TPU v7x, 32 devices: a whole 2x2x4 slice. The times are simulated.
32 devices in a mesh: dp: 4 (over z), seq: 4 (over y, core), mp: 2 (over x).
Axes of the slice: x: 2, y: 2, z: 4, core: 2. Of those that a mesh axis runs over, the one named last changes fastest.
Arguments:
- tokens: bfloat16 [8, 2048, 2048], P('dp', 'seq'), may hold values from -6 to 6
- lengths: int32 [8], P('dp'), may hold values from 102 to 2048, as said below
- qkv_weight: bfloat16 [3, 2048, 2048], P(None, ('dp', 'seq'), 'mp'), may hold values from -0.125 to 0.125
- out_weight: bfloat16 [2048, 2048], P('mp', ('dp', 'seq')), may hold values from -0.125 to 0.125
- in_weight: bfloat16 [2048, 8192], P(('dp', 'seq'), 'mp'), may hold values from -0.125 to 0.125
- down_weight: bfloat16 [8192, 2048], P('mp', ('dp', 'seq')), may hold values from -0.0625 to 0.0625
- gain_in: bfloat16 [2048], P(('dp', 'seq')), may hold values from 0.099609375 to 1.8984375
- gain_attn: bfloat16 [32, 64], P('mp', ('dp', 'seq')), may hold values from 0.099609375 to 1.8984375
- gain_mid: bfloat16 [2048], P(('dp', 'seq')), may hold values from 0.099609375 to 1.8984375
- gain_ffn: bfloat16 [128, 64], P('mp', ('dp', 'seq')), may hold values from 0.099609375 to 1.8984375
- out_grad: bfloat16 [8, 2048, 2048], P('dp', 'seq'), may hold values from -6 to 6
Outputs:
- result: bfloat16 [8, 2048, 2048], P('dp', 'seq')
- grad_input: bfloat16 [8, 2048, 2048], P('dp', 'seq')
- grad_qkv: float32 [3, 2048, 2048], P(None, ('dp', 'seq'), 'mp')
- grad_out: float32 [2048, 2048], P('mp', ('dp', 'seq'))
- grad_in: float32 [2048, 8192], P(('dp', 'seq'), 'mp')
- grad_down: float32 [8192, 2048], P('mp', ('dp', 'seq'))
- grad_gain_in: float32 [2048], P(('dp', 'seq'))
- grad_gain_attn: float32 [32, 64], P('mp', ('dp', 'seq'))
- grad_gain_mid: float32 [2048], P(('dp', 'seq'))
- grad_gain_ffn: float32 [128, 64], P('mp', ('dp', 'seq'))
Inputs may be any that keep to these rules, and one draw needn't show every extreme that they name: `lengths`: in each aligned group of 2 sequences (those of one index of dp) one sequence, drawn, has all 2048 tokens valid.
All inputs are finite; a program needn't handle non-finite values.
Results may differ from a plain program's by a relative error of at most 0.023.
Values may be sent and summed in bfloat16 or wider, within the bound.
No kernel may reach another device: no remote copies, remote signals or barrier semaphores. Data moves between devices by JAX's collectives and lax.ppermute only.
A program may use at most 512 MiB of HBM per device.

v0:
```python
from functools import partial

import jax
import jax.numpy as jnp
from jax import lax
from jax.sharding import PartitionSpec as P

D = 2048
HEAD_DIM = 64
FF = 8192
SEQ_LEN = 2048
XPOS_BASE = 512


EPSILON = 1e-05


def gather_attention(qkv_weight, out_weight, gain_in, gain_attn):
    return (
        lax.all_gather(qkv_weight, ("dp", "seq"), axis=1, tiled=True),
        lax.all_gather(out_weight, ("dp", "seq"), axis=1, tiled=True),
        lax.all_gather(gain_in, ("dp", "seq"), axis=0, tiled=True),
        lax.all_gather(gain_attn, ("dp", "seq"), axis=1, tiled=True),
    )


def gather_ffn(in_weight, down_weight, gain_mid, gain_ffn):
    return (
        lax.all_gather(in_weight, ("dp", "seq"), axis=0, tiled=True),
        lax.all_gather(down_weight, ("dp", "seq"), axis=1, tiled=True),
        lax.all_gather(gain_mid, ("dp", "seq"), axis=0, tiled=True),
        lax.all_gather(gain_ffn, ("dp", "seq"), axis=1, tiled=True),
    )


def gather_keys(keys_flat, values_flat):
    return (
        lax.all_gather(keys_flat, "seq", axis=1, tiled=True),
        lax.all_gather(values_flat, "seq", axis=1, tiled=True),
    )


def across_units(first_sum, second_sum):
    return lax.psum((first_sum, second_sum), "mp")


def unit_sum(terms):
    return lax.psum(terms.astype(jnp.bfloat16), "mp").astype(jnp.float32)


def full_norm(inputs, scales):
    row_mean = jnp.mean(inputs, axis=-1, keepdims=True)
    centered = inputs - row_mean
    row_var = jnp.mean(centered * centered, axis=-1, keepdims=True)
    inv_std = lax.rsqrt(row_var + EPSILON)
    normal = centered * inv_std
    return (normal * scales, normal, inv_std)


def full_norm_back(grad_out, normal, inv_std, scales):
    scaled = grad_out * scales
    grad_in = inv_std * (
        scaled
        - jnp.mean(scaled, axis=-1, keepdims=True)
        - normal * jnp.mean(scaled * normal, axis=-1, keepdims=True)
    )
    return (grad_in, jnp.sum(grad_out * normal, axis=0))


def split_norm(inputs, scales, full_width):
    moment_sums = across_units(jnp.sum(inputs, axis=-1), jnp.sum(inputs * inputs, axis=-1))
    row_mean = moment_sums[0][:, None] / full_width
    row_var = moment_sums[1][:, None] / full_width - row_mean * row_mean
    inv_std = lax.rsqrt(row_var + EPSILON)
    normal = (inputs - row_mean) * inv_std
    return (normal * scales, normal, inv_std)


def split_norm_back(grad_out, normal, inv_std, scales, full_width):
    scaled = grad_out * scales
    moment_sums = across_units(jnp.sum(scaled, axis=-1), jnp.sum(scaled * normal, axis=-1))
    grad_in = inv_std * (
        scaled
        - moment_sums[0][:, None] / full_width
        - normal * moment_sums[1][:, None] / full_width
    )
    return (grad_in, jnp.sum(grad_out * normal, axis=0))


def xpos_tables(positions):
    half_dim = HEAD_DIM // 2
    pair_index = jnp.arange(half_dim, dtype=jnp.float32)
    frequency = 1.0 / 10000.0 ** (2.0 * pair_index / HEAD_DIM)
    angles = positions[:, None] * frequency[None, :]
    base_ratio = (2.0 * pair_index + 0.4 * HEAD_DIM) / (1.4 * HEAD_DIM)
    growth = base_ratio[None, :] ** ((positions[:, None] - SEQ_LEN // 2) / XPOS_BASE)
    return (jnp.cos(angles), jnp.sin(angles), growth)


def rotate(tensor, cosine_table, sine_table, factor):
    half_dim = HEAD_DIM // 2
    cos_scaled = (cosine_table * factor)[:, None, :]
    sin_scaled = (sine_table * factor)[:, None, :]
    front_half = tensor[..., :half_dim]
    back_half = tensor[..., half_dim:]
    return jnp.concatenate(
        [
            front_half * cos_scaled - back_half * sin_scaled,
            back_half * cos_scaled + front_half * sin_scaled,
        ],
        axis=-1,
    )


def rotate_back(tensor, cosine_table, sine_table, factor):
    half_dim = HEAD_DIM // 2
    cos_scaled = (cosine_table * factor)[:, None, :]
    sin_scaled = (sine_table * factor)[:, None, :]
    front_half = tensor[..., :half_dim]
    back_half = tensor[..., half_dim:]
    return jnp.concatenate(
        [
            front_half * cos_scaled + back_half * sin_scaled,
            back_half * cos_scaled - front_half * sin_scaled,
        ],
        axis=-1,
    )


def allowed_keys(query_pos, key_count, length):
    key_pos = jnp.arange(key_count, dtype=jnp.int32)
    return (key_pos[None, :] <= query_pos[:, None]) & (key_pos[None, :] < length)


def softmax_parts(query_seq, key_seq, allowed):
    scores = (
        jnp.einsum("qhe,khe->hqk", query_seq, key_seq, preferred_element_type=jnp.float32) * 0.125
    )
    masked = jnp.where(allowed[None], scores, -1e30)
    row_max = jnp.max(masked, axis=-1, keepdims=True)
    exponent = jnp.where(allowed[None], jnp.exp(masked - row_max), 0.0)
    return (exponent, row_max)


def body(
    tokens,
    lengths,
    qkv_weight,
    out_weight,
    in_weight,
    down_weight,
    gain_in,
    gain_attn,
    gain_mid,
    gain_ffn,
    out_grad,
):
    seq_count, span_len, model_width = tokens.shape
    row_count = seq_count * span_len
    qkv_full, out_full, gain_one, gain_two = gather_attention(
        qkv_weight, out_weight, gain_in, gain_attn
    )
    local_width = qkv_full.shape[2]
    heads_here = local_width // HEAD_DIM
    gain_two_flat = gain_two.reshape(local_width)
    inputs = tokens.reshape(row_count, model_width).astype(jnp.float32)
    normed_one, plain_one, std_one = full_norm(inputs, gain_one)
    normed_low = normed_one.astype(jnp.bfloat16)
    projected = jnp.einsum("td,jde->jte", normed_low, qkv_full, preferred_element_type=jnp.float32)
    shaped = projected.reshape(3, seq_count, span_len, heads_here, HEAD_DIM)
    query_pos = lax.axis_index("seq") * span_len + jnp.arange(span_len, dtype=jnp.int32)
    cosine_table, sine_table, growth = xpos_tables(query_pos.astype(jnp.float32))
    inverse_growth = 1.0 / growth
    queries = rotate(shaped[0], cosine_table, sine_table, growth).astype(jnp.bfloat16)
    keys_here = rotate(shaped[1], cosine_table, sine_table, inverse_growth).astype(jnp.bfloat16)
    values_here = shaped[2].astype(jnp.bfloat16)
    keys_flat = keys_here.reshape(seq_count, span_len, local_width)
    values_flat = values_here.reshape(seq_count, span_len, local_width)
    keys_all, values_all = gather_keys(keys_flat, values_flat)
    key_count = keys_all.shape[1]

    def attend(operands):
        query_seq, key_seq, value_seq, length = operands
        key_seq = key_seq.reshape(key_count, heads_here, HEAD_DIM)
        value_seq = value_seq.reshape(key_count, heads_here, HEAD_DIM)
        allowed = allowed_keys(query_pos, key_count, length)
        exponent, row_max = softmax_parts(query_seq, key_seq, allowed)
        row_total = jnp.sum(exponent, axis=-1, keepdims=True)
        attn_probs = (exponent / row_total).astype(jnp.bfloat16)
        output = jnp.einsum(
            "hqk,khe->qhe", attn_probs, value_seq, preferred_element_type=jnp.float32
        )
        return (output, row_max, row_total)

    mixed_out, row_maxes, row_totals = lax.map(attend, (queries, keys_all, values_all, lengths))
    attended = mixed_out.reshape(row_count, local_width)
    normed_two, plain_two, std_two = split_norm(attended, gain_two_flat, D)
    normed_two_low = normed_two.astype(jnp.bfloat16)
    branch_attn = jnp.dot(normed_two_low, out_full, preferred_element_type=jnp.float32)
    hidden = inputs + unit_sum(branch_attn)
    in_full, down_full, gain_three, gain_four = gather_ffn(
        in_weight, down_weight, gain_mid, gain_ffn
    )
    ffn_width = in_full.shape[1]
    gain_four_flat = gain_four.reshape(ffn_width)
    normed_three, plain_three, std_three = full_norm(hidden, gain_three)
    normed_three_low = normed_three.astype(jnp.bfloat16)
    pre_act = jnp.dot(normed_three_low, in_full, preferred_element_type=jnp.float32)
    activated, gelu_back = jax.vjp(partial(jax.nn.gelu, approximate=False), pre_act)
    normed_four, plain_four, std_four = split_norm(activated, gain_four_flat, FF)
    normed_four_low = normed_four.astype(jnp.bfloat16)
    branch_ffn = jnp.dot(normed_four_low, down_full, preferred_element_type=jnp.float32)
    result_low = (hidden + unit_sum(branch_ffn)).astype(jnp.bfloat16)
    grad_out_low = out_grad.reshape(row_count, model_width)
    in_full, down_full, gain_three, gain_four = gather_ffn(
        in_weight, down_weight, gain_mid, gain_ffn
    )
    gain_four_flat = gain_four.reshape(ffn_width)
    grad_down_w = jnp.einsum(
        "tf,td->fd", normed_four_low, grad_out_low, preferred_element_type=jnp.float32
    )
    grad_wide = jnp.einsum("td,fd->tf", grad_out_low, down_full, preferred_element_type=jnp.float32)
    grad_act, grad_gain_four = split_norm_back(grad_wide, plain_four, std_four, gain_four_flat, FF)
    grad_pre_low = gelu_back(grad_act)[0].astype(jnp.bfloat16)
    grad_in_w = jnp.einsum(
        "td,tf->df", normed_three_low, grad_pre_low, preferred_element_type=jnp.float32
    )
    ffn_back_terms = jnp.einsum(
        "tf,df->td", grad_pre_low, in_full, preferred_element_type=jnp.float32
    )
    grad_normed_three = unit_sum(ffn_back_terms)
    grad_base = grad_out_low.astype(jnp.float32)
    grad_hidden_norm, grad_gain_three = full_norm_back(
        grad_normed_three, plain_three, std_three, gain_three
    )
    grad_hidden = grad_base + grad_hidden_norm
    grad_hidden_low = grad_hidden.astype(jnp.bfloat16)
    gain_four_grad = grad_gain_four.reshape(ffn_width // HEAD_DIM, HEAD_DIM)
    ffn_summed = (
        lax.psum_scatter(
            grad_in_w.astype(jnp.bfloat16), ("dp", "seq"), scatter_dimension=0, tiled=True
        ).astype(jnp.float32),
        lax.psum_scatter(
            grad_down_w.astype(jnp.bfloat16), ("dp", "seq"), scatter_dimension=1, tiled=True
        ).astype(jnp.float32),
        lax.psum_scatter(
            grad_gain_three.astype(jnp.bfloat16), ("dp", "seq"), scatter_dimension=0, tiled=True
        ).astype(jnp.float32),
        lax.psum_scatter(
            gain_four_grad.astype(jnp.bfloat16), ("dp", "seq"), scatter_dimension=1, tiled=True
        ).astype(jnp.float32),
    )
    qkv_full, out_full, gain_one, gain_two = gather_attention(
        qkv_weight, out_weight, gain_in, gain_attn
    )
    gain_two_flat = gain_two.reshape(local_width)
    keys_all, values_all = gather_keys(keys_flat, values_flat)
    grad_out_w = jnp.einsum(
        "te,td->ed", normed_two_low, grad_hidden_low, preferred_element_type=jnp.float32
    )
    grad_inner = jnp.einsum(
        "td,ed->te", grad_hidden_low, out_full, preferred_element_type=jnp.float32
    )
    grad_attended, grad_gain_two = split_norm_back(grad_inner, plain_two, std_two, gain_two_flat, D)
    grad_mixed = grad_attended.astype(jnp.bfloat16).reshape(
        seq_count, span_len, heads_here, HEAD_DIM
    )

    def attend_back(operands):
        query_seq, key_seq, value_seq, length, row_max, row_total, grad_seq = operands
        key_seq = key_seq.reshape(key_count, heads_here, HEAD_DIM)
        value_seq = value_seq.reshape(key_count, heads_here, HEAD_DIM)
        allowed = allowed_keys(query_pos, key_count, length)
        scores = (
            jnp.einsum("qhe,khe->hqk", query_seq, key_seq, preferred_element_type=jnp.float32)
            * 0.125
        )
        masked = jnp.where(allowed[None], scores, -1e30)
        exponent = jnp.where(allowed[None], jnp.exp(masked - row_max), 0.0)
        attn_probs = exponent / row_total
        probs_low = attn_probs.astype(jnp.bfloat16)
        grad_probs = jnp.einsum(
            "qhe,khe->hqk", grad_seq, value_seq, preferred_element_type=jnp.float32
        )
        inner_sum = jnp.sum(attn_probs * grad_probs, axis=-1, keepdims=True)
        grad_scores = (attn_probs * (grad_probs - inner_sum)).astype(jnp.bfloat16)
        grad_query = (
            jnp.einsum("hqk,khe->qhe", grad_scores, key_seq, preferred_element_type=jnp.float32)
            * 0.125
        )
        grad_key = (
            jnp.einsum("hqk,qhe->khe", grad_scores, query_seq, preferred_element_type=jnp.float32)
            * 0.125
        )
        grad_value = jnp.einsum(
            "hqk,qhe->khe", probs_low, grad_seq, preferred_element_type=jnp.float32
        )
        return (
            grad_query,
            grad_key.reshape(key_count, local_width),
            grad_value.reshape(key_count, local_width),
        )

    grad_queries, grad_keys_all, grad_values_all = lax.map(
        attend_back, (queries, keys_all, values_all, lengths, row_maxes, row_totals, grad_mixed)
    )
    grad_keys_here, grad_values_here = (
        lax.psum_scatter(
            grad_keys_all.astype(jnp.bfloat16), "seq", scatter_dimension=1, tiled=True
        ).astype(jnp.float32),
        lax.psum_scatter(
            grad_values_all.astype(jnp.bfloat16), "seq", scatter_dimension=1, tiled=True
        ).astype(jnp.float32),
    )
    grad_keys_here = grad_keys_here.reshape(seq_count, span_len, heads_here, HEAD_DIM)
    grad_q_low = rotate_back(grad_queries, cosine_table, sine_table, growth).astype(jnp.bfloat16)
    grad_k_low = rotate_back(grad_keys_here, cosine_table, sine_table, inverse_growth).astype(
        jnp.bfloat16
    )
    grad_v_low = grad_values_here.astype(jnp.bfloat16)
    stacked = jnp.stack(
        [
            grad_q_low.reshape(row_count, local_width),
            grad_k_low.reshape(row_count, local_width),
            grad_v_low.reshape(row_count, local_width),
        ]
    )
    grad_qkv_w = jnp.einsum("td,jte->jde", normed_low, stacked, preferred_element_type=jnp.float32)
    attn_back_terms = jnp.einsum(
        "jte,jde->td", stacked, qkv_full, preferred_element_type=jnp.float32
    )
    grad_normed_one = unit_sum(attn_back_terms)
    grad_first, grad_gain_one = full_norm_back(grad_normed_one, plain_one, std_one, gain_one)
    grad_input = (grad_hidden + grad_first).astype(jnp.bfloat16)
    gain_two_grad = grad_gain_two.reshape(heads_here, HEAD_DIM)
    attn_summed = (
        lax.psum_scatter(
            grad_qkv_w.astype(jnp.bfloat16), ("dp", "seq"), scatter_dimension=1, tiled=True
        ).astype(jnp.float32),
        lax.psum_scatter(
            grad_out_w.astype(jnp.bfloat16), ("dp", "seq"), scatter_dimension=1, tiled=True
        ).astype(jnp.float32),
        lax.psum_scatter(
            grad_gain_one.astype(jnp.bfloat16), ("dp", "seq"), scatter_dimension=0, tiled=True
        ).astype(jnp.float32),
        lax.psum_scatter(
            gain_two_grad.astype(jnp.bfloat16), ("dp", "seq"), scatter_dimension=1, tiled=True
        ).astype(jnp.float32),
    )
    return (
        result_low.reshape(seq_count, span_len, model_width),
        grad_input.reshape(seq_count, span_len, model_width),
        attn_summed[0],
        attn_summed[1],
        ffn_summed[0],
        ffn_summed[1],
        attn_summed[2],
        attn_summed[3],
        ffn_summed[2],
        ffn_summed[3],
    )


def solution(mesh):
    in_specs = (
        P("dp", "seq", None),
        P("dp"),
        P(None, ("dp", "seq"), "mp"),
        P("mp", ("dp", "seq")),
        P(("dp", "seq"), "mp"),
        P("mp", ("dp", "seq")),
        P(("dp", "seq")),
        P("mp", ("dp", "seq")),
        P(("dp", "seq")),
        P("mp", ("dp", "seq")),
        P("dp", "seq", None),
    )
    out_specs = (
        P("dp", "seq", None),
        P("dp", "seq", None),
        P(None, ("dp", "seq"), "mp"),
        P("mp", ("dp", "seq")),
        P(("dp", "seq"), "mp"),
        P("mp", ("dp", "seq")),
        P(("dp", "seq")),
        P("mp", ("dp", "seq")),
        P(("dp", "seq")),
        P("mp", ("dp", "seq")),
    )
    return jax.shard_map(body, mesh=mesh, in_specs=in_specs, out_specs=out_specs, check_vma=False)
```

profile of v0, /device:TPU:0, one launch (start us, length us, event | category | flops | bytes accessed | tf_op | source)
XLA Modules:
  0.0 2468.1 jit_solution(1435643085086097799)
XLA Ops:
  14.4 23.3 all-gather
  41.3 72.5 %all-gather.11.cloned.1.call-done = bf16[3,2048,1024]{2,1,0:T(8,128)(2,1)} async-done(((bf16[3,128,1024]{2,1,0:T(8,128)(2,1)}), bf16[3,2048,1024]{2,1,0:T(8,128)(2,1)}) %all-gather.11.cloned.1.call-update) | async-done | bytes 12582928 | tf_op jit(solution)/shard_map/all_gather | solution.py:20
  113.8 17.0 convolution_bitcast_fusion
  139.3 9.7 fusion.74
  149.0 5.4 copy.57
  154.4 6.6 squeeze.33
  169.9 18.3 all-gather.1
  189.0 5.4 copy.56
  194.3 6.6 squeeze.32
  208.0 47.4 %all-gather.15.cloned.1.call-done = bf16[2,2048,1024]{1,2,0:T(8,128)(2,1)} async-done(((bf16[2,512,1024]{1,2,0:T(8,128)(2,1)}), bf16[2,2048,1024]{1,2,0:T(8,128)(2,1)}) %all-gather.15.cloned.1.call-update) | async-done | bytes 8388624 | tf_op jit(solution)/shard_map/all_gather | solution.py:38
  255.4 165.1 %while.30 = (s32[]{:T(128)}, f32[2,512,16,64]{1,3,2,0:T(8,128)}, f32[2,16,512,1]{2,1,3,0:T(8,128)S(1)}, f32[2,16,512,1]{2,1,3,0:T(8,128)S(1)}, bf16[2,2048,1024]...) while((s32[]{:T(128)}, f32[2,512,16,64]{1,3,2,0:T(8,128)}, ...), condition=%wide.region_5.6_spmd.clone, body=%wide.region_2.5_spmd.clone.sunk | while | flops 4531931648 | bytes 267690160 | solution.py:195
  262.8 24.3 fusion.116
  287.1 22.3 fusion.117
  309.4 28.8 %bitcast_dynamic-update-slice_fusion.5 = f32[2,512,16,64]{1,3,2,0:T(8,128)} fusion(f32[2,512,16,64]{1,3,2,0:T(8,128)} %get-tuple-element.535, s32[]{:T(128)S(6)} %copy.124, bf16[2048,16,64]{0,2,1:T(8,128)(2,1)} %bitcast.221, f32[16,512,2048]{2,1,0:T(8,128)} %get-tuple-element.502, f32[16,512]{1,0:T(8,128)S(1)} %fusion.117, ...), kind=kOutput, calls=%fused_computation.10.clone.1 | convolution fusion | flops 2248146944 | bytes 74514432 | tf_op jit(solution)/shard_map/while/body/eval_jaxpr/hqk,khe->qhe/dot_general | solution.py:190
  345.4 23.8 fusion.116
  369.2 22.1 fusion.117
  391.3 28.8 %bitcast_dynamic-update-slice_fusion.5 = f32[2,512,16,64]{1,3,2,0:T(8,128)} fusion(f32[2,512,16,64]{1,3,2,0:T(8,128)} %get-tuple-element.535, s32[]{:T(128)S(6)} %copy.124, bf16[2048,16,64]{0,2,1:T(8,128)(2,1)} %bitcast.221, f32[16,512,2048]{2,1,0:T(8,128)} %get-tuple-element.502, f32[16,512]{1,0:T(8,128)S(1)} %fusion.117, ...), kind=kOutput, calls=%fused_computation.10.clone.1 | convolution fusion | flops 2248146944 | bytes 74514432 | tf_op jit(solution)/shard_map/while/body/eval_jaxpr/hqk,khe->qhe/dot_general | solution.py:190
  420.6 6.3 copy.60
  435.6 10.3 convolution_convert_fusion.5
  447.3 20.4 all-gather.2
  467.8 17.4 all-gather.3
  485.9 68.1 %all-reduce.14.cloned.1.call-done = bf16[1024,2048]{1,0:T(8,128)(2,1)} async-done(((bf16[1024,2048]{1,0:T(8,128)(2,1)}), bf16[1024,2048]{1,0:T(8,128)(2,1)}) %all-reduce.14.cloned.1.call-update) | async-done | bytes 4194320 | tf_op jit(solution)/shard_map/psum | solution.py:48
  567.1 116.1 %all-gather.19.cloned.1.call-done = bf16[2048,4096]{1,0:T(8,128)(2,1)} async-done(((bf16[128,4096]{1,0:T(8,128)(2,1)}), bf16[2048,4096]{1,0:T(8,128)(2,1)}) %all-gather.19.cloned.1.call-update) | async-done | bytes 16777232 | tf_op jit(solution)/shard_map/all_gather | solution.py:29
  683.2 60.8 %fusion.71 = (f32[1024]{0:T(1024)S(1)}, f32[1024]{0:T(1024)S(1)}, f32[1024,4096]{1,0:T(8,128)}, f32[1024,4096]{1,0:T(8,128)}, f32[1024,4096]{1,0:T(8,128)}) fusion(bf16[2048,4096]{1,0:T(8,128)(2,1)} %all-gather.19.cloned.1.call-done, f32[1024,2048]{1,0:T(8,128)} %subtract_multiply_fusion.1, f32[2048]{0:T(1024)S(1)} %bitcast.247), kind=kOutput, calls=%fused_computation.181 | convolution fusion | flops 17465081856 | bytes 75513856 | tf_op jit(solution)/shard_map/dot_general | solution.py:208
  749.0 65.2 %all-gather.21.cloned.1.call-done = bf16[4096,2048]{1,0:T(8,128)(2,1)} async-done(((bf16[4096,128]{1,0:T(8,128)(2,1)}), bf16[4096,2048]{1,0:T(8,128)(2,1)}) %all-gather.21.cloned.1.call-update) | async-done | bytes 16777232 | tf_op jit(solution)/shard_map/all_gather | solution.py:30
  814.2 27.3 %multiply_reduce_fusion.1 = (bf16[4096]{0:T(1024)(128)(2,1)}, f32[1024]{0:T(1024)S(1)}, f32[1024]{0:T(1024)S(1)}, f32[1024,4096]{1,0:T(8,128)}) fusion(f32[1024,4096]{1,0:T(8,128)} %get-tuple-element.333, f32[1024]{0:T(1024)S(1)} %get-tuple-element.362, f32[1024]{0:T(1024)S(1)} %get-tuple-element.361, f32[4096]{0:T(1024)S(1)} %copy-done.38, ...), kind=kOutput, calls=%fused_computation.56 | convolution fusion | flops 17213419520 | bytes 54566912 | tf_op jit(solution)/shard_map/td,fd->tf/dot_general | solution.py:222
  846.5 23.7 add_convert_fusion
  873.4 21.3 convolution_convert_fusion.2
  894.8 106.1 %all-reduce.16.cloned.1.call-done = bf16[1024,2048]{1,0:T(8,128)(2,1)} async-done(((bf16[1024,2048]{1,0:T(8,128)(2,1)}), bf16[1024,2048]{1,0:T(8,128)(2,1)}) %all-reduce.16.cloned.1.call-update) | async-done | bytes 4194320 | tf_op jit(solution)/shard_map/psum | solution.py:48
  1000.9 7.3 fusion.47
  1008.3 5.2 fusion.45
  1014.2 7.3 multiply_reduce_fusion.6
  1036.0 493.1 %while.31 = (s32[]{:T(128)}, f32[2,512,16,64]{1,0,3,2:T(2,128)}, bf16[2,2048,1024]{1,2,0:T(8,128)(2,1)}, bf16[2,2048,1024]{1,2,0:T(8,128)(2,1)}, bf16[2,2048,102...) while((s32[]{:T(128)}, f32[2,512,16,64]{1,0,3,2:T(2,128)}, ...), condition=%wide.region_31.32_spmd.clone, body=%wide.region_29.31_spmd.clone.sunk | while | flops 10928777216 | bytes 641999104 | solution.py:304
  1044.0 23.1 fusion.127
  1067.1 53.6 %multiply_reduce_fusion.11 = (f32[16,512]{1,0:T(8,128)S(1)}, f32[16,512,2048]{2,1,0:T(8,128)}) fusion(f32[16,512,2048]{2,1,0:T(8,128)} %fusion.127, f32[16,512]{1,0:T(8,128)S(1)} %get-tuple-element.520, f32[16,512]{1,0:T(8,128)S(1)} %get-tuple-element.521, bf16[2048,16,64]{0,2,1:T(8,128)(2,1)S(1)} %bitcast.218, ...), kind=kOutput, calls=%fused_computation.25.clone.2 | convolution fusion | flops 2264915968 | bytes 140607488 | tf_op jit(solution)/shard_map/while/body/eval_jaxpr/qhe,khe->hqk/dot_general | solution.py:275
  1120.7 52.8 %multiply_convert_fusion.12 = bf16[16,512,2048]{2,1,0:T(8,128)(2,1)} fusion(f32[16,512,2048]{2,1,0:T(8,128)} %get-tuple-element.522, f32[16,512,2048]{2,1,0:T(8,128)} %fusion.127, f32[16,512]{1,0:T(8,128)S(1)} %get-tuple-element.523), kind=kLoop, calls=%fused_computation.24.clone.1 | loop fusion | flops 50331648 | bytes 167804928 | tf_op jit(solution)/shard_map/while/body/eval_jaxpr/convert_element_type | solution.py:286
  1173.5 24.2 fusion.129
  1197.7 17.2 multiply_bitcast_fusion.2
  1214.9 18.8 broadcast_multiply_fusion.12
  1237.3 38.0 %dynamic_update_slice.41 = f32[2,512,16,64]{1,0,3,2:T(2,128)} dynamic-update-slice(f32[2,512,16,64]{1,0,3,2:T(2,128)} %get-tuple-element.569, f32[1,512,16,64]{1,0,3,2:T(1,128)} %copy.113, s32[]{:T(128)S(6)} %copy.138, s32[]{:T(128)} %constant.50.clone.1..sunk, s32[]{:T(128)} %constant.50.clone.1..sunk, s32[]{:T(128)} %constant.50.clone.1..sunk) | dynamic-update-slice | bytes 4194308 | tf_op jit(solution)/shard_map/while/body/jit(dynamic_update_index_in_dim)/dynamic_update_slice | solution.py:195
  1290.3 23.1 fusion.127
  1313.4 53.6 %multiply_reduce_fusion.11 = (f32[16,512]{1,0:T(8,128)S(1)}, f32[16,512,2048]{2,1,0:T(8,128)}) fusion(f32[16,512,2048]{2,1,0:T(8,128)} %fusion.127, f32[16,512]{1,0:T(8,128)S(1)} %get-tuple-element.520, f32[16,512]{1,0:T(8,128)S(1)} %get-tuple-element.521, bf16[2048,16,64]{0,2,1:T(8,128)(2,1)S(1)} %bitcast.218, ...), kind=kOutput, calls=%fused_computation.25.clone.2 | convolution fusion | flops 2264915968 | bytes 140607488 | tf_op jit(solution)/shard_map/while/body/eval_jaxpr/qhe,khe->hqk/dot_general | solution.py:275
  1367.0 52.8 %multiply_convert_fusion.12 = bf16[16,512,2048]{2,1,0:T(8,128)(2,1)} fusion(f32[16,512,2048]{2,1,0:T(8,128)} %get-tuple-element.522, f32[16,512,2048]{2,1,0:T(8,128)} %fusion.127, f32[16,512]{1,0:T(8,128)S(1)} %get-tuple-element.523), kind=kLoop, calls=%fused_computation.24.clone.1 | loop fusion | flops 50331648 | bytes 167804928 | tf_op jit(solution)/shard_map/while/body/eval_jaxpr/convert_element_type | solution.py:286
  1419.8 24.2 fusion.129
  1444.0 17.2 multiply_bitcast_fusion.2
  1461.2 18.8 broadcast_multiply_fusion.12
  1483.5 38.0 %dynamic_update_slice.41 = f32[2,512,16,64]{1,0,3,2:T(2,128)} dynamic-update-slice(f32[2,512,16,64]{1,0,3,2:T(2,128)} %get-tuple-element.569, f32[1,512,16,64]{1,0,3,2:T(1,128)} %copy.113, s32[]{:T(128)S(6)} %copy.138, s32[]{:T(128)} %constant.50.clone.1..sunk, s32[]{:T(128)} %constant.50.clone.1..sunk, s32[]{:T(128)} %constant.50.clone.1..sunk) | dynamic-update-slice | bytes 4194308 | tf_op jit(solution)/shard_map/while/body/jit(dynamic_update_index_in_dim)/dynamic_update_slice | solution.py:195
  1529.8 11.7 convolution_convert_fusion.4
  1541.5 6.7 copy.78
  1548.3 26.8 %convolution_convert_fusion = bf16[4096,2048]{1,0:T(8,128)(2,1)} fusion(bf16[1024,2048]{1,0:T(8,128)(2,1)} %bitcast.238, f32[1024,4096]{1,0:T(8,128)} %get-tuple-element.333, f32[4096]{0:T(1024)S(1)} %copy-done.39, f32[1024]{0:T(1024)S(1)} %copy-done.55, f32[1024]{0:T(1024)S(1)} %copy-done.53), kind=kOutput, calls=%fused_computation.76 | convolution fusion | flops 17205035008 | bytes 37773312 | tf_op jit(solution)/shard_map/tf,td->fd/dot_general | solution.py:219
  1575.1 20.7 copy.80
  1596.6 26.0 %convolution_convert_fusion.1 = bf16[2048,4096]{1,0:T(8,128)(2,1)} fusion(bf16[1024,4096]{1,0:T(8,128)(2,1)} %copy-done.16, f32[1024,2048]{1,0:T(8,128)} %subtract_multiply_fusion.1, f32[2048]{0:T(1024)S(1)} %bitcast.250), kind=kOutput, calls=%fused_computation.77 | convolution fusion | flops 17192452096 | bytes 33562624 | tf_op jit(solution)/shard_map/td,tf->df/dot_general | solution.py:225
  1622.7 27.3 %convolution_convert_fusion.3 = bf16[1024,2048]{1,0:T(8,128)(2,1)} fusion(bf16[4096,2048]{1,0:T(8,128)(2,1)} %all-gather.21.cloned.1.call-done, f32[1024,4096]{1,0:T(8,128)} %get-tuple-element.333, f32[4096]{0:T(1024)S(1)} %copy-done.39, f32[1024]{0:T(1024)S(1)} %copy-done.55, f32[1024]{0:T(1024)S(1)} %copy-done.53), kind=kOutput, calls=%fused_computation.129 | convolution fusion | flops 17198743552 | bytes 37773312 | tf_op jit(solution)/shard_map/dot_general | solution.py:212
  1681.6 18.9 bitcast_convert_fusion
  1700.6 19.2 convert_bitcast_fusion
  1719.7 27.7 %copy.76 = bf16[3,2048,1024]{2,0,1:T(4,128)(2,1)} copy(bf16[3,2048,1024]{1,2,0:T(8,128)(2,1)} %convert_bitcast_fusion) | data formatting | bytes 25165824
  1747.4 15.8 copy.111
  1767.9 165.9 %reduce-scatter.25.cloned.1.call-done = bf16[128,4096]{1,0:T(8,128)(2,1)} async-done(((bf16[2048,4096]{1,0:T(8,128)(2,1)}), bf16[128,4096]{1,0:T(8,128)(2,1)}) %reduce-scatter.25.cloned.1.call-update) | async-done | bytes 1048592
  1936.9 179.2 %reduce-scatter.19.cloned.1.call-done = bf16[128,4096]{1,0:T(8,128)(2,1)} async-done(((bf16[2048,4096]{1,0:T(8,128)(2,1)}), bf16[128,4096]{1,0:T(8,128)(2,1)}) %reduce-scatter.19.cloned.1.call-update) | async-done | bytes 1048592 | tf_op jit(solution)/shard_map/reduce_scatter | solution.py:240
  2118.8 197.9 %all-reduce.18.cloned.1.call-done = (bf16[1024,2048]{1,0:T(8,128)(2,1)}, bf16[1024,2048]{1,0:T(8,128)(2,1)}) async-done(((bf16[1024,2048]{1,0:T(8,128)(2,1)}, bf16[1024,2048]{1,0:T(8,128)(2,1)}), (bf16[1024,2048]{1,0:T(8,128)(2,1)}, bf16[1024,2048]{1,0:T(8,128)(2,1)})) %all-reduce.18.cloned.1.call-update) | async-done | bytes 8388624 | tf_op jit(solution)/shard_map/psum | solution.py:48
  2316.7 6.0 fusion.53
  2322.7 63.0 %all-reduce.8 = (bf16[2048]{0:T(1024)(128)(2,1)S(1)}, bf16[16,64]{1,0:T(8,128)(2,1)S(1)}, bf16[2048]{0:T(1024)(128)(2,1)S(1)}, bf16[64,64]{1,0:T(8,128)(2,1)S(1)}) all-reduce(bf16[2048]{0:T(1024)(128)(2,1)S(1)} %get-tuple-element.270, ...), channel_id=8, replica_groups=mesh['dp'=4,'seq'=4,'mp'=2] {'dp','seq'}, use_global_device_ids=true, to_apply=%region_42.43.clone | all-reduce | flops 9216 | bytes 36864
  2388.3 13.7 fusion.51
  2402.0 54.4 %reduce-scatter.21.cloned.1.call-done = bf16[128,3072]{1,0:T(8,128)(2,1)} async-done(((bf16[2048,3072]{1,0:T(8,128)(2,1)}), bf16[128,3072]{1,0:T(8,128)(2,1)}) %reduce-scatter.21.cloned.1.call-update) | async-done | bytes 786448
  (293 shorter events, 189.0 us)
Async XLA Ops:
  7.2 7.2 copy-start.60
  7.2 106.6 %all-gather.11.cloned.1.call-start = ((), (), s32[]{:S(2)}) async-start(), calls=%async_computation.6 | async-start | bytes 13369344 | tf_op jit(solution)/shard_map/all_gather | solution.py:20
  7.9 200.0 %all-gather.13.cloned.1.call-start = ((), (), s32[]{:S(2)}) async-start(), calls=%async_computation.7 | async-start | bytes 10485760 | tf_op jit(solution)/shard_map/all_gather | solution.py:39
  8.0 30.4 %copy-start.2 = (bf16[2,512,2048]{2,1,0:T(8,128)(2,1)S(1)}, bf16[2,512,2048]{2,1,0:T(8,128)(2,1)}, u32[]{:S(2)}) copy-start(bf16[2,512,2048]{2,1,0:T(8,128)(2,1)} %param.15) | copy-start | bytes 12582916
  11.0 26.8 %copy-start.34 = (f32[1,4,2,128]{3,1,2,0:T(4,128)}, f32[1,4,2,128]{3,1,2,0:T(4,128)S(1)}, u32[]{:S(2)}) copy-start(f32[1,4,2,128]{3,1,2,0:T(4,128)S(1)} %copy.106) | copy-start | bytes 12292
  14.4 23.4 copy-start.36
  138.1 117.2 %all-gather.15.cloned.1.call-start = ((), (), s32[]{:S(2)}) async-start(), calls=%async_computation.8 | async-start | bytes 10485760 | tf_op jit(solution)/shard_map/all_gather | solution.py:38
  139.2 21.8 copy-start.20
  139.2 21.8 copy-start.22
  139.2 61.7 %copy-start.24 = (f32[512,32]{0,1:T(8,128)}, f32[512,32]{0,1:T(8,128)S(1)}, u32[]{:S(2)}) copy-start(f32[512,32]{0,1:T(8,128)S(1)} %get-tuple-element.367) | copy-start | bytes 196612
  139.3 61.7 %copy-start.26 = (f32[512,32]{0,1:T(8,128)}, f32[512,32]{0,1:T(8,128)S(1)}, u32[]{:S(2)}) copy-start(f32[512,32]{0,1:T(8,128)S(1)} %get-tuple-element.368) | copy-start | bytes 196612
  161.1 8.9 copy-start.58
  169.3 266.3 %all-gather.17.cloned.1.call-start = ((), (), s32[]{:S(2)}) async-start(), calls=%async_computation.9 | async-start | bytes 4456448 | tf_op jit(solution)/shard_map/all_gather | solution.py:21
  169.9 384.2 %all-reduce.14.cloned.1.call-start = ((), (), s32[]{:S(2)}) async-start(), calls=%async_computation.10 | async-start | bytes 8388608 | tf_op jit(solution)/shard_map/psum | solution.py:48
  200.9 54.5 %copy-start.63 = (s32[2]{0:T(128)S(1)}, s32[2]{0:T(128)}, u32[]{:S(2)}) copy-start(s32[2]{0:T(128)} %param.16) | copy-start | bytes 28
  420.5 9.3 copy-start.8
  420.6 9.3 copy-start.28
  420.6 9.3 copy-start.29
  420.6 9.3 copy-start.13
  426.9 8.7 copy-start.42
  435.5 10.3 copy-start.46
  435.5 10.3 copy-start.49
  435.6 11.7 copy-start.61
  435.6 32.2 %copy-start.59 = (bf16[64,4]{0,1:T(4,128)(2,1)S(1)}, bf16[64,4]{0,1:T(4,128)(2,1)}, u32[]{:S(2)}) copy-start(bf16[64,4]{0,1:T(4,128)(2,1)} %param.24) | copy-start | bytes 1540
  445.9 237.3 %all-gather.19.cloned.1.call-start = ((), (), s32[]{:S(2)}) async-start(), calls=%async_computation.11 | async-start | bytes 17825792 | tf_op jit(solution)/shard_map/all_gather | solution.py:29
  446.5 367.7 %all-gather.21.cloned.1.call-start = ((), (), s32[]{:S(2)}) async-start(), calls=%async_computation.12 | async-start | bytes 17825792 | tf_op jit(solution)/shard_map/all_gather | solution.py:30
  447.2 553.7 %all-reduce.16.cloned.1.call-start = ((), (), s32[]{:S(2)}) async-start(), calls=%async_computation.13 | async-start | bytes 8388608 | tf_op jit(solution)/shard_map/psum | solution.py:48
  467.7 540.5 %copy-start.32 = (f32[16,1,128]{2,1,0:T(1,128)}, f32[16,1,128]{2,1,0:T(1,128)S(1)}, u32[]{:S(2)}) copy-start(f32[16,1,128]{2,1,0:T(1,128)S(1)} %convert_element_type.271) | copy-start | bytes 24580
  683.2 130.9 %copy-start.38 = (f32[4096]{0:T(1024)S(1)}, f32[4096]{0:T(1024)}, u32[]{:S(2)}) copy-start(f32[4096]{0:T(1024)} %reshape.535) | copy-start | bytes 49156
  749.0 97.5 %copy-start.52 = (f32[1024]{0:T(1024)}, f32[1024]{0:T(1024)S(1)}, u32[]{:S(2)}) copy-start(f32[1024]{0:T(1024)S(1)} %get-tuple-element.361) | copy-start | bytes 12292
  749.0 97.5 %copy-start.54 = (f32[1024]{0:T(1024)}, f32[1024]{0:T(1024)S(1)}, u32[]{:S(2)}) copy-start(f32[1024]{0:T(1024)S(1)} %get-tuple-element.362) | copy-start | bytes 12292
  894.7 113.5 %copy-start.41 = (f32[1024]{0:T(1024)S(1)}, f32[1024]{0:T(1024)}, u32[]{:S(2)}) copy-start(f32[1024]{0:T(1024)} %copy-done.40) | copy-start | bytes 12292
  894.7 767.0 %reduce-scatter.15.cloned.1.call-start = ((), (), s32[]{:S(2)}) async-start(), calls=%async_computation.14 | async-start | bytes 10485760 | tf_op jit(solution)/shard_map/reduce_scatter | solution.py:308
  1000.9 7.3 copy-start.14
  1000.9 7.3 copy-start.18
  1014.2 7.3 copy-start.11
  1036.2 7.8 copy-start.5
  1044.0 23.2 copy-start
  1044.0 23.1 copy-start.9
  1120.7 52.8 %copy-start.6 = (bf16[2,512,16,64]{1,3,2,0:T(8,128)(2,1)S(1)}, bf16[2,512,16,64]{1,3,2,0:T(8,128)(2,1)}, u32[]{:S(2)}) copy-start(bf16[2,512,16,64]{1,3,2,0:T(8,128)(2,1)} %copy-done.5) | copy-start | bytes 6291460 | tf_op jit(solution)/shard_map/while
  1275.2 7.2 copy-start.7
  1282.5 7.8 copy-start.5
  1290.2 23.2 copy-start
  1290.3 23.1 copy-start.9
  1367.0 52.8 %copy-start.6 = (bf16[2,512,16,64]{1,3,2,0:T(8,128)(2,1)S(1)}, bf16[2,512,16,64]{1,3,2,0:T(8,128)(2,1)}, u32[]{:S(2)}) copy-start(bf16[2,512,16,64]{1,3,2,0:T(8,128)(2,1)} %copy-done.5) | copy-start | bytes 6291460 | tf_op jit(solution)/shard_map/while
  1521.5 7.1 copy-start.7
  1529.1 148.6 %reduce-scatter.17.cloned.1.call-start = ((), (), s32[]{:S(2)}) async-start(), calls=%async_computation.15 | async-start | bytes 10485760 | tf_op jit(solution)/shard_map/reduce_scatter | solution.py:311
  1529.7 236.2 %reduce-scatter.23.cloned.1.call-start = ((), (), s32[]{:S(2)}) async-start(), calls=%async_computation.18 | async-start | bytes 4456448
  1541.5 6.8 copy-start.53
  1541.5 6.8 copy-start.55
  1548.2 385.6 %reduce-scatter.25.cloned.1.call-start = ((), (), s32[]{:S(2)}) async-start(), calls=%async_computation.19 | async-start | bytes 17825792
  1595.9 520.1 %reduce-scatter.19.cloned.1.call-start = ((), (), s32[]{:S(2)}) async-start(), calls=%async_computation.16 | async-start | bytes 17825792 | tf_op jit(solution)/shard_map/reduce_scatter | solution.py:240
  1622.6 27.4 %copy-start.25 = (f32[512,32]{0,1:T(8,128)S(1)}, f32[512,32]{0,1:T(8,128)}, u32[]{:S(2)}) copy-start(f32[512,32]{0,1:T(8,128)} %copy-done.24) | copy-start | bytes 196612
  1622.6 27.4 %copy-start.27 = (f32[512,32]{0,1:T(8,128)S(1)}, f32[512,32]{0,1:T(8,128)}, u32[]{:S(2)}) copy-start(f32[512,32]{0,1:T(8,128)} %copy-done.26) | copy-start | bytes 196612
  1622.6 694.0 %all-reduce.18.cloned.1.call-start = ((), (), s32[]{:S(2)}) async-start(), calls=%async_computation.20 | async-start | bytes 16777216 | tf_op jit(solution)/shard_map/psum | solution.py:48
  1622.7 27.3 %copy-start.17 = (f32[2,512,16,64]{1,0,3,2:T(2,128)S(1)}, f32[2,512,16,64]{1,0,3,2:T(2,128)}, u32[]{:S(2)}) copy-start(f32[2,512,16,64]{1,0,3,2:T(2,128)} %get-tuple-element.126) | copy-start | bytes 12582916
  1655.0 10.5 copy-start.21
  1655.0 10.5 copy-start.23
  1673.6 8.0 copy-start.19
  1700.5 755.9 %reduce-scatter.21.cloned.1.call-start = ((), (), s32[]{:S(2)}) async-start(), calls=%async_computation.17 | async-start | bytes 13369344
  1763.2 553.5 %copy-start.31 = (f32[16,1,128]{2,1,0:T(1,128)S(1)}, f32[16,1,128]{2,1,0:T(1,128)}, u32[]{:S(2)}) copy-start(f32[16,1,128]{2,1,0:T(1,128)} %copy-done.30) | copy-start | bytes 24580
  1763.2 553.5 %copy-start.35 = (f32[1,4,2,128]{3,1,2,0:T(4,128)S(1)}, f32[1,4,2,128]{3,1,2,0:T(4,128)}, u32[]{:S(2)}) copy-start(f32[1,4,2,128]{3,1,2,0:T(4,128)} %copy-done.34) | copy-start | bytes 12292
  1763.2 553.5 %copy-start.37 = (f32[1,4,2,128]{3,1,2,0:T(4,128)S(1)}, f32[1,4,2,128]{3,1,2,0:T(4,128)}, u32[]{:S(2)}) copy-start(f32[1,4,2,128]{3,1,2,0:T(4,128)} %copy-done.36) | copy-start | bytes 12292
  1933.8 388.9 %copy-start.45 = (bf16[2048]{0:T(1024)(128)(2,1)S(1)}, bf16[2048]{0:T(1024)(128)(2,1)}, u32[]{:S(2)}) copy-start(bf16[2048]{0:T(1024)(128)(2,1)} %get-tuple-element.266) | copy-start | bytes 12292
  (23 other events, 81.5 us)
Sparse Core Ops, SparseCore 0:
  10.2 103.5 all-gather.10
  138.3 56.6 all-gather.12
  197.1 58.2 all-gather.14
  257.4 53.2 all-gather.16
  446.0 107.9 all-reduce.13
  556.3 126.8 all-gather.18
  685.6 128.5 all-gather.20
  894.8 106.0 all-reduce.15
  1529.2 71.7 reduce-scatter.14
  1603.6 71.6 reduce-scatter.16
  1679.2 72.3 reduce-scatter.22
  1756.1 177.6 reduce-scatter.24
  1938.5 177.5 reduce-scatter.18
  2119.1 197.5 all-reduce.17
  2321.1 135.2 reduce-scatter.20
where the time goes:
time: 2480 us; the launch traced here: 2470 us
  waiting for transfers between devices  1080 us (44%)
  matrix products  654 us (26%)
  local copies, waits for them, and re-layouts  289 us (12%)
  other arithmetic  268 us (11%)
  blocking collectives  162 us (7%)
    psum x3, waiting for transfers between devices, unit_sum(): return lax.psum(terms.astype(jnp.bfloat16), 'mp').astype(jnp.float32)  372 us
    unnamed x18, waiting for transfers between devices  223 us
    reduce_scatter x1, waiting for transfers between devices, body(): lax.psum_scatter(grad_in_w.astype(jnp.bfloat16), ('dp', 'seq'), scatter_d...  179 us
    all_gather x1, waiting for transfers between devices, gather_ffn(): lax.all_gather(in_weight, ('dp', 'seq'), axis=0, tiled=True)  116 us
    dot_general x2, matrix products, attend_back(): jnp.einsum('qhe,khe->hqk', query_seq, key_seq, preferred_element_type=jnp...  107 us
    convert_element_type x2, other arithmetic, attend_back(): grad_scores = (attn_probs * (grad_probs - inner_sum)).astype(jnp.bfloat16)  106 us
    unnamed x135, local copies, waits for them, and re-layouts  98.2 us
    dynamic_update_slice x6, local copies, waits for them, and re-layouts, body(): lax.map(attend, (queries, keys_all, values_all, lengths))  82.9 us
  transfers between devices with their start and end apart: 15, of which 10 were waited for; matrix products, arithmetic and copies ran while one was open for 23% of the time, Pallas kernels for 0%

commit v1 on v0

v1 whole, which is shorter than its diff:
```python
from functools import partial

import jax
import jax.numpy as jnp
from jax import lax
from jax.experimental import pallas as pl
from jax.experimental.pallas import tpu as pltpu
from jax.sharding import PartitionSpec as P

HEAD_DIM = 64
HALF = HEAD_DIM // 2
XPOS_BASE = 512
EPSILON = 1e-05
NEGATIVE = -1e30
LOG2_E = 1.4426950408889634
SCORE_SCALE = 0.125
VMEM = 56 * 2**20
BF16 = jnp.bfloat16
F32 = jnp.float32


def params(limit=VMEM):
    return pltpu.CompilerParams(vmem_limit_bytes=limit)


def dot(left, right, left_dim, right_dim):
    return lax.dot_general(
        left, right, (((left_dim,), (right_dim,)), ((), ())), preferred_element_type=F32
    )


def swap_halves(block):
    width = block.shape[1]
    if width % 128:
        pieces = []
        for start in range(0, width, HEAD_DIM):
            pieces += [block[:, start + HALF : start + HEAD_DIM], block[:, start : start + HALF]]
        return jnp.concatenate(pieces, axis=1)
    lane = lax.broadcasted_iota(jnp.int32, (block.shape[0], 128), 1) % HEAD_DIM
    pieces = []
    for start in range(0, width, 128):
        part = block[:, start : start + 128]
        pieces.append(
            jnp.where(lane < HALF, pltpu.roll(part, 128 - HALF, 1), pltpu.roll(part, HALF, 1))
        )
    return pieces[0] if len(pieces) == 1 else jnp.concatenate(pieces, axis=1)


def turned(block, cosine, sine, sign):
    lanes = cosine.shape[1]
    pieces = []
    for start in range(0, block.shape[1], lanes):
        part = block[:, start : start + lanes]
        pieces.append(part * cosine + sign * (swap_halves(part) * sine))
    return pieces[0] if len(pieces) == 1 else jnp.concatenate(pieces, axis=1)


def project_kernel(place, rows, weight, cos_q, sin_q, cos_k, sin_k, *outs):
    step = pl.program_id(0)
    block = rows[...]
    made = [dot(block, weight[j], 1, 0) for j in range(3)]
    made[0] = turned(made[0], cos_q[...], sin_q[...], 1)
    made[1] = turned(made[1], cos_k[...], sin_k[...], 1)
    for offset, out in enumerate(outs):

        @pl.when(step == offset)
        def _(out=out):
            for j in range(3):
                out[j] = made[j].astype(BF16)


def project(place, rows, qkv_full, tables, groups):
    span, width = rows.shape
    local = qkv_full.shape[2]
    share = local // groups
    if share % 128:
        weight = qkv_full.reshape(3, width, groups, share).transpose(2, 0, 1, 3)
        weight_spec = pl.BlockSpec(
            (None, 3, width, share), lambda o, p: (jnp.bitwise_xor(o, p[0]), 0, 0, 0)
        )
    else:
        weight = qkv_full
        weight_spec = pl.BlockSpec(
            (3, width, share), lambda o, p: (0, 0, jnp.bitwise_xor(o, p[0]))
        )
    table_spec = pl.BlockSpec(tables[0].shape, lambda o, p: (0, 0))
    return pl.pallas_call(
        project_kernel,
        grid_spec=pltpu.PrefetchScalarGridSpec(
            num_scalar_prefetch=1,
            grid=(groups,),
            in_specs=[pl.BlockSpec((span, width), lambda o, p: (0, 0)), weight_spec]
            + [table_spec] * 4,
            out_specs=[pl.BlockSpec((3, span, share), lambda o, p: (0, 0, 0))] * groups,
        ),
        out_shape=[jax.ShapeDtypeStruct((3, span, share), BF16)] * groups,
        compiler_params=params(),
        cost_estimate=pl.CostEstimate(
            flops=2 * 3 * span * width * local,
            bytes_accessed=2 * 3 * width * local,
            transcendentals=0,
        ),
        name="project",
    )(place, rows, weight, *tables)


def attend_kernel(meta, *refs, groups, heads, block):
    messages, rest = refs[:groups], refs[groups:]
    outs, log_ref = rest[:groups], rest[groups]
    q_all, k_all, vt_all, o_all = rest[groups + 1 :]
    step = pl.program_id(0)
    length, place = meta[0], meta[1]
    span = messages[0].shape[1]

    @pl.when(step == 0)
    def _():
        for offset, message in enumerate(messages):
            at = pl.multiple_of(jnp.bitwise_xor(place, offset) * span, span)
            q_all[pl.ds(at, span), :] = message[0]
            k_all[pl.ds(at, span), :] = message[1]
            for h in range(heads):
                lanes = slice(h * HEAD_DIM, (h + 1) * HEAD_DIM)
                vt_all[h, :, pl.ds(at, span)] = message[2, :, lanes].T

    start = pl.multiple_of(step * block, block)
    queries = [
        q_all[pl.ds(start, block), h * HEAD_DIM : (h + 1) * HEAD_DIM] for h in range(heads)
    ]
    scale = SCORE_SCALE * LOG2_E

    def keys_block(index, carry, masked):
        at = pl.multiple_of(index * block, block)
        if masked:
            key_pos = at + lax.broadcasted_iota(jnp.int32, (block, block), 0)
            query_pos = start + lax.broadcasted_iota(jnp.int32, (block, block), 1)
            allowed = (key_pos <= query_pos) & (key_pos < length)
        new = []
        for h in range(heads):
            top, total, mixed = carry[h]
            keys = k_all[pl.ds(at, block), h * HEAD_DIM : (h + 1) * HEAD_DIM]
            scores = dot(keys, queries[h], 1, 1)
            if masked:
                scores = jnp.where(allowed, scores, NEGATIVE)
            higher = jnp.maximum(top, jnp.max(scores, axis=0, keepdims=True))
            fade = jnp.exp2((top - higher) * scale)
            weights = jnp.exp2((scores - higher) * scale)
            total = total * fade + jnp.sum(weights, axis=0, keepdims=True)
            added = dot(vt_all[h, :, pl.ds(at, block)], weights.astype(BF16), 1, 0)
            new.append((higher, total, mixed * fade + added))
        return tuple(new)

    carry = tuple(
        (
            jnp.full((1, block), NEGATIVE, F32),
            jnp.zeros((1, block), F32),
            jnp.zeros((HEAD_DIM, block), F32),
        )
        for _ in range(heads)
    )
    whole = jnp.minimum(step, length // block)
    end = jnp.minimum(step + 1, (length + block - 1) // block)
    carry = lax.fori_loop(0, whole, lambda n, c: keys_block(n, c, False), carry)
    carry = lax.fori_loop(whole, end, lambda n, c: keys_block(n, c, True), carry)
    pieces = []
    for h in range(heads):
        top, total, mixed = carry[h]
        pieces.append((mixed / total).T)
        log_ref[h : h + 1, :] = top * scale + jnp.log2(total)
    o_all[pl.ds(start, block), :] = jnp.concatenate(pieces, axis=1).astype(BF16)

    @pl.when(step == pl.num_programs(0) - 1)
    def _():
        for offset, out in enumerate(outs):
            at = pl.multiple_of(jnp.bitwise_xor(place, offset) * span, span)
            out[...] = o_all[pl.ds(at, span), :]


def attend(meta, messages):
    groups = len(messages)
    _, span, share = messages[0].shape
    heads = share // HEAD_DIM
    count = groups * span
    block = min(512, span)
    message_spec = pl.BlockSpec((3, span, share), lambda n, m: (0, 0, 0))
    out_spec = pl.BlockSpec((span, share), lambda n, m: (0, 0))
    results = pl.pallas_call(
        partial(attend_kernel, groups=groups, heads=heads, block=block),
        grid_spec=pltpu.PrefetchScalarGridSpec(
            num_scalar_prefetch=1,
            grid=(count // block,),
            in_specs=[message_spec] * groups,
            out_specs=[out_spec] * groups + [pl.BlockSpec((heads, block), lambda n, m: (0, n))],
            scratch_shapes=[
                pltpu.VMEM((count, share), BF16),
                pltpu.VMEM((count, share), BF16),
                pltpu.VMEM((heads, HEAD_DIM, count), BF16),
                pltpu.VMEM((count, share), BF16),
            ],
        ),
        out_shape=[jax.ShapeDtypeStruct((span, share), BF16)] * groups
        + [jax.ShapeDtypeStruct((heads, count), F32)],
        compiler_params=params(),
        cost_estimate=pl.CostEstimate(
            flops=8 * count * count * share, bytes_accessed=8 * count * share, transcendentals=0
        ),
        name="attend",
    )(meta, *messages)
    return results[:groups], results[groups]


def attend_back_kernel(meta, *refs, groups, heads, block):
    messages, grads, mixed = refs[:groups], refs[groups : 2 * groups], refs[2 * groups : 3 * groups]
    log_ref, cos_q, sin_q, cos_k, sin_k = refs[3 * groups : 3 * groups + 5]
    outs = refs[3 * groups + 5 : 4 * groups + 5]
    scratch = refs[4 * groups + 5 :]
    q_all, k_all, v_all, g_all, kt_all, dot_all, dqt_all, dk_sum, dv_sum, out_all = scratch
    length, place = meta[0], meta[1]
    span = messages[0].shape[1]
    count = groups * span
    scale = SCORE_SCALE * LOG2_E

    def lanes(h):
        return slice(h * HEAD_DIM, (h + 1) * HEAD_DIM)

    for offset in range(groups):
        at = pl.multiple_of(jnp.bitwise_xor(place, offset) * span, span)
        message = messages[offset]
        q_all[pl.ds(at, span), :] = message[0]
        k_all[pl.ds(at, span), :] = message[1]
        v_all[pl.ds(at, span), :] = message[2]
        g_all[pl.ds(at, span), :] = grads[offset][...]
        both = grads[offset][...].astype(F32) * mixed[offset][...].astype(F32)
        for h in range(heads):
            kt_all[h, :, pl.ds(at, span)] = message[1, :, lanes(h)].T
            dot_all[h : h + 1, pl.ds(at, span)] = jnp.sum(
                both[:, lanes(h)].T, axis=0, keepdims=True
            )
    dqt_all[...] = jnp.zeros_like(dqt_all)
    query_blocks = count // block

    def keys_block(index, _):
        key_at = pl.multiple_of(index * block, block)
        keys = [k_all[pl.ds(key_at, block), lanes(h)] for h in range(heads)]
        values = [v_all[pl.ds(key_at, block), lanes(h)] for h in range(heads)]
        dk_sum[...] = jnp.zeros_like(dk_sum)
        dv_sum[...] = jnp.zeros_like(dv_sum)

        def query_block(index, _, masked):
            at = pl.multiple_of(index * block, block)
            if masked:
                key_pos = key_at + lax.broadcasted_iota(jnp.int32, (block, block), 0)
                query_pos = at + lax.broadcasted_iota(jnp.int32, (block, block), 1)
                allowed = (key_pos <= query_pos) & (key_pos < length)
            for h in range(heads):
                query = q_all[pl.ds(at, block), lanes(h)]
                grad = g_all[pl.ds(at, block), lanes(h)]
                scores = dot(keys[h], query, 1, 1)
                weights = jnp.exp2(scores * scale - log_ref[h : h + 1, pl.ds(at, block)])
                if masked:
                    weights = jnp.where(allowed, weights, 0.0)
                grad_weights = dot(values[h], grad, 1, 1)
                grad_scores = weights * (grad_weights - dot_all[h : h + 1, pl.ds(at, block)])
                grad_scores = grad_scores.astype(BF16)
                dv_sum[h] += dot(weights.astype(BF16), grad, 1, 0)
                dk_sum[h] += dot(grad_scores, query, 1, 0)
                dqt_all[h, :, pl.ds(at, block)] += dot(
                    kt_all[h, :, pl.ds(key_at, block)], grad_scores, 1, 0
                )
            return 0

        crosses = key_at + block > length
        whole = jnp.where(crosses, query_blocks, index + 1)
        lax.fori_loop(index, whole, partial(query_block, masked=True), 0)
        lax.fori_loop(whole, query_blocks, partial(query_block, masked=False), 0)
        dk = jnp.concatenate([dk_sum[h] for h in range(heads)], axis=1) * SCORE_SCALE
        dv = jnp.concatenate([dv_sum[h] for h in range(heads)], axis=1)
        turn = (cos_k[pl.ds(key_at, block), :], sin_k[pl.ds(key_at, block), :])
        out_all[1, pl.ds(key_at, block), :] = turned(dk, *turn, -1).astype(BF16)
        out_all[2, pl.ds(key_at, block), :] = dv.astype(BF16)
        return 0

    used = (length + block - 1) // block
    lax.fori_loop(0, used, keys_block, 0)

    def no_keys(index, _):
        at = pl.multiple_of(index * block, block)
        for j in (1, 2):
            out_all[j, pl.ds(at, block), :] = jnp.zeros((block, heads * HEAD_DIM), BF16)
        return 0

    lax.fori_loop(used, query_blocks, no_keys, 0)
    for index in range(query_blocks):
        at = slice(index * block, (index + 1) * block)
        dq = jnp.concatenate([dqt_all[h, :, at].T for h in range(heads)], axis=1) * SCORE_SCALE
        out_all[0, at, :] = turned(dq, cos_q[at, :], sin_q[at, :], -1).astype(BF16)
    for offset, out in enumerate(outs):
        at = pl.multiple_of(jnp.bitwise_xor(place, offset) * span, span)
        out[...] = out_all[:, pl.ds(at, span), :]


def attend_back(meta, messages, grads, mixed, logs, tables):
    groups = len(messages)
    _, span, share = messages[0].shape
    heads = share // HEAD_DIM
    count = groups * span
    block = min(512, span)
    message_spec = pl.BlockSpec((3, span, share), lambda n, m: (0, 0, 0))
    row_spec = pl.BlockSpec((span, share), lambda n, m: (0, 0))
    table_spec = pl.BlockSpec(tables[0].shape, lambda n, m: (0, 0))
    return pl.pallas_call(
        partial(attend_back_kernel, groups=groups, heads=heads, block=block),
        grid_spec=pltpu.PrefetchScalarGridSpec(
            num_scalar_prefetch=1,
            grid=(1,),
            in_specs=[message_spec] * groups
            + [row_spec] * (2 * groups)
            + [pl.BlockSpec(logs.shape, lambda n, m: (0, 0))]
            + [table_spec] * 4,
            out_specs=[message_spec] * groups,
            scratch_shapes=[pltpu.VMEM((count, share), BF16)] * 4
            + [
                pltpu.VMEM((heads, HEAD_DIM, count), BF16),
                pltpu.VMEM((heads, count), F32),
                pltpu.VMEM((heads, HEAD_DIM, count), F32),
                pltpu.VMEM((heads, block, HEAD_DIM), F32),
                pltpu.VMEM((heads, block, HEAD_DIM), F32),
                pltpu.VMEM((3, count, share), BF16),
            ],
        ),
        out_shape=[jax.ShapeDtypeStruct((3, span, share), BF16)] * groups,
        compiler_params=params(),
        cost_estimate=pl.CostEstimate(
            flops=16 * count * count * share, bytes_accessed=16 * count * share, transcendentals=0
        ),
        name="attend_back",
    )(meta, *messages, *grads, *mixed, logs, *tables)


def weight_grad_kernel(place, *refs, sequences, devices, groups, chunk):
    lefts, rights = refs[:sequences], refs[sequences : 2 * sequences]
    away, near, own = refs[2 * sequences : 2 * sequences + 3]
    turned_left = refs[2 * sequences + 3]
    span = lefts[0].shape[0]

    @pl.when(pl.program_id(0) == 0)
    def _():
        row = 0
        for offset in (3, 1, 2, 0):
            target = jnp.bitwise_xor(place[0], offset)
            for device in range(devices):
                at = pl.multiple_of((device * groups + target) * chunk, chunk)
                for s in range(sequences):
                    turned_left[row : row + chunk, s * span : (s + 1) * span] = lefts[s][
                        :, pl.ds(at, chunk)
                    ].T
                row += chunk

    block = devices * chunk
    parts = [away.at[:block], away.at[block:], near, own]
    for n, part in enumerate(parts):
        rows = slice(n * block, (n + 1) * block)
        total = dot(turned_left[rows, :span], rights[0][...], 1, 0)
        for s in range(1, sequences):
            total += dot(turned_left[rows, s * span : (s + 1) * span], rights[s][...], 1, 0)
        part[...] = total.astype(BF16)


def weight_grad(place, lefts, rights, devices, groups):
    sequences = len(lefts)
    span, width = lefts[0].shape
    columns = rights[0].shape[1]
    chunk = width // (devices * groups)
    tile = 512 if columns % 512 == 0 else 256
    half, quarter = width // 2, width // 4
    return pl.pallas_call(
        partial(
            weight_grad_kernel, sequences=sequences, devices=devices, groups=groups, chunk=chunk
        ),
        grid_spec=pltpu.PrefetchScalarGridSpec(
            num_scalar_prefetch=1,
            grid=(columns // tile,),
            in_specs=[pl.BlockSpec((span, width), lambda n, p: (0, 0))] * sequences
            + [pl.BlockSpec((span, tile), lambda n, p: (0, n))] * sequences,
            out_specs=[
                pl.BlockSpec((half, tile), lambda n, p: (0, n)),
                pl.BlockSpec((quarter, tile), lambda n, p: (0, n)),
                pl.BlockSpec((quarter, tile), lambda n, p: (0, n)),
            ],
            scratch_shapes=[pltpu.VMEM((width, sequences * span), BF16)],
        ),
        out_shape=[
            jax.ShapeDtypeStruct((half, columns), BF16),
            jax.ShapeDtypeStruct((quarter, columns), BF16),
            jax.ShapeDtypeStruct((quarter, columns), BF16),
        ],
        compiler_params=params(),
        cost_estimate=pl.CostEstimate(
            flops=2 * sequences * span * width * columns,
            bytes_accessed=2 * width * columns,
            transcendentals=0,
        ),
        name="weight_grad",
    )(place, *lefts, *rights)


def exchange(array, axis, size, offset):
    return lax.ppermute(array, axis, [(n, n ^ offset) for n in range(size)])


def scatter_sum(parts, groups):
    away, near, own = parts
    quarter = own.shape[0]
    got = exchange(away, "seq", groups, 1)
    near = (near.astype(F32) + got[:quarter].astype(F32)).astype(BF16)
    far = exchange(near, "seq", groups, 2)
    own = own.astype(F32) + got[quarter:].astype(F32) + far.astype(F32)
    return lax.psum_scatter(own.astype(BF16), "dp", scatter_dimension=0, tiled=True).astype(F32)


def unit_sum(low, units):
    if units != 2:
        return lax.psum(low, "mp").astype(F32)
    other = exchange(low, "mp", 2, 1)
    return low.astype(F32) + other.astype(F32)


def rounded(terms):
    return lax.optimization_barrier(terms.astype(BF16))


def gathered(pieces, place, groups):
    stacked = jnp.stack(pieces)
    ordered = [
        lax.dynamic_index_in_dim(stacked, jnp.bitwise_xor(place, n), 0, False)
        for n in range(groups)
    ]
    return jnp.concatenate([piece.transpose(1, 0, 2) for piece in ordered], axis=2)


def split_up(rows, place, groups):
    share = rows.shape[1] // groups
    return [
        lax.dynamic_slice_in_dim(rows, jnp.bitwise_xor(place, n) * share, share, 1)
        for n in range(groups)
    ]


def pass_round(pieces, groups):
    return [pieces[0]] + [exchange(pieces[n], "seq", groups, n) for n in range(1, groups)]


def full_norm(inputs, scales):
    row_mean = jnp.mean(inputs, axis=-1, keepdims=True)
    centered = inputs - row_mean
    row_var = jnp.mean(centered * centered, axis=-1, keepdims=True)
    inv_std = lax.rsqrt(row_var + EPSILON)
    normal = centered * inv_std
    return (normal * scales, normal, inv_std)


def full_norm_back(grad_out, normal, inv_std, scales):
    scaled = grad_out * scales
    return inv_std * (
        scaled
        - jnp.mean(scaled, axis=-1, keepdims=True)
        - normal * jnp.mean(scaled * normal, axis=-1, keepdims=True)
    )


def across_units(first_sum, second_sum, units):
    if units != 2:
        return lax.psum((first_sum, second_sum), "mp")
    sums = jnp.stack([first_sum, second_sum])
    return sums + exchange(sums, "mp", 2, 1)


def split_norm(inputs, scales, full_width, units):
    moment_sums = across_units(
        jnp.sum(inputs, axis=-1), jnp.sum(inputs * inputs, axis=-1), units
    )
    row_mean = moment_sums[0][:, None] / full_width
    row_var = moment_sums[1][:, None] / full_width - row_mean * row_mean
    inv_std = lax.rsqrt(row_var + EPSILON)
    normal = (inputs - row_mean) * inv_std
    return (normal * scales, normal, inv_std)


def split_norm_back(grad_out, normal, inv_std, scales, full_width, units):
    scaled = grad_out * scales
    moment_sums = across_units(
        jnp.sum(scaled, axis=-1), jnp.sum(scaled * normal, axis=-1), units
    )
    grad_in = inv_std * (
        scaled
        - moment_sums[0][:, None] / full_width
        - normal * moment_sums[1][:, None] / full_width
    )
    return (grad_in, jnp.sum(grad_out * normal, axis=0))


def xpos_tables(count, lanes):
    positions = jnp.arange(count, dtype=F32)
    pair_index = jnp.arange(HALF, dtype=F32)
    frequency = 1.0 / 10000.0 ** (2.0 * pair_index / HEAD_DIM)
    angles = positions[:, None] * frequency[None, :]
    base_ratio = (2.0 * pair_index + 0.4 * HEAD_DIM) / (1.4 * HEAD_DIM)
    growth = base_ratio[None, :] ** ((positions[:, None] - count // 2) / XPOS_BASE)
    cosine, sine = jnp.cos(angles), jnp.sin(angles)
    tables = []
    for factor in (growth, 1.0 / growth):
        tables.append(jnp.tile(cosine * factor, (1, lanes // HALF)))
        tables.append(
            jnp.tile(jnp.concatenate([-sine * factor, sine * factor], axis=1), (1, lanes // HEAD_DIM))
        )
    return tables


def body(
    devices,
    groups,
    units,
    tokens,
    lengths,
    qkv_weight,
    out_weight,
    in_weight,
    down_weight,
    gain_in,
    gain_attn,
    gain_mid,
    gain_ffn,
    out_grad,
):
    sequences, span, model = tokens.shape
    each = range(sequences)
    data = ("dp", "seq")
    shards = devices * groups
    place = lax.axis_index("seq").astype(jnp.int32)
    local_width = qkv_weight.shape[2]
    heads_here = local_width // HEAD_DIM
    ffn_width = in_weight.shape[1]
    share = local_width // groups

    sizes = [gain_in.size, gain_mid.size, gain_attn.size, gain_ffn.size]
    flat = jnp.concatenate(
        [gain_in, gain_mid, gain_attn.reshape(-1), gain_ffn.reshape(-1)]
    ).reshape(1, -1)
    all_gains = lax.all_gather(flat, data, axis=0, tiled=True).astype(F32)
    cuts = [sum(sizes[:n]) for n in range(5)]
    pieces = [all_gains[:, cuts[n] : cuts[n + 1]] for n in range(4)]
    gain_one, gain_three = pieces[0].reshape(-1), pieces[1].reshape(-1)
    gain_two = pieces[2].reshape(shards, heads_here, -1).transpose(1, 0, 2).reshape(-1)
    gain_four = (
        pieces[3].reshape(shards, ffn_width // HEAD_DIM, -1).transpose(1, 0, 2).reshape(-1)
    )

    qkv_full = lax.all_gather(qkv_weight, data, axis=1, tiled=True)
    out_full = lax.all_gather(out_weight, data, axis=1, tiled=True)
    in_full = lax.all_gather(in_weight, data, axis=0, tiled=True)
    down_full = lax.all_gather(down_weight, data, axis=1, tiled=True)

    count = span * groups
    tables = xpos_tables(count, min(128, share))
    tables_here = [lax.dynamic_slice_in_dim(t, place * span, span, 0) for t in tables]
    spot = place.reshape(1)
    metas = [jnp.stack([lengths[s], place]) for s in each]

    inputs = [tokens[s].astype(F32) for s in each]
    first = [full_norm(inputs[s], gain_one) for s in each]
    first_low = [first[s][0].astype(BF16) for s in each]

    messages = []
    for s in each:
        made = project(spot, first_low[s], qkv_full, tables_here, groups)
        messages.append(pass_round(made, groups))
    mixed, logs = [], []
    hidden, second, second_low = [], [], []
    for s in each:
        outs, log = attend(metas[s], messages[s])
        mixed.append(outs)
        logs.append(log)
        back = pass_round(outs, groups)
        attended = gathered([b[None] for b in back], place, groups).reshape(span, local_width)
        normed, plain, std = split_norm(attended.astype(F32), gain_two, model, units)
        second.append((plain, std))
        second_low.append(normed.astype(BF16))
        branch = rounded(jnp.dot(second_low[s], out_full, preferred_element_type=F32))
        hidden.append(inputs[s] + unit_sum(branch, units))

    third, third_low, fourth, fourth_low, gelu_backs, results = [], [], [], [], [], []
    for s in each:
        normed, plain, std = full_norm(hidden[s], gain_three)
        third.append((plain, std))
        third_low.append(normed.astype(BF16))
        pre_act = jnp.dot(third_low[s], in_full, preferred_element_type=F32)
        activated, gelu_back = jax.vjp(partial(jax.nn.gelu, approximate=False), pre_act)
        gelu_backs.append(gelu_back)
        normed, plain, std = split_norm(activated, gain_four, ffn_width * units, units)
        fourth.append((plain, std))
        fourth_low.append(normed.astype(BF16))

    grad_low = [out_grad[s] for s in each]
    pre_low, base_terms = [], []
    gain_four_grad = 0.0
    for s in each:
        grad_wide = dot(grad_low[s], down_full, 1, 1)
        grad_act, gain_part = split_norm_back(
            grad_wide, *fourth[s], gain_four, ffn_width * units, units
        )
        gain_four_grad += gain_part
        pre_low.append(gelu_backs[s](grad_act)[0].astype(BF16))
        base_terms.append(rounded(dot(pre_low[s], in_full, 1, 1)))
    grad_third = [unit_sum(base_terms[s], units) for s in each]

    in_parts = weight_grad(spot, third_low, pre_low, devices, groups)
    grad_in_w = scatter_sum(in_parts, groups)
    down_parts = weight_grad(spot, grad_low, fourth_low, devices, groups)
    grad_down_w = scatter_sum(down_parts, groups).T

    for s in each:
        branch = rounded(jnp.dot(fourth_low[s], down_full, preferred_element_type=F32))
        results.append((hidden[s] + unit_sum(branch, units)).astype(BF16))

    gain_three_grad, gain_two_grad = 0.0, 0.0
    grad_hidden, hidden_low, returned = [], [], []
    for s in each:
        gain_three_grad += jnp.sum(grad_third[s] * third[s][0], axis=0)
        grad_hidden.append(
            grad_low[s].astype(F32) + full_norm_back(grad_third[s], *third[s], gain_three)
        )
        hidden_low.append(grad_hidden[s].astype(BF16))
        grad_inner = dot(hidden_low[s], out_full, 1, 1)
        grad_attended, gain_part = split_norm_back(grad_inner, *second[s], gain_two, model, units)
        gain_two_grad += gain_part
        grads = pass_round(split_up(grad_attended.astype(BF16), place, groups), groups)
        made = attend_back(metas[s], messages[s], grads, mixed[s], logs[s], tables)
        back = pass_round(made, groups)
        returned.append(gathered(back, place, groups))
    out_parts = weight_grad(spot, hidden_low, second_low, devices, groups)
    grad_out_w = scatter_sum(out_parts, groups).T

    flat_returned = [returned[s].reshape(span, 3 * local_width) for s in each]
    gain_one_grad = 0.0
    first_terms = []
    for s in each:
        terms = jnp.einsum("tje,jde->td", returned[s], qkv_full, preferred_element_type=F32)
        gain_one_grad += jnp.sum(terms * first[s][1], axis=0)
        first_terms.append(rounded(terms))
    qkv_parts = weight_grad(spot, first_low, flat_returned, devices, groups)
    grad_qkv_w = scatter_sum(qkv_parts, groups).reshape(-1, 3, local_width).transpose(1, 0, 2)
    grad_inputs = []
    for s in each:
        grad_first = full_norm_back(
            unit_sum(first_terms[s], units), first[s][1], first[s][2], gain_one
        )
        grad_inputs.append((grad_hidden[s] + grad_first).astype(BF16))

    gain_rows = jnp.concatenate(
        [
            gain_one_grad.reshape(shards, -1),
            gain_three_grad.reshape(shards, -1),
            gain_two_grad.reshape(heads_here, shards, -1).transpose(1, 0, 2).reshape(shards, -1),
            gain_four_grad.reshape(ffn_width // HEAD_DIM, shards, -1)
            .transpose(1, 0, 2)
            .reshape(shards, -1),
        ],
        axis=1,
    )
    gain_sums = lax.psum_scatter(gain_rows, data, scatter_dimension=0, tiled=True).reshape(-1)
    one, three, two, four = [gain_sums[cuts[n] : cuts[n + 1]] for n in range(4)]
    return (
        jnp.stack(results),
        jnp.stack(grad_inputs),
        grad_qkv_w,
        grad_out_w,
        grad_in_w,
        grad_down_w,
        lax.psum(one, "mp"),
        two.reshape(gain_attn.shape),
        three,
        four.reshape(gain_ffn.shape),
    )


def solution(mesh):
    sizes = mesh.shape
    data = ("dp", "seq")
    in_specs = (
        P("dp", "seq", None),
        P("dp"),
        P(None, data, "mp"),
        P("mp", data),
        P(data, "mp"),
        P("mp", data),
        P(data),
        P("mp", data),
        P(data),
        P("mp", data),
        P("dp", "seq", None),
    )
    out_specs = (
        P("dp", "seq", None),
        P("dp", "seq", None),
        P(None, data, "mp"),
        P("mp", data),
        P(data, "mp"),
        P("mp", data),
        P(data),
        P("mp", data),
        P(data),
        P("mp", data),
    )
    run = partial(body, sizes["dp"], sizes["seq"], sizes["mp"])
    return jax.shard_map(run, mesh=mesh, in_specs=in_specs, out_specs=out_specs, check_vma=False)
```

time: 2480 us -> 1480 us (0.60)
  matrix products: 654 us -> 205 us
  waiting for transfers between devices: 1080 us -> 632 us
  Pallas kernels: 0 us -> 252 us
  local copies, waits for them, and re-layouts: 289 us -> 51.4 us
  other arithmetic: 268 us -> 145 us
  starting transfers between devices: 1.13 us -> 43.4 us
  blocking collectives: 162 us -> 132 us
    ppermute x0 -> x48, waiting for transfers between devices: none -> 612 us  [exchange(): return lax.ppermute(array, axis, [(n, n ^ offset) for n in range(size)])]
    dot_general x26 -> x14, matrix products: 654 us -> 205 us  [the longest x6 76.6 us: dot(): lax.dot_general(left, right, (((left_dim,), (right_dim,)), ((), ())), pre...]
    psum x3 -> x0, waiting for transfers between devices: 372 us -> none  [unit_sum(): return lax.psum(terms.astype(jnp.bfloat16), 'mp').astype(jnp.float32)]
    all_gather x6 -> x4, waiting for transfers between devices: 301 us -> 17.4 us  [the longest x1 17.4 us: body(): qkv_full = lax.all_gather(qkv_weight, data, axis=1, tiled=True)]
    pallas_call x0 -> x10, Pallas kernels: none -> 252 us  [the longest x2 88.5 us: attend_back(): pl.pallas_call(partial(attend_back_kernel, groups=groups, heads=heads, bl...]
    unnamed x18 -> x8, waiting for transfers between devices: 223 us -> 2.65 us
    reduce_scatter x3 -> x4, waiting for transfers between devices: 179 us -> 0.01 us  [scatter_sum(): lax.psum_scatter(own.astype(BF16), 'dp', scatter_dimension=0, tiled=True)]
    dynamic_update_slice x10 -> x0, local copies, waits for them, and re-layouts: 97.3 us -> none  [the longest x6 82.9 us: body(): lax.map(attend, (queries, keys_all, values_all, lengths))]
  transfers between devices with their start and end apart: 15 -> 56, of which waited for: 10 -> 25; matrix products, arithmetic and copies ran while one was open for 23% -> 19% of each run, Pallas kernels for 0% -> 16%
where the time goes in v1:
time: 1480 us
  waiting for transfers between devices  632 us (43%)
  Pallas kernels  252 us (17%)
  matrix products  205 us (14%)
  other arithmetic  145 us (10%)
  blocking collectives  132 us (9%)
  local copies, waits for them, and re-layouts  51.4 us (3%)
  starting transfers between devices  43.4 us (3%)
  between operations  16.8 us (1%)
    ppermute x48, waiting for transfers between devices, exchange(): return lax.ppermute(array, axis, [(n, n ^ offset) for n in range(size)])  612 us
    unnamed x2, blocking collectives  127 us
    pallas_call x2, Pallas kernels, attend_back(): pl.pallas_call(partial(attend_back_kernel, groups=groups, heads=heads, bl...  88.5 us
    dot_general x6, matrix products, dot(): lax.dot_general(left, right, (((left_dim,), (right_dim,)), ((), ())), pre...  76.6 us
    pallas_call x4, Pallas kernels, weight_grad(): pl.pallas_call(partial(weight_grad_kernel, sequences=sequences, devices=d...  75.9 us
    dot_general x2, matrix products, body(): pre_act = jnp.dot(third_low[s], in_full, preferred_element_type=F32)  63.8 us
    pallas_call x2, Pallas kernels, attend(): pl.pallas_call(partial(attend_kernel, groups=groups, heads=heads, block=b...  61.6 us
    ppermute x48, starting transfers between devices, exchange(): return lax.ppermute(array, axis, [(n, n ^ offset) for n in range(size)])  43.1 us
  transfers between devices with their start and end apart: 56, of which 25 were waited for; matrix products, arithmetic and copies ran while one was open for 19% of the time, Pallas kernels for 16%

profile of v1, /device:TPU:0, one launch (start us, length us, event | category | flops | bytes accessed | tf_op | source)
XLA Modules:
  0.0 1478.1 jit_solution(13432100905495590811)
XLA Ops:
  18.6 65.4 %all-reduce = bf16[9216]{0:T(1024)(128)(2,1)S(1)} all-reduce(bf16[9216]{0:T(1024)(128)(2,1)S(1)} %dynamic-update-slice), channel_id=2, replica_groups=mesh['dp'=4,'seq'=4,'mp'=2] {'dp','seq'}, use_global_device_ids=true, to_apply=%add | all-reduce | flops 9216 | bytes 36864
  97.0 17.4 %all-gather.6.cloned.1.call-done.weight = bf16[3,2048,1024]{2,1,0:T(8,128)(2,1)} async-done(((bf16[3,128,1024]{2,1,0:T(8,128)(2,1)}), bf16[3,2048,1024]{2,1,0:T(8,128)(2,1)}) %all-gather.6.cloned.1.call-update) | async-done | bytes 12582928 | tf_op jit(solution)/shard_map/all_gather | solution.py:557
  114.4 13.0 project.3
  131.8 13.0 project.2
  146.7 4.6 collective-permute-done.11.refs_2_
  151.4 23.6 %collective-permute-done.12.refs_3_ = bf16[3,512,256]{2,1,0:T(8,128)(2,1)S(1)} collective-permute-done((bf16[3,512,256]{2,1,0:T(8,128)(2,1)}, bf16[3,512,256]{2,1,0:T(8,128)(2,1)S(1)}, u32[]{:S(2)}, u32[]{:S(2)}) %collective-permute-start.12) | collective-permute-done | bytes 786464 | tf_op jit(solution)/shard_map/ppermute | solution.py:407
  175.9 31.9 %attend.3 = (bf16[512,256]{1,0:T(8,128)(2,1)}, bf16[512,256]{1,0:T(8,128)(2,1)}, bf16[512,256]{1,0:T(8,128)(2,1)}, bf16[512,256]{1,0:T(8,128)(2,1)}, f32[4,2048]{1,0:T(4,128)}) custom-call(s32[2]{0:T(128)} %get-tuple-element.279.meta, bf16[3,512,256]{2,1,0:T(8,128)(2,1)} %get-tuple-element.56.refs_0_, bf16[3,512,256]{2,1,0:T(8,128)(2,1)} %copy-done.96, ...), custom_call_target="tpu_custom_call" | custom-call | flops 8589934592 | bytes 4194304 | tf_op jit(solution)/shard_map/attend/pallas_call | solution.py:186
  210.6 9.3 collective-permute-done.2.refs_3_
  220.9 29.7 %attend.2 = (bf16[512,256]{1,0:T(8,128)(2,1)}, bf16[512,256]{1,0:T(8,128)(2,1)}, bf16[512,256]{1,0:T(8,128)(2,1)}, bf16[512,256]{1,0:T(8,128)(2,1)}, f32[4,2048]{1,0:T(4,128)}) custom-call(s32[2]{0:T(128)} %get-tuple-element.278.meta, bf16[3,512,256]{2,1,0:T(8,128)(2,1)} %get-tuple-element.48.refs_0_, bf16[3,512,256]{2,1,0:T(8,128)(2,1)} %copy-done.93, ...), custom_call_target="tpu_custom_call" | custom-call | flops 8589934592 | bytes 4194304 | tf_op jit(solution)/shard_map/attend/pallas_call | solution.py:186
  255.9 9.5 collective-permute-done.4
  265.4 11.9 collective-permute-done.5
  283.7 5.0 convolution_convert_fusion
  290.3 3.7 convolution_convert_fusion.1
  296.1 41.5 %collective-permute-done.17 = bf16[512,2048]{1,0:T(8,128)(2,1)} collective-permute-done((bf16[512,2048]{1,0:T(8,128)(2,1)S(1)}, bf16[512,2048]{1,0:T(8,128)(2,1)}, u32[]{:S(2)}, u32[]{:S(2)}) %collective-permute-start.17) | collective-permute-done | bytes 2097184 | tf_op jit(solution)/shard_map/ppermute | solution.py:407
  337.6 42.8 %collective-permute-done.7 = bf16[512,2048]{1,0:T(8,128)(2,1)} collective-permute-done((bf16[512,2048]{1,0:T(8,128)(2,1)}, bf16[512,2048]{1,0:T(8,128)(2,1)}, u32[]{:S(2)}, u32[]{:S(2)}) %collective-permute-start.7) | collective-permute-done | bytes 2097184 | tf_op jit(solution)/shard_map/ppermute | solution.py:407
  380.4 5.6 fusion.105
  391.5 34.2 %fusion.101 = (f32[512]{0:T(512)S(1)}, f32[512]{0:T(512)S(1)}, f32[512,4096]{1,0:T(8,128)}, f32[512,4096]{1,0:T(8,128)}, f32[512,4096]{1,0:T(8,128)}) fusion(bf16[512,2048]{1,0:T(8,128)(2,1)} %get-tuple-element.239.refs_1_, bf16[2048,4096]{1,0:T(8,128)(2,1)} %all-gather.10.cloned.1.call-done), kind=kOutput, calls=%fused_computation.285 | convolution fusion | flops 8730443776 | bytes 44044288 | tf_op jit(solution)/shard_map/dot_general | solution.py:595
  427.2 29.6 %fusion.100 = (f32[512]{0:T(512)S(1)}, f32[512]{0:T(512)S(1)}, f32[512,4096]{1,0:T(8,128)}, f32[512,4096]{1,0:T(8,128)}, f32[512,4096]{1,0:T(8,128)}) fusion(bf16[512,2048]{1,0:T(8,128)(2,1)S(1)} %get-tuple-element.238.refs_0_, bf16[2048,4096]{1,0:T(8,128)(2,1)S(1)} %copy-done.90), kind=kOutput, calls=%fused_computation.284 | convolution fusion | flops 8730443776 | bytes 44044288 | tf_op jit(solution)/shard_map/dot_general | solution.py:595
  457.5 15.4 %fusion.97 = f32[512,4096]{1,0:T(8,128)} fusion(bf16[4096,2048]{1,0:T(8,128)(2,1)} %all-gather.12.cloned.1.call-done, bf16[2,512,2048]{2,1,0:T(8,128)(2,1)} %param.21), kind=kOutput, calls=%fused_computation.281 | convolution fusion | flops 8589934592 | bytes 27262976 | tf_op jit(solution)/shard_map/dot_general | solution.py:27
  473.0 23.5 %multiply_reduce_fusion.1 = (f32[4096]{0:T(1024)}, f32[512]{0:T(512)S(1)}, f32[512]{0:T(512)S(1)}, f32[512]{0:T(512)S(1)}, f32[512]{0:T(512)S(1)}, /*index=5*/f32[4096]{0:T(1024)}, f32[512,4096]{1,0:T(8,128)}) fusion(f32[512,4096]{1,0:T(8,128)} %get-tuple-element.174, f32[512]{0:T(512)S(1)} %add_rsqrt_fusion.4, f32[512]{0:T(512)S(1)} %bitcast.363, ...), kind=kOutput, calls=%fused_computation.5 | convolution fusion | flops 8623480832 | bytes 52494336 | tf_op jit(solution)/shard_map/dot_general | solution.py:27
  501.7 28.5 %add_convert_fusion.5 = (bf16[512,4096]{1,0:T(8,128)(2,1)S(1)}, bf16[512,4096]{1,0:T(8,128)(2,1)}, bf16[512,4096]{1,0:T(8,128)(2,1)}, bf16[512,4096]{1,0:T(8,128)(2,1)}) fusion(f32[512,4096]{1,0:T(8,128)} %get-tuple-element.175, f32[512,4096]{1,0:T(8,128)} %get-tuple-element.270, f32[512,4096]{1,0:T(8,128)} %get-tuple-element.272, ...), kind=kLoop, calls=%fused_computation.12 | loop fusion | flops 100663296 | bytes 83918848 | tf_op jit(solution)/shard_map/convert_element_type | solution.py:611
  530.2 15.1 %convolution_convert_fusion.2 = bf16[512,2048]{1,0:T(8,128)(2,1)S(1)} fusion(bf16[512,4096]{1,0:T(8,128)(2,1)} %get-tuple-element.225.refs_3_, bf16[2048,4096]{1,0:T(8,128)(2,1)} %all-gather.10.cloned.1.call-done), kind=kOutput, calls=%fused_computation.122 | convolution fusion | flops 8590983168 | bytes 23068672 | tf_op jit(solution)/shard_map/dot_general | solution.py:27
  546.0 14.6 convolution_convert_fusion.5
  562.0 13.5 convolution_convert_fusion.3
  576.1 13.9 convolution_convert_fusion.4
  594.1 44.9 %collective-permute-done.9 = bf16[512,2048]{1,0:T(8,128)(2,1)} collective-permute-done((bf16[512,2048]{1,0:T(8,128)(2,1)}, bf16[512,2048]{1,0:T(8,128)(2,1)}, u32[]{:S(2)}, u32[]{:S(2)}) %collective-permute-start.9) | collective-permute-done | bytes 2097184 | tf_op jit(solution)/shard_map/ppermute | solution.py:407
  639.0 44.8 %collective-permute-done.21 = bf16[512,2048]{1,0:T(8,128)(2,1)S(1)} collective-permute-done((bf16[512,2048]{1,0:T(8,128)(2,1)}, bf16[512,2048]{1,0:T(8,128)(2,1)S(1)}, u32[]{:S(2)}, u32[]{:S(2)}) %collective-permute-start.21) | collective-permute-done | bytes 2097184 | tf_op jit(solution)/shard_map/ppermute | solution.py:407
  683.9 8.9 multiply_reduce_fusion.9
  692.9 31.3 %collective-permute-done.19 = bf16[512,2048]{1,0:T(8,128)(2,1)} collective-permute-done((bf16[512,2048]{1,0:T(8,128)(2,1)S(1)}, bf16[512,2048]{1,0:T(8,128)(2,1)}, u32[]{:S(2)}, u32[]{:S(2)}) %collective-permute-start.19) | collective-permute-done | bytes 2097184 | tf_op jit(solution)/shard_map/ppermute | solution.py:407
  724.1 10.8 fusion.103
  735.0 5.3 fusion.112
  740.5 3.8 fusion.79
  755.6 4.5 collective-permute-done.34.refs_6_
  760.2 4.8 collective-permute-done.35.refs_7_
  765.7 46.1 %attend_back.3 = (bf16[3,512,256]{2,1,0:T(8,128)(2,1)}, bf16[3,512,256]{2,1,0:T(8,128)(2,1)}, bf16[3,512,256]{2,1,0:T(8,128)(2,1)}, bf16[3,512,256]{2,1,0:T(8,128)(2,1)}) custom-call(s32[2]{0:T(128)} %get-tuple-element.279.meta, bf16[3,512,256]{2,1,0:T(8,128)(2,1)} %get-tuple-element.56.refs_0_, bf16[3,512,256]{2,1,0:T(8,128)(2,1)} %copy-done.96, ...), custom_call_target="tpu_custom_call" | custom-call | flops 17179869184 | bytes 8388608 | tf_op jit(solution)/shard_map/attend_back/pallas_call | solution.py:310
  814.8 42.4 %attend_back.2 = (bf16[3,512,256]{2,1,0:T(8,128)(2,1)}, bf16[3,512,256]{2,1,0:T(8,128)(2,1)}, bf16[3,512,256]{2,1,0:T(8,128)(2,1)}, bf16[3,512,256]{2,1,0:T(8,128)(2,1)}) custom-call(s32[2]{0:T(128)} %get-tuple-element.278.meta, bf16[3,512,256]{2,1,0:T(8,128)(2,1)} %get-tuple-element.48.refs_0_, bf16[3,512,256]{2,1,0:T(8,128)(2,1)} %copy-done.93, ...), custom_call_target="tpu_custom_call" | custom-call | flops 17179869184 | bytes 8388608 | tf_op jit(solution)/shard_map/attend_back/pallas_call | solution.py:310
  860.2 18.1 %collective-permute-done.27 = bf16[3,512,256]{2,1,0:T(8,128)(2,1)S(1)} collective-permute-done((bf16[3,512,256]{2,1,0:T(8,128)(2,1)}, bf16[3,512,256]{2,1,0:T(8,128)(2,1)S(1)}, u32[]{:S(2)}, u32[]{:S(2)}) %collective-permute-start.27) | collective-permute-done | bytes 786464 | tf_op jit(solution)/shard_map/ppermute | solution.py:407
  878.3 15.1 %collective-permute-done.28 = bf16[3,512,256]{2,1,0:T(8,128)(2,1)S(1)} collective-permute-done((bf16[3,512,256]{2,1,0:T(8,128)(2,1)}, bf16[3,512,256]{2,1,0:T(8,128)(2,1)S(1)}, u32[]{:S(2)}, u32[]{:S(2)}) %collective-permute-start.28) | collective-permute-done | bytes 786464 | tf_op jit(solution)/shard_map/ppermute | solution.py:407
  897.4 3.2 copy.140
  900.6 3.1 copy.142.refs_3_
  903.7 3.3 pad_maximum_fusion.3
  907.0 3.2 copy.139
  910.2 3.0 copy.141.refs_2_
  913.2 18.9 %weight_grad.4 = (bf16[1024,3072]{1,0:T(8,128)(2,1)}, bf16[512,3072]{1,0:T(8,128)(2,1)}, bf16[512,3072]{1,0:T(8,128)(2,1)}) custom-call(s32[1]{0:T(128)} %bitcast.1.place, bf16[512,2048]{1,0:T(8,128)(2,1)} %get-tuple-element.190.rows.refs_0_, bf16[512,2048]{1,0:T(8,128)(2,1)} %get-tuple-element.191.rows.refs_1_, bf16[512,3072]{1,0:T(8,128)(2,1)} %copy.141.refs_2_, ...), custom_call_target="tpu_custom_call" | custom-call | flops 12884901888 | bytes 12582912 | tf_op jit(solution)/shard_map/weight_grad/pallas_call | solution.py:375
  935.4 23.6 %weight_grad.7 = (bf16[1024,4096]{1,0:T(8,128)(2,1)}, bf16[512,4096]{1,0:T(8,128)(2,1)}, bf16[512,4096]{1,0:T(8,128)(2,1)}) custom-call(s32[1]{0:T(128)} %bitcast.1.place, bf16[512,2048]{1,0:T(8,128)(2,1)} %get-tuple-element.194.refs_0_, bf16[512,2048]{1,0:T(8,128)(2,1)} %get-tuple-element.193.refs_1_, bf16[512,4096]{1,0:T(8,128)(2,1)} %get-tuple-element.183.refs_2_, ...), custom_call_target="tpu_custom_call" | custom-call | flops 17179869184 | bytes 16777216 | tf_op jit(solution)/shard_map/weight_grad/pallas_call | solution.py:375
  959.0 9.8 weight_grad.5
  969.5 4.8 add_convert_fusion.7
  977.4 89.6 %collective-permute-done.43 = bf16[512,1024]{1,0:T(8,128)(2,1)S(1)} collective-permute-done((bf16[512,1024]{1,0:T(8,128)(2,1)S(1)}, bf16[512,1024]{1,0:T(8,128)(2,1)S(1)}, u32[]{:S(2)}, u32[]{:S(2)}) %collective-permute-start.43) | collective-permute-done | bytes 1048608 | tf_op jit(solution)/shard_map/ppermute | solution.py:407
  1068.7 23.6 %weight_grad.6 = (bf16[1024,4096]{1,0:T(8,128)(2,1)}, bf16[512,4096]{1,0:T(8,128)(2,1)}, bf16[512,4096]{1,0:T(8,128)(2,1)}) custom-call(s32[1]{0:T(128)} %bitcast.1.place, bf16[512,2048]{1,0:T(8,128)(2,1)} %copy-done.38, bf16[512,2048]{1,0:T(8,128)(2,1)} %get-tuple-element.239.refs_1_, bf16[512,4096]{1,0:T(8,128)(2,1)} %copy-done.26, ...), custom_call_target="tpu_custom_call" | custom-call | flops 17179869184 | bytes 16777216 | tf_op jit(solution)/shard_map/weight_grad/pallas_call | solution.py:375
  1092.3 6.4 add_convert_fusion.6
  1098.8 5.1 add_convert_fusion.1
  1105.6 91.5 %collective-permute-done.47 = bf16[512,4096]{1,0:T(8,128)(2,1)S(1)} collective-permute-done((bf16[512,4096]{1,0:T(8,128)(2,1)S(1)}, bf16[512,4096]{1,0:T(8,128)(2,1)S(1)}, u32[]{:S(2)}, u32[]{:S(2)}) %collective-permute-start.47) | collective-permute-done | bytes 4194336 | tf_op jit(solution)/shard_map/ppermute | solution.py:407
  1197.0 5.0 add_convert_fusion
  1202.1 7.3 add_convert_fusion.3
  1210.9 13.4 bitcast_convert_fusion
  1225.8 76.2 %collective-permute-done.45 = bf16[512,4096]{1,0:T(8,128)(2,1)} collective-permute-done((bf16[512,4096]{1,0:T(8,128)(2,1)}, bf16[512,4096]{1,0:T(8,128)(2,1)}, u32[]{:S(2)}, u32[]{:S(2)}) %collective-permute-start.45) | collective-permute-done | bytes 4194336 | tf_op jit(solution)/shard_map/ppermute | solution.py:407
  1302.0 7.3 add_convert_fusion.2
  1310.4 14.3 bitcast_convert_fusion.1
  1327.6 4.8 pad_maximum_fusion
  1332.5 38.2 %collective-permute-done.29 = bf16[512,2048]{1,0:T(8,128)(2,1)} collective-permute-done((bf16[512,2048]{1,0:T(8,128)(2,1)}, bf16[512,2048]{1,0:T(8,128)(2,1)}, u32[]{:S(2)}, u32[]{:S(2)}) %collective-permute-start.29) | collective-permute-done | bytes 2097184 | tf_op jit(solution)/shard_map/ppermute | solution.py:407
  1370.7 7.0 fusion.48
  1377.8 61.3 %all-reduce.1 = f32[16,576]{0,1:T(8,128)S(1)} all-reduce(f32[16,576]{0,1:T(8,128)S(1)} %pad_maximum_fusion.12), channel_id=7, replica_groups=mesh['dp'=4,'seq'=4,'mp'=2] {'dp','seq'}, use_global_device_ids=true, to_apply=%region_44.45.clone | all-reduce | flops 9216 | bytes 73728
  1443.7 5.6 psum.7
  1449.3 8.3 fusion.82
  (443 shorter events, 126.5 us)
Async XLA Ops:
  7.2 107.3 %all-gather.6.cloned.1.call-start = ((), (), s32[]{:S(2)}) async-start(), calls=%async_computation.4 | async-start | bytes 13369344 | tf_op jit(solution)/shard_map/all_gather | solution.py:557
  7.9 275.8 %all-gather.8.cloned.1.call-start = ((), (), s32[]{:S(2)}) async-start(), calls=%async_computation.5 | async-start | bytes 4456448 | tf_op jit(solution)/shard_map/all_gather | solution.py:558
  8.7 382.9 %all-gather.10.cloned.1.call-start = ((), (), s32[]{:S(2)}) async-start(), calls=%async_computation.6 | async-start | bytes 17825792 | tf_op jit(solution)/shard_map/all_gather | solution.py:559
  9.4 448.1 %all-gather.12.cloned.1.call-start = ((), (), s32[]{:S(2)}) async-start(), calls=%async_computation.7 | async-start | bytes 17825792 | tf_op jit(solution)/shard_map/all_gather | solution.py:560
  10.0 1450.1 %reduce-scatter.8.cloned.1.call-start = ((), (), s32[]{:S(2)}) async-start(), calls=%async_computation.9 | async-start | bytes 1310720 | tf_op jit(solution)/shard_map/reduce_scatter | solution.py:417
  84.4 197.3 %copy-start.60 = (f32[1024]{0:T(1024)}, f32[1024]{0:T(1024)S(1)}, u32[]{:S(2)}) copy-start(f32[1024]{0:T(1024)S(1)} %mul.632) | copy-start | bytes 12292
  93.7 293.5 %copy-start.49 = (f32[2048]{0:T(1024)}, f32[2048]{0:T(1024)S(1)}, u32[]{:S(2)}) copy-start(f32[2048]{0:T(1024)S(1)} %get-tuple-element.222) | copy-start | bytes 24580
  127.4 18.5 %collective-permute-start.10 = (bf16[3,512,256]{2,1,0:T(8,128)(2,1)}, bf16[3,512,256]{2,1,0:T(8,128)(2,1)S(1)}, u32[]{:S(2)}, u32[]{:S(2)}) collective-permute-start(bf16[3,512,256]{2,1,0:T(8,128)(2,1)} %get-tuple-element.57), channel_id=1, source_target_pairs={{0,2},{2,0},{4,6},{6,4},{1,3},{3,1},{5,7},{7,5},{8,10},{10,8},{12,... | collective-permute-start | bytes 2359304 | tf_op jit(solution)/shard_map/ppermute | solution.py:407
  127.7 23.7 %collective-permute-start.11 = (bf16[3,512,256]{2,1,0:T(8,128)(2,1)}, bf16[3,512,256]{2,1,0:T(8,128)(2,1)S(1)}, u32[]{:S(2)}, u32[]{:S(2)}) collective-permute-start(bf16[3,512,256]{2,1,0:T(8,128)(2,1)} %get-tuple-element.58), channel_id=1, source_target_pairs={{0,4},{2,6},{4,0},{6,2},{1,5},{3,7},{5,1},{7,3},{8,12},{10,14},{12... | collective-permute-start | bytes 2359304 | tf_op jit(solution)/shard_map/ppermute | solution.py:407
  128.3 46.7 %collective-permute-start.12 = (bf16[3,512,256]{2,1,0:T(8,128)(2,1)}, bf16[3,512,256]{2,1,0:T(8,128)(2,1)S(1)}, u32[]{:S(2)}, u32[]{:S(2)}) collective-permute-start(bf16[3,512,256]{2,1,0:T(8,128)(2,1)} %get-tuple-element.59), channel_id=1, source_target_pairs={{0,6},{2,4},{4,2},{6,0},{1,7},{3,5},{5,3},{7,1},{8,14},{10,12},{12... | collective-permute-start | bytes 2359304 | tf_op jit(solution)/shard_map/ppermute | solution.py:407
  144.8 65.0 %collective-permute-start = (bf16[3,512,256]{2,1,0:T(8,128)(2,1)}, bf16[3,512,256]{2,1,0:T(8,128)(2,1)S(1)}, u32[]{:S(2)}, u32[]{:S(2)}) collective-permute-start(bf16[3,512,256]{2,1,0:T(8,128)(2,1)} %get-tuple-element.49), channel_id=1, source_target_pairs={{0,2},{2,0},{4,6},{6,4},{1,3},{3,1},{5,7},{7,5},{8,10},{10,8},{12,... | collective-permute-start | bytes 2359304 | tf_op jit(solution)/shard_map/ppermute | solution.py:407
  145.4 65.2 %collective-permute-start.1 = (bf16[3,512,256]{2,1,0:T(8,128)(2,1)}, bf16[3,512,256]{2,1,0:T(8,128)(2,1)S(1)}, u32[]{:S(2)}, u32[]{:S(2)}) collective-permute-start(bf16[3,512,256]{2,1,0:T(8,128)(2,1)} %get-tuple-element.50), channel_id=1, source_target_pairs={{0,4},{2,6},{4,0},{6,2},{1,5},{3,7},{5,1},{7,3},{8,12},{10,14},{12... | collective-permute-start | bytes 2359304 | tf_op jit(solution)/shard_map/ppermute | solution.py:407
  145.9 73.9 %collective-permute-start.2 = (bf16[3,512,256]{2,1,0:T(8,128)(2,1)}, bf16[3,512,256]{2,1,0:T(8,128)(2,1)S(1)}, u32[]{:S(2)}, u32[]{:S(2)}) collective-permute-start(bf16[3,512,256]{2,1,0:T(8,128)(2,1)} %get-tuple-element.51), channel_id=1, source_target_pairs={{0,6},{2,4},{4,2},{6,0},{1,7},{3,5},{5,3},{7,1},{8,14},{10,12},{12... | collective-permute-start | bytes 2359304 | tf_op jit(solution)/shard_map/ppermute | solution.py:407
  207.7 45.9 %collective-permute-start.13 = (bf16[512,256]{1,0:T(8,128)(2,1)}, bf16[512,256]{1,0:T(8,128)(2,1)S(1)}, u32[]{:S(2)}, u32[]{:S(2)}) collective-permute-start(bf16[512,256]{1,0:T(8,128)(2,1)} %get-tuple-element.61.refs_9_), channel_id=1, source_target_pairs={{0,2},{2,0},{4,6},{6,4},{1,3},{3,1},{5,7},{7,5},{8,10},{10,8},{12,... | collective-permute-start | bytes 786440 | tf_op jit(solution)/shard_map/ppermute | solution.py:407
  209.2 44.5 %collective-permute-start.14 = (bf16[512,256]{1,0:T(8,128)(2,1)}, bf16[512,256]{1,0:T(8,128)(2,1)S(1)}, u32[]{:S(2)}, u32[]{:S(2)}) collective-permute-start(bf16[512,256]{1,0:T(8,128)(2,1)} %get-tuple-element.62.refs_10_), channel_id=1, source_target_pairs={{0,4},{2,6},{4,0},{6,2},{1,5},{3,7},{5,1},{7,3},{8,12},{10,14},{12... | collective-permute-start | bytes 786440 | tf_op jit(solution)/shard_map/ppermute | solution.py:407
  209.7 43.9 %collective-permute-start.15 = (bf16[512,256]{1,0:T(8,128)(2,1)}, bf16[512,256]{1,0:T(8,128)(2,1)S(1)}, u32[]{:S(2)}, u32[]{:S(2)}) collective-permute-start(bf16[512,256]{1,0:T(8,128)(2,1)} %get-tuple-element.63.refs_11_), channel_id=1, source_target_pairs={{0,6},{2,4},{4,2},{6,0},{1,7},{3,5},{5,3},{7,1},{8,14},{10,12},{12... | collective-permute-start | bytes 786440 | tf_op jit(solution)/shard_map/ppermute | solution.py:407
  250.6 14.8 %collective-permute-start.4 = (bf16[512,256]{1,0:T(8,128)(2,1)}, bf16[512,256]{1,0:T(8,128)(2,1)S(1)}, u32[]{:S(2)}, u32[]{:S(2)}) collective-permute-start(bf16[512,256]{1,0:T(8,128)(2,1)} %get-tuple-element.54.refs_10_), channel_id=1, source_target_pairs={{0,4},{2,6},{4,0},{6,2},{1,5},{3,7},{5,1},{7,3},{8,12},{10,14},{12... | collective-permute-start | bytes 786440 | tf_op jit(solution)/shard_map/ppermute | solution.py:407
  251.7 25.6 %collective-permute-start.5 = (bf16[512,256]{1,0:T(8,128)(2,1)}, bf16[512,256]{1,0:T(8,128)(2,1)S(1)}, u32[]{:S(2)}, u32[]{:S(2)}) collective-permute-start(bf16[512,256]{1,0:T(8,128)(2,1)} %get-tuple-element.55.refs_11_), channel_id=1, source_target_pairs={{0,6},{2,4},{4,2},{6,0},{1,7},{3,5},{5,3},{7,1},{8,14},{10,12},{12... | collective-permute-start | bytes 786440 | tf_op jit(solution)/shard_map/ppermute | solution.py:407
  253.6 23.7 %collective-permute-start.3 = (bf16[512,256]{1,0:T(8,128)(2,1)}, bf16[512,256]{1,0:T(8,128)(2,1)S(1)}, u32[]{:S(2)}, u32[]{:S(2)}) collective-permute-start(bf16[512,256]{1,0:T(8,128)(2,1)} %get-tuple-element.53.refs_9_), channel_id=1, source_target_pairs={{0,2},{2,0},{4,6},{6,4},{1,3},{3,1},{5,7},{7,5},{8,10},{10,8},{12,... | collective-permute-start | bytes 786440 | tf_op jit(solution)/shard_map/ppermute | solution.py:407
  254.4 25.1 %collective-permute-start.16 = (f32[2,512]{1,0:T(2,128)S(1)}, f32[2,512]{1,0:T(2,128)S(1)}, u32[]{:S(2)}, u32[]{:S(2)}) collective-permute-start(f32[2,512]{1,0:T(2,128)S(1)} %pad_maximum_fusion.15), channel_id=1, source_target_pairs={{0,1},{1,0},{2,3},{3,2},{4,5},{5,4},{6,7},{7,6},{8,9},{9,8},{10,11... | collective-permute-start | bytes 12296 | tf_op jit(solution)/shard_map/ppermute | solution.py:407
  278.1 3.7 collective-permute-start.6
  288.8 48.7 %collective-permute-start.17 = (bf16[512,2048]{1,0:T(8,128)(2,1)S(1)}, bf16[512,2048]{1,0:T(8,128)(2,1)}, u32[]{:S(2)}, u32[]{:S(2)}) collective-permute-start(bf16[512,2048]{1,0:T(8,128)(2,1)S(1)} %convolution_convert_fusion), channel_id=1, source_target_pairs={{0,1},{1,0},{2,3},{3,2},{4,5},{5,4},{6,7},{7,6},{8,9},{9,8},{10,11... | collective-permute-start | bytes 6291464 | tf_op jit(solution)/shard_map/ppermute | solution.py:407
  294.0 86.4 %collective-permute-start.7 = (bf16[512,2048]{1,0:T(8,128)(2,1)}, bf16[512,2048]{1,0:T(8,128)(2,1)}, u32[]{:S(2)}, u32[]{:S(2)}) collective-permute-start(bf16[512,2048]{1,0:T(8,128)(2,1)} %convolution_convert_fusion.1), channel_id=1, source_target_pairs={{0,1},{1,0},{2,3},{3,2},{4,5},{5,4},{6,7},{7,6},{8,9},{9,8},{10,11... | collective-permute-start | bytes 6291464 | tf_op jit(solution)/shard_map/ppermute | solution.py:407
  425.7 47.2 %collective-permute-start.18 = (f32[2,512]{1,0:T(2,128)S(1)}, f32[2,512]{1,0:T(2,128)S(1)}, u32[]{:S(2)}, u32[]{:S(2)}) collective-permute-start(f32[2,512]{1,0:T(2,128)S(1)} %pad_maximum_fusion.16), channel_id=1, source_target_pairs={{0,1},{1,0},{2,3},{3,2},{4,5},{5,4},{6,7},{7,6},{8,9},{9,8},{10,11... | collective-permute-start | bytes 12296 | tf_op jit(solution)/shard_map/ppermute | solution.py:407
  456.9 16.1 %collective-permute-start.8 = (f32[2,512]{1,0:T(2,128)S(1)}, f32[2,512]{1,0:T(2,128)S(1)}, u32[]{:S(2)}, u32[]{:S(2)}) collective-permute-start(f32[2,512]{1,0:T(2,128)S(1)} %pad_maximum_fusion.14), channel_id=1, source_target_pairs={{0,1},{1,0},{2,3},{3,2},{4,5},{5,4},{6,7},{7,6},{8,9},{9,8},{10,11... | collective-permute-start | bytes 12296 | tf_op jit(solution)/shard_map/ppermute | solution.py:407
  496.5 3.6 collective-permute-start.30
  498.0 3.7 collective-permute-start.20
  545.3 48.7 %collective-permute-start.31 = (bf16[512,2048]{1,0:T(8,128)(2,1)S(1)}, bf16[512,2048]{1,0:T(8,128)(2,1)}, u32[]{:S(2)}, u32[]{:S(2)}) collective-permute-start(bf16[512,2048]{1,0:T(8,128)(2,1)S(1)} %convolution_convert_fusion.2), channel_id=1, source_target_pairs={{0,1},{1,0},{2,3},{3,2},{4,5},{5,4},{6,7},{7,6},{8,9},{9,8},{10,11... | collective-permute-start | bytes 6291464 | tf_op jit(solution)/shard_map/ppermute | solution.py:407
  560.6 78.4 %collective-permute-start.9 = (bf16[512,2048]{1,0:T(8,128)(2,1)}, bf16[512,2048]{1,0:T(8,128)(2,1)}, u32[]{:S(2)}, u32[]{:S(2)}) collective-permute-start(bf16[512,2048]{1,0:T(8,128)(2,1)} %convolution_convert_fusion.5), channel_id=1, source_target_pairs={{0,1},{1,0},{2,3},{3,2},{4,5},{5,4},{6,7},{7,6},{8,9},{9,8},{10,11... | collective-permute-start | bytes 6291464 | tf_op jit(solution)/shard_map/ppermute | solution.py:407
  575.5 108.3 %collective-permute-start.21 = (bf16[512,2048]{1,0:T(8,128)(2,1)}, bf16[512,2048]{1,0:T(8,128)(2,1)S(1)}, u32[]{:S(2)}, u32[]{:S(2)}) collective-permute-start(bf16[512,2048]{1,0:T(8,128)(2,1)} %convolution_convert_fusion.3), channel_id=1, source_target_pairs={{0,1},{1,0},{2,3},{3,2},{4,5},{5,4},{6,7},{7,6},{8,9},{9,8},{10,11... | collective-permute-start | bytes 6291464 | tf_op jit(solution)/shard_map/ppermute | solution.py:407
  576.1 107.8 %copy-start.50 = (f32[2048]{0:T(1024)S(1)}, f32[2048]{0:T(1024)}, u32[]{:S(2)}) copy-start(f32[2048]{0:T(1024)} %copy-done.49) | copy-start | bytes 24580
  576.1 107.8 %copy-start.57 = (f32[512]{0:T(512)S(1)}, f32[512]{0:T(512)}, u32[]{:S(2)}) copy-start(f32[512]{0:T(512)} %copy-done.56) | copy-start | bytes 6148
  576.1 107.8 %copy-start.59 = (f32[512]{0:T(512)S(1)}, f32[512]{0:T(512)}, u32[]{:S(2)}) copy-start(f32[512]{0:T(512)} %copy-done.58) | copy-start | bytes 6148
  576.1 107.8 %copy-start.73 = (f32[512]{0:T(512)S(1)}, f32[512]{0:T(512)}, u32[]{:S(2)}) copy-start(f32[512]{0:T(512)} %copy-done.72) | copy-start | bytes 6148
  576.1 107.8 %copy-start.75 = (f32[512]{0:T(512)S(1)}, f32[512]{0:T(512)}, u32[]{:S(2)}) copy-start(f32[512]{0:T(512)} %copy-done.74) | copy-start | bytes 6148
  590.1 134.0 %copy-start.6 = (bf16[2,512,2048]{2,1,0:T(8,128)(2,1)S(1)}, bf16[2,512,2048]{2,1,0:T(8,128)(2,1)}, u32[]{:S(2)}) copy-start(bf16[2,512,2048]{2,1,0:T(8,128)(2,1)} %param.21) | copy-start | bytes 12582916
  590.1 134.0 %collective-permute-start.19 = (bf16[512,2048]{1,0:T(8,128)(2,1)S(1)}, bf16[512,2048]{1,0:T(8,128)(2,1)}, u32[]{:S(2)}, u32[]{:S(2)}) collective-permute-start(bf16[512,2048]{1,0:T(8,128)(2,1)S(1)} %convolution_convert_fusion.4), channel_id=1, source_target_pairs={{0,1},{1,0},{2,3},{3,2},{4,5},{5,4},{6,7},{7,6},{8,9},{9,8},{10,11... | collective-permute-start | bytes 6291464 | tf_op jit(solution)/shard_map/ppermute | solution.py:407
  744.3 3.6 collective-permute-start.22
  744.9 3.7 collective-permute-start.32
  751.1 4.5 collective-permute-start.33
  751.1 9.1 collective-permute-start.34
  752.6 12.4 collective-permute-start.35
  753.8 60.1 %collective-permute-start.23 = (bf16[512,256]{1,0:T(8,128)(2,1)S(1)}, bf16[512,256]{1,0:T(8,128)(2,1)S(1)}, u32[]{:S(2)}, u32[]{:S(2)}) collective-permute-start(bf16[512,256]{1,0:T(8,128)(2,1)S(1)} %get-tuple-element.212), channel_id=1, source_target_pairs={{0,2},{2,0},{4,6},{6,4},{1,3},{3,1},{5,7},{7,5},{8,10},{10,8},{12,... | collective-permute-start | bytes 786440 | tf_op jit(solution)/shard_map/ppermute | solution.py:407
  754.1 59.8 %collective-permute-start.24 = (bf16[512,256]{1,0:T(8,128)(2,1)S(1)}, bf16[512,256]{1,0:T(8,128)(2,1)S(1)}, u32[]{:S(2)}, u32[]{:S(2)}) collective-permute-start(bf16[512,256]{1,0:T(8,128)(2,1)S(1)} %get-tuple-element.211), channel_id=1, source_target_pairs={{0,4},{2,6},{4,0},{6,2},{1,5},{3,7},{5,1},{7,3},{8,12},{10,14},{12... | collective-permute-start | bytes 786440 | tf_op jit(solution)/shard_map/ppermute | solution.py:407
  755.6 58.3 %collective-permute-start.25 = (bf16[512,256]{1,0:T(8,128)(2,1)S(1)}, bf16[512,256]{1,0:T(8,128)(2,1)S(1)}, u32[]{:S(2)}, u32[]{:S(2)}) collective-permute-start(bf16[512,256]{1,0:T(8,128)(2,1)S(1)} %get-tuple-element.210), channel_id=1, source_target_pairs={{0,6},{2,4},{4,2},{6,0},{1,7},{3,5},{5,3},{7,1},{8,14},{10,12},{12... | collective-permute-start | bytes 786440 | tf_op jit(solution)/shard_map/ppermute | solution.py:407
  811.8 47.5 %collective-permute-start.36 = (bf16[3,512,256]{2,1,0:T(8,128)(2,1)}, bf16[3,512,256]{2,1,0:T(8,128)(2,1)S(1)}, u32[]{:S(2)}, u32[]{:S(2)}) collective-permute-start(bf16[3,512,256]{2,1,0:T(8,128)(2,1)} %get-tuple-element.71), channel_id=1, source_target_pairs={{0,2},{2,0},{4,6},{6,4},{1,3},{3,1},{5,7},{7,5},{8,10},{10,8},{12,... | collective-permute-start | bytes 2359304 | tf_op jit(solution)/shard_map/ppermute | solution.py:407
  812.4 46.9 %collective-permute-start.37 = (bf16[3,512,256]{2,1,0:T(8,128)(2,1)}, bf16[3,512,256]{2,1,0:T(8,128)(2,1)S(1)}, u32[]{:S(2)}, u32[]{:S(2)}) collective-permute-start(bf16[3,512,256]{2,1,0:T(8,128)(2,1)} %get-tuple-element.72), channel_id=1, source_target_pairs={{0,4},{2,6},{4,0},{6,2},{1,5},{3,7},{5,1},{7,3},{8,12},{10,14},{12... | collective-permute-start | bytes 2359304 | tf_op jit(solution)/shard_map/ppermute | solution.py:407
  813.9 45.4 %collective-permute-start.38 = (bf16[3,512,256]{2,1,0:T(8,128)(2,1)}, bf16[3,512,256]{2,1,0:T(8,128)(2,1)S(1)}, u32[]{:S(2)}, u32[]{:S(2)}) collective-permute-start(bf16[3,512,256]{2,1,0:T(8,128)(2,1)} %get-tuple-element.73), channel_id=1, source_target_pairs={{0,6},{2,4},{4,2},{6,0},{1,7},{3,5},{5,3},{7,1},{8,14},{10,12},{12... | collective-permute-start | bytes 2359304 | tf_op jit(solution)/shard_map/ppermute | solution.py:407
  857.2 3.0 collective-permute-start.26
  857.7 20.6 %collective-permute-start.27 = (bf16[3,512,256]{2,1,0:T(8,128)(2,1)}, bf16[3,512,256]{2,1,0:T(8,128)(2,1)S(1)}, u32[]{:S(2)}, u32[]{:S(2)}) collective-permute-start(bf16[3,512,256]{2,1,0:T(8,128)(2,1)} %get-tuple-element.67), channel_id=1, source_target_pairs={{0,4},{2,6},{4,0},{6,2},{1,5},{3,7},{5,1},{7,3},{8,12},{10,14},{12... | collective-permute-start | bytes 2359304 | tf_op jit(solution)/shard_map/ppermute | solution.py:407
  859.2 34.2 %collective-permute-start.28 = (bf16[3,512,256]{2,1,0:T(8,128)(2,1)}, bf16[3,512,256]{2,1,0:T(8,128)(2,1)S(1)}, u32[]{:S(2)}, u32[]{:S(2)}) collective-permute-start(bf16[3,512,256]{2,1,0:T(8,128)(2,1)} %get-tuple-element.68), channel_id=1, source_target_pairs={{0,6},{2,4},{4,2},{6,0},{1,7},{3,5},{5,3},{7,1},{8,14},{10,12},{12... | collective-permute-start | bytes 2359304 | tf_op jit(solution)/shard_map/ppermute | solution.py:407
  932.1 37.3 %collective-permute-start.40 = (bf16[1024,3072]{1,0:T(8,128)(2,1)}, bf16[1024,3072]{1,0:T(8,128)(2,1)}, u32[]{:S(2)}, u32[]{:S(2)}) collective-permute-start(bf16[1024,3072]{1,0:T(8,128)(2,1)} %get-tuple-element.75), channel_id=1, source_target_pairs={{0,2},{2,0},{4,6},{6,4},{1,3},{3,1},{5,7},{7,5},{8,10},{10,8},{12,... | collective-permute-start | bytes 18874376 | tf_op jit(solution)/shard_map/ppermute | solution.py:407
  959.0 139.8 %collective-permute-start.46 = (bf16[1024,4096]{1,0:T(8,128)(2,1)}, bf16[1024,4096]{1,0:T(8,128)(2,1)}, u32[]{:S(2)}, u32[]{:S(2)}) collective-permute-start(bf16[1024,4096]{1,0:T(8,128)(2,1)} %get-tuple-element.84), channel_id=1, source_target_pairs={{0,2},{2,0},{4,6},{6,4},{1,3},{3,1},{5,7},{7,5},{8,10},{10,8},{12,... | collective-permute-start | bytes 25165832 | tf_op jit(solution)/shard_map/ppermute | solution.py:407
  968.8 7.0 collective-permute-start.42
  974.3 118.1 %collective-permute-start.41 = (bf16[512,3072]{1,0:T(8,128)(2,1)}, bf16[512,3072]{1,0:T(8,128)(2,1)}, u32[]{:S(2)}, u32[]{:S(2)}) collective-permute-start(bf16[512,3072]{1,0:T(8,128)(2,1)} %add_convert_fusion.7), channel_id=1, source_target_pairs={{0,4},{2,6},{4,0},{6,2},{1,5},{3,7},{5,1},{7,3},{8,12},{10,14},{12... | collective-permute-start | bytes 9437192 | tf_op jit(solution)/shard_map/ppermute | solution.py:407
  976.2 90.8 %collective-permute-start.43 = (bf16[512,1024]{1,0:T(8,128)(2,1)S(1)}, bf16[512,1024]{1,0:T(8,128)(2,1)S(1)}, u32[]{:S(2)}, u32[]{:S(2)}) collective-permute-start(bf16[512,1024]{1,0:T(8,128)(2,1)S(1)} %add_convert_fusion.11), channel_id=1, source_target_pairs={{0,4},{2,6},{4,0},{6,2},{1,5},{3,7},{5,1},{7,3},{8,12},{10,14},{12... | collective-permute-start | bytes 3145736 | tf_op jit(solution)/shard_map/ppermute | solution.py:407
  1068.7 393.4 %reduce-scatter.6.cloned.1.call-start = ((), (), s32[]{:S(2)}) async-start(), calls=%async_computation.8 | async-start | bytes 3932160 | tf_op jit(solution)/shard_map/reduce_scatter | solution.py:417
  1092.3 109.8 %collective-permute-start.44 = (bf16[1024,4096]{1,0:T(8,128)(2,1)}, bf16[1024,4096]{1,0:T(8,128)(2,1)}, u32[]{:S(2)}, u32[]{:S(2)}) collective-permute-start(bf16[1024,4096]{1,0:T(8,128)(2,1)} %get-tuple-element.81), channel_id=1, source_target_pairs={{0,2},{2,0},{4,6},{6,4},{1,3},{3,1},{5,7},{7,5},{8,10},{10,8},{12,... | collective-permute-start | bytes 25165832 | tf_op jit(solution)/shard_map/ppermute | solution.py:407
  1098.8 366.3 %reduce-scatter.12.cloned.1.call-start = ((), (), s32[]{:S(2)}) async-start(), calls=%async_computation.11 | async-start | bytes 5242880 | tf_op jit(solution)/shard_map/reduce_scatter | solution.py:417
  1104.0 93.0 %collective-permute-start.47 = (bf16[512,4096]{1,0:T(8,128)(2,1)S(1)}, bf16[512,4096]{1,0:T(8,128)(2,1)S(1)}, u32[]{:S(2)}, u32[]{:S(2)}) collective-permute-start(bf16[512,4096]{1,0:T(8,128)(2,1)S(1)} %add_convert_fusion.1), channel_id=1, source_target_pairs={{0,4},{2,6},{4,0},{6,2},{1,5},{3,7},{5,1},{7,3},{8,12},{10,14},{12... | collective-permute-start | bytes 12582920 | tf_op jit(solution)/shard_map/ppermute | solution.py:407
  1202.1 266.2 %reduce-scatter.10.cloned.1.call-start = ((), (), s32[]{:S(2)}) async-start(), calls=%async_computation.10 | async-start | bytes 5242880 | tf_op jit(solution)/shard_map/reduce_scatter | solution.py:417
  1209.4 92.5 %collective-permute-start.45 = (bf16[512,4096]{1,0:T(8,128)(2,1)}, bf16[512,4096]{1,0:T(8,128)(2,1)}, u32[]{:S(2)}, u32[]{:S(2)}) collective-permute-start(bf16[512,4096]{1,0:T(8,128)(2,1)} %add_convert_fusion.3), channel_id=1, source_target_pairs={{0,4},{2,6},{4,0},{6,2},{1,5},{3,7},{5,1},{7,3},{8,12},{10,14},{12... | collective-permute-start | bytes 12582920 | tf_op jit(solution)/shard_map/ppermute | solution.py:407
  1224.3 108.2 %collective-permute-start.39 = (bf16[512,2048]{1,0:T(8,128)(2,1)S(1)}, bf16[512,2048]{1,0:T(8,128)(2,1)}, u32[]{:S(2)}, u32[]{:S(2)}) collective-permute-start(bf16[512,2048]{1,0:T(8,128)(2,1)S(1)} %get-tuple-element.276), channel_id=1, source_target_pairs={{0,1},{1,0},{2,3},{3,2},{4,5},{5,4},{6,7},{7,6},{8,9},{9,8},{10,11... | collective-permute-start | bytes 6291464 | tf_op jit(solution)/shard_map/ppermute | solution.py:407
  1324.7 45.9 %collective-permute-start.29 = (bf16[512,2048]{1,0:T(8,128)(2,1)}, bf16[512,2048]{1,0:T(8,128)(2,1)}, u32[]{:S(2)}, u32[]{:S(2)}) collective-permute-start(bf16[512,2048]{1,0:T(8,128)(2,1)} %get-tuple-element.274), channel_id=1, source_target_pairs={{0,1},{1,0},{2,3},{3,2},{4,5},{5,4},{6,7},{7,6},{8,9},{9,8},{10,11... | collective-permute-start | bytes 6291464 | tf_op jit(solution)/shard_map/ppermute | solution.py:407
  (97 other events, 1893.1 us)
Sparse Core Ops, SparseCore 0:
  10.2 104.1 all-gather.5
  116.6 62.8 all-gather.7
  181.7 140.4 all-gather.9
  324.2 128.4 all-gather.11
  1068.8 26.1 reduce-scatter.7
  1098.9 59.4 reduce-scatter.5
  1202.2 75.7 reduce-scatter.11
  1309.4 75.9 reduce-scatter.9

commit v2 on v1

v2 whole, which is shorter than its diff:
```python
from functools import partial

import jax
import jax.numpy as jnp
from jax import lax
from jax.experimental import pallas as pl
from jax.experimental.pallas import tpu as pltpu
from jax.sharding import PartitionSpec as P

HEAD_DIM = 64
HALF = HEAD_DIM // 2
XPOS_BASE = 512
EPSILON = 1e-05
NEGATIVE = -1e30
LOG2_E = 1.4426950408889634
SCORE_SCALE = 0.125
VMEM = 56 * 2**20
Z_FIRST = True
BF16 = jnp.bfloat16
KERNEL_RATE = 0.25e9
BACK_WEIGHT = 25


def lasting(us):
    return pl.CostEstimate(flops=int(us * KERNEL_RATE), bytes_accessed=0, transcendentals=0)


F32 = jnp.float32


def params(limit=VMEM):
    return pltpu.CompilerParams(vmem_limit_bytes=limit)


def dot(left, right, left_dim, right_dim):
    return lax.dot_general(
        left, right, (((left_dim,), (right_dim,)), ((), ())), preferred_element_type=F32
    )


def swap_halves(block):
    width = block.shape[1]
    if width % 128:
        pieces = []
        for start in range(0, width, HEAD_DIM):
            pieces += [block[:, start + HALF : start + HEAD_DIM], block[:, start : start + HALF]]
        return jnp.concatenate(pieces, axis=1)
    lane = lax.broadcasted_iota(jnp.int32, (block.shape[0], 128), 1) % HEAD_DIM
    pieces = []
    for start in range(0, width, 128):
        part = block[:, start : start + 128]
        pieces.append(
            jnp.where(lane < HALF, pltpu.roll(part, 128 - HALF, 1), pltpu.roll(part, HALF, 1))
        )
    return pieces[0] if len(pieces) == 1 else jnp.concatenate(pieces, axis=1)


def turned(block, cosine, sine, sign):
    lanes = cosine.shape[1]
    pieces = []
    for start in range(0, block.shape[1], lanes):
        part = block[:, start : start + lanes]
        pieces.append(part * cosine + sign * (swap_halves(part) * sine))
    return pieces[0] if len(pieces) == 1 else jnp.concatenate(pieces, axis=1)


def project_kernel(place, rows, weight, cos_q, sin_q, cos_k, sin_k, *outs, extra):
    outs = outs[extra:]
    step = pl.program_id(0)
    block = rows[...]
    made = [dot(block, weight[j], 1, 0) for j in range(3)]
    made[0] = turned(made[0], cos_q[...], sin_q[...], 1)
    made[1] = turned(made[1], cos_k[...], sin_k[...], 1)
    for offset, out in enumerate(outs):

        @pl.when(step == offset)
        def _(out=out):
            for j in range(3):
                out[j] = made[j].astype(BF16)


def project(place, rows, qkv_full, tables, groups, after=()):
    span, width = rows.shape
    local = qkv_full.shape[2]
    share = local // groups
    if share % 128:
        weight = qkv_full.reshape(3, width, groups, share).transpose(2, 0, 1, 3)
        weight_spec = pl.BlockSpec(
            (None, 3, width, share), lambda o, p: (jnp.bitwise_xor(o, p[0]), 0, 0, 0)
        )
    else:
        weight = qkv_full
        weight_spec = pl.BlockSpec(
            (3, width, share), lambda o, p: (0, 0, jnp.bitwise_xor(o, p[0]))
        )
    table_spec = pl.BlockSpec(tables[0].shape, lambda o, p: (0, 0))
    return pl.pallas_call(
        partial(project_kernel, extra=len(after)),
        grid_spec=pltpu.PrefetchScalarGridSpec(
            num_scalar_prefetch=1,
            grid=(groups,),
            in_specs=[pl.BlockSpec((span, width), lambda o, p: (0, 0)), weight_spec]
            + [table_spec] * 4
            + [pl.BlockSpec(memory_space=pl.ANY)] * len(after),
            out_specs=[pl.BlockSpec((3, span, share), lambda o, p: (0, 0, 0))] * groups,
        ),
        out_shape=[jax.ShapeDtypeStruct((3, span, share), BF16)] * groups,
        compiler_params=params(),
        cost_estimate=lasting(1.2e-8 * span * width * local),
        name="project",
    )(place, rows, weight, *tables, *after)


def attend_kernel(meta, *refs, groups, heads, block, extra):
    messages, rest = refs[:groups], refs[groups + extra :]
    outs, log_ref = rest[:groups], rest[groups]
    q_all, k_all, vt_all, o_all = rest[groups + 1 :]
    step = pl.program_id(0)
    length, place = meta[0], meta[1]
    span = messages[0].shape[1]

    @pl.when(step == 0)
    def _():
        for offset, message in enumerate(messages):
            at = pl.multiple_of(jnp.bitwise_xor(place, offset) * span, span)
            q_all[pl.ds(at, span), :] = message[0]
            k_all[pl.ds(at, span), :] = message[1]
            for h in range(heads):
                lanes = slice(h * HEAD_DIM, (h + 1) * HEAD_DIM)
                vt_all[h, :, pl.ds(at, span)] = message[2, :, lanes].T

    start = pl.multiple_of(step * block, block)
    queries = [
        q_all[pl.ds(start, block), h * HEAD_DIM : (h + 1) * HEAD_DIM] for h in range(heads)
    ]
    scale = SCORE_SCALE * LOG2_E

    def keys_block(index, carry, masked):
        at = pl.multiple_of(index * block, block)
        if masked:
            key_pos = at + lax.broadcasted_iota(jnp.int32, (block, block), 0)
            query_pos = start + lax.broadcasted_iota(jnp.int32, (block, block), 1)
            allowed = (key_pos <= query_pos) & (key_pos < length)
        new = []
        for h in range(heads):
            top, total, mixed = carry[h]
            keys = k_all[pl.ds(at, block), h * HEAD_DIM : (h + 1) * HEAD_DIM]
            scores = dot(keys, queries[h], 1, 1)
            if masked:
                scores = jnp.where(allowed, scores, NEGATIVE)
            higher = jnp.maximum(top, jnp.max(scores, axis=0, keepdims=True))
            fade = jnp.exp2((top - higher) * scale)
            weights = jnp.exp2((scores - higher) * scale)
            total = total * fade + jnp.sum(weights, axis=0, keepdims=True)
            added = dot(vt_all[h, :, pl.ds(at, block)], weights.astype(BF16), 1, 0)
            new.append((higher, total, mixed * fade + added))
        return tuple(new)

    carry = tuple(
        (
            jnp.full((1, block), NEGATIVE, F32),
            jnp.zeros((1, block), F32),
            jnp.zeros((HEAD_DIM, block), F32),
        )
        for _ in range(heads)
    )
    whole = jnp.minimum(step, length // block)
    end = jnp.minimum(step + 1, (length + block - 1) // block)
    carry = lax.fori_loop(0, whole, lambda n, c: keys_block(n, c, False), carry)
    carry = lax.fori_loop(whole, end, lambda n, c: keys_block(n, c, True), carry)
    pieces = []
    for h in range(heads):
        top, total, mixed = carry[h]
        pieces.append((mixed / total).T)
        log_ref[h : h + 1, :] = top * scale + jnp.log2(total)
    o_all[pl.ds(start, block), :] = jnp.concatenate(pieces, axis=1).astype(BF16)

    @pl.when(step == pl.num_programs(0) - 1)
    def _():
        for offset, out in enumerate(outs):
            at = pl.multiple_of(jnp.bitwise_xor(place, offset) * span, span)
            out[...] = o_all[pl.ds(at, span), :]


def attend(meta, messages, after=()):
    groups = len(messages)
    _, span, share = messages[0].shape
    heads = share // HEAD_DIM
    count = groups * span
    block = min(512, span)
    message_spec = pl.BlockSpec((3, span, share), lambda n, m: (0, 0, 0))
    out_spec = pl.BlockSpec((span, share), lambda n, m: (0, 0))
    results = pl.pallas_call(
        partial(attend_kernel, groups=groups, heads=heads, block=block, extra=len(after)),
        grid_spec=pltpu.PrefetchScalarGridSpec(
            num_scalar_prefetch=1,
            grid=(count // block,),
            in_specs=[message_spec] * groups
            + [pl.BlockSpec(memory_space=pl.ANY)] * len(after),
            out_specs=[out_spec] * groups + [pl.BlockSpec((heads, block), lambda n, m: (0, n))],
            scratch_shapes=[
                pltpu.VMEM((count, share), BF16),
                pltpu.VMEM((count, share), BF16),
                pltpu.VMEM((heads, HEAD_DIM, count), BF16),
                pltpu.VMEM((count, share), BF16),
            ],
        ),
        out_shape=[jax.ShapeDtypeStruct((span, share), BF16)] * groups
        + [jax.ShapeDtypeStruct((heads, count), F32)],
        compiler_params=params(),
        cost_estimate=lasting(2.9e-8 * count * count * share),
        name="attend",
    )(meta, *messages, *after)
    return results[:groups], results[groups]


def attend_back_kernel(meta, *refs, groups, heads, block, extra):
    messages, grads, mixed = refs[:groups], refs[groups : 2 * groups], refs[2 * groups : 3 * groups]
    log_ref, cos_q, sin_q, cos_k, sin_k = refs[3 * groups : 3 * groups + 5]
    refs = refs[3 * groups + 5 + extra :]
    outs, scratch = refs[:groups], refs[groups:]
    q_all, k_all, v_all, g_all, kt_all, dot_all, dqt_all, dk_sum, dv_sum, out_all = scratch
    length, place = meta[0], meta[1]
    span = messages[0].shape[1]
    count = groups * span
    scale = SCORE_SCALE * LOG2_E

    def lanes(h):
        return slice(h * HEAD_DIM, (h + 1) * HEAD_DIM)

    for offset in range(groups):
        at = pl.multiple_of(jnp.bitwise_xor(place, offset) * span, span)
        message = messages[offset]
        q_all[pl.ds(at, span), :] = message[0]
        k_all[pl.ds(at, span), :] = message[1]
        v_all[pl.ds(at, span), :] = message[2]
        g_all[pl.ds(at, span), :] = grads[offset][...]
        both = grads[offset][...].astype(F32) * mixed[offset][...].astype(F32)
        for h in range(heads):
            kt_all[h, :, pl.ds(at, span)] = message[1, :, lanes(h)].T
            dot_all[h : h + 1, pl.ds(at, span)] = jnp.sum(
                both[:, lanes(h)].T, axis=0, keepdims=True
            )
    dqt_all[...] = jnp.zeros_like(dqt_all)
    query_blocks = count // block

    def keys_block(index, _):
        key_at = pl.multiple_of(index * block, block)
        keys = [k_all[pl.ds(key_at, block), lanes(h)] for h in range(heads)]
        values = [v_all[pl.ds(key_at, block), lanes(h)] for h in range(heads)]
        dk_sum[...] = jnp.zeros_like(dk_sum)
        dv_sum[...] = jnp.zeros_like(dv_sum)

        def query_block(index, _, masked):
            at = pl.multiple_of(index * block, block)
            if masked:
                key_pos = key_at + lax.broadcasted_iota(jnp.int32, (block, block), 0)
                query_pos = at + lax.broadcasted_iota(jnp.int32, (block, block), 1)
                allowed = (key_pos <= query_pos) & (key_pos < length)
            for h in range(heads):
                query = q_all[pl.ds(at, block), lanes(h)]
                grad = g_all[pl.ds(at, block), lanes(h)]
                scores = dot(keys[h], query, 1, 1)
                weights = jnp.exp2(scores * scale - log_ref[h : h + 1, pl.ds(at, block)])
                if masked:
                    weights = jnp.where(allowed, weights, 0.0)
                grad_weights = dot(values[h], grad, 1, 1)
                grad_scores = weights * (grad_weights - dot_all[h : h + 1, pl.ds(at, block)])
                grad_scores = grad_scores.astype(BF16)
                dv_sum[h] += dot(weights.astype(BF16), grad, 1, 0)
                dk_sum[h] += dot(grad_scores, query, 1, 0)
                dqt_all[h, :, pl.ds(at, block)] += dot(
                    kt_all[h, :, pl.ds(key_at, block)], grad_scores, 1, 0
                )
            return 0

        crosses = key_at + block > length
        whole = jnp.where(crosses, query_blocks, index + 1)
        lax.fori_loop(index, whole, partial(query_block, masked=True), 0)
        lax.fori_loop(whole, query_blocks, partial(query_block, masked=False), 0)
        dk = jnp.concatenate([dk_sum[h] for h in range(heads)], axis=1) * SCORE_SCALE
        dv = jnp.concatenate([dv_sum[h] for h in range(heads)], axis=1)
        turn = (cos_k[pl.ds(key_at, block), :], sin_k[pl.ds(key_at, block), :])
        out_all[1, pl.ds(key_at, block), :] = turned(dk, *turn, -1).astype(BF16)
        out_all[2, pl.ds(key_at, block), :] = dv.astype(BF16)
        return 0

    used = (length + block - 1) // block
    lax.fori_loop(0, used, keys_block, 0)

    def no_keys(index, _):
        at = pl.multiple_of(index * block, block)
        for j in (1, 2):
            out_all[j, pl.ds(at, block), :] = jnp.zeros((block, heads * HEAD_DIM), BF16)
        return 0

    lax.fori_loop(used, query_blocks, no_keys, 0)
    for index in range(query_blocks):
        at = slice(index * block, (index + 1) * block)
        dq = jnp.concatenate([dqt_all[h, :, at].T for h in range(heads)], axis=1) * SCORE_SCALE
        out_all[0, at, :] = turned(dq, cos_q[at, :], sin_q[at, :], -1).astype(BF16)
    for offset, out in enumerate(outs):
        at = pl.multiple_of(jnp.bitwise_xor(place, offset) * span, span)
        out[...] = out_all[:, pl.ds(at, span), :]


def attend_back(meta, messages, grads, mixed, logs, tables, after=(), weight=1):
    groups = len(messages)
    _, span, share = messages[0].shape
    heads = share // HEAD_DIM
    count = groups * span
    block = min(512, span)
    message_spec = pl.BlockSpec((3, span, share), lambda n, m: (0, 0, 0))
    row_spec = pl.BlockSpec((span, share), lambda n, m: (0, 0))
    table_spec = pl.BlockSpec(tables[0].shape, lambda n, m: (0, 0))
    return pl.pallas_call(
        partial(
            attend_back_kernel, groups=groups, heads=heads, block=block, extra=len(after)
        ),
        grid_spec=pltpu.PrefetchScalarGridSpec(
            num_scalar_prefetch=1,
            grid=(1,),
            in_specs=[message_spec] * groups
            + [row_spec] * (2 * groups)
            + [pl.BlockSpec(logs.shape, lambda n, m: (0, 0))]
            + [table_spec] * 4
            + [pl.BlockSpec(memory_space=pl.ANY)] * len(after),
            out_specs=[message_spec] * groups,
            scratch_shapes=[pltpu.VMEM((count, share), BF16)] * 4
            + [
                pltpu.VMEM((heads, HEAD_DIM, count), BF16),
                pltpu.VMEM((heads, count), F32),
                pltpu.VMEM((heads, HEAD_DIM, count), F32),
                pltpu.VMEM((heads, block, HEAD_DIM), F32),
                pltpu.VMEM((heads, block, HEAD_DIM), F32),
                pltpu.VMEM((3, count, share), BF16),
            ],
        ),
        out_shape=[jax.ShapeDtypeStruct((3, span, share), BF16)] * groups,
        compiler_params=params(),
        cost_estimate=lasting(4.2e-8 * count * count * share * weight),
        name="attend_back",
    )(meta, *messages, *grads, *mixed, logs, *tables, *after)


def normed_rows(block, column_mean, column_std, gain):
    return (block.astype(F32) - column_mean) * column_std * gain


def moments(own, other, width):
    total = own + other
    mean = total[0:1] / width
    return mean, lax.rsqrt(total[1:2] / width - mean * mean + EPSILON)


def as_column(row):
    return jnp.broadcast_to(row, (128, row.shape[1])).T[:, 0:1]


def as_row(block):
    width = block.shape[1]
    part = block[:, 0:128]
    for start in range(128, width, 128):
        part = part + block[:, start : start + 128]
    return jnp.sum(part.T, axis=0, keepdims=True)


def weight_grad_kernel(place, *refs, sequences, devices, groups, chunk, offsets, normed, extra):
    lefts, refs = refs[:sequences], refs[sequences:]
    rights, refs = refs[:sequences], refs[sequences:]
    if normed:
        own_sums, other_sums, gain = refs[:sequences], refs[sequences : 2 * sequences], refs[2 * sequences]
        refs = refs[2 * sequences + 1 :]
    away, kept, turned_left = refs[extra : extra + 3]
    columns_ref = refs[extra + 3] if normed else None
    span = lefts[0].shape[0]

    @pl.when(pl.program_id(0) == 0)
    def _():
        row = 0
        for device, offset in offsets:
            target = jnp.bitwise_xor(place[0], offset)
            at = pl.multiple_of((device * groups + target) * chunk, chunk)
            for s in range(sequences):
                turned_left[row : row + chunk, s * span : (s + 1) * span] = lefts[s][
                    :, pl.ds(at, chunk)
                ].T
            row += chunk
        if normed:
            for s in range(sequences):
                mean, std = moments(own_sums[s][...], other_sums[s][...], normed)
                columns_ref[2 * s] = jnp.broadcast_to(as_column(mean), (span, 128))
                columns_ref[2 * s + 1] = jnp.broadcast_to(as_column(std), (span, 128))

    values = []
    for s in range(sequences):
        block = rights[s][...]
        if normed:
            block = normed_rows(
                block, columns_ref[2 * s, :, 0:1], columns_ref[2 * s + 1, :, 0:1], gain[...]
            ).astype(BF16)
        values.append(block)
    block = turned_left.shape[0] // 4
    parts = [away.at[:block], away.at[block:], kept.at[:block], kept.at[block:]]
    for n, part in enumerate(parts):
        rows = slice(n * block, (n + 1) * block)
        total = dot(turned_left[rows, :span], values[0], 1, 0)
        for s in range(1, sequences):
            total += dot(turned_left[rows, s * span : (s + 1) * span], values[s], 1, 0)
        part[...] = total.astype(BF16)


def weight_grad(place, lefts, rights, devices, groups, norm=None, z_first=False, after=()):
    sequences = len(lefts)
    span, width = lefts[0].shape
    layers = rights[0].ndim == 3
    columns = rights[0].shape[0] * rights[0].shape[2] if layers else rights[0].shape[1]
    chunk = width // (devices * groups)
    tile = 512 if rights[0].shape[-1] % 512 == 0 else rights[0].shape[-1]
    half = width // 2
    if z_first:
        offsets = [(d, o) for core in (1, 0) for d in range(devices) for o in (2 + core, core)]
    else:
        offsets = [(d, o) for o in (3, 1, 2, 0) for d in range(devices)]
    if layers:
        tiles = rights[0].shape[2] // tile
        right_spec = pl.BlockSpec((None, span, tile), lambda n, p: (n // tiles, 0, n % tiles))
    else:
        right_spec = pl.BlockSpec((span, tile), lambda n, p: (0, n))
    in_specs = [pl.BlockSpec((span, width), lambda n, p: (0, 0))] * sequences
    in_specs += [right_spec] * sequences
    operands = [*lefts, *rights]
    scratch = [pltpu.VMEM((width, sequences * span), BF16)]
    full = 0
    if norm:
        own_sums, other_sums, gain, full = norm
        in_specs += [pl.BlockSpec((2, span), lambda n, p: (0, 0))] * (2 * sequences)
        in_specs += [pl.BlockSpec((1, tile), lambda n, p: (0, n))]
        operands += [*own_sums, *other_sums, gain]
        scratch += [pltpu.VMEM((2 * sequences, span, 128), F32)]
    in_specs += [pl.BlockSpec(memory_space=pl.ANY)] * len(after)
    return pl.pallas_call(
        partial(
            weight_grad_kernel,
            sequences=sequences,
            devices=devices,
            groups=groups,
            chunk=chunk,
            offsets=offsets,
            normed=full,
            extra=len(after),
        ),
        grid_spec=pltpu.PrefetchScalarGridSpec(
            num_scalar_prefetch=1,
            grid=(columns // tile,),
            in_specs=in_specs,
            out_specs=[pl.BlockSpec((half, tile), lambda n, p: (0, n))] * 2,
            scratch_shapes=scratch,
        ),
        out_shape=[jax.ShapeDtypeStruct((half, columns), BF16)] * 2,
        compiler_params=params(),
        cost_estimate=lasting(2.9e-9 * sequences * span * width * columns),
        name="weight_grad",
    )(place, *operands, *after)


def call(kernel, name, grid, ins, outs, scratch, us, after=(), scalars=None):
    extra = len(after)
    first = 0 if scalars is None else 1
    count = first + len(ins)

    def run(*refs):
        kernel(*refs[:count], *refs[count + extra :])

    def spec(block, index):
        if index is None:
            return pl.BlockSpec(block, lambda *_: (0,) * len(block))
        return pl.BlockSpec(block, index)

    return pl.pallas_call(
        run,
        grid_spec=pltpu.PrefetchScalarGridSpec(
            num_scalar_prefetch=first,
            grid=grid,
            in_specs=[spec(block, index) for _, block, index in ins]
            + [pl.BlockSpec(memory_space=pl.ANY)] * extra,
            out_specs=[spec(block, index) for _, _, block, index in outs],
            scratch_shapes=scratch,
        ),
        out_shape=[jax.ShapeDtypeStruct(shape, dtype) for shape, dtype, _, _ in outs],
        compiler_params=params(),
        cost_estimate=lasting(us),
        name=name,
    )(*(() if scalars is None else (scalars,)), *[array for array, _, _ in ins], *after)


def collect_kernel(place, *refs, groups):
    pieces, (whole, sums) = refs[:groups], refs[groups:]
    share = pieces[0].shape[1]
    total, squares = 0.0, 0.0
    for offset, piece in enumerate(pieces):
        at = pl.multiple_of(jnp.bitwise_xor(place[0], offset) * share, share)
        block = piece[...]
        whole[:, pl.ds(at, share)] = block
        wide = block.astype(F32)
        total += as_row(wide)
        squares += as_row(wide * wide)
    sums[...] = jnp.concatenate([total, squares], axis=0)


def collect(place, pieces, after=()):
    groups = len(pieces)
    span, share = pieces[0].shape
    if share % 128:
        stacked = jnp.stack(pieces)
        whole = jnp.concatenate(
            [
                lax.dynamic_index_in_dim(stacked, jnp.bitwise_xor(place[0], n), 0, False)
                for n in range(groups)
            ],
            axis=1,
        )
        wide = whole.astype(F32)
        return whole, jnp.stack([jnp.sum(wide, axis=1), jnp.sum(wide * wide, axis=1)])
    width = groups * share
    return call(
        partial(collect_kernel, groups=groups),
        "collect",
        (1,),
        [(piece, (span, share), None) for piece in pieces],
        [((span, width), BF16, (span, width), None), ((2, span), F32, (2, span), None)],
        [],
        5e-6 * span * width,
        after,
        place,
    )


def out_kernel(mixed, own, other, gain, weight, inner, branch, *, full):
    mean, std = moments(own[...], other[...], full)
    low = normed_rows(mixed[...], as_column(mean), as_column(std), gain[...]).astype(BF16)
    inner[...] = low
    branch[...] = dot(low, weight[...], 1, 1).astype(BF16)


def out_branch(mixed, own, other, gain, near_full, full, after=()):
    span, width = mixed.shape
    model = near_full.shape[0]
    place = near_full.shape[1] // width - 1
    rows = min(256, span)
    return call(
        partial(out_kernel, full=full),
        "out_branch",
        (span // rows,),
        [
            (mixed, (rows, width), lambda n: (n, 0)),
            (own, (2, rows), lambda n: (0, n)),
            (other, (2, rows), lambda n: (0, n)),
            (gain, (1, width), None),
            (near_full, (model, width), lambda n: (0, place)),
        ],
        [
            ((span, width), BF16, (rows, width), lambda n: (n, 0)),
            ((span, model), BF16, (rows, model), lambda n: (n, 0)),
        ],
        [],
        6e-9 * span * width * model,
        after,
    )


def row_norm(block):
    mean = jnp.mean(block, axis=-1, keepdims=True)
    centered = block - mean
    std = lax.rsqrt(jnp.mean(centered * centered, axis=-1, keepdims=True) + EPSILON)
    return centered * std, std


def widen_kernel(tokens, own, other, gain, weight, hidden, low, active, slope, sums, total, squares):
    step = pl.program_id(0)

    @pl.when(step == 0)
    def _():
        block = tokens[...].astype(F32) + (own[...].astype(F32) + other[...].astype(F32))
        hidden[...] = block
        normal, _ = row_norm(block)
        low[...] = (normal * gain[...]).astype(BF16)
        total[...] = jnp.zeros_like(total)
        squares[...] = jnp.zeros_like(squares)

    pre = dot(low[...], weight[...], 1, 0)
    below = 0.5 + 0.5 * lax.erf(pre * 0.7071067811865476)
    value = pre * below
    active[...] = value.astype(BF16)
    slope[...] = (below + pre * (0.3989422804014327 * jnp.exp2(pre * pre * (-0.5 * LOG2_E)))).astype(
        BF16
    )
    part, square = total[...], squares[...]
    for start in range(0, value.shape[1], 128):
        piece = value[:, start : start + 128]
        part += piece
        square += piece * piece
    total[...] = part
    squares[...] = square

    @pl.when(step == pl.num_programs(0) - 1)
    def _():
        sums[...] = jnp.concatenate([as_row(total[...]), as_row(squares[...])], axis=0)


def widen(tokens, own, other, gain, weight, units, after=()):
    span, model = tokens.shape
    tile = 512
    rows = (span, model)
    across = (span, tile)
    return call(
        widen_kernel,
        "widen",
        (units // tile,),
        [
            (tokens, rows, None),
            (own, rows, None),
            (other, rows, None),
            (gain, (1, model), None),
            (weight, (model, tile), lambda n: (0, n)),
        ],
        [
            (rows, F32, rows, None),
            (rows, BF16, rows, None),
            ((span, units), BF16, across, lambda n: (0, n)),
            ((span, units), BF16, across, lambda n: (0, n)),
            ((2, span), F32, (2, span), None),
        ],
        [pltpu.VMEM((span, 128), F32)] * 2,
        5.4e-9 * span * model * units,
        after,
    )


def narrow_kernel(active, own, other, gain, weight, branch, total, columns, *, full):
    step = pl.program_id(0)

    @pl.when(step == 0)
    def _():
        mean, std = moments(own[...], other[...], full)
        columns[0] = jnp.broadcast_to(as_column(mean), columns.shape[1:])
        columns[1] = jnp.broadcast_to(as_column(std), columns.shape[1:])
        total[...] = jnp.zeros_like(total)

    low = normed_rows(active[...], columns[0, :, 0:1], columns[1, :, 0:1], gain[...]).astype(BF16)
    total[...] += dot(low, weight[...], 1, 0)

    @pl.when(step == pl.num_programs(0) - 1)
    def _():
        branch[...] = total[...].astype(BF16)


def narrow(active, own, other, gain, weight, full, after=()):
    span, units = active.shape
    model = weight.shape[1]
    tile = 512
    sums = (2, span)
    return call(
        partial(narrow_kernel, full=full),
        "narrow",
        (units // tile,),
        [
            (active, (span, tile), lambda n: (0, n)),
            (own, sums, None),
            (other, sums, None),
            (gain, (1, tile), lambda n: (0, n)),
            (weight, (tile, model), lambda n: (n, 0)),
        ],
        [((span, model), BF16, (span, model), None)],
        [pltpu.VMEM((span, model), F32), pltpu.VMEM((2, span, 128), F32)],
        3.7e-9 * span * model * units,
        after,
    )[0]


def wide_back_kernel(
    grads, weight, active, own, other, gain, scaled, sums, gain_grad, columns, total, weighted, *, full
):
    step = pl.program_id(0)

    @pl.when(step == 0)
    def _():
        mean, std = moments(own[...], other[...], full)
        columns[0] = jnp.broadcast_to(as_column(mean), columns.shape[1:])
        columns[1] = jnp.broadcast_to(as_column(std), columns.shape[1:])
        total[...] = jnp.zeros_like(total)
        weighted[...] = jnp.zeros_like(weighted)

    grad = dot(grads[...], weight[...], 1, 1)
    normal = (active[...].astype(F32) - columns[0, :, 0:1]) * columns[1, :, 0:1]
    product = grad * normal
    gain_grad[...] = jnp.sum(product, axis=0, keepdims=True)
    scaled[...] = (grad * gain[...]).astype(BF16)
    product = product * gain[...]
    part, other_part = total[...], weighted[...]
    for start in range(0, grad.shape[1], 128):
        at = slice(start, start + 128)
        part += grad[:, at] * gain[:, at]
        other_part += product[:, at]
    total[...] = part
    weighted[...] = other_part

    @pl.when(step == pl.num_programs(0) - 1)
    def _():
        sums[...] = jnp.concatenate([as_row(total[...]), as_row(weighted[...])], axis=0)


def wide_back(grads, weight, active, own, other, gain, full, after=()):
    span, units = active.shape
    model = weight.shape[1]
    tile = 512
    sums = (2, span)
    across = (span, tile)
    return call(
        partial(wide_back_kernel, full=full),
        "wide_back",
        (units // tile,),
        [
            (grads, (span, model), None),
            (weight, (tile, model), lambda n: (n, 0)),
            (active, across, lambda n: (0, n)),
            (own, sums, None),
            (other, sums, None),
            (gain, (1, tile), lambda n: (0, n)),
        ],
        [
            ((span, units), BF16, across, lambda n: (0, n)),
            (sums, F32, sums, None),
            ((1, units), F32, (1, tile), lambda n: (0, n)),
        ],
        [pltpu.VMEM((2, span, 128), F32)] + [pltpu.VMEM((span, 128), F32)] * 2,
        4.2e-9 * span * model * units,
        after,
    )


def pre_back_kernel(
    scaled, active, slope, own, other, own_back, other_back, weight, grads, branch, total, columns, *, full
):
    step = pl.program_id(0)

    @pl.when(step == 0)
    def _():
        mean, std = moments(own[...], other[...], full)
        back = (own_back[...] + other_back[...]) / full
        for n, row in enumerate((mean, std, back[0:1], back[1:2])):
            columns[n] = jnp.broadcast_to(as_column(row), columns.shape[1:])
        total[...] = jnp.zeros_like(total)

    std = columns[1, :, 0:1]
    normal = (active[...].astype(F32) - columns[0, :, 0:1]) * std
    grad = std * (scaled[...].astype(F32) - columns[2, :, 0:1] - normal * columns[3, :, 0:1])
    low = (grad * slope[...].astype(F32)).astype(BF16)
    grads[...] = low
    total[...] += dot(low, weight[...], 1, 1)

    @pl.when(step == pl.num_programs(0) - 1)
    def _():
        branch[...] = total[...].astype(BF16)


def pre_back(scaled, active, slope, own, other, own_back, other_back, weight, full, after=()):
    span, units = active.shape
    model = weight.shape[0]
    tile = 512
    sums = (2, span)
    across = (span, tile)
    tiled = lambda n: (0, n)
    return call(
        partial(pre_back_kernel, full=full),
        "pre_back",
        (units // tile,),
        [
            (scaled, across, tiled),
            (active, across, tiled),
            (slope, across, tiled),
            (own, sums, None),
            (other, sums, None),
            (own_back, sums, None),
            (other_back, sums, None),
            (weight, (model, tile), tiled),
        ],
        [((span, units), BF16, across, tiled), ((span, model), BF16, (span, model), None)],
        [pltpu.VMEM((span, model), F32), pltpu.VMEM((4, span, 128), F32)],
        4.6e-9 * span * model * units,
        after,
    )


def middle_kernel(
    grads, own, other, hidden, gain, weight, mixed, own_sums, other_sums, gain_attn,
    grad_hidden, low, scaled, sums, gain_grad, gain_attn_grad, *, full
):
    step = pl.program_id(0)

    @pl.when(step == 0)
    def _():
        gain_grad[...] = jnp.zeros_like(gain_grad)
        gain_attn_grad[...] = jnp.zeros_like(gain_attn_grad)

    normal, std = row_norm(hidden[...])
    grad = own[...].astype(F32) + other[...].astype(F32)
    gain_grad[...] += jnp.sum(grad * normal, axis=0, keepdims=True)
    part = grad * gain[...]
    back = std * (
        part
        - jnp.mean(part, axis=-1, keepdims=True)
        - normal * jnp.mean(part * normal, axis=-1, keepdims=True)
    )
    total = grads[...].astype(F32) + back
    grad_hidden[...] = total
    rows = total.astype(BF16)
    low[...] = rows
    inner = dot(rows, weight[...], 1, 0)
    mean, deviation = moments(own_sums[...], other_sums[...], full)
    normal = (mixed[...].astype(F32) - as_column(mean)) * as_column(deviation)
    gain_attn_grad[...] += jnp.sum(inner * normal, axis=0, keepdims=True)
    inner = inner * gain_attn[...]
    scaled[...] = inner
    sums[...] = jnp.concatenate([as_row(inner), as_row(inner * normal)], axis=0)


def middle(
    grads, own, other, hidden, gain, near_full, mixed, own_sums, other_sums, gain_attn, full, after=()
):
    span, model = grads.shape
    width = mixed.shape[1]
    place = near_full.shape[1] // width - 1
    rows = min(256, span)
    by_row = lambda n: (n, 0)
    by_column = lambda n: (0, n)
    return call(
        partial(middle_kernel, full=full),
        "middle",
        (span // rows,),
        [
            (grads, (rows, model), by_row),
            (own, (rows, model), by_row),
            (other, (rows, model), by_row),
            (hidden, (rows, model), by_row),
            (gain, (1, model), None),
            (near_full, (model, width), lambda n: (0, place)),
            (mixed, (rows, width), by_row),
            (own_sums, (2, rows), by_column),
            (other_sums, (2, rows), by_column),
            (gain_attn, (1, width), None),
        ],
        [
            ((span, model), F32, (rows, model), by_row),
            ((span, model), BF16, (rows, model), by_row),
            ((span, width), F32, (rows, width), by_row),
            ((2, span), F32, (2, rows), by_column),
            ((1, model), F32, (1, model), None),
            ((1, width), F32, (1, width), None),
        ],
        [],
        1.2e-8 * span * width * model,
        after,
    )


def share_out_kernel(place, scaled, mixed, own, other, own_back, other_back, *outs, full):
    mean, std = moments(own[...], other[...], full)
    back = (own_back[...] + other_back[...]) / full
    mean, std, first, second = [as_column(row) for row in (mean, std, back[0:1], back[1:2])]
    share = outs[0].shape[1]
    for offset, out in enumerate(outs):
        at = pl.multiple_of(jnp.bitwise_xor(place[0], offset) * share, share)
        normal = (mixed[:, pl.ds(at, share)].astype(F32) - mean) * std
        out[...] = (std * (scaled[:, pl.ds(at, share)] - first - normal * second)).astype(BF16)


def share_out(place, scaled, mixed, own, other, own_back, other_back, full, groups, after=()):
    span, width = scaled.shape
    share = width // groups
    if share % 128:
        mean, std = moments(own, other, full)
        back = (own_back + other_back) / full
        mean, std, first, second = [row.reshape(-1, 1) for row in (mean, std, back[0], back[1])]
        normal = (mixed.astype(F32) - mean) * std
        grads = (std * (scaled - first - normal * second)).astype(BF16)
        return [
            lax.dynamic_slice_in_dim(grads, jnp.bitwise_xor(place[0], n) * share, share, 1)
            for n in range(groups)
        ]
    sums = (2, span)
    return call(
        partial(share_out_kernel, full=full),
        "share_out",
        (1,),
        [
            (scaled, (span, width), None),
            (mixed, (span, width), None),
            (own, sums, None),
            (other, sums, None),
            (own_back, sums, None),
            (other_back, sums, None),
        ],
        [((span, share), BF16, (span, share), None)] * groups,
        [],
        7.6e-6 * span * width,
        after,
        place,
    )


def first_back_kernel(place, *refs, groups):
    pieces, (weight, tokens, whole, branch, gain_grad, total) = refs[:groups], refs[groups:]
    step = pl.program_id(0)
    for offset, piece in enumerate(pieces):

        @pl.when(step == offset)
        def _(piece=piece, offset=offset):
            whole[...] = piece[...]
            made = dot(piece[0], weight[0], 1, 1)
            for j in (1, 2):
                made += dot(piece[j], weight[j], 1, 1)
            if offset:
                total[...] += made
            else:
                total[...] = made

    @pl.when(step == groups - 1)
    def _():
        normal, _ = row_norm(tokens[...].astype(F32))
        grad = total[...]
        gain_grad[...] = jnp.sum(grad * normal, axis=0, keepdims=True)
        branch[...] = grad.astype(BF16)


def first_back(place, pieces, qkv_full, tokens, after=()):
    groups = len(pieces)
    _, span, share = pieces[0].shape
    model, local = qkv_full.shape[1:]
    if share % 128:
        stacked = jnp.stack(pieces)
        whole = jnp.concatenate(
            [
                lax.dynamic_index_in_dim(stacked, jnp.bitwise_xor(place[0], n), 0, False)
                for n in range(groups)
            ],
            axis=2,
        )
        grad = jnp.einsum("jte,jde->td", whole, qkv_full, preferred_element_type=F32)
        normal, _ = row_norm(tokens.astype(F32))
        return whole, grad.astype(BF16), jnp.sum(grad * normal, axis=0, keepdims=True)
    across = lambda o, p: (0, 0, jnp.bitwise_xor(o, p[0]))
    return call(
        partial(first_back_kernel, groups=groups),
        "first_back",
        (groups,),
        [(piece, (3, span, share), None) for piece in pieces]
        + [(qkv_full, (3, model, share), across), (tokens, (span, model), None)],
        [
            ((3, span, local), BF16, (3, span, share), across),
            ((span, model), BF16, (span, model), None),
            ((1, model), F32, (1, model), None),
        ],
        [pltpu.VMEM((span, model), F32)],
        1.34e-8 * span * model * local,
        after,
        place,
    )


def exchange(array, axis, size, offset):
    return lax.ppermute(array, axis, [(n, n ^ offset) for n in range(size)])


def add_kernel(*refs):
    total = refs[0][...].astype(F32)
    for ref in refs[1:-1]:
        total += ref[...].astype(F32)
    refs[-1][...] = total.astype(BF16)


def add(arrays, rows, after=()):
    width = arrays[0][0].shape[1]
    tile = 128

    def from_row(first):
        return lambda n: (n + first // tile, 0)

    return call(
        add_kernel,
        "add",
        (rows // tile,),
        [(array, (tile, width), from_row(first)) for array, first in arrays],
        [((rows, width), BF16, (tile, width), lambda n: (n, 0))],
        [],
        1.5e-6 * rows * width,
        after,
    )[0]


class ScatterSum:
    def __init__(self, parts, groups, z_first=False):
        away, self.kept = parts
        self.groups, self.z_first = groups, z_first
        self.got = exchange(away, "seq", groups, 1)

    def mates(self, after=()):
        rows = self.kept.shape[0]
        pair = [(self.kept, 0), (self.got, 0)]
        if self.z_first:
            near = add(pair, rows, after)
            self.rows = lax.psum_scatter(near, "dp", scatter_dimension=0, tiled=True)
        else:
            near = add(pair, rows // 2, after)
            self.far = exchange(near, "seq", self.groups, 2)
        return near

    def chips(self, after=()):
        if self.z_first:
            half = self.rows.shape[0] // 2
            far = exchange(self.rows[:half], "seq", self.groups, 2)
            self.out = self.rows[half:].astype(F32) + far.astype(F32)
            return self.out
        half = self.kept.shape[0] // 2
        own = add([(self.kept, half), (self.got, half), (self.far, 0)], half, after)
        self.out = lax.psum_scatter(own, "dp", scatter_dimension=0, tiled=True).astype(F32)
        return own


def mp_sum(low, units):
    if units != 2:
        return lax.psum(low, "mp"), jnp.zeros_like(low)
    return low, exchange(low, "mp", 2, 1)


def mp_rows(sums, units):
    if units != 2:
        return lax.psum(sums, "mp"), jnp.zeros_like(sums)
    return sums, exchange(sums, "mp", 2, 1)


def data_sum(array, devices, groups):
    for axis, size in (("seq", groups), ("dp", devices)):
        offset = 1
        while offset < size:
            array = array + exchange(array, axis, size, offset)
            offset *= 2
    return array


def pass_round(pieces, groups):
    return [pieces[0]] + [exchange(pieces[n], "seq", groups, n) for n in range(1, groups)]


def xpos_tables(count, lanes):
    positions = jnp.arange(count, dtype=F32)
    pair_index = jnp.arange(HALF, dtype=F32)
    frequency = 1.0 / 10000.0 ** (2.0 * pair_index / HEAD_DIM)
    angles = positions[:, None] * frequency[None, :]
    base_ratio = (2.0 * pair_index + 0.4 * HEAD_DIM) / (1.4 * HEAD_DIM)
    growth = base_ratio[None, :] ** ((positions[:, None] - count // 2) / XPOS_BASE)
    cosine, sine = jnp.cos(angles), jnp.sin(angles)
    tables = []
    for factor in (growth, 1.0 / growth):
        tables.append(jnp.tile(cosine * factor, (1, lanes // HALF)))
        tables.append(
            jnp.tile(jnp.concatenate([-sine * factor, sine * factor], axis=1), (1, lanes // HEAD_DIM))
        )
    return tables


def body(
    devices,
    groups,
    units,
    tokens,
    lengths,
    qkv_weight,
    out_weight,
    in_weight,
    down_weight,
    gain_in,
    gain_attn,
    gain_mid,
    gain_ffn,
    out_grad,
):
    sequences, span, model = tokens.shape
    each = range(sequences)
    data = ("dp", "seq")
    shards = devices * groups
    place = lax.axis_index("seq").astype(jnp.int32)
    local_width = qkv_weight.shape[2]
    heads_here = local_width // HEAD_DIM
    ffn_width = in_weight.shape[1]
    share = local_width // groups

    number = lax.axis_index("dp") * groups + place
    sizes = [gain_in.size, gain_mid.size, gain_attn.size, gain_ffn.size]
    cuts = [sum(sizes[:n]) for n in range(5)]
    flat = jnp.concatenate(
        [gain_in, gain_mid, gain_attn.reshape(-1), gain_ffn.reshape(-1)]
    ).reshape(1, -1)
    row = lax.broadcasted_iota(jnp.int32, (shards, 1), 0)
    all_gains = data_sum(jnp.where(row == number, flat, 0).astype(F32), devices, groups)
    pieces = [all_gains[:, cuts[n] : cuts[n + 1]] for n in range(4)]
    gain_one, gain_three = pieces[0].reshape(1, -1), pieces[1].reshape(1, -1)
    gain_two = pieces[2].reshape(shards, heads_here, -1).transpose(1, 0, 2).reshape(1, -1)
    gain_four = (
        pieces[3].reshape(shards, ffn_width // HEAD_DIM, -1).transpose(1, 0, 2).reshape(1, -1)
    )

    qkv_full = lax.all_gather(qkv_weight, data, axis=1, tiled=True)
    near_full = lax.all_gather(
        jnp.concatenate([in_weight, out_weight.T], axis=1), data, axis=0, tiled=True
    )
    down_full = lax.all_gather(down_weight, data, axis=1, tiled=True)

    count = span * groups
    tables = xpos_tables(count, min(128, share))
    tables_here = [lax.dynamic_slice_in_dim(t, place * span, span, 0) for t in tables]
    spot = place.reshape(1)
    metas = [jnp.stack([lengths[s], place]) for s in each]
    full_units = ffn_width * units

    first_low = []
    for s in each:
        normal, _ = row_norm(tokens[s].astype(F32))
        first_low.append((normal * gain_one).astype(BF16))
    messages, mixed, logs, attended, att_sums, inner, branch = [], [], [], [], [], [], []
    last = ()
    for s in each:
        made = project(spot, first_low[s], qkv_full, tables_here, groups, last)
        messages.append(pass_round(made, groups))
        last = [made[0]]
    for s in each:
        outs, log = attend(metas[s], messages[s], last)
        mixed.append(outs)
        logs.append(log)
        last = [log]
    for s in each:
        whole, sums = collect(spot, pass_round(mixed[s], groups), last)
        attended.append(whole)
        att_sums.append(mp_rows(sums, units))
        low, terms = out_branch(whole, *att_sums[s], gain_two, near_full, model)
        inner.append(low)
        branch.append(mp_sum(terms, units))
        last = [terms]

    hidden, third_low, active, slope, act_sums = [], [], [], [], []
    for s in each:
        made = widen(tokens[s], *branch[s], gain_three, near_full, ffn_width, last)
        hidden.append(made[0])
        third_low.append(made[1])
        active.append(made[2])
        slope.append(made[3])
        act_sums.append(mp_rows(made[4], units))
        last = [made[4]]

    grad_low = [out_grad[s] for s in each]
    norm = ([a for a, _ in act_sums], [b for _, b in act_sums], gain_four, full_units)
    down_parts = weight_grad(spot, grad_low, active, devices, groups, norm, False, last)
    down_sum = ScatterSum(down_parts, groups)
    last = [down_parts[0]]
    pre_low, third_terms, scaled, back_sums = [], [], [], []
    gain_four_grad = 0.0
    for s in each:
        part, sums, gain_part = wide_back(
            grad_low[s], down_full, active[s], *act_sums[s], gain_four, full_units, last
        )
        scaled.append(part)
        gain_four_grad += gain_part
        back_sums.append(mp_rows(sums, units))
        last = [sums]
    last = [down_sum.mates(last)] + [other for _, other in back_sums]
    for s in each:
        low, terms = pre_back(
            scaled[s], active[s], slope[s], *act_sums[s], *back_sums[s], near_full, full_units,
            last,
        )
        pre_low.append(low)
        third_terms.append(mp_sum(terms, units))
        last = [terms]

    def finish(s, after):
        terms = narrow(active[s], *act_sums[s], gain_four, down_full, full_units, after)
        return mp_sum(terms, units)

    def result(s, after):
        own, other = wide_terms[s]
        return add([(own, 0), (other, 0), (hidden[s], 0)], span, after)

    gain_three_grad, gain_two_grad = 0.0, 0.0
    grad_hidden, hidden_low, grads, returned = [], [], [], []
    wide_terms = [finish(0, last)]
    last = [wide_terms[0][0]]
    for s in each:
        made = middle(
            grad_low[s], *third_terms[s], hidden[s], gain_three, near_full, attended[s],
            *att_sums[s], gain_two, model, last
        )
        grad_hidden.append(made[0])
        hidden_low.append(made[1])
        gain_three_grad += made[4]
        gain_two_grad += made[5]
        if s == 0:
            in_parts = weight_grad(
                spot, third_low, pre_low, devices, groups, None, Z_FIRST, [made[3]]
            )
            in_sum = ScatterSum(in_parts, groups, Z_FIRST)
            last = [down_sum.chips([in_parts[0], third_terms[1][1]])]
        else:
            wide_terms.append(finish(s, [made[3]]))
            last = [in_sum.mates([wide_terms[s][0]])]
        parts = share_out(
            spot, made[2], attended[s], *att_sums[s], *mp_rows(made[3], units), model, groups,
            last,
        )
        last = [parts[0]]
        grads.append(pass_round(parts, groups))
    for s in each:
        made = attend_back(
            metas[s], messages[s], grads[s], mixed[s], logs[s], tables, last,
            BACK_WEIGHT if s == 0 else 1,
        )
        returned.append(pass_round(made, groups))
        last = [made[0]]
        if s == 0:
            out_parts = weight_grad(spot, hidden_low, inner, devices, groups, None, False, last)
            out_sum = ScatterSum(out_parts, groups)
            last = [out_parts[0], down_sum.out]

    early = jnp.concatenate(
        [
            gain_three_grad.reshape(shards, -1),
            gain_two_grad.reshape(heads_here, shards, -1).transpose(1, 0, 2).reshape(shards, -1),
            gain_four_grad.reshape(ffn_width // HEAD_DIM, shards, -1)
            .transpose(1, 0, 2)
            .reshape(shards, -1),
        ],
        axis=1,
    )
    early = lax.dynamic_index_in_dim(data_sum(early, devices, groups), number, 0, False)
    cuts = [cut - cuts[1] for cut in cuts]
    three, two, four = [early[cuts[n] : cuts[n + 1]] for n in (1, 2, 3)]

    gain_one_grad = 0.0
    stacked, first_terms = [], []
    results = [result(0, last)]
    last = [out_sum.mates([results[0]])]
    for s in each:
        whole, terms, gain_part = first_back(spot, returned[s], qkv_full, tokens[s], last)
        stacked.append(whole)
        gain_one_grad += gain_part
        first_terms.append(mp_sum(terms, units))
        last = [terms]
    results.append(result(1, last))
    last = [out_sum.chips([results[1]])]
    qkv_parts = weight_grad(spot, first_low, stacked, devices, groups, None, False, last)
    qkv_sum = ScatterSum(qkv_parts, groups)
    grad_inputs = []
    for s in each:
        normal, std = row_norm(tokens[s].astype(F32))
        own, other = first_terms[s]
        part = (own.astype(F32) + other.astype(F32)) * gain_one
        grad_first = std * (
            part
            - jnp.mean(part, axis=-1, keepdims=True)
            - normal * jnp.mean(part * normal, axis=-1, keepdims=True)
        )
        grad_inputs.append((grad_hidden[s] + grad_first).astype(BF16))
    qkv_sum.mates([in_sum.chips()])
    qkv_sum.chips([grad_inputs[0]])
    grad_qkv_w = qkv_sum.out.reshape(-1, 3, local_width).transpose(1, 0, 2)
    own, other = mp_rows(gain_one_grad.reshape(shards, -1), units)
    one = lax.dynamic_index_in_dim(data_sum(own + other, devices, groups), number, 0, False)
    return (
        jnp.stack(results),
        jnp.stack(grad_inputs),
        grad_qkv_w,
        out_sum.out.T,
        in_sum.out,
        down_sum.out.T,
        one,
        two.reshape(gain_attn.shape),
        three,
        four.reshape(gain_ffn.shape),
    )


def solution(mesh):
    sizes = mesh.shape
    data = ("dp", "seq")
    in_specs = (
        P("dp", "seq", None),
        P("dp"),
        P(None, data, "mp"),
        P("mp", data),
        P(data, "mp"),
        P("mp", data),
        P(data),
        P("mp", data),
        P(data),
        P("mp", data),
        P("dp", "seq", None),
    )
    out_specs = (
        P("dp", "seq", None),
        P("dp", "seq", None),
        P(None, data, "mp"),
        P("mp", data),
        P(data, "mp"),
        P("mp", data),
        P(data),
        P("mp", data),
        P(data),
        P("mp", data),
    )
    run = partial(body, sizes["dp"], sizes["seq"], sizes["mp"])
    return jax.shard_map(run, mesh=mesh, in_specs=in_specs, out_specs=out_specs, check_vma=False)
```

time: 1480 us -> 1080 us (0.73)
  Pallas kernels: 252 us -> 543 us
  waiting for transfers between devices: 632 us -> 380 us
  matrix products: 205 us -> 0 us
  blocking collectives: 132 us -> 0 us
  other arithmetic: 145 us -> 45.2 us
    ppermute x48 -> x61, waiting for transfers between devices: 612 us -> 295 us  [exchange(): return lax.ppermute(array, axis, [(n, n ^ offset) for n in range(size)])]
    pallas_call x2 -> x29, Pallas kernels: 25.9 us -> 315 us  [the longest x27 289 us: call(): pl.pallas_call(run, grid_spec=pltpu.PrefetchScalarGridSpec(num_scalar_pre...]
    dot_general x14 -> x0, matrix products: 205 us -> none  [the longest x6 76.6 us: dot(): lax.dot_general(left, right, (((left_dim,), (right_dim,)), ((), ())), pre...]
    unnamed x2 -> x0, blocking collectives: 127 us -> none
    convert_element_type x15 -> x3, other arithmetic: 88.4 us -> 12.2 us  [the longest x1 7.55 us: body(): grad_inputs.append((grad_hidden[s] + grad_first).astype(BF16))]
    all_gather x1, waiting for transfers between devices: 17.4 us -> 65.8 us  [body(): qkv_full = lax.all_gather(qkv_weight, data, axis=1, tiled=True)]
    reduce_scatter x4, waiting for transfers between devices: 0.01 us -> 17.8 us  [the longest x3 17.8 us: chips(): lax.psum_scatter(own, 'dp', scatter_dimension=0, tiled=True).astype(F32)]
    reduce_sum x11 -> x4, other arithmetic: 27.9 us -> 11.8 us  [the longest x1 5.85 us: body(): jnp.mean(part, axis=-1, keepdims=True)]
  transfers between devices with their start and end apart: 56 -> 68, of which waited for: 25 -> 32; matrix products, arithmetic and copies ran while one was open for 19% -> 7% of each run, Pallas kernels for 16% -> 50%
where the time goes in v2:
time: 1080 us
  Pallas kernels  543 us (50%)
  waiting for transfers between devices  380 us (35%)
  starting transfers between devices  49.3 us (5%)
  local copies, waits for them, and re-layouts  45.5 us (4%)
  other arithmetic  45.2 us (4%)
  between operations  15.5 us (1%)
    ppermute x61, waiting for transfers between devices, exchange(): return lax.ppermute(array, axis, [(n, n ^ offset) for n in range(size)])  295 us
    pallas_call x27, Pallas kernels, call(): pl.pallas_call(run, grid_spec=pltpu.PrefetchScalarGridSpec(num_scalar_pre...  289 us
    pallas_call x2, Pallas kernels, attend_back(): pl.pallas_call(partial(attend_back_kernel, groups=groups, heads=heads, bl...  89.1 us
    pallas_call x4, Pallas kernels, weight_grad(): pl.pallas_call(partial(weight_grad_kernel, sequences=sequences, devices=d...  78.2 us
    all_gather x1, waiting for transfers between devices, body(): qkv_full = lax.all_gather(qkv_weight, data, axis=1, tiled=True)  65.8 us
    pallas_call x2, Pallas kernels, attend(): pl.pallas_call(partial(attend_kernel, groups=groups, heads=heads, block=b...  60.8 us
    ppermute x61, starting transfers between devices, exchange(): return lax.ppermute(array, axis, [(n, n ^ offset) for n in range(size)])  49 us
    pallas_call x2, Pallas kernels, project(): pl.pallas_call(partial(project_kernel, extra=len(after)), grid_spec=pltpu...  26 us
  transfers between devices with their start and end apart: 68, of which 32 were waited for; matrix products, arithmetic and copies ran while one was open for 7% of the time, Pallas kernels for 50%

profile of v2, /device:TPU:0, one launch (start us, length us, event | category | flops | bytes accessed | tf_op | source)
XLA Modules:
  0.0 1079.1 jit_solution(754234075577848348)
XLA Ops:
  15.4 3.3 fusion.23
  33.1 3.0 collective-permute-done.2
  39.0 5.4 collective-permute-done.3
  45.1 4.6 fusion.17
  49.7 65.8 %all-gather.4.cloned.1.call-done.weight.refs_5_ = bf16[3,2048,1024]{2,1,0:T(8,128)(2,1)} async-done(((bf16[3,128,1024]{2,1,0:T(8,128)(2,1)}), bf16[3,2048,1024]{2,1,0:T(8,128)(2,1)}) %all-gather.4.cloned.1.call-update) | async-done | bytes 12582928 | tf_op jit(solution)/shard_map/all_gather | solution.py:1113
  115.5 12.9 %project.2 = (bf16[3,512,256]{2,1,0:T(8,128)(2,1)}, bf16[3,512,256]{2,1,0:T(8,128)(2,1)}, bf16[3,512,256]{2,1,0:T(8,128)(2,1)}, bf16[3,512,256]{2,1,0:T(8,128)(2,1)}) custom-call(s32[1]{0:T(128)} %bitcast.1.place.refs_0_, bf16[512,2048]{1,0:T(8,128)(2,1)} %get-tuple-element.234.rows.refs_0_, ...), custom_call_target="tpu_custom_call" | custom-call | flops 3221225472 | tf_op jit(solution)/shard_map/project/pallas_call | solution.py:97
  130.9 13.1 %project.3 = (bf16[3,512,256]{2,1,0:T(8,128)(2,1)}, bf16[3,512,256]{2,1,0:T(8,128)(2,1)}, bf16[3,512,256]{2,1,0:T(8,128)(2,1)}, bf16[3,512,256]{2,1,0:T(8,128)(2,1)}) custom-call(s32[1]{0:T(128)} %bitcast.1.place.refs_0_, bf16[512,2048]{1,0:T(8,128)(2,1)} %get-tuple-element.235.rows.refs_1_, ...), custom_call_target="tpu_custom_call" | custom-call | flops 3221225472 | tf_op jit(solution)/shard_map/project/pallas_call | solution.py:97
  148.0 18.1 %collective-permute-done.5.refs_2_ = bf16[3,512,256]{2,1,0:T(8,128)(2,1)S(1)} collective-permute-done((bf16[3,512,256]{2,1,0:T(8,128)(2,1)}, bf16[3,512,256]{2,1,0:T(8,128)(2,1)S(1)}, u32[]{:S(2)}, u32[]{:S(2)}) %collective-permute-start.5) | collective-permute-done | bytes 786464 | tf_op jit(solution)/shard_map/ppermute | solution.py:972
  166.1 32.8 %collective-permute-done.6.refs_3_ = bf16[3,512,256]{2,1,0:T(8,128)(2,1)S(1)} collective-permute-done((bf16[3,512,256]{2,1,0:T(8,128)(2,1)}, bf16[3,512,256]{2,1,0:T(8,128)(2,1)S(1)}, u32[]{:S(2)}, u32[]{:S(2)}) %collective-permute-start.6) | collective-permute-done | bytes 786464 | tf_op jit(solution)/shard_map/ppermute | solution.py:972
  199.7 31.4 %attend.2 = (bf16[512,256]{1,0:T(8,128)(2,1)}, bf16[512,256]{1,0:T(8,128)(2,1)}, bf16[512,256]{1,0:T(8,128)(2,1)}, bf16[512,256]{1,0:T(8,128)(2,1)}, f32[4,2048]{1,0:T(4,128)}) custom-call(s32[2]{0:T(128)} %get-tuple-element.255.meta, bf16[3,512,256]{2,1,0:T(8,128)(2,1)} %get-tuple-element.98.outs_0_.refs_0_, bf16[3,512,256]{2,1,0:T(8,128)(2,1)} %copy-done.62, ...), custom_call_target="tpu_custom_call" | custom-call | flops 7784628224 | tf_op jit(solution)/shard_map/attend/pallas_call | solution.py:193
  233.8 32.5 %collective-permute-done.12.refs_3_ = bf16[3,512,256]{2,1,0:T(8,128)(2,1)S(1)} collective-permute-done((bf16[3,512,256]{2,1,0:T(8,128)(2,1)}, bf16[3,512,256]{2,1,0:T(8,128)(2,1)S(1)}, u32[]{:S(2)}, u32[]{:S(2)}) %collective-permute-start.12) | collective-permute-done | bytes 786464 | tf_op jit(solution)/shard_map/ppermute | solution.py:972
  267.3 29.5 %attend.3 = (bf16[512,256]{1,0:T(8,128)(2,1)}, bf16[512,256]{1,0:T(8,128)(2,1)}, bf16[512,256]{1,0:T(8,128)(2,1)}, bf16[512,256]{1,0:T(8,128)(2,1)}, f32[4,2048]{1,0:T(4,128)}) custom-call(s32[2]{0:T(128)} %get-tuple-element.256.meta, bf16[3,512,256]{2,1,0:T(8,128)(2,1)} %get-tuple-element.102.refs_4_.refs_0_, bf16[3,512,256]{2,1,0:T(8,128)(2,1)} %copy-done.59, ...), custom_call_target="tpu_custom_call" | custom-call | flops 7784628224 | tf_op jit(solution)/shard_map/attend/pallas_call | solution.py:193
  304.6 6.4 out_branch.2
  314.5 12.5 %collective-permute-done.16.refs_3_ = bf16[512,256]{1,0:T(8,128)(2,1)S(1)} collective-permute-done((bf16[512,256]{1,0:T(8,128)(2,1)S(1)}, bf16[512,256]{1,0:T(8,128)(2,1)S(1)}, u32[]{:S(2)}, u32[]{:S(2)}) %collective-permute-start.16) | collective-permute-done | bytes 262176 | tf_op jit(solution)/shard_map/ppermute | solution.py:972
  327.0 9.6 collective-permute-done.17.refs_4_
  339.9 19.2 %collective-permute-done.18.refs_2_.refs_8_.refs_4_ = f32[2,512]{1,0:T(2,128)S(1)} collective-permute-done((f32[2,512]{1,0:T(2,128)}, f32[2,512]{1,0:T(2,128)S(1)}, u32[]{:S(2)}, u32[]{:S(2)}) %collective-permute-start.18) | collective-permute-done | bytes 4128 | tf_op jit(solution)/shard_map/ppermute | solution.py:972
  359.6 6.5 out_branch.3
  371.6 23.5 %widen.2 = (f32[512,2048]{1,0:T(8,128)}, bf16[512,2048]{1,0:T(8,128)(2,1)}, bf16[512,4096]{1,0:T(8,128)(2,1)}, bf16[512,4096]{1,0:T(8,128)(2,1)}, f32[2,512]{1,0:T(2,128)}) custom-call(bf16[512,2048]{1,0:T(8,128)(2,1)} %get-tuple-element.238.refs_0_.refs_6_, bf16[512,2048]{1,0:T(8,128)(2,1)} %get-tuple-element.114.refs_5_.refs_1_, ...), custom_call_target="tpu_custom_call" | custom-call | flops 5798205952 | tf_op jit(solution)/shard_map/widen/pallas_call | solution.py:480
  396.4 16.9 %collective-permute-done.20.refs_2_ = bf16[512,2048]{1,0:T(8,128)(2,1)} collective-permute-done((bf16[512,2048]{1,0:T(8,128)(2,1)}, bf16[512,2048]{1,0:T(8,128)(2,1)}, u32[]{:S(2)}, u32[]{:S(2)}) %collective-permute-start.20) | collective-permute-done | bytes 2097184 | tf_op jit(solution)/shard_map/ppermute | solution.py:972
  413.3 23.6 %widen.3 = (f32[512,2048]{1,0:T(8,128)}, bf16[512,2048]{1,0:T(8,128)(2,1)}, bf16[512,4096]{1,0:T(8,128)(2,1)}, bf16[512,4096]{1,0:T(8,128)(2,1)}, f32[2,512]{1,0:T(2,128)}) custom-call(bf16[512,2048]{1,0:T(8,128)(2,1)} %get-tuple-element.239.refs_0_.refs_6_, bf16[512,2048]{1,0:T(8,128)(2,1)} %get-tuple-element.121.refs_5_.refs_1_, ...), custom_call_target="tpu_custom_call" | custom-call | flops 5798205952 | tf_op jit(solution)/shard_map/widen/pallas_call | solution.py:480
  443.3 25.8 %weight_grad.4 = (bf16[1024,4096]{1,0:T(8,128)(2,1)}, bf16[1024,4096]{1,0:T(8,128)(2,1)}) custom-call(s32[1]{0:T(128)} %bitcast.1.place.refs_0_, bf16[512,2048]{1,0:T(8,128)(2,1)} %get-tuple-element.236.refs_0_, bf16[512,2048]{1,0:T(8,128)(2,1)} %get-tuple-element.237.refs_1_.refs_0_, bf16[512,4096]{1,0:T(8,128)(2,1)} %get-tuple-element.122.refs_2_.refs_1_.refs_0_, ...), custom_call_target="tpu_custom_call" | custom-call | flops 6227702784 | tf_op jit(solution)/shard_map/weight_grad/pallas_call | solution.py:442
  469.1 17.7 %wide_back.2 = (bf16[512,4096]{1,0:T(8,128)(2,1)}, f32[2,512]{1,0:T(2,128)}, f32[1,4096]{1,0:T(1,128)}) custom-call(bf16[512,2048]{1,0:T(8,128)(2,1)} %get-tuple-element.236.refs_0_, bf16[4096,2048]{1,0:T(8,128)(2,1)} %all-gather.8.cloned.1.call-done.refs_1_.refs_4_, bf16[512,4096]{1,0:T(8,128)(2,1)} %get-tuple-element.122.refs_2_.refs_1_.refs_0_, ...), custom_call_target="tpu_custom_call" | custom-call | flops 4509715456 | tf_op jit(solution)/shard_map/wide_back/pallas_call | solution.py:480
  486.8 17.5 %wide_back.3 = (bf16[512,4096]{1,0:T(8,128)(2,1)}, f32[2,512]{1,0:T(2,128)}, f32[1,4096]{1,0:T(1,128)}) custom-call(bf16[512,2048]{1,0:T(8,128)(2,1)} %get-tuple-element.237.refs_1_.refs_0_, bf16[4096,2048]{1,0:T(8,128)(2,1)} %all-gather.8.cloned.1.call-done.refs_1_.refs_4_, bf16[512,4096]{1,0:T(8,128)(2,1)} %get-tuple-element.124.refs_3_.refs_2_.refs_1_.refs_0_, ...), custom_call_target="tpu_custom_call" | custom-call | flops 4509715456 | tf_op jit(solution)/shard_map/wide_back/pallas_call | solution.py:480
  504.3 6.0 add.241.refs_8_
  516.5 19.8 %pre_back.2 = (bf16[512,4096]{1,0:T(8,128)(2,1)}, bf16[512,2048]{1,0:T(8,128)(2,1)}) custom-call(bf16[512,4096]{1,0:T(8,128)(2,1)} %get-tuple-element.131.refs_0_, bf16[512,4096]{1,0:T(8,128)(2,1)} %get-tuple-element.122.refs_2_.refs_1_.refs_0_, bf16[512,4096]{1,0:T(8,128)(2,1)} %get-tuple-element.132.refs_2_, ...), custom_call_target="tpu_custom_call" | custom-call | flops 4939212288 | tf_op jit(solution)/shard_map/pre_back/pallas_call | solution.py:480
  537.3 19.7 %pre_back.3 = (bf16[512,4096]{1,0:T(8,128)(2,1)}, bf16[512,2048]{1,0:T(8,128)(2,1)}) custom-call(bf16[512,4096]{1,0:T(8,128)(2,1)} %get-tuple-element.128.refs_0_, bf16[512,4096]{1,0:T(8,128)(2,1)} %get-tuple-element.124.refs_3_.refs_2_.refs_1_.refs_0_, bf16[512,4096]{1,0:T(8,128)(2,1)} %get-tuple-element.129.refs_2_, ...), custom_call_target="tpu_custom_call" | custom-call | flops 4939212288 | tf_op jit(solution)/shard_map/pre_back/pallas_call | solution.py:480
  558.1 16.1 %narrow.2.refs_10_.refs_0_ = bf16[512,2048]{1,0:T(8,128)(2,1)} custom-call(bf16[512,4096]{1,0:T(8,128)(2,1)} %get-tuple-element.122.refs_2_.refs_1_.refs_0_, f32[2,512]{1,0:T(2,128)} %get-tuple-element.123.refs_5_.refs_4_.refs_3_.refs_1_, f32[2,512]{1,0:T(2,128)} %copy-done.31, f32[1,4096]{1,0:T(1,128)} %reshape.262.refs_8_.refs_5_.refs_3_, ...), custom_call_target="tpu_custom_call" | custom-call | flops 3972844800 | tf_op jit(solution)/shard_map/narrow/pallas_call | solution.py:480
  574.2 11.0 %collective-permute-done.27.refs_2_ = bf16[512,2048]{1,0:T(8,128)(2,1)} collective-permute-done((bf16[512,2048]{1,0:T(8,128)(2,1)}, bf16[512,2048]{1,0:T(8,128)(2,1)}, u32[]{:S(2)}, u32[]{:S(2)}) %collective-permute-start.27) | collective-permute-done | bytes 2097184 | tf_op jit(solution)/shard_map/ppermute | solution.py:972
  585.2 13.2 %middle.2 = (f32[512,2048]{1,0:T(8,128)}, bf16[512,2048]{1,0:T(8,128)(2,1)}, f32[512,1024]{1,0:T(8,128)}, f32[2,512]{1,0:T(2,128)}, f32[1,2048]{1,0:T(1,128)}, /*index=5*/f32[1,1024]{1,0:T(1,128)}) custom-call(bf16[512,2048]{1,0:T(8,128)(2,1)} %get-tuple-element.236.refs_0_, bf16[512,2048]{1,0:T(8,128)(2,1)} %get-tuple-element.134.refs_8_.refs_1_, ...), custom_call_target="tpu_custom_call" | custom-call | flops 3221225472 | tf_op jit(solution)/shard_map/middle/pallas_call | solution.py:480
  598.5 23.7 %weight_grad.5 = (bf16[1024,4096]{1,0:T(8,128)(2,1)}, bf16[1024,4096]{1,0:T(8,128)(2,1)}) custom-call(s32[1]{0:T(128)} %bitcast.1.place.refs_0_, bf16[512,2048]{1,0:T(8,128)(2,1)} %get-tuple-element.140.refs_0_, bf16[512,2048]{1,0:T(8,128)(2,1)} %get-tuple-element.141.refs_1_, bf16[512,4096]{1,0:T(8,128)(2,1)} %get-tuple-element.142.refs_2_, ...), custom_call_target="tpu_custom_call" | custom-call | flops 6227702784 | tf_op jit(solution)/shard_map/weight_grad/pallas_call | solution.py:442
  622.2 6.0 collective-permute-done.26.refs_4_.refs_2_
  631.4 7.2 add.242.refs_7_
  643.6 4.1 share_out.2
  649.5 13.1 %middle.3 = (f32[512,2048]{1,0:T(8,128)}, bf16[512,2048]{1,0:T(8,128)(2,1)}, f32[512,1024]{1,0:T(8,128)}, f32[2,512]{1,0:T(2,128)}, f32[1,2048]{1,0:T(1,128)}, /*index=5*/f32[1,1024]{1,0:T(1,128)}) custom-call(bf16[512,2048]{1,0:T(8,128)(2,1)} %get-tuple-element.237.refs_1_.refs_0_, bf16[512,2048]{1,0:T(8,128)(2,1)} %get-tuple-element.135.refs_5_.refs_1_, ...), custom_call_target="tpu_custom_call" | custom-call | flops 3221225472 | tf_op jit(solution)/shard_map/middle/pallas_call | solution.py:480
  662.6 16.1 %narrow.3.refs_2_.refs_0_ = bf16[512,2048]{1,0:T(8,128)(2,1)} custom-call(bf16[512,4096]{1,0:T(8,128)(2,1)} %get-tuple-element.124.refs_3_.refs_2_.refs_1_.refs_0_, f32[2,512]{1,0:T(2,128)} %get-tuple-element.125.refs_5_.refs_9_.refs_3_.refs_1_, f32[2,512]{1,0:T(2,128)} %copy-done.30, f32[1,4096]{1,0:T(1,128)} %reshape.262.refs_8_.refs_5_.refs_3_, ...), custom_call_target="tpu_custom_call" | custom-call | flops 3972844800 | tf_op jit(solution)/shard_map/narrow/pallas_call | solution.py:480
  679.7 11.4 %add.243.refs_7_ = bf16[1024,4096]{1,0:T(8,128)(2,1)} custom-call(bf16[1024,4096]{1,0:T(8,128)(2,1)} %get-tuple-element.148.refs_0_, bf16[1024,4096]{1,0:T(8,128)(2,1)} %collective-permute-done.31.refs_1_, bf16[512,2048]{1,0:T(8,128)(2,1)} %narrow.3.refs_2_.refs_0_), custom_call_target="tpu_custom_call" | custom-call | flops 1572864000 | tf_op jit(solution)/shard_map/add/pallas_call | solution.py:480
  691.8 4.0 share_out.3
  696.7 46.2 %attend_back.2 = (bf16[3,512,256]{2,1,0:T(8,128)(2,1)}, bf16[3,512,256]{2,1,0:T(8,128)(2,1)}, bf16[3,512,256]{2,1,0:T(8,128)(2,1)}, bf16[3,512,256]{2,1,0:T(8,128)(2,1)}) custom-call(s32[2]{0:T(128)} %get-tuple-element.255.meta, bf16[3,512,256]{2,1,0:T(8,128)(2,1)} %get-tuple-element.98.outs_0_.refs_0_, bf16[3,512,256]{2,1,0:T(8,128)(2,1)} %copy-done.62, ...), custom_call_target="tpu_custom_call" | custom-call | flops 281857228800 | tf_op jit(solution)/shard_map/attend_back/pallas_call | solution.py:316
  743.0 9.5 weight_grad.6
  754.5 3.7 convert_bitcast_fusion.1
  763.3 3.1 collective-permute-done.34.refs_7_
  768.8 42.8 %attend_back.3 = (bf16[3,512,256]{2,1,0:T(8,128)(2,1)}, bf16[3,512,256]{2,1,0:T(8,128)(2,1)}, bf16[3,512,256]{2,1,0:T(8,128)(2,1)}, bf16[3,512,256]{2,1,0:T(8,128)(2,1)}) custom-call(s32[2]{0:T(128)} %get-tuple-element.256.meta, bf16[3,512,256]{2,1,0:T(8,128)(2,1)} %get-tuple-element.102.refs_4_.refs_0_, bf16[3,512,256]{2,1,0:T(8,128)(2,1)} %copy-done.59, ...), custom_call_target="tpu_custom_call" | custom-call | flops 11274289152 | tf_op jit(solution)/shard_map/attend_back/pallas_call | solution.py:316
  813.6 5.3 add.244.refs_2_
  818.9 3.6 add.245.refs_7_
  823.5 14.3 %first_back.2 = (bf16[3,512,1024]{2,1,0:T(8,128)(2,1)}, bf16[512,2048]{1,0:T(8,128)(2,1)}, f32[1,2048]{1,0:T(1,128)}) custom-call(s32[1]{0:T(128)} %bitcast.1.place.refs_0_, bf16[3,512,256]{2,1,0:T(8,128)(2,1)} %get-tuple-element.160.refs_4_.refs_1_, bf16[3,512,256]{2,1,0:T(8,128)(2,1)} %copy-done.18, bf16[3,512,256]{2,1,0:T(8,128)(2,1)} %copy-done.19, ...), custom_call_target="tpu_custom_call" | custom-call | flops 3597035008 | tf_op jit(solution)/shard_map/first_back/pallas_call | solution.py:480
  837.8 10.6 collective-permute-done.41.refs_4_
  848.3 14.5 %first_back.3 = (bf16[3,512,1024]{2,1,0:T(8,128)(2,1)}, bf16[512,2048]{1,0:T(8,128)(2,1)}, f32[1,2048]{1,0:T(1,128)}) custom-call(s32[1]{0:T(128)} %bitcast.1.place.refs_0_, bf16[3,512,256]{2,1,0:T(8,128)(2,1)} %get-tuple-element.162.refs_3_.refs_1_, bf16[3,512,256]{2,1,0:T(8,128)(2,1)} %collective-permute-done.39.refs_2_, ...), custom_call_target="tpu_custom_call" | custom-call | flops 3597035008 | tf_op jit(solution)/shard_map/first_back/pallas_call | solution.py:480
  864.2 5.3 add.246.refs_3_
  872.1 3.9 add.247.refs_4_
  876.0 19.2 %weight_grad.7 = (bf16[1024,3072]{1,0:T(8,128)(2,1)}, bf16[1024,3072]{1,0:T(8,128)(2,1)}) custom-call(s32[1]{0:T(128)} %bitcast.1.place.refs_0_, bf16[512,2048]{1,0:T(8,128)(2,1)} %get-tuple-element.234.rows.refs_0_, bf16[512,2048]{1,0:T(8,128)(2,1)} %get-tuple-element.235.rows.refs_1_, bf16[3,512,1024]{2,1,0:T(8,128)(2,1)} %get-tuple-element.174.refs_2_, ...), custom_call_target="tpu_custom_call" | custom-call | flops 4670776832 | tf_op jit(solution)/shard_map/weight_grad/pallas_call | solution.py:442
  899.5 22.6 %collective-permute-done.50 = bf16[128,4096]{1,0:T(8,128)(2,1)S(1)} collective-permute-done((bf16[128,4096]{1,0:T(8,128)(2,1)S(1)}, bf16[128,4096]{1,0:T(8,128)(2,1)S(1)}, u32[]{:S(2)}, u32[]{:S(2)}) %collective-permute-start.50) | collective-permute-done | bytes 1048608 | tf_op jit(solution)/shard_map/ppermute | solution.py:972
  922.1 2.8 convert_add_fusion.refs_2_
  925.0 5.1 add.248
  931.1 15.2 %collective-permute-done.46 = bf16[512,2048]{1,0:T(8,128)(2,1)} collective-permute-done((bf16[512,2048]{1,0:T(8,128)(2,1)}, bf16[512,2048]{1,0:T(8,128)(2,1)}, u32[]{:S(2)}, u32[]{:S(2)}) %collective-permute-start.46) | collective-permute-done | bytes 2097184 | tf_op jit(solution)/shard_map/ppermute | solution.py:972
  946.3 44.2 %collective-permute-done.47 = bf16[512,2048]{1,0:T(8,128)(2,1)} collective-permute-done((bf16[512,2048]{1,0:T(8,128)(2,1)S(1)}, bf16[512,2048]{1,0:T(8,128)(2,1)}, u32[]{:S(2)}, u32[]{:S(2)}) %collective-permute-start.47) | collective-permute-done | bytes 2097184 | tf_op jit(solution)/shard_map/ppermute | solution.py:972
  990.5 5.9 fusion.24
  996.4 7.5 fusion.22
  1004.0 6.1 add.249
  1014.3 2.8 collective-permute-done.58
  1017.1 6.6 collective-permute-done.59
  1023.8 5.6 collective-permute-done.60
  1035.9 2.9 copy.110
  1039.7 4.2 pad_maximum_fusion
  1050.9 17.8 %reduce-scatter.9.cloned.1.call-done = bf16[128,3072]{1,0:T(8,128)(2,1)} async-done(((bf16[512,3072]{1,0:T(8,128)(2,1)}), bf16[128,3072]{1,0:T(8,128)(2,1)}) %reduce-scatter.9.cloned.1.call-update) | async-done | bytes 786448 | tf_op jit(solution)/shard_map/reduce_scatter | solution.py:1026
  (367 shorter events, 129.1 us)
Async XLA Ops:
  7.2 108.3 %all-gather.4.cloned.1.call-start = ((), (), s32[]{:S(2)}) async-start(), calls=%async_computation.4 | async-start | bytes 13369344 | tf_op jit(solution)/shard_map/all_gather | solution.py:1113
  8.0 296.1 %all-gather.6.cloned.1.call-start = ((), (), s32[]{:S(2)}) async-start(), calls=%async_computation.5 | async-start | bytes 22282240 | tf_op jit(solution)/shard_map/all_gather | solution.py:1114
  11.5 457.6 %all-gather.8.cloned.1.call-start = ((), (), s32[]{:S(2)}) async-start(), calls=%async_computation.6 | async-start | bytes 17825792 | tf_op jit(solution)/shard_map/all_gather | solution.py:1117
  12.2 742.2 %reduce-scatter.5.cloned.1.call-start = ((), (), s32[]{:S(2)}) async-start(), calls=%async_computation.7 | async-start | bytes 5242880 | tf_op jit(solution)/shard_map/reduce_scatter | solution.py:1026
  12.9 10.2 collective-permute-start
  23.2 5.7 collective-permute-start.1
  29.0 7.2 collective-permute-start.2
  36.1 8.3 collective-permute-start.3
  128.4 17.2 %collective-permute-start.4 = (bf16[3,512,256]{2,1,0:T(8,128)(2,1)}, bf16[3,512,256]{2,1,0:T(8,128)(2,1)S(1)}, u32[]{:S(2)}, u32[]{:S(2)}) collective-permute-start(bf16[3,512,256]{2,1,0:T(8,128)(2,1)} %get-tuple-element.99), channel_id=1, source_target_pairs={{0,2},{2,0},{4,6},{6,4},{1,3},{3,1},{5,7},{7,5},{8,10},{10,8},{12,... | collective-permute-start | bytes 2359304 | tf_op jit(solution)/shard_map/ppermute | solution.py:972
  128.7 37.4 %collective-permute-start.5 = (bf16[3,512,256]{2,1,0:T(8,128)(2,1)}, bf16[3,512,256]{2,1,0:T(8,128)(2,1)S(1)}, u32[]{:S(2)}, u32[]{:S(2)}) collective-permute-start(bf16[3,512,256]{2,1,0:T(8,128)(2,1)} %get-tuple-element.100), channel_id=1, source_target_pairs={{0,4},{2,6},{4,0},{6,2},{1,5},{3,7},{5,1},{7,3},{8,12},{10,14},{12... | collective-permute-start | bytes 2359304 | tf_op jit(solution)/shard_map/ppermute | solution.py:972
  129.7 69.2 %collective-permute-start.6 = (bf16[3,512,256]{2,1,0:T(8,128)(2,1)}, bf16[3,512,256]{2,1,0:T(8,128)(2,1)S(1)}, u32[]{:S(2)}, u32[]{:S(2)}) collective-permute-start(bf16[3,512,256]{2,1,0:T(8,128)(2,1)} %get-tuple-element.101), channel_id=1, source_target_pairs={{0,6},{2,4},{4,2},{6,0},{1,7},{3,5},{5,3},{7,1},{8,14},{10,12},{12... | collective-permute-start | bytes 2359304 | tf_op jit(solution)/shard_map/ppermute | solution.py:972
  144.1 89.2 %collective-permute-start.10 = (bf16[3,512,256]{2,1,0:T(8,128)(2,1)}, bf16[3,512,256]{2,1,0:T(8,128)(2,1)S(1)}, u32[]{:S(2)}, u32[]{:S(2)}) collective-permute-start(bf16[3,512,256]{2,1,0:T(8,128)(2,1)} %get-tuple-element.107), channel_id=1, source_target_pairs={{0,2},{2,0},{4,6},{6,4},{1,3},{3,1},{5,7},{7,5},{8,10},{10,8},{12,... | collective-permute-start | bytes 2359304 | tf_op jit(solution)/shard_map/ppermute | solution.py:972
  144.7 89.1 %collective-permute-start.11 = (bf16[3,512,256]{2,1,0:T(8,128)(2,1)}, bf16[3,512,256]{2,1,0:T(8,128)(2,1)S(1)}, u32[]{:S(2)}, u32[]{:S(2)}) collective-permute-start(bf16[3,512,256]{2,1,0:T(8,128)(2,1)} %get-tuple-element.108), channel_id=1, source_target_pairs={{0,4},{2,6},{4,0},{6,2},{1,5},{3,7},{5,1},{7,3},{8,12},{10,14},{12... | collective-permute-start | bytes 2359304 | tf_op jit(solution)/shard_map/ppermute | solution.py:972
  145.6 120.6 %collective-permute-start.12 = (bf16[3,512,256]{2,1,0:T(8,128)(2,1)}, bf16[3,512,256]{2,1,0:T(8,128)(2,1)S(1)}, u32[]{:S(2)}, u32[]{:S(2)}) collective-permute-start(bf16[3,512,256]{2,1,0:T(8,128)(2,1)} %get-tuple-element.109), channel_id=1, source_target_pairs={{0,6},{2,4},{4,2},{6,0},{1,7},{3,5},{5,3},{7,1},{8,14},{10,12},{12... | collective-permute-start | bytes 2359304 | tf_op jit(solution)/shard_map/ppermute | solution.py:972
  231.1 65.6 %collective-permute-start.7 = (bf16[512,256]{1,0:T(8,128)(2,1)}, bf16[512,256]{1,0:T(8,128)(2,1)S(1)}, u32[]{:S(2)}, u32[]{:S(2)}) collective-permute-start(bf16[512,256]{1,0:T(8,128)(2,1)} %get-tuple-element.104.refs_9_), channel_id=1, source_target_pairs={{0,2},{2,0},{4,6},{6,4},{1,3},{3,1},{5,7},{7,5},{8,10},{10,8},{12,... | collective-permute-start | bytes 786440 | tf_op jit(solution)/shard_map/ppermute | solution.py:972
  232.3 64.4 %collective-permute-start.8 = (bf16[512,256]{1,0:T(8,128)(2,1)}, bf16[512,256]{1,0:T(8,128)(2,1)S(1)}, u32[]{:S(2)}, u32[]{:S(2)}) collective-permute-start(bf16[512,256]{1,0:T(8,128)(2,1)} %get-tuple-element.105.refs_10_), channel_id=1, source_target_pairs={{0,4},{2,6},{4,0},{6,2},{1,5},{3,7},{5,1},{7,3},{8,12},{10,14},{12... | collective-permute-start | bytes 786440 | tf_op jit(solution)/shard_map/ppermute | solution.py:972
  233.3 63.4 %collective-permute-start.9 = (bf16[512,256]{1,0:T(8,128)(2,1)}, bf16[512,256]{1,0:T(8,128)(2,1)S(1)}, u32[]{:S(2)}, u32[]{:S(2)}) collective-permute-start(bf16[512,256]{1,0:T(8,128)(2,1)} %get-tuple-element.106.refs_11_), channel_id=1, source_target_pairs={{0,6},{2,4},{4,2},{6,0},{1,7},{3,5},{5,3},{7,1},{8,14},{10,12},{12... | collective-permute-start | bytes 786440 | tf_op jit(solution)/shard_map/ppermute | solution.py:972
  300.2 3.8 collective-permute-start.13
  311.1 59.2 %collective-permute-start.14 = (bf16[512,2048]{1,0:T(8,128)(2,1)}, bf16[512,2048]{1,0:T(8,128)(2,1)S(1)}, u32[]{:S(2)}, u32[]{:S(2)}) collective-permute-start(bf16[512,2048]{1,0:T(8,128)(2,1)} %get-tuple-element.114.refs_5_.refs_1_), channel_id=1, source_target_pairs={{0,1},{1,0},{2,3},{3,2},{4,5},{5,4},{6,7},{7,6},{8,9},{9,8},{10,11... | collective-permute-start | bytes 6291464 | tf_op jit(solution)/shard_map/ppermute | solution.py:972
  312.6 14.4 %collective-permute-start.16 = (bf16[512,256]{1,0:T(8,128)(2,1)S(1)}, bf16[512,256]{1,0:T(8,128)(2,1)S(1)}, u32[]{:S(2)}, u32[]{:S(2)}) collective-permute-start(bf16[512,256]{1,0:T(8,128)(2,1)S(1)} %copy-done.66), channel_id=1, source_target_pairs={{0,4},{2,6},{4,0},{6,2},{1,5},{3,7},{5,1},{7,3},{8,12},{10,14},{12... | collective-permute-start | bytes 786440 | tf_op jit(solution)/shard_map/ppermute | solution.py:972
  313.6 23.0 %collective-permute-start.17 = (bf16[512,256]{1,0:T(8,128)(2,1)S(1)}, bf16[512,256]{1,0:T(8,128)(2,1)S(1)}, u32[]{:S(2)}, u32[]{:S(2)}) collective-permute-start(bf16[512,256]{1,0:T(8,128)(2,1)S(1)} %copy-done.67), channel_id=1, source_target_pairs={{0,6},{2,4},{4,2},{6,0},{1,7},{3,5},{5,3},{7,1},{8,14},{10,12},{12... | collective-permute-start | bytes 786440 | tf_op jit(solution)/shard_map/ppermute | solution.py:972
  339.9 19.2 %collective-permute-start.18 = (f32[2,512]{1,0:T(2,128)}, f32[2,512]{1,0:T(2,128)S(1)}, u32[]{:S(2)}, u32[]{:S(2)}) collective-permute-start(f32[2,512]{1,0:T(2,128)} %get-tuple-element.120.refs_1_.refs_7_.refs_3_), channel_id=1, source_target_pairs={{0,1},{1,0},{2,3},{3,2},{4,5},{5,4},{6,7},{7,6},{8,9},{9,8},{10,11... | collective-permute-start | bytes 12296 | tf_op jit(solution)/shard_map/ppermute | solution.py:972
  366.2 47.2 %collective-permute-start.20 = (bf16[512,2048]{1,0:T(8,128)(2,1)}, bf16[512,2048]{1,0:T(8,128)(2,1)}, u32[]{:S(2)}, u32[]{:S(2)}) collective-permute-start(bf16[512,2048]{1,0:T(8,128)(2,1)} %get-tuple-element.121.refs_5_.refs_1_), channel_id=1, source_target_pairs={{0,1},{1,0},{2,3},{3,2},{4,5},{5,4},{6,7},{7,6},{8,9},{9,8},{10,11... | collective-permute-start | bytes 6291464 | tf_op jit(solution)/shard_map/ppermute | solution.py:972
  395.1 47.6 %collective-permute-start.19 = (f32[2,512]{1,0:T(2,128)}, f32[2,512]{1,0:T(2,128)S(1)}, u32[]{:S(2)}, u32[]{:S(2)}) collective-permute-start(f32[2,512]{1,0:T(2,128)} %get-tuple-element.123.refs_5_.refs_4_.refs_3_.refs_1_), channel_id=1, source_target_pairs={{0,1},{1,0},{2,3},{3,2},{4,5},{5,4},{6,7},{7,6},{8,9},{9,8},{10,11... | collective-permute-start | bytes 12296 | tf_op jit(solution)/shard_map/ppermute | solution.py:972
  437.0 5.7 collective-permute-start.21
  469.0 35.3 %collective-permute-start.24 = (bf16[1024,4096]{1,0:T(8,128)(2,1)}, bf16[1024,4096]{1,0:T(8,128)(2,1)}, u32[]{:S(2)}, u32[]{:S(2)}) collective-permute-start(bf16[1024,4096]{1,0:T(8,128)(2,1)} %get-tuple-element.126.refs_6_), channel_id=1, source_target_pairs={{0,2},{2,0},{4,6},{6,4},{1,3},{3,1},{5,7},{7,5},{8,10},{10,8},{12,... | collective-permute-start | bytes 25165832 | tf_op jit(solution)/shard_map/ppermute | solution.py:972
  510.4 117.8 %collective-permute-start.29 = (bf16[512,4096]{1,0:T(8,128)(2,1)}, bf16[512,4096]{1,0:T(8,128)(2,1)S(1)}, u32[]{:S(2)}, u32[]{:S(2)}) collective-permute-start(bf16[512,4096]{1,0:T(8,128)(2,1)} %add.241.refs_8_), channel_id=1, source_target_pairs={{0,4},{2,6},{4,0},{6,2},{1,5},{3,7},{5,1},{7,3},{8,12},{10,14},{12... | collective-permute-start | bytes 12582920 | tf_op jit(solution)/shard_map/ppermute | solution.py:972
  511.2 3.6 collective-permute-start.22
  536.3 48.9 %collective-permute-start.27 = (bf16[512,2048]{1,0:T(8,128)(2,1)}, bf16[512,2048]{1,0:T(8,128)(2,1)}, u32[]{:S(2)}, u32[]{:S(2)}) collective-permute-start(bf16[512,2048]{1,0:T(8,128)(2,1)} %get-tuple-element.134.refs_8_.refs_1_), channel_id=1, source_target_pairs={{0,1},{1,0},{2,3},{3,2},{4,5},{5,4},{6,7},{7,6},{8,9},{9,8},{10,11... | collective-permute-start | bytes 6291464 | tf_op jit(solution)/shard_map/ppermute | solution.py:972
  557.0 71.1 %collective-permute-start.26 = (bf16[512,2048]{1,0:T(8,128)(2,1)}, bf16[512,2048]{1,0:T(8,128)(2,1)S(1)}, u32[]{:S(2)}, u32[]{:S(2)}) collective-permute-start(bf16[512,2048]{1,0:T(8,128)(2,1)} %get-tuple-element.135.refs_5_.refs_1_), channel_id=1, source_target_pairs={{0,1},{1,0},{2,3},{3,2},{4,5},{5,4},{6,7},{7,6},{8,9},{9,8},{10,11... | collective-permute-start | bytes 6291464 | tf_op jit(solution)/shard_map/ppermute | solution.py:972
  622.2 56.6 %collective-permute-start.31 = (bf16[1024,4096]{1,0:T(8,128)(2,1)}, bf16[1024,4096]{1,0:T(8,128)(2,1)}, u32[]{:S(2)}, u32[]{:S(2)}) collective-permute-start(bf16[1024,4096]{1,0:T(8,128)(2,1)} %get-tuple-element.144.refs_3_), channel_id=1, source_target_pairs={{0,2},{2,0},{4,6},{6,4},{1,3},{3,1},{5,7},{7,5},{8,10},{10,8},{12,... | collective-permute-start | bytes 25165832 | tf_op jit(solution)/shard_map/ppermute | solution.py:972
  638.7 256.6 %reduce-scatter.7.cloned.1.call-start = ((), (), s32[]{:S(2)}) async-start(), calls=%async_computation.8 | async-start | bytes 10485760 | tf_op jit(solution)/shard_map/reduce_scatter | solution.py:1012
  639.3 3.7 collective-permute-start.28
  640.2 117.9 %collective-permute-start.25 = (bf16[512,2048]{1,0:T(8,128)(2,1)}, bf16[512,2048]{1,0:T(8,128)(2,1)}, u32[]{:S(2)}, u32[]{:S(2)}) collective-permute-start(bf16[512,2048]{1,0:T(8,128)(2,1)} %narrow.2.refs_10_.refs_0_), channel_id=1, source_target_pairs={{0,1},{1,0},{2,3},{3,2},{4,5},{5,4},{6,7},{7,6},{8,9},{9,8},{10,11... | collective-permute-start | bytes 6291464 | tf_op jit(solution)/shard_map/ppermute | solution.py:972
  647.7 48.2 %collective-permute-start.35 = (bf16[512,256]{1,0:T(8,128)(2,1)}, bf16[512,256]{1,0:T(8,128)(2,1)S(1)}, u32[]{:S(2)}, u32[]{:S(2)}) collective-permute-start(bf16[512,256]{1,0:T(8,128)(2,1)} %get-tuple-element.157), channel_id=1, source_target_pairs={{0,2},{2,0},{4,6},{6,4},{1,3},{3,1},{5,7},{7,5},{8,10},{10,8},{12,... | collective-permute-start | bytes 786440 | tf_op jit(solution)/shard_map/ppermute | solution.py:972
  647.7 48.2 %collective-permute-start.36 = (bf16[512,256]{1,0:T(8,128)(2,1)}, bf16[512,256]{1,0:T(8,128)(2,1)S(1)}, u32[]{:S(2)}, u32[]{:S(2)}) collective-permute-start(bf16[512,256]{1,0:T(8,128)(2,1)} %get-tuple-element.158), channel_id=1, source_target_pairs={{0,4},{2,6},{4,0},{6,2},{1,5},{3,7},{5,1},{7,3},{8,12},{10,14},{12... | collective-permute-start | bytes 786440 | tf_op jit(solution)/shard_map/ppermute | solution.py:972
  648.4 47.5 %collective-permute-start.37 = (bf16[512,256]{1,0:T(8,128)(2,1)}, bf16[512,256]{1,0:T(8,128)(2,1)S(1)}, u32[]{:S(2)}, u32[]{:S(2)}) collective-permute-start(bf16[512,256]{1,0:T(8,128)(2,1)} %get-tuple-element.159), channel_id=1, source_target_pairs={{0,6},{2,4},{4,2},{6,0},{1,7},{3,5},{5,3},{7,1},{8,14},{10,12},{12... | collective-permute-start | bytes 786440 | tf_op jit(solution)/shard_map/ppermute | solution.py:972
  678.8 12.4 %collective-permute-start.30 = (f32[2,512]{1,0:T(2,128)S(1)}, f32[2,512]{1,0:T(2,128)S(1)}, u32[]{:S(2)}, u32[]{:S(2)}) collective-permute-start(f32[2,512]{1,0:T(2,128)S(1)} %copy-done.38), channel_id=1, source_target_pairs={{0,1},{1,0},{2,3},{3,2},{4,5},{5,4},{6,7},{7,6},{8,9},{9,8},{10,11... | collective-permute-start | bytes 12296 | tf_op jit(solution)/shard_map/ppermute | solution.py:972
  691.1 357.8 %reduce-scatter.11.cloned.1.call-start = ((), (), s32[]{:S(2)}) async-start(), calls=%async_computation.10 | async-start | bytes 1310720 | tf_op jit(solution)/shard_map/reduce_scatter | solution.py:1026
  752.5 60.2 %collective-permute-start.45 = (bf16[1024,1024]{1,0:T(8,128)(2,1)}, bf16[1024,1024]{1,0:T(8,128)(2,1)}, u32[]{:S(2)}, u32[]{:S(2)}) collective-permute-start(bf16[1024,1024]{1,0:T(8,128)(2,1)} %get-tuple-element.161.refs_17_), channel_id=1, source_target_pairs={{0,2},{2,0},{4,6},{6,4},{1,3},{3,1},{5,7},{7,5},{8,10},{10,8},{12,... | collective-permute-start | bytes 6291464 | tf_op jit(solution)/shard_map/ppermute | solution.py:972
  752.5 6.7 collective-permute-start.32
  753.0 9.2 collective-permute-start.33
  754.2 12.3 %collective-permute-start.34 = (bf16[512,256]{1,0:T(8,128)(2,1)S(1)}, bf16[512,256]{1,0:T(8,128)(2,1)}, u32[]{:S(2)}, u32[]{:S(2)}) collective-permute-start(bf16[512,256]{1,0:T(8,128)(2,1)S(1)} %copy-done.68), channel_id=1, source_target_pairs={{0,6},{2,4},{4,2},{6,0},{1,7},{3,5},{5,3},{7,1},{8,14},{10,12},{12... | collective-permute-start | bytes 786440 | tf_op jit(solution)/shard_map/ppermute | solution.py:972
  758.1 104.7 %collective-permute-start.38 = (bf16[512,2048]{1,0:T(8,128)(2,1)S(1)}, bf16[512,2048]{1,0:T(8,128)(2,1)S(1)}, u32[]{:S(2)}, u32[]{:S(2)}) collective-permute-start(bf16[512,2048]{1,0:T(8,128)(2,1)S(1)} %copy-done.6), channel_id=1, source_target_pairs={{0,1},{1,0},{2,3},{3,2},{4,5},{5,4},{6,7},{7,6},{8,9},{9,8},{10,11... | collective-permute-start | bytes 6291464 | tf_op jit(solution)/shard_map/ppermute | solution.py:972
  759.3 52.3 %collective-permute-start.42 = (bf16[3,512,256]{2,1,0:T(8,128)(2,1)}, bf16[3,512,256]{2,1,0:T(8,128)(2,1)S(1)}, u32[]{:S(2)}, u32[]{:S(2)}) collective-permute-start(bf16[3,512,256]{2,1,0:T(8,128)(2,1)} %get-tuple-element.166), channel_id=1, source_target_pairs={{0,2},{2,0},{4,6},{6,4},{1,3},{3,1},{5,7},{7,5},{8,10},{10,8},{12,... | collective-permute-start | bytes 2359304 | tf_op jit(solution)/shard_map/ppermute | solution.py:972
  762.2 49.5 %collective-permute-start.43 = (bf16[3,512,256]{2,1,0:T(8,128)(2,1)}, bf16[3,512,256]{2,1,0:T(8,128)(2,1)S(1)}, u32[]{:S(2)}, u32[]{:S(2)}) collective-permute-start(bf16[3,512,256]{2,1,0:T(8,128)(2,1)} %get-tuple-element.167), channel_id=1, source_target_pairs={{0,4},{2,6},{4,0},{6,2},{1,5},{3,7},{5,1},{7,3},{8,12},{10,14},{12... | collective-permute-start | bytes 2359304 | tf_op jit(solution)/shard_map/ppermute | solution.py:972
  766.5 56.0 %collective-permute-start.44 = (bf16[3,512,256]{2,1,0:T(8,128)(2,1)}, bf16[3,512,256]{2,1,0:T(8,128)(2,1)S(1)}, u32[]{:S(2)}, u32[]{:S(2)}) collective-permute-start(bf16[3,512,256]{2,1,0:T(8,128)(2,1)} %get-tuple-element.168), channel_id=1, source_target_pairs={{0,6},{2,4},{4,2},{6,0},{1,7},{3,5},{5,3},{7,1},{8,14},{10,12},{12... | collective-permute-start | bytes 2359304 | tf_op jit(solution)/shard_map/ppermute | solution.py:972
  811.6 26.1 %collective-permute-start.39 = (bf16[3,512,256]{2,1,0:T(8,128)(2,1)}, bf16[3,512,256]{2,1,0:T(8,128)(2,1)}, u32[]{:S(2)}, u32[]{:S(2)}) collective-permute-start(bf16[3,512,256]{2,1,0:T(8,128)(2,1)} %get-tuple-element.163), channel_id=1, source_target_pairs={{0,2},{2,0},{4,6},{6,4},{1,3},{3,1},{5,7},{7,5},{8,10},{10,8},{12,... | collective-permute-start | bytes 2359304 | tf_op jit(solution)/shard_map/ppermute | solution.py:972
  811.7 26.0 %collective-permute-start.40 = (bf16[3,512,256]{2,1,0:T(8,128)(2,1)}, bf16[3,512,256]{2,1,0:T(8,128)(2,1)}, u32[]{:S(2)}, u32[]{:S(2)}) collective-permute-start(bf16[3,512,256]{2,1,0:T(8,128)(2,1)} %get-tuple-element.164), channel_id=1, source_target_pairs={{0,4},{2,6},{4,0},{6,2},{1,5},{3,7},{5,1},{7,3},{8,12},{10,14},{12... | collective-permute-start | bytes 2359304 | tf_op jit(solution)/shard_map/ppermute | solution.py:972
  812.7 35.7 %collective-permute-start.41 = (bf16[3,512,256]{2,1,0:T(8,128)(2,1)}, bf16[3,512,256]{2,1,0:T(8,128)(2,1)}, u32[]{:S(2)}, u32[]{:S(2)}) collective-permute-start(bf16[3,512,256]{2,1,0:T(8,128)(2,1)} %get-tuple-element.165), channel_id=1, source_target_pairs={{0,6},{2,4},{4,2},{6,0},{1,7},{3,5},{5,3},{7,1},{8,14},{10,12},{12... | collective-permute-start | bytes 2359304 | tf_op jit(solution)/shard_map/ppermute | solution.py:972
  822.5 48.7 %collective-permute-start.48 = (bf16[512,1024]{1,0:T(8,128)(2,1)}, bf16[512,1024]{1,0:T(8,128)(2,1)S(1)}, u32[]{:S(2)}, u32[]{:S(2)}) collective-permute-start(bf16[512,1024]{1,0:T(8,128)(2,1)} %add.245.refs_7_), channel_id=1, source_target_pairs={{0,4},{2,6},{4,0},{6,2},{1,5},{3,7},{5,1},{7,3},{8,12},{10,14},{12... | collective-permute-start | bytes 3145736 | tf_op jit(solution)/shard_map/ppermute | solution.py:972
  895.2 29.7 %collective-permute-start.49 = (bf16[1024,3072]{1,0:T(8,128)(2,1)}, bf16[1024,3072]{1,0:T(8,128)(2,1)}, u32[]{:S(2)}, u32[]{:S(2)}) collective-permute-start(bf16[1024,3072]{1,0:T(8,128)(2,1)} %get-tuple-element.177), channel_id=1, source_target_pairs={{0,2},{2,0},{4,6},{6,4},{1,3},{3,1},{5,7},{7,5},{8,10},{10,8},{12,... | collective-permute-start | bytes 18874376 | tf_op jit(solution)/shard_map/ppermute | solution.py:972
  896.5 25.6 %collective-permute-start.50 = (bf16[128,4096]{1,0:T(8,128)(2,1)S(1)}, bf16[128,4096]{1,0:T(8,128)(2,1)S(1)}, u32[]{:S(2)}, u32[]{:S(2)}) collective-permute-start(bf16[128,4096]{1,0:T(8,128)(2,1)S(1)} %slice.77), channel_id=1, source_target_pairs={{0,4},{2,6},{4,0},{6,2},{1,5},{3,7},{5,1},{7,3},{8,12},{10,14},{12... | collective-permute-start | bytes 3145736 | tf_op jit(solution)/shard_map/ppermute | solution.py:972
  897.5 48.8 %collective-permute-start.46 = (bf16[512,2048]{1,0:T(8,128)(2,1)}, bf16[512,2048]{1,0:T(8,128)(2,1)}, u32[]{:S(2)}, u32[]{:S(2)}) collective-permute-start(bf16[512,2048]{1,0:T(8,128)(2,1)} %get-tuple-element.170.refs_7_), channel_id=1, source_target_pairs={{0,1},{1,0},{2,3},{3,2},{4,5},{5,4},{6,7},{7,6},{8,9},{9,8},{10,11... | collective-permute-start | bytes 6291464 | tf_op jit(solution)/shard_map/ppermute | solution.py:972
  898.6 91.9 %collective-permute-start.47 = (bf16[512,2048]{1,0:T(8,128)(2,1)S(1)}, bf16[512,2048]{1,0:T(8,128)(2,1)}, u32[]{:S(2)}, u32[]{:S(2)}) collective-permute-start(bf16[512,2048]{1,0:T(8,128)(2,1)S(1)} %copy-done.5), channel_id=1, source_target_pairs={{0,1},{1,0},{2,3},{3,2},{4,5},{5,4},{6,7},{7,6},{8,9},{9,8},{10,11... | collective-permute-start | bytes 6291464 | tf_op jit(solution)/shard_map/ppermute | solution.py:972
  930.1 73.9 %collective-permute-start.51 = (bf16[512,3072]{1,0:T(8,128)(2,1)}, bf16[512,3072]{1,0:T(8,128)(2,1)}, u32[]{:S(2)}, u32[]{:S(2)}) collective-permute-start(bf16[512,3072]{1,0:T(8,128)(2,1)} %add.248), channel_id=1, source_target_pairs={{0,4},{2,6},{4,0},{6,2},{1,5},{3,7},{5,1},{7,3},{8,12},{10,14},{12... | collective-permute-start | bytes 9437192 | tf_op jit(solution)/shard_map/ppermute | solution.py:972
  931.0 137.8 %reduce-scatter.9.cloned.1.call-start = ((), (), s32[]{:S(2)}) async-start(), calls=%async_computation.9 | async-start | bytes 3932160 | tf_op jit(solution)/shard_map/reduce_scatter | solution.py:1026
  1013.1 3.9 collective-permute-start.58
  1017.0 6.7 collective-permute-start.59
  1023.7 5.8 collective-permute-start.60
  1023.8 5.7 collective-permute-start.52
  1030.7 3.7 collective-permute-start.54
  1034.4 4.4 collective-permute-start.55
  1038.8 7.2 collective-permute-start.56
  (83 other events, 1182.8 us)
Sparse Core Ops, SparseCore 0:
  10.2 105.2 all-gather.3
  117.7 185.4 all-gather.5
  305.3 140.7 all-gather.7
  638.8 77.5 reduce-scatter.4
  718.7 144.9 reduce-scatter.6
  931.1 24.0 reduce-scatter.10
  1010.3 58.4 reduce-scatter.8

commit v3 on v2

--- a/solution.py
+++ b/solution.py
@@ -64,75 +64,68 @@
     return pieces[0] if len(pieces) == 1 else jnp.concatenate(pieces, axis=1)
 
 
-def project_kernel(place, rows, weight, cos_q, sin_q, cos_k, sin_k, *outs, extra):
-    outs = outs[extra:]
-    step = pl.program_id(0)
-    block = rows[...]
-    made = [dot(block, weight[j], 1, 0) for j in range(3)]
-    made[0] = turned(made[0], cos_q[...], sin_q[...], 1)
-    made[1] = turned(made[1], cos_k[...], sin_k[...], 1)
-    for offset, out in enumerate(outs):
-
-        @pl.when(step == offset)
-        def _(out=out):
-            for j in range(3):
-                out[j] = made[j].astype(BF16)
-
-
-def project(place, rows, qkv_full, tables, groups, after=()):
-    span, width = rows.shape
-    local = qkv_full.shape[2]
-    share = local // groups
-    if share % 128:
-        weight = qkv_full.reshape(3, width, groups, share).transpose(2, 0, 1, 3)
-        weight_spec = pl.BlockSpec(
-            (None, 3, width, share), lambda o, p: (jnp.bitwise_xor(o, p[0]), 0, 0, 0)
-        )
-    else:
-        weight = qkv_full
-        weight_spec = pl.BlockSpec(
-            (3, width, share), lambda o, p: (0, 0, jnp.bitwise_xor(o, p[0]))
-        )
-    table_spec = pl.BlockSpec(tables[0].shape, lambda o, p: (0, 0))
-    return pl.pallas_call(
-        partial(project_kernel, extra=len(after)),
-        grid_spec=pltpu.PrefetchScalarGridSpec(
-            num_scalar_prefetch=1,
-            grid=(groups,),
-            in_specs=[pl.BlockSpec((span, width), lambda o, p: (0, 0)), weight_spec]
-            + [table_spec] * 4
-            + [pl.BlockSpec(memory_space=pl.ANY)] * len(after),
-            out_specs=[pl.BlockSpec((3, span, share), lambda o, p: (0, 0, 0))] * groups,
-        ),
-        out_shape=[jax.ShapeDtypeStruct((3, span, share), BF16)] * groups,
-        compiler_params=params(),
-        cost_estimate=lasting(1.2e-8 * span * width * local),
-        name="project",
-    )(place, rows, weight, *tables, *after)
-
-
-def attend_kernel(meta, *refs, groups, heads, block, extra):
-    messages, rest = refs[:groups], refs[groups + extra :]
-    outs, log_ref = rest[:groups], rest[groups]
-    q_all, k_all, vt_all, o_all = rest[groups + 1 :]
+def project_kernel(place, *refs, groups, share):
+    blocks, refs = refs[:groups], refs[groups:]
+    gain, weight, cos_q, sin_q, cos_k, sin_k, low, made, held = refs
+    for offset, block in enumerate(blocks):
+
+        @pl.when(pl.program_id(0) == offset)
+        def _(block=block):
+            held[...] = block[...]
+
+    normal, _ = row_norm(held[...].astype(F32))
+    rows = (normal * gain[...]).astype(BF16)
+    low[...] = rows
+    out = dot(rows, weight[...], 1, 0)
+    queries = turned(out[:, :share], cos_q[...], sin_q[...], 1)
+    keys = turned(out[:, share : 2 * share], cos_k[...], sin_k[...], 1)
+    made[...] = jnp.concatenate([queries, keys, out[:, 2 * share :]], axis=1).astype(BF16)
+
+
+def project(place, blocks, gain, weight, tables, after=()):
+    groups = len(blocks)
+    span, model = blocks[0].shape
+    width = weight.shape[1]
+    lanes = tables[0].shape[1]
+
+    def here(n, p):
+        return (jnp.bitwise_xor(n, p[0]), 0)
+
+    return call(
+        partial(project_kernel, groups=groups, share=width // 3),
+        "project",
+        (groups,),
+        [(block, (span, model), None) for block in blocks]
+        + [(gain, (1, model), None), (weight, (model, width), None)]
+        + [(table, (span, lanes), here) for table in tables],
+        [
+            ((groups * span, model), BF16, (span, model), here),
+            ((groups * span, width), BF16, (span, width), here),
+        ],
+        [pltpu.VMEM((span, model), BF16)],
+        5e-9 * groups * span * model * width,
+        after,
+        place,
+    )
+
+
+def attend_kernel(meta, projected, *refs, groups, heads, block):
+    outs, log_ref, vt_all, o_all = refs[:groups], refs[groups], refs[groups + 1], refs[groups + 2]
     step = pl.program_id(0)
     length, place = meta[0], meta[1]
-    span = messages[0].shape[1]
+    share = heads * HEAD_DIM
+    span = outs[0].shape[0]
+
+    def lanes(part, h):
+        return slice(part * share + h * HEAD_DIM, part * share + (h + 1) * HEAD_DIM)
 
     @pl.when(step == 0)
     def _():
-        for offset, message in enumerate(messages):
-            at = pl.multiple_of(jnp.bitwise_xor(place, offset) * span, span)
-            q_all[pl.ds(at, span), :] = message[0]
-            k_all[pl.ds(at, span), :] = message[1]
-            for h in range(heads):
-                lanes = slice(h * HEAD_DIM, (h + 1) * HEAD_DIM)
-                vt_all[h, :, pl.ds(at, span)] = message[2, :, lanes].T
+        for h in range(heads):
+            vt_all[h] = projected[:, lanes(2, h)].T
 
     start = pl.multiple_of(step * block, block)
-    queries = [
-        q_all[pl.ds(start, block), h * HEAD_DIM : (h + 1) * HEAD_DIM] for h in range(heads)
-    ]
+    queries = [projected[pl.ds(start, block), lanes(0, h)] for h in range(heads)]
     scale = SCORE_SCALE * LOG2_E
 
     def keys_block(index, carry, masked):
@@ -144,8 +137,7 @@
         new = []
         for h in range(heads):
             top, total, mixed = carry[h]
-            keys = k_all[pl.ds(at, block), h * HEAD_DIM : (h + 1) * HEAD_DIM]
-            scores = dot(keys, queries[h], 1, 1)
+            scores = dot(projected[pl.ds(at, block), lanes(1, h)], queries[h], 1, 1)
             if masked:
                 scores = jnp.where(allowed, scores, NEGATIVE)
             higher = jnp.maximum(top, jnp.max(scores, axis=0, keepdims=True))
@@ -182,72 +174,57 @@
             out[...] = o_all[pl.ds(at, span), :]
 
 
-def attend(meta, messages, after=()):
-    groups = len(messages)
-    _, span, share = messages[0].shape
+def attend(meta, projected, groups, after=()):
+    count, width = projected.shape
+    share = width // 3
+    span = count // groups
     heads = share // HEAD_DIM
+    block = min(512, span)
+    results = call(
+        partial(attend_kernel, groups=groups, heads=heads, block=block),
+        "attend",
+        (count // block,),
+        [(projected, (count, width), None)],
+        [((span, share), BF16, (span, share), None)] * groups
+        + [((heads, count), F32, (heads, block), lambda n, m: (0, n))],
+        [pltpu.VMEM((heads, HEAD_DIM, count), BF16), pltpu.VMEM((count, share), BF16)],
+        2.9e-8 * count * count * share,
+        after,
+        meta,
+    )
+    return results[:groups], results[groups]
+
+
+def attend_back_kernel(meta, projected, *refs, groups, heads, block):
+    grads, mixed = refs[:groups], refs[groups : 2 * groups]
+    log_ref, cos_q, sin_q, cos_k, sin_k, out = refs[2 * groups : 2 * groups + 6]
+    g_all, kt_all, dot_all, dqt_all, dk_sum, dv_sum = refs[2 * groups + 6 :]
+    length, place = meta[0], meta[1]
+    span = grads[0].shape[0]
     count = groups * span
-    block = min(512, span)
-    message_spec = pl.BlockSpec((3, span, share), lambda n, m: (0, 0, 0))
-    out_spec = pl.BlockSpec((span, share), lambda n, m: (0, 0))
-    results = pl.pallas_call(
-        partial(attend_kernel, groups=groups, heads=heads, block=block, extra=len(after)),
-        grid_spec=pltpu.PrefetchScalarGridSpec(
-            num_scalar_prefetch=1,
-            grid=(count // block,),
-            in_specs=[message_spec] * groups
-            + [pl.BlockSpec(memory_space=pl.ANY)] * len(after),
-            out_specs=[out_spec] * groups + [pl.BlockSpec((heads, block), lambda n, m: (0, n))],
-            scratch_shapes=[
-                pltpu.VMEM((count, share), BF16),
-                pltpu.VMEM((count, share), BF16),
-                pltpu.VMEM((heads, HEAD_DIM, count), BF16),
-                pltpu.VMEM((count, share), BF16),
-            ],
-        ),
-        out_shape=[jax.ShapeDtypeStruct((span, share), BF16)] * groups
-        + [jax.ShapeDtypeStruct((heads, count), F32)],
-        compiler_params=params(),
-        cost_estimate=lasting(2.9e-8 * count * count * share),
-        name="attend",
-    )(meta, *messages, *after)
-    return results[:groups], results[groups]
-
-
-def attend_back_kernel(meta, *refs, groups, heads, block, extra):
-    messages, grads, mixed = refs[:groups], refs[groups : 2 * groups], refs[2 * groups : 3 * groups]
-    log_ref, cos_q, sin_q, cos_k, sin_k = refs[3 * groups : 3 * groups + 5]
-    refs = refs[3 * groups + 5 + extra :]
-    outs, scratch = refs[:groups], refs[groups:]
-    q_all, k_all, v_all, g_all, kt_all, dot_all, dqt_all, dk_sum, dv_sum, out_all = scratch
-    length, place = meta[0], meta[1]
-    span = messages[0].shape[1]
-    count = groups * span
+    share = heads * HEAD_DIM
     scale = SCORE_SCALE * LOG2_E
 
-    def lanes(h):
-        return slice(h * HEAD_DIM, (h + 1) * HEAD_DIM)
-
+    def lanes(part, h):
+        return slice(part * share + h * HEAD_DIM, part * share + (h + 1) * HEAD_DIM)
+
+    for h in range(heads):
+        kt_all[h] = projected[:, lanes(1, h)].T
     for offset in range(groups):
         at = pl.multiple_of(jnp.bitwise_xor(place, offset) * span, span)
-        message = messages[offset]
-        q_all[pl.ds(at, span), :] = message[0]
-        k_all[pl.ds(at, span), :] = message[1]
-        v_all[pl.ds(at, span), :] = message[2]
         g_all[pl.ds(at, span), :] = grads[offset][...]
         both = grads[offset][...].astype(F32) * mixed[offset][...].astype(F32)
         for h in range(heads):
-            kt_all[h, :, pl.ds(at, span)] = message[1, :, lanes(h)].T
             dot_all[h : h + 1, pl.ds(at, span)] = jnp.sum(
-                both[:, lanes(h)].T, axis=0, keepdims=True
+                both[:, lanes(0, h)].T, axis=0, keepdims=True
             )
     dqt_all[...] = jnp.zeros_like(dqt_all)
     query_blocks = count // block
 
     def keys_block(index, _):
         key_at = pl.multiple_of(index * block, block)
-        keys = [k_all[pl.ds(key_at, block), lanes(h)] for h in range(heads)]
-        values = [v_all[pl.ds(key_at, block), lanes(h)] for h in range(heads)]
+        keys = [projected[pl.ds(key_at, block), lanes(1, h)] for h in range(heads)]
+        values = [projected[pl.ds(key_at, block), lanes(2, h)] for h in range(heads)]
         dk_sum[...] = jnp.zeros_like(dk_sum)
         dv_sum[...] = jnp.zeros_like(dv_sum)
 
@@ -258,8 +235,8 @@
                 query_pos = at + lax.broadcasted_iota(jnp.int32, (block, block), 1)
                 allowed = (key_pos <= query_pos) & (key_pos < length)
             for h in range(heads):
-                query = q_all[pl.ds(at, block), lanes(h)]
-                grad = g_all[pl.ds(at, block), lanes(h)]
+                query = projected[pl.ds(at, block), lanes(0, h)]
+                grad = g_all[pl.ds(at, block), lanes(0, h)]
                 scores = dot(keys[h], query, 1, 1)
                 weights = jnp.exp2(scores * scale - log_ref[h : h + 1, pl.ds(at, block)])
                 if masked:
@@ -281,8 +258,8 @@
         dk = jnp.concatenate([dk_sum[h] for h in range(heads)], axis=1) * SCORE_SCALE
         dv = jnp.concatenate([dv_sum[h] for h in range(heads)], axis=1)
         turn = (cos_k[pl.ds(key_at, block), :], sin_k[pl.ds(key_at, block), :])
-        out_all[1, pl.ds(key_at, block), :] = turned(dk, *turn, -1).astype(BF16)
-        out_all[2, pl.ds(key_at, block), :] = dv.astype(BF16)
+        out[pl.ds(key_at, block), share : 2 * share] = turned(dk, *turn, -1).astype(BF16)
+        out[pl.ds(key_at, block), 2 * share :] = dv.astype(BF16)
         return 0
 
     used = (length + block - 1) // block
@@ -290,57 +267,82 @@
 
     def no_keys(index, _):
         at = pl.multiple_of(index * block, block)
-        for j in (1, 2):
-            out_all[j, pl.ds(at, block), :] = jnp.zeros((block, heads * HEAD_DIM), BF16)
+        out[pl.ds(at, block), share:] = jnp.zeros((block, 2 * share), BF16)
         return 0
 
     lax.fori_loop(used, query_blocks, no_keys, 0)
     for index in range(query_blocks):
         at = slice(index * block, (index + 1) * block)
         dq = jnp.concatenate([dqt_all[h, :, at].T for h in range(heads)], axis=1) * SCORE_SCALE
-        out_all[0, at, :] = turned(dq, cos_q[at, :], sin_q[at, :], -1).astype(BF16)
-    for offset, out in enumerate(outs):
-        at = pl.multiple_of(jnp.bitwise_xor(place, offset) * span, span)
-        out[...] = out_all[:, pl.ds(at, span), :]
-
-
-def attend_back(meta, messages, grads, mixed, logs, tables, after=(), weight=1):
-    groups = len(messages)
-    _, span, share = messages[0].shape
+        out[at, :share] = turned(dq, cos_q[at, :], sin_q[at, :], -1).astype(BF16)
+
+
+def attend_back(meta, projected, grads, mixed, logs, tables, after=(), weight=1):
+    groups = len(grads)
+    count, width = projected.shape
+    share = width // 3
+    span = count // groups
     heads = share // HEAD_DIM
-    count = groups * span
     block = min(512, span)
-    message_spec = pl.BlockSpec((3, span, share), lambda n, m: (0, 0, 0))
-    row_spec = pl.BlockSpec((span, share), lambda n, m: (0, 0))
-    table_spec = pl.BlockSpec(tables[0].shape, lambda n, m: (0, 0))
-    return pl.pallas_call(
-        partial(
-            attend_back_kernel, groups=groups, heads=heads, block=block, extra=len(after)
-        ),
-        grid_spec=pltpu.PrefetchScalarGridSpec(
-            num_scalar_prefetch=1,
-            grid=(1,),
-            in_specs=[message_spec] * groups
-            + [row_spec] * (2 * groups)
-            + [pl.BlockSpec(logs.shape, lambda n, m: (0, 0))]
-            + [table_spec] * 4
-            + [pl.BlockSpec(memory_space=pl.ANY)] * len(after),
-            out_specs=[message_spec] * groups,
-            scratch_shapes=[pltpu.VMEM((count, share), BF16)] * 4
-            + [
-                pltpu.VMEM((heads, HEAD_DIM, count), BF16),
-                pltpu.VMEM((heads, count), F32),
-                pltpu.VMEM((heads, HEAD_DIM, count), F32),
-                pltpu.VMEM((heads, block, HEAD_DIM), F32),
-                pltpu.VMEM((heads, block, HEAD_DIM), F32),
-                pltpu.VMEM((3, count, share), BF16),
-            ],
-        ),
-        out_shape=[jax.ShapeDtypeStruct((3, span, share), BF16)] * groups,
-        compiler_params=params(),
-        cost_estimate=lasting(4.2e-8 * count * count * share * weight),
-        name="attend_back",
-    )(meta, *messages, *grads, *mixed, logs, *tables, *after)
+    return call(
+        partial(attend_back_kernel, groups=groups, heads=heads, block=block),
+        "attend_back",
+        (1,),
+        [(projected, (count, width), None)]
+        + [(piece, (span, share), None) for piece in (*grads, *mixed)]
+        + [(logs, logs.shape, None)]
+        + [(table, table.shape, None) for table in tables],
+        [((count, width), BF16, (count, width), None)],
+        [
+            pltpu.VMEM((count, share), BF16),
+            pltpu.VMEM((heads, HEAD_DIM, count), BF16),
+            pltpu.VMEM((heads, count), F32),
+            pltpu.VMEM((heads, HEAD_DIM, count), F32),
+            pltpu.VMEM((heads, block, HEAD_DIM), F32),
+            pltpu.VMEM((heads, block, HEAD_DIM), F32),
+        ],
+        4.2e-8 * count * count * share * weight,
+        after,
+        meta,
+    )[0]
+
+
+def heads_grad_kernel(*refs, sequences):
+    grads, lows, out, turned_grads = (
+        refs[:sequences],
+        refs[sequences : 2 * sequences],
+        refs[2 * sequences],
+        refs[2 * sequences + 1],
+    )
+    count = grads[0].shape[0]
+
+    @pl.when(pl.program_id(0) == 0)
+    def _():
+        for s in range(sequences):
+            turned_grads[:, s * count : (s + 1) * count] = grads[s][...].T
+
+    total = dot(turned_grads[:, :count], lows[0][...], 1, 0)
+    for s in range(1, sequences):
+        total += dot(turned_grads[:, s * count : (s + 1) * count], lows[s][...], 1, 0)
+    out[...] = total.T.astype(BF16)
+
+
+def heads_grad(lows, grads, after=()):
+    sequences = len(lows)
+    count, model = lows[0].shape
+    width = grads[0].shape[1]
+    tile = 512
+    return call(
+        partial(heads_grad_kernel, sequences=sequences),
+        "heads_grad",
+        (model // tile,),
+        [(grad, (count, width), None) for grad in grads]
+        + [(low, (count, tile), lambda n: (0, n)) for low in lows],
+        [((model, width), BF16, (tile, width), lambda n: (n, 0))],
+        [pltpu.VMEM((width, sequences * count), BF16)],
+        3e-9 * sequences * count * model * width,
+        after,
+    )[0]
 
 
 def normed_rows(block, column_mean, column_std, gain):
@@ -464,7 +466,9 @@
     )(place, *operands, *after)
 
 
-def call(kernel, name, grid, ins, outs, scratch, us, after=(), scalars=None):
+def call(kernel, name, grid, ins, outs, scratch, us, after=(), scalars=None, into=None):
+    if into is not None:
+        after = [into, *after]
     extra = len(after)
     first = 0 if scalars is None else 1
     count = first + len(ins)
@@ -488,10 +492,32 @@
             scratch_shapes=scratch,
         ),
         out_shape=[jax.ShapeDtypeStruct(shape, dtype) for shape, dtype, _, _ in outs],
+        input_output_aliases={} if into is None else {count: 0},
         compiler_params=params(),
         cost_estimate=lasting(us),
         name=name,
     )(*(() if scalars is None else (scalars,)), *[array for array, _, _ in ins], *after)
+
+
+def pack_kernel(columns, rows, out):
+    width = columns.shape[1]
+    out[:, :width] = columns[...]
+    out[:, width:] = rows[...].T
+
+
+def pack(columns, rows, after=()):
+    height, width = columns.shape
+    total = width + rows.shape[0]
+    return call(
+        pack_kernel,
+        "pack",
+        (1,),
+        [(columns, columns.shape, None), (rows, rows.shape, None)],
+        [((height, total), BF16, (height, total), None)],
+        [],
+        1,
+        after,
+    )[0]
 
 
 def collect_kernel(place, *refs, groups):
@@ -909,63 +935,74 @@
     )
 
 
-def first_back_kernel(place, *refs, groups):
-    pieces, (weight, tokens, whole, branch, gain_grad, total) = refs[:groups], refs[groups:]
+def first_back_kernel(order, grads, low, weight, gain, away, kept, gain_grad, total):
     step = pl.program_id(0)
-    for offset, piece in enumerate(pieces):
-
-        @pl.when(step == offset)
-        def _(piece=piece, offset=offset):
-            whole[...] = piece[...]
-            made = dot(piece[0], weight[0], 1, 1)
-            for j in (1, 2):
-                made += dot(piece[j], weight[j], 1, 1)
-            if offset:
-                total[...] += made
-            else:
-                total[...] = made
-
-    @pl.when(step == groups - 1)
-    def _():
-        normal, _ = row_norm(tokens[...].astype(F32))
-        grad = total[...]
-        gain_grad[...] = jnp.sum(grad * normal, axis=0, keepdims=True)
-        branch[...] = grad.astype(BF16)
-
-
-def first_back(place, pieces, qkv_full, tokens, after=()):
-    groups = len(pieces)
-    _, span, share = pieces[0].shape
-    model, local = qkv_full.shape[1:]
-    if share % 128:
-        stacked = jnp.stack(pieces)
-        whole = jnp.concatenate(
-            [
-                lax.dynamic_index_in_dim(stacked, jnp.bitwise_xor(place[0], n), 0, False)
-                for n in range(groups)
-            ],
-            axis=2,
-        )
-        grad = jnp.einsum("jte,jde->td", whole, qkv_full, preferred_element_type=F32)
-        normal, _ = row_norm(tokens.astype(F32))
-        return whole, grad.astype(BF16), jnp.sum(grad * normal, axis=0, keepdims=True)
-    across = lambda o, p: (0, 0, jnp.bitwise_xor(o, p[0]))
-    return call(
-        partial(first_back_kernel, groups=groups),
+    grad = dot(grads[...], weight[...], 1, 1)
+    made = grad.astype(BF16)
+
+    @pl.when(step < 2)
+    def _():
+        away[...] = made
+
+    @pl.when(step >= 2)
+    def _():
+        kept[...] = made
+
+    @pl.when(step == 0)
+    def _():
+        total[...] = jnp.zeros_like(total)
+
+    total[...] += jnp.sum(grad * low[...].astype(F32), axis=0, keepdims=True)
+
+    @pl.when(step == pl.num_programs(0) - 1)
+    def _():
+        gain_grad[...] = total[...] / gain[...]
+
+
+def first_back(order, grads, low, weight, gain, groups, after=()):
+    count, width = grads.shape
+    model = weight.shape[0]
+    span = count // groups
+    rows = (span, model)
+    return call(
+        first_back_kernel,
         "first_back",
         (groups,),
-        [(piece, (3, span, share), None) for piece in pieces]
-        + [(qkv_full, (3, model, share), across), (tokens, (span, model), None)],
-        [
-            ((3, span, local), BF16, (3, span, share), across),
-            ((span, model), BF16, (span, model), None),
+        [
+            (grads, (span, width), lambda n, p: (p[n], 0)),
+            (low, rows, lambda n, p: (p[n], 0)),
+            (weight, (model, width), None),
+            (gain, (1, model), None),
+        ],
+        [
+            ((2 * span, model), BF16, rows, lambda n, p: (jnp.minimum(n, 1), 0)),
+            ((2 * span, model), BF16, rows, lambda n, p: (jnp.maximum(n - 2, 0), 0)),
             ((1, model), F32, (1, model), None),
         ],
-        [pltpu.VMEM((span, model), F32)],
-        1.34e-8 * span * model * local,
-        after,
-        place,
-    )
+        [pltpu.VMEM((1, model), F32)],
+        4.5e-9 * count * model * width,
+        after,
+        order,
+    )
+
+
+def relay_kernel(array, out):
+    out[...] = array[...]
+
+
+def relay(array, after):
+    rows = min(128, array.shape[0])
+    block = (rows, array.shape[1])
+    return call(
+        relay_kernel,
+        "relay",
+        (array.shape[0] // rows,),
+        [(array, block, lambda n: (n, 0))],
+        [(array.shape, array.dtype, block, lambda n: (n, 0))],
+        [],
+        1,
+        after,
+    )[0]
 
 
 def exchange(array, axis, size, offset):
@@ -995,6 +1032,64 @@
         [],
         1.5e-6 * rows * width,
         after,
+    )[0]
+
+
+def result_kernel(own, other, hidden, out):
+    out[...] = (hidden[...] + (own[...].astype(F32) + other[...].astype(F32))).astype(BF16)
+
+
+def result_rows(number, count, own, other, hidden, into, after=()):
+    span, model = hidden.shape
+    tile = min(128, span)
+    block = (tile, model)
+    return call(
+        result_kernel,
+        "result",
+        (span // tile,),
+        [(array, block, lambda n: (n, 0)) for array in (own, other, hidden)],
+        [((count, span, model), BF16, (None, *block), lambda n: (number, n, 0))],
+        [],
+        1.5e-6 * span * model,
+        after,
+        None,
+        into,
+    )[0]
+
+
+def input_kernel(tokens, own, other, gain, grads, out):
+    normal, std = row_norm(tokens[...].astype(F32))
+    part = (own[...].astype(F32) + other[...].astype(F32)) * gain[...]
+    first = std * (
+        part
+        - jnp.mean(part, axis=-1, keepdims=True)
+        - normal * jnp.mean(part * normal, axis=-1, keepdims=True)
+    )
+    out[...] = (grads[...] + first).astype(BF16)
+
+
+def input_rows(number, count, tokens, own, other, gain, grads, into, after=()):
+    span, model = tokens.shape
+    tile = min(128, span)
+    block = (tile, model)
+    by_row = lambda n: (n, 0)
+    return call(
+        input_kernel,
+        "input_grad",
+        (span // tile,),
+        [
+            (tokens, block, by_row),
+            (own, block, by_row),
+            (other, block, by_row),
+            (gain, (1, model), None),
+            (grads, block, by_row),
+        ],
+        [((count, span, model), BF16, (None, *block), lambda n: (number, n, 0))],
+        [],
+        2e-6 * span * model,
+        after,
+        None,
+        into,
     )[0]
 
 
@@ -1015,14 +1110,17 @@
             self.far = exchange(near, "seq", self.groups, 2)
         return near
 
+    def own(self, after=()):
+        half = self.kept.shape[0] // 2
+        return add([(self.kept, half), (self.got, half), (self.far, 0)], half, after)
+
     def chips(self, after=()):
         if self.z_first:
             half = self.rows.shape[0] // 2
             far = exchange(self.rows[:half], "seq", self.groups, 2)
             self.out = self.rows[half:].astype(F32) + far.astype(F32)
             return self.out
-        half = self.kept.shape[0] // 2
-        own = add([(self.kept, half), (self.got, half), (self.far, 0)], half, after)
+        own = self.own(after)
         self.out = lax.psum_scatter(own, "dp", scatter_dimension=0, tiled=True).astype(F32)
         return own
 
@@ -1039,13 +1137,25 @@
     return sums, exchange(sums, "mp", 2, 1)
 
 
+def axis_sum(array, axis, size):
+    offset = 1
+    while offset < size:
+        array = array + exchange(array, axis, size, offset)
+        offset *= 2
+    return array
+
+
 def data_sum(array, devices, groups):
-    for axis, size in (("seq", groups), ("dp", devices)):
-        offset = 1
-        while offset < size:
-            array = array + exchange(array, axis, size, offset)
-            offset *= 2
-    return array
+    array = axis_sum(array + exchange(array, "seq", groups, 1), "dp", devices)
+    return array + exchange(array, "seq", groups, 2)
+
+
+def in_order(pieces, place):
+    stacked = jnp.stack(pieces)
+    return [
+        lax.dynamic_index_in_dim(stacked, jnp.bitwise_xor(place, n), 0, False)
+        for n in range(len(pieces))
+    ]
 
 
 def pass_round(pieces, groups):
@@ -1095,14 +1205,37 @@
     ffn_width = in_weight.shape[1]
     share = local_width // groups
 
+    blocks = []
+    for s in each:
+        far = exchange(tokens[s], "seq", groups, 2)
+        blocks.append([tokens[s], exchange(tokens[s], "seq", groups, 1), far])
+    blocks[0].append(exchange(blocks[0][2], "seq", groups, 1))
+
     number = lax.axis_index("dp") * groups + place
     sizes = [gain_in.size, gain_mid.size, gain_attn.size, gain_ffn.size]
     cuts = [sum(sizes[:n]) for n in range(5)]
-    flat = jnp.concatenate(
-        [gain_in, gain_mid, gain_attn.reshape(-1), gain_ffn.reshape(-1)]
-    ).reshape(1, -1)
-    row = lax.broadcasted_iota(jnp.int32, (shards, 1), 0)
-    all_gains = data_sum(jnp.where(row == number, flat, 0).astype(F32), devices, groups)
+    chunk = qkv_weight.shape[1]
+    by_device = qkv_weight.reshape(3, chunk, groups, share).transpose(2, 1, 0, 3)
+    by_device = by_device.reshape(groups, chunk, 3 * share)
+    flat = jnp.concatenate([gain_in, gain_mid, gain_attn.reshape(-1), gain_ffn.reshape(-1)])
+    flat = jnp.pad(flat, (0, 16 * 3 * share - cuts[4])).reshape(16, 3 * share)
+    pieces = [
+        jnp.concatenate(
+            [
+                lax.dynamic_index_in_dim(by_device, jnp.bitwise_xor(place, n), 0, False),
+                flat,
+            ]
+        )
+        for n in range(groups)
+    ]
+    pieces = in_order(pass_round(pieces, groups), place)
+    rows = jnp.concatenate([piece[:chunk] for piece in pieces], axis=0)
+    heads_weight = lax.all_gather(rows, "dp", axis=0, tiled=True)
+
+    flat = jnp.stack([piece[chunk:].reshape(-1)[: cuts[4]] for piece in pieces]).reshape(1, -1)
+    row = lax.broadcasted_iota(jnp.int32, (devices, 1), 0)
+    all_gains = jnp.where(row == lax.axis_index("dp"), flat, 0).astype(F32)
+    all_gains = axis_sum(all_gains, "dp", devices).reshape(shards, cuts[4])
     pieces = [all_gains[:, cuts[n] : cuts[n + 1]] for n in range(4)]
     gain_one, gain_three = pieces[0].reshape(1, -1), pieces[1].reshape(1, -1)
     gain_two = pieces[2].reshape(shards, heads_here, -1).transpose(1, 0, 2).reshape(1, -1)
@@ -1110,39 +1243,42 @@
         pieces[3].reshape(shards, ffn_width // HEAD_DIM, -1).transpose(1, 0, 2).reshape(1, -1)
     )
 
-    qkv_full = lax.all_gather(qkv_weight, data, axis=1, tiled=True)
     near_full = lax.all_gather(
-        jnp.concatenate([in_weight, out_weight.T], axis=1), data, axis=0, tiled=True
+        pack(in_weight, out_weight, [all_gains, blocks[0][2]]), data, axis=0, tiled=True
     )
     down_full = lax.all_gather(down_weight, data, axis=1, tiled=True)
 
     count = span * groups
     tables = xpos_tables(count, min(128, share))
-    tables_here = [lax.dynamic_slice_in_dim(t, place * span, span, 0) for t in tables]
     spot = place.reshape(1)
     metas = [jnp.stack([lengths[s], place]) for s in each]
     full_units = ffn_width * units
 
-    first_low = []
-    for s in each:
-        normal, _ = row_norm(tokens[s].astype(F32))
-        first_low.append((normal * gain_one).astype(BF16))
-    messages, mixed, logs, attended, att_sums, inner, branch = [], [], [], [], [], [], []
+    first_low, projected = [], []
+    mixed, logs, attended, att_sums, inner, branch = [], [], [], [], [], []
     last = ()
     for s in each:
-        made = project(spot, first_low[s], qkv_full, tables_here, groups, last)
-        messages.append(pass_round(made, groups))
-        last = [made[0]]
-    for s in each:
-        outs, log = attend(metas[s], messages[s], last)
+        low, made = project(spot, blocks[s], gain_one, heads_weight, tables, last)
+        first_low.append(low)
+        projected.append(made)
+        outs, log = attend(metas[s], made, groups)
         mixed.append(outs)
         logs.append(log)
         last = [log]
+        if s == 0:
+            far = relay(blocks[1][2], last)
+            blocks[1].append(exchange(far, "seq", groups, 1))
+            last = [far]
+    passed = [pass_round(mixed[s], groups) for s in each]
+    last = [*last, *passed[-1][1:]]
     for s in each:
-        whole, sums = collect(spot, pass_round(mixed[s], groups), last)
+        whole, sums = collect(spot, passed[s], last)
         attended.append(whole)
         att_sums.append(mp_rows(sums, units))
-        low, terms = out_branch(whole, *att_sums[s], gain_two, near_full, model)
+        last = [sums]
+    last = [other for _, other in att_sums]
+    for s in each:
+        low, terms = out_branch(attended[s], *att_sums[s], gain_two, near_full, model, last)
         inner.append(low)
         branch.append(mp_sum(terms, units))
         last = [terms]
@@ -1186,12 +1322,13 @@
         terms = narrow(active[s], *act_sums[s], gain_four, down_full, full_units, after)
         return mp_sum(terms, units)
 
-    def result(s, after):
-        own, other = wide_terms[s]
-        return add([(own, 0), (other, 0), (hidden[s], 0)], span, after)
-
-    gain_three_grad, gain_two_grad = 0.0, 0.0
-    grad_hidden, hidden_low, grads, returned = [], [], [], []
+    def result(s, into, after):
+        return result_rows(s, sequences, *wide_terms[s], hidden[s], into, after)
+
+    gain_three_grad, gain_two_grad, gain_one_grad = 0.0, 0.0, 0.0
+    order = jnp.bitwise_xor(place, jnp.array([3, 1, 2, 0], jnp.int32))
+    first_sums = []
+    grad_hidden, hidden_low, grads, projected_grads = [], [], [], []
     wide_terms = [finish(0, last)]
     last = [wide_terms[0][0]]
     for s in each:
@@ -1220,18 +1357,46 @@
         grads.append(pass_round(parts, groups))
     for s in each:
         made = attend_back(
-            metas[s], messages[s], grads[s], mixed[s], logs[s], tables, last,
+            metas[s], projected[s], grads[s], mixed[s], logs[s], tables, last,
             BACK_WEIGHT if s == 0 else 1,
         )
-        returned.append(pass_round(made, groups))
-        last = [made[0]]
+        projected_grads.append(made)
+        last = [made]
         if s == 0:
-            out_parts = weight_grad(spot, hidden_low, inner, devices, groups, None, False, last)
+            out_parts = weight_grad(
+                spot, hidden_low, inner, devices, groups, None, False, last + grads[1][1:]
+            )
             out_sum = ScatterSum(out_parts, groups)
-            last = [out_parts[0], down_sum.out]
-
-    early = jnp.concatenate(
-        [
+            results = result(0, None, [out_parts[0], down_sum.out])
+            last = [results]
+        else:
+            first_terms = [mp_sum(first_sums[0].own(last), units)]
+            results = result(1, results, [first_terms[0][0]])
+            last = [out_sum.chips([results])]
+        away, kept, gain_part = first_back(
+            order, made, first_low[s], heads_weight, gain_one, groups, last
+        )
+        gain_one_grad += gain_part
+        first_sums.append(ScatterSum((away, kept), groups))
+        if s == 0:
+            last = [first_sums[0].mates([away])]
+            last = [out_sum.mates(last)]
+        else:
+            last = [away, in_sum.rows]
+
+    heads_part = heads_grad(first_low, projected_grads, last)
+    heads_rows = lax.psum_scatter(heads_part, "dp", scatter_dimension=0, tiled=True)
+    last = [first_sums[1].mates([heads_part])]
+    gain_one_sums = mp_rows(gain_one_grad, units)
+
+    def input_grad(s, into, after):
+        return input_rows(
+            s, sequences, tokens[s], *first_terms[s], gain_one, grad_hidden[s], into, after
+        )
+
+    gain_rows = jnp.concatenate(
+        [
+            (gain_one_sums[0] + gain_one_sums[1]).reshape(shards, -1),
             gain_three_grad.reshape(shards, -1),
             gain_two_grad.reshape(heads_here, shards, -1).transpose(1, 0, 2).reshape(shards, -1),
             gain_four_grad.reshape(ffn_width // HEAD_DIM, shards, -1)
@@ -1240,43 +1405,25 @@
         ],
         axis=1,
     )
-    early = lax.dynamic_index_in_dim(data_sum(early, devices, groups), number, 0, False)
-    cuts = [cut - cuts[1] for cut in cuts]
-    three, two, four = [early[cuts[n] : cuts[n + 1]] for n in (1, 2, 3)]
-
-    gain_one_grad = 0.0
-    stacked, first_terms = [], []
-    results = [result(0, last)]
-    last = [out_sum.mates([results[0]])]
-    for s in each:
-        whole, terms, gain_part = first_back(spot, returned[s], qkv_full, tokens[s], last)
-        stacked.append(whole)
-        gain_one_grad += gain_part
-        first_terms.append(mp_sum(terms, units))
-        last = [terms]
-    results.append(result(1, last))
-    last = [out_sum.chips([results[1]])]
-    qkv_parts = weight_grad(spot, first_low, stacked, devices, groups, None, False, last)
-    qkv_sum = ScatterSum(qkv_parts, groups)
-    grad_inputs = []
-    for s in each:
-        normal, std = row_norm(tokens[s].astype(F32))
-        own, other = first_terms[s]
-        part = (own.astype(F32) + other.astype(F32)) * gain_one
-        grad_first = std * (
-            part
-            - jnp.mean(part, axis=-1, keepdims=True)
-            - normal * jnp.mean(part * normal, axis=-1, keepdims=True)
-        )
-        grad_inputs.append((grad_hidden[s] + grad_first).astype(BF16))
-    qkv_sum.mates([in_sum.chips()])
-    qkv_sum.chips([grad_inputs[0]])
-    grad_qkv_w = qkv_sum.out.reshape(-1, 3, local_width).transpose(1, 0, 2)
-    own, other = mp_rows(gain_one_grad.reshape(shards, -1), units)
-    one = lax.dynamic_index_in_dim(data_sum(own + other, devices, groups), number, 0, False)
+    gain_rows = data_sum(gain_rows, devices, groups)
+
+    grad_input = input_grad(0, None, last)
+    first_terms.append(mp_sum(first_sums[1].own([grad_input, gain_rows]), units))
+    in_sum.chips()
+    pieces = [
+        lax.dynamic_slice_in_dim(heads_rows, jnp.bitwise_xor(place, n) * chunk, chunk, 0)
+        for n in range(groups)
+    ]
+    pieces = pass_round(pieces, groups)
+    grad_input = input_grad(1, grad_input, [*last, *pieces[1:]])
+    rows = jnp.stack(in_order(pieces, place)).astype(F32)
+    grad_qkv_w = rows.reshape(groups, chunk, 3, share).transpose(2, 1, 0, 3)
+    grad_qkv_w = grad_qkv_w.reshape(3, chunk, local_width)
+    gain_sums = lax.dynamic_index_in_dim(gain_rows, number, 0, False)
+    one, three, two, four = [gain_sums[cuts[n] : cuts[n + 1]] for n in range(4)]
     return (
-        jnp.stack(results),
-        jnp.stack(grad_inputs),
+        results,
+        grad_input,
         grad_qkv_w,
         out_sum.out.T,
         in_sum.out,

time: 1080 us -> 1010 us (0.935)
  waiting for transfers between devices: 380 us -> 278 us
  Pallas kernels: 543 us -> 588 us
  other arithmetic: 45.2 us -> 16.4 us
    pallas_call x27 -> x40, Pallas kernels: 289 us -> 529 us  [call(): pl.pallas_call(run, grid_spec=pltpu.PrefetchScalarGridSpec(num_scalar_pre...]
    pallas_call x6 -> x0, Pallas kernels: 176 us -> none  [the longest x2 89.1 us: attend_back(): pl.pallas_call(partial(attend_back_kernel, groups=groups, heads=heads, bl...]
    all_gather x2, waiting for transfers between devices: 65.8 us -> 0.01 us  [the longest x1 0.01 us: body(): heads_weight = lax.all_gather(rows, 'dp', axis=0, tiled=True)]
    pallas_call x4 -> x3, Pallas kernels: 78.2 us -> 59.2 us  [weight_grad(): pl.pallas_call(partial(weight_grad_kernel, sequences=sequences, devices=d...]
    reduce_scatter x3 -> x2, waiting for transfers between devices: 17.8 us -> 0.01 us  [chips(): lax.psum_scatter(own, 'dp', scatter_dimension=0, tiled=True).astype(F32)]
    ppermute x61 -> x57, waiting for transfers between devices: 295 us -> 277 us  [exchange(): return lax.ppermute(array, axis, [(n, n ^ offset) for n in range(size)])]
    convert_element_type x3 -> x1, other arithmetic: 12.2 us -> 0.08 us  [body(): all_gains = jnp.where(row == lax.axis_index('dp'), flat, 0).astype(F32)]
    reduce_sum x4 -> x0, other arithmetic: 11.8 us -> none  [the longest x1 5.85 us: body(): jnp.mean(part, axis=-1, keepdims=True)]
  transfers between devices with their start and end apart: 68 -> 64, of which waited for: 32 -> 26; matrix products, arithmetic and copies ran while one was open for 7% -> 5% of each run, Pallas kernels for 50% -> 57%
where the time goes in v3:
time: 1010 us; the launch traced here: 1000 us
  Pallas kernels  588 us (58%)
  waiting for transfers between devices  278 us (28%)
  local copies, waits for them, and re-layouts  56.3 us (6%)
  starting transfers between devices  47.6 us (5%)
  other arithmetic  16.4 us (2%)
  between operations  15.4 us (2%)
    pallas_call x40, Pallas kernels, call(): pl.pallas_call(run, grid_spec=pltpu.PrefetchScalarGridSpec(num_scalar_pre...  529 us
    ppermute x57, waiting for transfers between devices, exchange(): return lax.ppermute(array, axis, [(n, n ^ offset) for n in range(size)])  277 us
    pallas_call x3, Pallas kernels, weight_grad(): pl.pallas_call(partial(weight_grad_kernel, sequences=sequences, devices=d...  59.2 us
    ppermute x57, starting transfers between devices, exchange(): return lax.ppermute(array, axis, [(n, n ^ offset) for n in range(size)])  46.8 us
    unnamed x124, local copies, waits for them, and re-layouts  26.9 us
  transfers between devices with their start and end apart: 64, of which 26 were waited for; matrix products, arithmetic and copies ran while one was open for 5% of the time, Pallas kernels for 57%

profile of v3, /device:TPU:0, one launch (start us, length us, event | category | flops | bytes accessed | tf_op | source)
XLA Modules:
  0.0 1001.8 jit_solution(10722035075515067317)
XLA Ops:
  10.2 3.0 collective-permute-start.6
  13.4 6.1 collective-permute-done.6
  19.5 3.2 collective-permute-done.7
  23.9 4.0 slice_bitcast_fusion.2
  36.5 5.6 collective-permute-done.9
  42.9 33.4 %collective-permute-done.3.refs_3_ = bf16[512,2048]{1,0:T(8,128)(2,1)} collective-permute-done((bf16[512,2048]{1,0:T(8,128)(2,1)}, bf16[512,2048]{1,0:T(8,128)(2,1)}, u32[]{:S(2)}, u32[]{:S(2)}) %collective-permute-start.3) | collective-permute-done | bytes 2097184 | tf_op jit(solution)/shard_map/ppermute | solution.py:1009
  95.7 19.2 %project.2 = (bf16[2048,2048]{1,0:T(8,128)(2,1)}, bf16[2048,768]{1,0:T(8,128)(2,1)}) custom-call(s32[1]{0:T(128)} %bitcast.1.refs_0_.place, bf16[512,2048]{1,0:T(8,128)(2,1)} %get-tuple-element.190.refs_1_.refs_0_, bf16[512,2048]{1,0:T(8,128)(2,1)} %collective-permute-done.2.refs_2_, bf16[512,2048]{1,0:T(8,128)(2,1)} %collective-permute-done.3.refs_3_, ...), custom_call_target="tpu_custom_call" | custom-call | flops 4026531840 | tf_op jit(solution)/shard_map/project/pallas_call | solution.py:484
  114.9 28.8 %attend.2 = (bf16[512,256]{1,0:T(8,128)(2,1)}, bf16[512,256]{1,0:T(8,128)(2,1)}, bf16[512,256]{1,0:T(8,128)(2,1)}, bf16[512,256]{1,0:T(8,128)(2,1)}, f32[4,2048]{1,0:T(4,128)}) custom-call(s32[2]{0:T(128)} %pad_add_fusion.1.refs_0_, bf16[2048,768]{1,0:T(8,128)(2,1)} %get-tuple-element.84.refs_1_), custom_call_target="tpu_custom_call" | custom-call | flops 7784628224 | tf_op jit(solution)/shard_map/attend/pallas_call | solution.py:484
  143.8 13.6 %collective-permute-done.1.refs_0_.refs_3_ = bf16[512,2048]{1,0:T(8,128)(2,1)} collective-permute-done((bf16[512,2048]{1,0:T(8,128)(2,1)S(1)}, bf16[512,2048]{1,0:T(8,128)(2,1)}, u32[]{:S(2)}, u32[]{:S(2)}) %collective-permute-start.1) | collective-permute-done | bytes 2097184 | tf_op jit(solution)/shard_map/ppermute | solution.py:1009
  157.4 3.9 relay.1.refs_11_
  167.0 18.7 %project.3 = (bf16[2048,2048]{1,0:T(8,128)(2,1)}, bf16[2048,768]{1,0:T(8,128)(2,1)}) custom-call(s32[1]{0:T(128)} %bitcast.1.refs_0_.place, bf16[512,2048]{1,0:T(8,128)(2,1)} %copy-done, bf16[512,2048]{1,0:T(8,128)(2,1)} %collective-permute-done.refs_2_, bf16[512,2048]{1,0:T(8,128)(2,1)} %collective-permute-done.1.refs_0_.refs_3_, ...), custom_call_target="tpu_custom_call" | custom-call | flops 4026531840 | tf_op jit(solution)/shard_map/project/pallas_call | solution.py:484
  185.7 31.2 %attend.3 = (bf16[512,256]{1,0:T(8,128)(2,1)}, bf16[512,256]{1,0:T(8,128)(2,1)}, bf16[512,256]{1,0:T(8,128)(2,1)}, bf16[512,256]{1,0:T(8,128)(2,1)}, f32[4,2048]{1,0:T(4,128)}) custom-call(s32[2]{0:T(128)} %pad_add_fusion.refs_0_, bf16[2048,768]{1,0:T(8,128)(2,1)} %get-tuple-element.86.refs_1_), custom_call_target="tpu_custom_call" | custom-call | flops 7784628224 | tf_op jit(solution)/shard_map/attend/pallas_call | solution.py:484
  219.8 12.8 %collective-permute-done.12.refs_7_.refs_3_ = bf16[512,256]{1,0:T(8,128)(2,1)S(1)} collective-permute-done((bf16[512,256]{1,0:T(8,128)(2,1)}, bf16[512,256]{1,0:T(8,128)(2,1)S(1)}, u32[]{:S(2)}, u32[]{:S(2)}) %collective-permute-start.12) | collective-permute-done | bytes 262176 | tf_op jit(solution)/shard_map/ppermute | solution.py:1009
  232.6 10.9 %collective-permute-done.13.refs_8_.refs_4_ = bf16[512,256]{1,0:T(8,128)(2,1)S(1)} collective-permute-done((bf16[512,256]{1,0:T(8,128)(2,1)}, bf16[512,256]{1,0:T(8,128)(2,1)S(1)}, u32[]{:S(2)}, u32[]{:S(2)}) %collective-permute-start.13) | collective-permute-done | bytes 262176 | tf_op jit(solution)/shard_map/ppermute | solution.py:1009
  254.9 6.4 out_branch.2
  262.1 7.1 out_branch.3
  270.5 39.6 %collective-permute-done.20.refs_2_ = bf16[512,2048]{1,0:T(8,128)(2,1)S(1)} collective-permute-done((bf16[512,2048]{1,0:T(8,128)(2,1)}, bf16[512,2048]{1,0:T(8,128)(2,1)S(1)}, u32[]{:S(2)}, u32[]{:S(2)}) %collective-permute-start.20) | collective-permute-done | bytes 2097184 | tf_op jit(solution)/shard_map/ppermute | solution.py:1009
  311.4 23.3 %widen.2 = (f32[512,2048]{1,0:T(8,128)}, bf16[512,2048]{1,0:T(8,128)(2,1)}, bf16[512,4096]{1,0:T(8,128)(2,1)}, bf16[512,4096]{1,0:T(8,128)(2,1)}, f32[2,512]{1,0:T(2,128)}) custom-call(bf16[512,2048]{1,0:T(8,128)(2,1)} %get-tuple-element.190.refs_1_.refs_0_, bf16[512,2048]{1,0:T(8,128)(2,1)} %get-tuple-element.100.refs_5_.refs_1_, ...), custom_call_target="tpu_custom_call" | custom-call | flops 5798205952 | tf_op jit(solution)/shard_map/widen/pallas_call | solution.py:484
  335.6 17.6 %collective-permute-done.19.refs_2_ = bf16[512,2048]{1,0:T(8,128)(2,1)S(1)} collective-permute-done((bf16[512,2048]{1,0:T(8,128)(2,1)}, bf16[512,2048]{1,0:T(8,128)(2,1)S(1)}, u32[]{:S(2)}, u32[]{:S(2)}) %collective-permute-start.19) | collective-permute-done | bytes 2097184 | tf_op jit(solution)/shard_map/ppermute | solution.py:1009
  354.5 23.4 %widen.3 = (f32[512,2048]{1,0:T(8,128)}, bf16[512,2048]{1,0:T(8,128)(2,1)}, bf16[512,4096]{1,0:T(8,128)(2,1)}, bf16[512,4096]{1,0:T(8,128)(2,1)}, f32[2,512]{1,0:T(2,128)}) custom-call(bf16[512,2048]{1,0:T(8,128)(2,1)} %copy-done, bf16[512,2048]{1,0:T(8,128)(2,1)} %get-tuple-element.101.refs_5_.refs_1_, bf16[512,2048]{1,0:T(8,128)(2,1)} %copy-done.12, ...), custom_call_target="tpu_custom_call" | custom-call | flops 5798205952 | tf_op jit(solution)/shard_map/widen/pallas_call | solution.py:484
  378.7 2.9 slice_bitcast_fusion
  383.7 26.0 %weight_grad.3 = (bf16[1024,4096]{1,0:T(8,128)(2,1)}, bf16[1024,4096]{1,0:T(8,128)(2,1)}) custom-call(s32[1]{0:T(128)} %bitcast.1.refs_0_.place, bf16[512,2048]{1,0:T(8,128)(2,1)} %get-tuple-element.188.refs_0_, bf16[512,2048]{1,0:T(8,128)(2,1)} %get-tuple-element.189.refs_1_.refs_0_, bf16[512,4096]{1,0:T(8,128)(2,1)} %get-tuple-element.105.refs_2_.refs_1_.refs_0_, ...), custom_call_target="tpu_custom_call" | custom-call | flops 6227702784 | tf_op jit(solution)/shard_map/weight_grad/pallas_call | solution.py:444
  409.8 17.5 %wide_back.2 = (bf16[512,4096]{1,0:T(8,128)(2,1)}, f32[2,512]{1,0:T(2,128)}, f32[1,4096]{1,0:T(1,128)}) custom-call(bf16[512,2048]{1,0:T(8,128)(2,1)} %get-tuple-element.188.refs_0_, bf16[4096,2048]{1,0:T(8,128)(2,1)} %all-gather.8.cloned.1.call-done.refs_1_.refs_4_, bf16[512,4096]{1,0:T(8,128)(2,1)} %get-tuple-element.105.refs_2_.refs_1_.refs_0_, ...), custom_call_target="tpu_custom_call" | custom-call | flops 4509715456 | tf_op jit(solution)/shard_map/wide_back/pallas_call | solution.py:484
  427.3 17.5 %wide_back.3 = (bf16[512,4096]{1,0:T(8,128)(2,1)}, f32[2,512]{1,0:T(2,128)}, f32[1,4096]{1,0:T(1,128)}) custom-call(bf16[512,2048]{1,0:T(8,128)(2,1)} %get-tuple-element.189.refs_1_.refs_0_, bf16[4096,2048]{1,0:T(8,128)(2,1)} %all-gather.8.cloned.1.call-done.refs_1_.refs_4_, bf16[512,4096]{1,0:T(8,128)(2,1)} %get-tuple-element.103.refs_3_.refs_2_.refs_1_.refs_0_, ...), custom_call_target="tpu_custom_call" | custom-call | flops 4509715456 | tf_op jit(solution)/shard_map/wide_back/pallas_call | solution.py:484
  444.8 6.0 add.197.refs_8_
  458.0 19.6 %pre_back.2 = (bf16[512,4096]{1,0:T(8,128)(2,1)}, bf16[512,2048]{1,0:T(8,128)(2,1)}) custom-call(bf16[512,4096]{1,0:T(8,128)(2,1)} %get-tuple-element.111.refs_0_, bf16[512,4096]{1,0:T(8,128)(2,1)} %get-tuple-element.105.refs_2_.refs_1_.refs_0_, bf16[512,4096]{1,0:T(8,128)(2,1)} %get-tuple-element.112.refs_2_, ...), custom_call_target="tpu_custom_call" | custom-call | flops 4939212288 | tf_op jit(solution)/shard_map/pre_back/pallas_call | solution.py:484
  478.6 19.6 %pre_back.3 = (bf16[512,4096]{1,0:T(8,128)(2,1)}, bf16[512,2048]{1,0:T(8,128)(2,1)}) custom-call(bf16[512,4096]{1,0:T(8,128)(2,1)} %get-tuple-element.108.refs_0_, bf16[512,4096]{1,0:T(8,128)(2,1)} %get-tuple-element.103.refs_3_.refs_2_.refs_1_.refs_0_, bf16[512,4096]{1,0:T(8,128)(2,1)} %get-tuple-element.109.refs_2_, ...), custom_call_target="tpu_custom_call" | custom-call | flops 4939212288 | tf_op jit(solution)/shard_map/pre_back/pallas_call | solution.py:484
  499.4 16.3 %narrow.2.refs_10_.refs_0_ = bf16[512,2048]{1,0:T(8,128)(2,1)} custom-call(bf16[512,4096]{1,0:T(8,128)(2,1)} %get-tuple-element.105.refs_2_.refs_1_.refs_0_, f32[2,512]{1,0:T(2,128)} %get-tuple-element.102.refs_5_.refs_4_.refs_3_.refs_1_, f32[2,512]{1,0:T(2,128)} %copy-done.22, f32[1,4096]{1,0:T(1,128)} %reshape.276.refs_8_.refs_5_.refs_3_, ...), custom_call_target="tpu_custom_call" | custom-call | flops 3972844800 | tf_op jit(solution)/shard_map/narrow/pallas_call | solution.py:484
  515.7 10.9 %collective-permute-done.27.refs_2_ = bf16[512,2048]{1,0:T(8,128)(2,1)} collective-permute-done((bf16[512,2048]{1,0:T(8,128)(2,1)}, bf16[512,2048]{1,0:T(8,128)(2,1)}, u32[]{:S(2)}, u32[]{:S(2)}) %collective-permute-start.27) | collective-permute-done | bytes 2097184 | tf_op jit(solution)/shard_map/ppermute | solution.py:1009
  526.6 12.9 %middle.2 = (f32[512,2048]{1,0:T(8,128)}, bf16[512,2048]{1,0:T(8,128)(2,1)}, f32[512,1024]{1,0:T(8,128)}, f32[2,512]{1,0:T(2,128)}, f32[1,2048]{1,0:T(1,128)}, /*index=5*/f32[1,1024]{1,0:T(1,128)}) custom-call(bf16[512,2048]{1,0:T(8,128)(2,1)} %get-tuple-element.188.refs_0_, bf16[512,2048]{1,0:T(8,128)(2,1)} %get-tuple-element.114.refs_8_.refs_1_, ...), custom_call_target="tpu_custom_call" | custom-call | flops 3221225472 | tf_op jit(solution)/shard_map/middle/pallas_call | solution.py:484
  539.5 23.7 %weight_grad.4 = (bf16[1024,4096]{1,0:T(8,128)(2,1)}, bf16[1024,4096]{1,0:T(8,128)(2,1)}) custom-call(s32[1]{0:T(128)} %bitcast.1.refs_0_.place, bf16[512,2048]{1,0:T(8,128)(2,1)} %get-tuple-element.120.refs_0_, bf16[512,2048]{1,0:T(8,128)(2,1)} %get-tuple-element.121.refs_1_, bf16[512,4096]{1,0:T(8,128)(2,1)} %get-tuple-element.122.refs_2_, ...), custom_call_target="tpu_custom_call" | custom-call | flops 6227702784 | tf_op jit(solution)/shard_map/weight_grad/pallas_call | solution.py:444
  563.2 6.3 collective-permute-done.26.refs_4_.refs_2_
  572.8 7.2 add.198.refs_7_
  585.1 4.7 share_out.2
  591.7 13.1 %middle.3 = (f32[512,2048]{1,0:T(8,128)}, bf16[512,2048]{1,0:T(8,128)(2,1)}, f32[512,1024]{1,0:T(8,128)}, f32[2,512]{1,0:T(2,128)}, f32[1,2048]{1,0:T(1,128)}, /*index=5*/f32[1,1024]{1,0:T(1,128)}) custom-call(bf16[512,2048]{1,0:T(8,128)(2,1)} %get-tuple-element.189.refs_1_.refs_0_, bf16[512,2048]{1,0:T(8,128)(2,1)} %get-tuple-element.115.refs_5_.refs_1_, ...), custom_call_target="tpu_custom_call" | custom-call | flops 3221225472 | tf_op jit(solution)/shard_map/middle/pallas_call | solution.py:484
  604.8 16.0 %narrow.3.refs_2_.refs_0_ = bf16[512,2048]{1,0:T(8,128)(2,1)} custom-call(bf16[512,4096]{1,0:T(8,128)(2,1)} %get-tuple-element.103.refs_3_.refs_2_.refs_1_.refs_0_, f32[2,512]{1,0:T(2,128)} %get-tuple-element.104.refs_5_.refs_9_.refs_3_.refs_1_, f32[2,512]{1,0:T(2,128)} %copy-done.21, f32[1,4096]{1,0:T(1,128)} %reshape.276.refs_8_.refs_5_.refs_3_, ...), custom_call_target="tpu_custom_call" | custom-call | flops 3972844800 | tf_op jit(solution)/shard_map/narrow/pallas_call | solution.py:484
  621.2 11.3 %add.199.refs_7_ = bf16[1024,4096]{1,0:T(8,128)(2,1)} custom-call(bf16[1024,4096]{1,0:T(8,128)(2,1)} %get-tuple-element.135.refs_0_, bf16[1024,4096]{1,0:T(8,128)(2,1)} %collective-permute-done.36.refs_1_, bf16[512,2048]{1,0:T(8,128)(2,1)} %narrow.3.refs_2_.refs_0_), custom_call_target="tpu_custom_call" | custom-call | flops 1572864000 | tf_op jit(solution)/shard_map/add/pallas_call | solution.py:484
  633.2 4.1 share_out.3
  639.8 41.9 %attend_back.2.refs_4_.refs_1_.refs_0_ = bf16[2048,768]{1,0:T(8,128)(2,1)} custom-call(s32[2]{0:T(128)} %pad_add_fusion.1.refs_0_, bf16[2048,768]{1,0:T(8,128)(2,1)} %get-tuple-element.84.refs_1_, bf16[512,256]{1,0:T(8,128)(2,1)} %get-tuple-element.125.refs_10_.refs_2_, bf16[512,256]{1,0:T(8,128)(2,1)} %copy-done.48, bf16[512,256]{1,0:T(8,128)(2,1)} %copy-done.49, ...), custom_call_target="tpu_custom_call" | custom-call | flops 281857228800 | tf_op jit(solution)/shard_map/attend_back/pallas_call | solution.py:484
  681.7 9.5 weight_grad.5
  691.3 3.8 convert_bitcast_fusion.2
  695.0 5.3 result.2.refs_5_.refs_3_
  700.3 16.7 %first_back.2 = (bf16[1024,2048]{1,0:T(8,128)(2,1)}, bf16[1024,2048]{1,0:T(8,128)(2,1)}, f32[1,2048]{1,0:T(1,128)}) custom-call(s32[4]{0:T(128)} %broadcast_xor_fusion.refs_0_, bf16[2048,768]{1,0:T(8,128)(2,1)} %attend_back.2.refs_4_.refs_1_.refs_0_, bf16[2048,2048]{1,0:T(8,128)(2,1)} %get-tuple-element.141.refs_2_, ...), custom_call_target="tpu_custom_call" | custom-call | flops 3623878656 | tf_op jit(solution)/shard_map/first_back/pallas_call | solution.py:484
  717.6 9.9 collective-permute-done.40.refs_1_
  729.5 4.5 add.200.refs_2_
  736.2 3.7 add.201.refs_15_
  741.4 45.1 %attend_back.3.refs_3_.refs_1_ = bf16[2048,768]{1,0:T(8,128)(2,1)} custom-call(s32[2]{0:T(128)} %pad_add_fusion.refs_0_, bf16[2048,768]{1,0:T(8,128)(2,1)} %get-tuple-element.86.refs_1_, bf16[512,256]{1,0:T(8,128)(2,1)} %get-tuple-element.136.refs_15_.refs_2_, bf16[512,256]{1,0:T(8,128)(2,1)} %collective-permute-done.37.refs_5_.refs_3_, ...), custom_call_target="tpu_custom_call" | custom-call | flops 11274289152 | tf_op jit(solution)/shard_map/attend_back/pallas_call | solution.py:484
  787.8 4.8 add.202.refs_4_.refs_1_
  794.0 5.3 result.3.refs_3_
  799.3 5.4 collective-permute-done.43.refs_2_
  805.6 3.9 add.203.refs_5_
  809.8 16.7 %first_back.3 = (bf16[1024,2048]{1,0:T(8,128)(2,1)}, bf16[1024,2048]{1,0:T(8,128)(2,1)}, f32[1,2048]{1,0:T(1,128)}) custom-call(s32[4]{0:T(128)} %broadcast_xor_fusion.refs_0_, bf16[2048,768]{1,0:T(8,128)(2,1)} %attend_back.3.refs_3_.refs_1_, bf16[2048,2048]{1,0:T(8,128)(2,1)} %get-tuple-element.145.refs_2_.refs_3_, ...), custom_call_target="tpu_custom_call" | custom-call | flops 3623878656 | tf_op jit(solution)/shard_map/first_back/pallas_call | solution.py:484
  826.7 20.9 %heads_grad.1.refs_2_ = bf16[2048,768]{1,0:T(8,128)(2,1)} custom-call(bf16[2048,768]{1,0:T(8,128)(2,1)} %attend_back.2.refs_4_.refs_1_.refs_0_, bf16[2048,768]{1,0:T(8,128)(2,1)} %attend_back.3.refs_3_.refs_1_, bf16[2048,2048]{1,0:T(8,128)(2,1)} %get-tuple-element.141.refs_2_, bf16[2048,2048]{1,0:T(8,128)(2,1)} %get-tuple-element.145.refs_2_.refs_3_, ...), custom_call_target="tpu_custom_call" | custom-call | flops 4831838208 | tf_op jit(solution)/shard_map/heads_grad/pallas_call | solution.py:484
  850.9 4.6 add.204.refs_5_.refs_6_
  857.8 39.5 %collective-permute-done.47 = f32[1,2048]{1,0:T(1,128)S(1)} collective-permute-done((f32[1,2048]{1,0:T(1,128)S(1)}, f32[1,2048]{1,0:T(1,128)S(1)}, u32[]{:S(2)}, u32[]{:S(2)}) %collective-permute-start.47) | collective-permute-done | bytes 8224 | tf_op jit(solution)/shard_map/ppermute | solution.py:1009
  900.1 5.6 collective-permute-done.49
  905.7 4.9 collective-permute-done.50
  912.2 14.7 %collective-permute-done.51 = f32[16,576]{1,0:T(8,128)S(1)} collective-permute-done((f32[16,576]{1,0:T(8,128)S(1)}, f32[16,576]{1,0:T(8,128)S(1)}, u32[]{:S(2)}, u32[]{:S(2)}) %collective-permute-start.51) | collective-permute-done | bytes 36896 | tf_op jit(solution)/shard_map/ppermute | solution.py:1009
  927.5 7.2 input_grad.2.refs_3_.refs_5_
  934.6 5.0 add.205.refs_1_
  955.2 3.1 collective-permute-done.54.refs_8_
  958.3 3.3 collective-permute-done.55.refs_9_
  964.3 22.9 %collective-permute-done.52.refs_2_ = bf16[512,2048]{1,0:T(8,128)(2,1)} collective-permute-done((bf16[512,2048]{1,0:T(8,128)(2,1)}, bf16[512,2048]{1,0:T(8,128)(2,1)}, u32[]{:S(2)}, u32[]{:S(2)}) %collective-permute-start.52) | collective-permute-done | bytes 2097184 | tf_op jit(solution)/shard_map/ppermute | solution.py:1009
  987.2 7.2 input_grad.3
  (336 shorter events, 123.5 us)
Async XLA Ops:
  7.2 88.5 %all-gather.4.cloned.1.call-start = ((), (), s32[]{:S(2)}) async-start(), calls=%async_computation.4 | async-start | bytes 3932160 | tf_op jit(solution)/shard_map/all_gather | solution.py:1233
  10.2 9.3 collective-permute-start.6
  13.2 9.4 collective-permute-start.7
  13.2 9.4 collective-permute-start.5
  23.8 230.5 %all-gather.6.cloned.1.call-start = ((), (), s32[]{:S(2)}) async-start(), calls=%async_computation.5 | async-start | bytes 22282240 | tf_op jit(solution)/shard_map/all_gather | solution.py:1246
  27.9 48.4 %collective-permute-start.3 = (bf16[512,2048]{1,0:T(8,128)(2,1)}, bf16[512,2048]{1,0:T(8,128)(2,1)}, u32[]{:S(2)}, u32[]{:S(2)}) collective-permute-start(bf16[512,2048]{1,0:T(8,128)(2,1)} %get-tuple-element.190.refs_1_.refs_0_), channel_id=1, source_target_pairs={{0,4},{2,6},{4,0},{6,2},{1,5},{3,7},{5,1},{7,3},{8,12},{10,14},{12... | collective-permute-start | bytes 6291464 | tf_op jit(solution)/shard_map/ppermute | solution.py:1009
  29.7 4.1 collective-permute-start.8
  33.9 8.2 collective-permute-start.9
  78.8 331.0 %all-gather.8.cloned.1.call-start = ((), (), s32[]{:S(2)}) async-start(), calls=%async_computation.6 | async-start | bytes 17825792 | tf_op jit(solution)/shard_map/all_gather | solution.py:1249
  79.5 611.8 %reduce-scatter.5.cloned.1.call-start = ((), (), s32[]{:S(2)}) async-start(), calls=%async_computation.7 | async-start | bytes 5242880 | tf_op jit(solution)/shard_map/reduce_scatter | solution.py:1124
  79.8 15.9 %collective-permute-start.2 = (bf16[512,2048]{1,0:T(8,128)(2,1)}, bf16[512,2048]{1,0:T(8,128)(2,1)}, u32[]{:S(2)}, u32[]{:S(2)}) collective-permute-start(bf16[512,2048]{1,0:T(8,128)(2,1)} %get-tuple-element.190.refs_1_.refs_0_), channel_id=1, source_target_pairs={{0,2},{2,0},{4,6},{6,4},{1,3},{3,1},{5,7},{7,5},{8,10},{10,8},{12,... | collective-permute-start | bytes 6291464 | tf_op jit(solution)/shard_map/ppermute | solution.py:1009
  79.8 15.8 %collective-permute-start.4 = (bf16[512,2048]{1,0:T(8,128)(2,1)}, bf16[512,2048]{1,0:T(8,128)(2,1)}, u32[]{:S(2)}, u32[]{:S(2)}) collective-permute-start(bf16[512,2048]{1,0:T(8,128)(2,1)} %collective-permute-done.3.refs_3_), channel_id=1, source_target_pairs={{0,2},{2,0},{4,6},{6,4},{1,3},{3,1},{5,7},{7,5},{8,10},{10,8},{12,... | collective-permute-start | bytes 6291464 | tf_op jit(solution)/shard_map/ppermute | solution.py:1009
  80.3 77.0 %collective-permute-start.1 = (bf16[512,2048]{1,0:T(8,128)(2,1)S(1)}, bf16[512,2048]{1,0:T(8,128)(2,1)}, u32[]{:S(2)}, u32[]{:S(2)}) collective-permute-start(bf16[512,2048]{1,0:T(8,128)(2,1)S(1)} %get-tuple-element.191.refs_1_.refs_0_), channel_id=1, source_target_pairs={{0,4},{2,6},{4,0},{6,2},{1,5},{3,7},{5,1},{7,3},{8,12},{10,14},{12... | collective-permute-start | bytes 6291464 | tf_op jit(solution)/shard_map/ppermute | solution.py:1009
  82.1 83.6 %collective-permute-start = (bf16[512,2048]{1,0:T(8,128)(2,1)S(1)}, bf16[512,2048]{1,0:T(8,128)(2,1)}, u32[]{:S(2)}, u32[]{:S(2)}) collective-permute-start(bf16[512,2048]{1,0:T(8,128)(2,1)S(1)} %get-tuple-element.191.refs_1_.refs_0_), channel_id=1, source_target_pairs={{0,2},{2,0},{4,6},{6,4},{1,3},{3,1},{5,7},{7,5},{8,10},{10,8},{12,... | collective-permute-start | bytes 6291464 | tf_op jit(solution)/shard_map/ppermute | solution.py:1009
  161.2 4.4 collective-permute-start.10
  162.5 57.2 %collective-permute-start.14 = (bf16[512,256]{1,0:T(8,128)(2,1)S(1)}, bf16[512,256]{1,0:T(8,128)(2,1)S(1)}, u32[]{:S(2)}, u32[]{:S(2)}) collective-permute-start(bf16[512,256]{1,0:T(8,128)(2,1)S(1)} %copy-done.45), channel_id=1, source_target_pairs={{0,2},{2,0},{4,6},{6,4},{1,3},{3,1},{5,7},{7,5},{8,10},{10,8},{12,... | collective-permute-start | bytes 786440 | tf_op jit(solution)/shard_map/ppermute | solution.py:1009
  163.0 56.8 %collective-permute-start.15 = (bf16[512,256]{1,0:T(8,128)(2,1)S(1)}, bf16[512,256]{1,0:T(8,128)(2,1)S(1)}, u32[]{:S(2)}, u32[]{:S(2)}) collective-permute-start(bf16[512,256]{1,0:T(8,128)(2,1)S(1)} %copy-done.46), channel_id=1, source_target_pairs={{0,4},{2,6},{4,0},{6,2},{1,5},{3,7},{5,1},{7,3},{8,12},{10,14},{12... | collective-permute-start | bytes 786440 | tf_op jit(solution)/shard_map/ppermute | solution.py:1009
  165.6 54.2 %collective-permute-start.16 = (bf16[512,256]{1,0:T(8,128)(2,1)S(1)}, bf16[512,256]{1,0:T(8,128)(2,1)S(1)}, u32[]{:S(2)}, u32[]{:S(2)}) collective-permute-start(bf16[512,256]{1,0:T(8,128)(2,1)S(1)} %copy-done.47), channel_id=1, source_target_pairs={{0,6},{2,4},{4,2},{6,0},{1,7},{3,5},{5,3},{7,1},{8,14},{10,12},{12... | collective-permute-start | bytes 786440 | tf_op jit(solution)/shard_map/ppermute | solution.py:1009
  216.9 2.9 collective-permute-start.11
  217.0 15.6 %collective-permute-start.12 = (bf16[512,256]{1,0:T(8,128)(2,1)}, bf16[512,256]{1,0:T(8,128)(2,1)S(1)}, u32[]{:S(2)}, u32[]{:S(2)}) collective-permute-start(bf16[512,256]{1,0:T(8,128)(2,1)} %get-tuple-element.89.refs_8_), channel_id=1, source_target_pairs={{0,4},{2,6},{4,0},{6,2},{1,5},{3,7},{5,1},{7,3},{8,12},{10,14},{12... | collective-permute-start | bytes 786440 | tf_op jit(solution)/shard_map/ppermute | solution.py:1009
  219.6 23.9 %collective-permute-start.13 = (bf16[512,256]{1,0:T(8,128)(2,1)}, bf16[512,256]{1,0:T(8,128)(2,1)S(1)}, u32[]{:S(2)}, u32[]{:S(2)}) collective-permute-start(bf16[512,256]{1,0:T(8,128)(2,1)} %get-tuple-element.90.refs_9_), channel_id=1, source_target_pairs={{0,6},{2,4},{4,2},{6,0},{1,7},{3,5},{5,3},{7,1},{8,14},{10,12},{12... | collective-permute-start | bytes 786440 | tf_op jit(solution)/shard_map/ppermute | solution.py:1009
  249.5 3.8 collective-permute-start.17
  250.7 3.6 collective-permute-start.18
  261.2 48.8 %collective-permute-start.20 = (bf16[512,2048]{1,0:T(8,128)(2,1)}, bf16[512,2048]{1,0:T(8,128)(2,1)S(1)}, u32[]{:S(2)}, u32[]{:S(2)}) collective-permute-start(bf16[512,2048]{1,0:T(8,128)(2,1)} %get-tuple-element.100.refs_5_.refs_1_), channel_id=1, source_target_pairs={{0,1},{1,0},{2,3},{3,2},{4,5},{5,4},{6,7},{7,6},{8,9},{9,8},{10,11... | collective-permute-start | bytes 6291464 | tf_op jit(solution)/shard_map/ppermute | solution.py:1009
  269.2 84.0 %collective-permute-start.19 = (bf16[512,2048]{1,0:T(8,128)(2,1)}, bf16[512,2048]{1,0:T(8,128)(2,1)S(1)}, u32[]{:S(2)}, u32[]{:S(2)}) collective-permute-start(bf16[512,2048]{1,0:T(8,128)(2,1)} %get-tuple-element.101.refs_5_.refs_1_), channel_id=1, source_target_pairs={{0,1},{1,0},{2,3},{3,2},{4,5},{5,4},{6,7},{7,6},{8,9},{9,8},{10,11... | collective-permute-start | bytes 6291464 | tf_op jit(solution)/shard_map/ppermute | solution.py:1009
  334.7 48.4 %collective-permute-start.22 = (f32[2,512]{1,0:T(2,128)}, f32[2,512]{1,0:T(2,128)S(1)}, u32[]{:S(2)}, u32[]{:S(2)}) collective-permute-start(f32[2,512]{1,0:T(2,128)} %get-tuple-element.102.refs_5_.refs_4_.refs_3_.refs_1_), channel_id=1, source_target_pairs={{0,1},{1,0},{2,3},{3,2},{4,5},{5,4},{6,7},{7,6},{8,9},{9,8},{10,11... | collective-permute-start | bytes 12296 | tf_op jit(solution)/shard_map/ppermute | solution.py:1009
  377.9 5.3 collective-permute-start.21
  409.8 35.0 %collective-permute-start.25 = (bf16[1024,4096]{1,0:T(8,128)(2,1)}, bf16[1024,4096]{1,0:T(8,128)(2,1)}, u32[]{:S(2)}, u32[]{:S(2)}) collective-permute-start(bf16[1024,4096]{1,0:T(8,128)(2,1)} %get-tuple-element.106.refs_6_), channel_id=1, source_target_pairs={{0,2},{2,0},{4,6},{6,4},{1,3},{3,1},{5,7},{7,5},{8,10},{10,8},{12,... | collective-permute-start | bytes 25165832 | tf_op jit(solution)/shard_map/ppermute | solution.py:1009
  450.9 118.6 %collective-permute-start.29 = (bf16[512,4096]{1,0:T(8,128)(2,1)}, bf16[512,4096]{1,0:T(8,128)(2,1)S(1)}, u32[]{:S(2)}, u32[]{:S(2)}) collective-permute-start(bf16[512,4096]{1,0:T(8,128)(2,1)} %add.197.refs_8_), channel_id=1, source_target_pairs={{0,4},{2,6},{4,0},{6,2},{1,5},{3,7},{5,1},{7,3},{8,12},{10,14},{12... | collective-permute-start | bytes 12582920 | tf_op jit(solution)/shard_map/ppermute | solution.py:1009
  452.8 3.6 collective-permute-start.23
  453.9 3.6 collective-permute-start.24
  477.7 48.9 %collective-permute-start.27 = (bf16[512,2048]{1,0:T(8,128)(2,1)}, bf16[512,2048]{1,0:T(8,128)(2,1)}, u32[]{:S(2)}, u32[]{:S(2)}) collective-permute-start(bf16[512,2048]{1,0:T(8,128)(2,1)} %get-tuple-element.114.refs_8_.refs_1_), channel_id=1, source_target_pairs={{0,1},{1,0},{2,3},{3,2},{4,5},{5,4},{6,7},{7,6},{8,9},{9,8},{10,11... | collective-permute-start | bytes 6291464 | tf_op jit(solution)/shard_map/ppermute | solution.py:1009
  498.3 71.2 %collective-permute-start.26 = (bf16[512,2048]{1,0:T(8,128)(2,1)}, bf16[512,2048]{1,0:T(8,128)(2,1)S(1)}, u32[]{:S(2)}, u32[]{:S(2)}) collective-permute-start(bf16[512,2048]{1,0:T(8,128)(2,1)} %get-tuple-element.115.refs_5_.refs_1_), channel_id=1, source_target_pairs={{0,1},{1,0},{2,3},{3,2},{4,5},{5,4},{6,7},{7,6},{8,9},{9,8},{10,11... | collective-permute-start | bytes 6291464 | tf_op jit(solution)/shard_map/ppermute | solution.py:1009
  563.1 57.7 %collective-permute-start.36 = (bf16[1024,4096]{1,0:T(8,128)(2,1)}, bf16[1024,4096]{1,0:T(8,128)(2,1)}, u32[]{:S(2)}, u32[]{:S(2)}) collective-permute-start(bf16[1024,4096]{1,0:T(8,128)(2,1)} %get-tuple-element.124.refs_3_), channel_id=1, source_target_pairs={{0,2},{2,0},{4,6},{6,4},{1,3},{3,1},{5,7},{7,5},{8,10},{10,8},{12,... | collective-permute-start | bytes 25165832 | tf_op jit(solution)/shard_map/ppermute | solution.py:1009
  580.1 246.6 %reduce-scatter.7.cloned.1.call-start = ((), (), s32[]{:S(2)}) async-start(), calls=%async_computation.8 | async-start | bytes 10485760 | tf_op jit(solution)/shard_map/reduce_scatter | solution.py:1107
  580.7 3.7 collective-permute-start.28
  582.2 112.9 %collective-permute-start.31 = (bf16[512,2048]{1,0:T(8,128)(2,1)}, bf16[512,2048]{1,0:T(8,128)(2,1)}, u32[]{:S(2)}, u32[]{:S(2)}) collective-permute-start(bf16[512,2048]{1,0:T(8,128)(2,1)} %narrow.2.refs_10_.refs_0_), channel_id=1, source_target_pairs={{0,1},{1,0},{2,3},{3,2},{4,5},{5,4},{6,7},{7,6},{8,9},{9,8},{10,11... | collective-permute-start | bytes 6291464 | tf_op jit(solution)/shard_map/ppermute | solution.py:1009
  589.8 47.6 %collective-permute-start.32 = (bf16[512,256]{1,0:T(8,128)(2,1)}, bf16[512,256]{1,0:T(8,128)(2,1)S(1)}, u32[]{:S(2)}, u32[]{:S(2)}) collective-permute-start(bf16[512,256]{1,0:T(8,128)(2,1)} %get-tuple-element.131), channel_id=1, source_target_pairs={{0,2},{2,0},{4,6},{6,4},{1,3},{3,1},{5,7},{7,5},{8,10},{10,8},{12,... | collective-permute-start | bytes 786440 | tf_op jit(solution)/shard_map/ppermute | solution.py:1009
  589.8 47.9 %collective-permute-start.33 = (bf16[512,256]{1,0:T(8,128)(2,1)}, bf16[512,256]{1,0:T(8,128)(2,1)S(1)}, u32[]{:S(2)}, u32[]{:S(2)}) collective-permute-start(bf16[512,256]{1,0:T(8,128)(2,1)} %get-tuple-element.132), channel_id=1, source_target_pairs={{0,4},{2,6},{4,0},{6,2},{1,5},{3,7},{5,1},{7,3},{8,12},{10,14},{12... | collective-permute-start | bytes 786440 | tf_op jit(solution)/shard_map/ppermute | solution.py:1009
  589.8 49.3 %collective-permute-start.34 = (bf16[512,256]{1,0:T(8,128)(2,1)}, bf16[512,256]{1,0:T(8,128)(2,1)S(1)}, u32[]{:S(2)}, u32[]{:S(2)}) collective-permute-start(bf16[512,256]{1,0:T(8,128)(2,1)} %get-tuple-element.133), channel_id=1, source_target_pairs={{0,6},{2,4},{4,2},{6,0},{1,7},{3,5},{5,3},{7,1},{8,14},{10,12},{12... | collective-permute-start | bytes 786440 | tf_op jit(solution)/shard_map/ppermute | solution.py:1009
  620.9 11.7 %collective-permute-start.35 = (f32[2,512]{1,0:T(2,128)S(1)}, f32[2,512]{1,0:T(2,128)S(1)}, u32[]{:S(2)}, u32[]{:S(2)}) collective-permute-start(f32[2,512]{1,0:T(2,128)S(1)} %copy-done.24), channel_id=1, source_target_pairs={{0,1},{1,0},{2,3},{3,2},{4,5},{5,4},{6,7},{7,6},{8,9},{9,8},{10,11... | collective-permute-start | bytes 12296 | tf_op jit(solution)/shard_map/ppermute | solution.py:1009
  632.5 314.6 %reduce-scatter.11.cloned.1.call-start = ((), (), s32[]{:S(2)}) async-start(), calls=%async_computation.10 | async-start | bytes 1310720 | tf_op jit(solution)/shard_map/reduce_scatter | solution.py:1124
  637.2 44.5 %collective-permute-start.37 = (bf16[512,256]{1,0:T(8,128)(2,1)}, bf16[512,256]{1,0:T(8,128)(2,1)}, u32[]{:S(2)}, u32[]{:S(2)}) collective-permute-start(bf16[512,256]{1,0:T(8,128)(2,1)} %get-tuple-element.137), channel_id=1, source_target_pairs={{0,2},{2,0},{4,6},{6,4},{1,3},{3,1},{5,7},{7,5},{8,10},{10,8},{12,... | collective-permute-start | bytes 786440 | tf_op jit(solution)/shard_map/ppermute | solution.py:1009
  637.4 44.4 %collective-permute-start.38 = (bf16[512,256]{1,0:T(8,128)(2,1)}, bf16[512,256]{1,0:T(8,128)(2,1)}, u32[]{:S(2)}, u32[]{:S(2)}) collective-permute-start(bf16[512,256]{1,0:T(8,128)(2,1)} %get-tuple-element.138), channel_id=1, source_target_pairs={{0,4},{2,6},{4,0},{6,2},{1,5},{3,7},{5,1},{7,3},{8,12},{10,14},{12... | collective-permute-start | bytes 786440 | tf_op jit(solution)/shard_map/ppermute | solution.py:1009
  637.7 44.1 %collective-permute-start.39 = (bf16[512,256]{1,0:T(8,128)(2,1)}, bf16[512,256]{1,0:T(8,128)(2,1)}, u32[]{:S(2)}, u32[]{:S(2)}) collective-permute-start(bf16[512,256]{1,0:T(8,128)(2,1)} %get-tuple-element.139), channel_id=1, source_target_pairs={{0,6},{2,4},{4,2},{6,0},{1,7},{3,5},{5,3},{7,1},{8,14},{10,12},{12... | collective-permute-start | bytes 786440 | tf_op jit(solution)/shard_map/ppermute | solution.py:1009
  717.0 10.5 %collective-permute-start.40 = (bf16[1024,2048]{1,0:T(8,128)(2,1)}, bf16[1024,2048]{1,0:T(8,128)(2,1)S(1)}, u32[]{:S(2)}, u32[]{:S(2)}) collective-permute-start(bf16[1024,2048]{1,0:T(8,128)(2,1)} %get-tuple-element.143.refs_2_), channel_id=1, source_target_pairs={{0,2},{2,0},{4,6},{6,4},{1,3},{3,1},{5,7},{7,5},{8,10},{10,8},{12,... | collective-permute-start | bytes 12582920 | tf_op jit(solution)/shard_map/ppermute | solution.py:1009
  717.5 18.7 %collective-permute-start.42 = (bf16[1024,1024]{1,0:T(8,128)(2,1)}, bf16[1024,1024]{1,0:T(8,128)(2,1)}, u32[]{:S(2)}, u32[]{:S(2)}) collective-permute-start(bf16[1024,1024]{1,0:T(8,128)(2,1)} %get-tuple-element.140.refs_3_), channel_id=1, source_target_pairs={{0,2},{2,0},{4,6},{6,4},{1,3},{3,1},{5,7},{7,5},{8,10},{10,8},{12,... | collective-permute-start | bytes 6291464 | tf_op jit(solution)/shard_map/ppermute | solution.py:1009
  734.0 52.5 %collective-permute-start.41 = (bf16[512,2048]{1,0:T(8,128)(2,1)}, bf16[512,2048]{1,0:T(8,128)(2,1)S(1)}, u32[]{:S(2)}, u32[]{:S(2)}) collective-permute-start(bf16[512,2048]{1,0:T(8,128)(2,1)} %add.200.refs_2_), channel_id=1, source_target_pairs={{0,4},{2,6},{4,0},{6,2},{1,5},{3,7},{5,1},{7,3},{8,12},{10,14},{12... | collective-permute-start | bytes 6291464 | tf_op jit(solution)/shard_map/ppermute | solution.py:1009
  734.5 58.1 %collective-permute-start.30 = (bf16[512,2048]{1,0:T(8,128)(2,1)S(1)}, bf16[512,2048]{1,0:T(8,128)(2,1)S(1)}, u32[]{:S(2)}, u32[]{:S(2)}) collective-permute-start(bf16[512,2048]{1,0:T(8,128)(2,1)S(1)} %copy-done.1), channel_id=1, source_target_pairs={{0,1},{1,0},{2,3},{3,2},{4,5},{5,4},{6,7},{7,6},{8,9},{9,8},{10,11... | collective-permute-start | bytes 6291464 | tf_op jit(solution)/shard_map/ppermute | solution.py:1009
  739.9 64.7 %collective-permute-start.43 = (bf16[512,1024]{1,0:T(8,128)(2,1)}, bf16[512,1024]{1,0:T(8,128)(2,1)S(1)}, u32[]{:S(2)}, u32[]{:S(2)}) collective-permute-start(bf16[512,1024]{1,0:T(8,128)(2,1)} %add.201.refs_15_), channel_id=1, source_target_pairs={{0,4},{2,6},{4,0},{6,2},{1,5},{3,7},{5,1},{7,3},{8,12},{10,14},{12... | collective-permute-start | bytes 3145736 | tf_op jit(solution)/shard_map/ppermute | solution.py:1009
  809.5 139.6 %reduce-scatter.9.cloned.1.call-start = ((), (), s32[]{:S(2)}) async-start(), calls=%async_computation.9 | async-start | bytes 3932160 | tf_op jit(solution)/shard_map/reduce_scatter | solution.py:1388
  826.6 24.2 %collective-permute-start.44 = (bf16[1024,2048]{1,0:T(8,128)(2,1)}, bf16[1024,2048]{1,0:T(8,128)(2,1)}, u32[]{:S(2)}, u32[]{:S(2)}) collective-permute-start(bf16[1024,2048]{1,0:T(8,128)(2,1)} %get-tuple-element.147.refs_4_), channel_id=1, source_target_pairs={{0,2},{2,0},{4,6},{6,4},{1,3},{3,1},{5,7},{7,5},{8,10},{10,8},{12,... | collective-permute-start | bytes 12582920 | tf_op jit(solution)/shard_map/ppermute | solution.py:1009
  849.1 78.3 %collective-permute-start.46 = (bf16[512,2048]{1,0:T(8,128)(2,1)S(1)}, bf16[512,2048]{1,0:T(8,128)(2,1)}, u32[]{:S(2)}, u32[]{:S(2)}) collective-permute-start(bf16[512,2048]{1,0:T(8,128)(2,1)S(1)} %copy-done.2), channel_id=1, source_target_pairs={{0,1},{1,0},{2,3},{3,2},{4,5},{5,4},{6,7},{7,6},{8,9},{9,8},{10,11... | collective-permute-start | bytes 6291464 | tf_op jit(solution)/shard_map/ppermute | solution.py:1009
  855.5 79.1 %collective-permute-start.45 = (bf16[512,2048]{1,0:T(8,128)(2,1)}, bf16[512,2048]{1,0:T(8,128)(2,1)}, u32[]{:S(2)}, u32[]{:S(2)}) collective-permute-start(bf16[512,2048]{1,0:T(8,128)(2,1)} %add.204.refs_5_.refs_6_), channel_id=1, source_target_pairs={{0,4},{2,6},{4,0},{6,2},{1,5},{3,7},{5,1},{7,3},{8,12},{10,14},{12... | collective-permute-start | bytes 6291464 | tf_op jit(solution)/shard_map/ppermute | solution.py:1009
  856.8 40.6 %collective-permute-start.47 = (f32[1,2048]{1,0:T(1,128)S(1)}, f32[1,2048]{1,0:T(1,128)S(1)}, u32[]{:S(2)}, u32[]{:S(2)}) collective-permute-start(f32[1,2048]{1,0:T(1,128)S(1)} %add.144), channel_id=1, source_target_pairs={{0,1},{1,0},{2,3},{3,2},{4,5},{5,4},{6,7},{7,6},{8,9},{9,8},{10,11... | collective-permute-start | bytes 24584 | tf_op jit(solution)/shard_map/ppermute | solution.py:1009
  897.4 2.6 collective-permute-start.48
  899.7 52.6 %collective-permute-start.56 = (bf16[128,4096]{1,0:T(8,128)(2,1)}, bf16[128,4096]{1,0:T(8,128)(2,1)}, u32[]{:S(2)}, u32[]{:S(2)}) collective-permute-start(bf16[128,4096]{1,0:T(8,128)(2,1)} %slice.159), channel_id=1, source_target_pairs={{0,4},{2,6},{4,0},{6,2},{1,5},{3,7},{5,1},{7,3},{8,12},{10,14},{12... | collective-permute-start | bytes 3145736 | tf_op jit(solution)/shard_map/ppermute | solution.py:1009
  900.1 5.6 collective-permute-start.49
  905.7 4.9 collective-permute-start.50
  910.6 16.2 %collective-permute-start.51 = (f32[16,576]{1,0:T(8,128)S(1)}, f32[16,576]{1,0:T(8,128)S(1)}, u32[]{:S(2)}, u32[]{:S(2)}) collective-permute-start(f32[16,576]{1,0:T(8,128)S(1)} %add.151), channel_id=1, source_target_pairs={{0,4},{2,6},{4,0},{6,2},{1,5},{3,7},{5,1},{7,3},{8,12},{10,14},{12... | collective-permute-start | bytes 110600 | tf_op jit(solution)/shard_map/ppermute | solution.py:1009
  939.6 47.6 %collective-permute-start.52 = (bf16[512,2048]{1,0:T(8,128)(2,1)}, bf16[512,2048]{1,0:T(8,128)(2,1)}, u32[]{:S(2)}, u32[]{:S(2)}) collective-permute-start(bf16[512,2048]{1,0:T(8,128)(2,1)} %add.205.refs_1_), channel_id=1, source_target_pairs={{0,1},{1,0},{2,3},{3,2},{4,5},{5,4},{6,7},{7,6},{8,9},{9,8},{10,11... | collective-permute-start | bytes 6291464 | tf_op jit(solution)/shard_map/ppermute | solution.py:1009
  950.4 4.7 collective-permute-start.53
  950.5 7.8 collective-permute-start.54
  950.9 10.6 %collective-permute-start.55 = (bf16[128,768]{1,0:T(8,128)(2,1)S(1)}, bf16[128,768]{1,0:T(8,128)(2,1)S(1)}, u32[]{:S(2)}, u32[]{:S(2)}) collective-permute-start(bf16[128,768]{1,0:T(8,128)(2,1)S(1)} %get-tuple-element.207), channel_id=1, source_target_pairs={{0,6},{2,4},{4,2},{6,0},{1,7},{3,5},{5,3},{7,1},{8,14},{10,12},{12... | collective-permute-start | bytes 589832 | tf_op jit(solution)/shard_map/ppermute | solution.py:1009
  (59 other events, 364.5 us)
Sparse Core Ops, SparseCore 0:
  23.9 66.3 all-gather.3
  92.5 158.0 all-gather.5
  252.7 131.8 all-gather.7
  580.2 76.5 reduce-scatter.4
  659.1 144.9 reduce-scatter.6
  809.7 25.1 reduce-scatter.10
  847.7 58.5 reduce-scatter.8

commit v4 on v3

--- a/solution.py
+++ b/solution.py
@@ -19,6 +19,8 @@
 BF16 = jnp.bfloat16
 KERNEL_RATE = 0.25e9
 BACK_WEIGHT = 25
+PAUSE = 300
+LONG_PAUSE = 200
 
 
 def lasting(us):
@@ -413,8 +415,9 @@
 
 
 def weight_grad(place, lefts, rights, devices, groups, norm=None, z_first=False, after=()):
-    sequences = len(lefts)
-    span, width = lefts[0].shape
+    sequences = len(rights)
+    span = rights[0].shape[-2]
+    width = lefts[0].shape[1]
     layers = rights[0].ndim == 3
     columns = rights[0].shape[0] * rights[0].shape[2] if layers else rights[0].shape[1]
     chunk = width // (devices * groups)
@@ -429,7 +432,13 @@
         right_spec = pl.BlockSpec((None, span, tile), lambda n, p: (n // tiles, 0, n % tiles))
     else:
         right_spec = pl.BlockSpec((span, tile), lambda n, p: (0, n))
-    in_specs = [pl.BlockSpec((span, width), lambda n, p: (0, 0))] * sequences
+    if len(lefts) == sequences:
+        in_specs = [pl.BlockSpec((span, width), lambda n, p: (0, 0))] * sequences
+    else:
+        lefts = lefts * sequences
+        in_specs = [
+            pl.BlockSpec((span, width), lambda n, p, s=s: (s, 0)) for s in range(sequences)
+        ]
     in_specs += [right_spec] * sequences
     operands = [*lefts, *rights]
     scratch = [pltpu.VMEM((width, sequences * span), BF16)]
@@ -634,8 +643,8 @@
         sums[...] = jnp.concatenate([as_row(total[...]), as_row(squares[...])], axis=0)
 
 
-def widen(tokens, own, other, gain, weight, units, after=()):
-    span, model = tokens.shape
+def widen(number, tokens, own, other, gain, weight, units, after=()):
+    span, model = own.shape
     tile = 512
     rows = (span, model)
     across = (span, tile)
@@ -644,7 +653,7 @@
         "widen",
         (units // tile,),
         [
-            (tokens, rows, None),
+            (tokens, rows, lambda n: (number, 0)),
             (own, rows, None),
             (other, rows, None),
             (gain, (1, model), None),
@@ -704,65 +713,77 @@
     )[0]
 
 
-def wide_back_kernel(
-    grads, weight, active, own, other, gain, scaled, sums, gain_grad, columns, total, weighted, *, full
-):
+def wide_back_kernel(grads, weight, gain, *refs, sequences, full):
+    active, refs = refs[:sequences], refs[sequences:]
+    own, refs = refs[:sequences], refs[sequences:]
+    other, refs = refs[:sequences], refs[sequences:]
+    scaled, refs = refs[:sequences], refs[sequences:]
+    sums, refs = refs[:sequences], refs[sequences:]
+    gain_grad, columns, totals = refs
     step = pl.program_id(0)
+    span = active[0].shape[0]
 
     @pl.when(step == 0)
     def _():
-        mean, std = moments(own[...], other[...], full)
-        columns[0] = jnp.broadcast_to(as_column(mean), columns.shape[1:])
-        columns[1] = jnp.broadcast_to(as_column(std), columns.shape[1:])
-        total[...] = jnp.zeros_like(total)
-        weighted[...] = jnp.zeros_like(weighted)
-
-    grad = dot(grads[...], weight[...], 1, 1)
-    normal = (active[...].astype(F32) - columns[0, :, 0:1]) * columns[1, :, 0:1]
-    product = grad * normal
-    gain_grad[...] = jnp.sum(product, axis=0, keepdims=True)
-    scaled[...] = (grad * gain[...]).astype(BF16)
-    product = product * gain[...]
-    part, other_part = total[...], weighted[...]
-    for start in range(0, grad.shape[1], 128):
-        at = slice(start, start + 128)
-        part += grad[:, at] * gain[:, at]
-        other_part += product[:, at]
-    total[...] = part
-    weighted[...] = other_part
+        for s in range(sequences):
+            mean, std = moments(own[s][...], other[s][...], full)
+            columns[2 * s] = jnp.broadcast_to(as_column(mean), columns.shape[1:])
+            columns[2 * s + 1] = jnp.broadcast_to(as_column(std), columns.shape[1:])
+        totals[...] = jnp.zeros_like(totals)
+
+    every = dot(grads[...], weight[...], 1, 1)
+    gain_part = 0.0
+    for s in range(sequences):
+        grad = every[s * span : (s + 1) * span]
+        normal = (active[s][...].astype(F32) - columns[2 * s, :, 0:1]) * columns[2 * s + 1, :, 0:1]
+        product = grad * normal
+        gain_part += jnp.sum(product, axis=0, keepdims=True)
+        grad = grad * gain[...]
+        scaled[s][...] = grad.astype(BF16)
+        product = product * gain[...]
+        part, other_part = totals[2 * s], totals[2 * s + 1]
+        for start in range(0, grad.shape[1], 128):
+            part += grad[:, start : start + 128]
+            other_part += product[:, start : start + 128]
+        totals[2 * s] = part
+        totals[2 * s + 1] = other_part
+    gain_grad[...] = gain_part
 
     @pl.when(step == pl.num_programs(0) - 1)
     def _():
-        sums[...] = jnp.concatenate([as_row(total[...]), as_row(weighted[...])], axis=0)
+        for s in range(sequences):
+            sums[s][...] = jnp.concatenate(
+                [as_row(totals[2 * s]), as_row(totals[2 * s + 1])], axis=0
+            )
 
 
 def wide_back(grads, weight, active, own, other, gain, full, after=()):
-    span, units = active.shape
+    sequences = len(active)
+    span, units = active[0].shape
     model = weight.shape[1]
     tile = 512
     sums = (2, span)
     across = (span, tile)
-    return call(
-        partial(wide_back_kernel, full=full),
+    tiled = lambda n: (0, n)
+    made = call(
+        partial(wide_back_kernel, sequences=sequences, full=full),
         "wide_back",
         (units // tile,),
         [
-            (grads, (span, model), None),
+            (grads, (sequences * span, model), None),
             (weight, (tile, model), lambda n: (n, 0)),
-            (active, across, lambda n: (0, n)),
-            (own, sums, None),
-            (other, sums, None),
-            (gain, (1, tile), lambda n: (0, n)),
-        ],
-        [
-            ((span, units), BF16, across, lambda n: (0, n)),
-            (sums, F32, sums, None),
-            ((1, units), F32, (1, tile), lambda n: (0, n)),
-        ],
-        [pltpu.VMEM((2, span, 128), F32)] + [pltpu.VMEM((span, 128), F32)] * 2,
-        4.2e-9 * span * model * units,
-        after,
-    )
+            (gain, (1, tile), tiled),
+        ]
+        + [(array, across, tiled) for array in active]
+        + [(array, sums, None) for array in (*own, *other)],
+        [((span, units), BF16, across, tiled)] * sequences
+        + [(sums, F32, sums, None)] * sequences
+        + [((1, units), F32, (1, tile), tiled)],
+        [pltpu.VMEM((2 * sequences, span, 128), F32)] * 2,
+        3.5e-9 * sequences * span * model * units,
+        after,
+    )
+    return made[:sequences], made[sequences : 2 * sequences], made[2 * sequences]
 
 
 def pre_back_kernel(
@@ -852,12 +873,13 @@
 
 
 def middle(
-    grads, own, other, hidden, gain, near_full, mixed, own_sums, other_sums, gain_attn, full, after=()
+    number, grads, own, other, hidden, gain, near_full, mixed, own_sums, other_sums, gain_attn, full, after=()
 ):
-    span, model = grads.shape
+    span, model = hidden.shape
     width = mixed.shape[1]
     place = near_full.shape[1] // width - 1
     rows = min(256, span)
+    below = number * (span // rows)
     by_row = lambda n: (n, 0)
     by_column = lambda n: (0, n)
     return call(
@@ -865,7 +887,7 @@
         "middle",
         (span // rows,),
         [
-            (grads, (rows, model), by_row),
+            (grads, (rows, model), lambda n: (n + below, 0)),
             (own, (rows, model), by_row),
             (other, (rows, model), by_row),
             (hidden, (rows, model), by_row),
@@ -1016,23 +1038,47 @@
     refs[-1][...] = total.astype(BF16)
 
 
-def add(arrays, rows, after=()):
-    width = arrays[0][0].shape[1]
+def add(arrays, rows, after=(), width=None, us=None):
+    width = width or arrays[0][0].shape[1]
     tile = 128
 
-    def from_row(first):
-        return lambda n: (n + first // tile, 0)
+    def place(row, column):
+        return lambda n: (n + row // tile, column // width)
 
     return call(
         add_kernel,
         "add",
         (rows // tile,),
-        [(array, (tile, width), from_row(first)) for array, first in arrays],
+        [(array, (tile, width), place(row, column)) for array, row, column in arrays],
         [((rows, width), BF16, (tile, width), lambda n: (n, 0))],
         [],
+        us or 1.5e-6 * rows * width,
+        after,
+    )[0]
+
+
+def add_halves_kernel(first, second, left, right):
+    total = (first[...].astype(F32) + second[...].astype(F32)).astype(BF16)
+    half = total.shape[1] // 2
+    left[...] = total[:, :half]
+    right[...] = total[:, half:]
+
+
+def add_halves(first, second, rows, after=()):
+    width = first.shape[1]
+    tile = 128
+    block = (tile, width)
+    half = ((rows, width // 2), BF16, (tile, width // 2), lambda n: (n, 0))
+    return call(
+        add_halves_kernel,
+        "add_halves",
+        (rows // tile,),
+        [(first, block, lambda n: (n, 0)), (second, block, lambda n: (n, 0))],
+        [half, half],
+        [],
         1.5e-6 * rows * width,
         after,
-    )[0]
+    )
 
 
 def result_kernel(own, other, hidden, out):
@@ -1057,9 +1103,15 @@
     )[0]
 
 
-def input_kernel(tokens, own, other, gain, grads, out):
+def input_kernel(tokens, gain, grads, *refs):
+    out = refs[-1]
+    pieces = [
+        own[...].astype(F32) + other[...].astype(F32)
+        for own, other in zip(refs[:-1:2], refs[1:-1:2])
+    ]
+    total = pieces[0] if len(pieces) == 1 else jnp.concatenate(pieces, axis=1)
     normal, std = row_norm(tokens[...].astype(F32))
-    part = (own[...].astype(F32) + other[...].astype(F32)) * gain[...]
+    part = total * gain[...]
     first = std * (
         part
         - jnp.mean(part, axis=-1, keepdims=True)
@@ -1068,22 +1120,23 @@
     out[...] = (grads[...] + first).astype(BF16)
 
 
-def input_rows(number, count, tokens, own, other, gain, grads, into, after=()):
-    span, model = tokens.shape
+def input_rows(number, count, tokens, terms, gain, grads, into, after=()):
+    span, model = grads.shape
     tile = min(128, span)
     block = (tile, model)
     by_row = lambda n: (n, 0)
+    below = number * (span // tile)
+    sums = [array for pair in terms for array in pair]
     return call(
         input_kernel,
         "input_grad",
         (span // tile,),
         [
-            (tokens, block, by_row),
-            (own, block, by_row),
-            (other, block, by_row),
+            (tokens, block, lambda n: (n + below, 0)),
             (gain, (1, model), None),
             (grads, block, by_row),
-        ],
+        ]
+        + [(array, (tile, array.shape[1]), by_row) for array in sums],
         [((count, span, model), BF16, (None, *block), lambda n: (number, n, 0))],
         [],
         2e-6 * span * model,
@@ -1101,7 +1154,7 @@
 
     def mates(self, after=()):
         rows = self.kept.shape[0]
-        pair = [(self.kept, 0), (self.got, 0)]
+        pair = [(self.kept, 0, 0), (self.got, 0, 0)]
         if self.z_first:
             near = add(pair, rows, after)
             self.rows = lax.psum_scatter(near, "dp", scatter_dimension=0, tiled=True)
@@ -1110,17 +1163,18 @@
             self.far = exchange(near, "seq", self.groups, 2)
         return near
 
-    def own(self, after=()):
+    def own(self, after=(), us=None):
         half = self.kept.shape[0] // 2
-        return add([(self.kept, half), (self.got, half), (self.far, 0)], half, after)
-
-    def chips(self, after=()):
+        pieces = [(self.kept, half, 0), (self.got, half, 0), (self.far, 0, 0)]
+        return add(pieces, half, after, None, us)
+
+    def chips(self, after=(), us=None):
         if self.z_first:
             half = self.rows.shape[0] // 2
             far = exchange(self.rows[:half], "seq", self.groups, 2)
             self.out = self.rows[half:].astype(F32) + far.astype(F32)
             return self.out
-        own = self.own(after)
+        own = self.own(after, us)
         self.out = lax.psum_scatter(own, "dp", scatter_dimension=0, tiled=True).astype(F32)
         return own
 
@@ -1143,11 +1197,6 @@
         array = array + exchange(array, axis, size, offset)
         offset *= 2
     return array
-
-
-def data_sum(array, devices, groups):
-    array = axis_sum(array + exchange(array, "seq", groups, 1), "dp", devices)
-    return array + exchange(array, "seq", groups, 2)
 
 
 def in_order(pieces, place):
@@ -1283,9 +1332,11 @@
         branch.append(mp_sum(terms, units))
         last = [terms]
 
+    flat_tokens = tokens.reshape(sequences * span, model)
+    flat_grads = out_grad.reshape(sequences * span, model)
     hidden, third_low, active, slope, act_sums = [], [], [], [], []
     for s in each:
-        made = widen(tokens[s], *branch[s], gain_three, near_full, ffn_width, last)
+        made = widen(s, flat_tokens, *branch[s], gain_three, near_full, ffn_width, last)
         hidden.append(made[0])
         third_low.append(made[1])
         active.append(made[2])
@@ -1293,21 +1344,17 @@
         act_sums.append(mp_rows(made[4], units))
         last = [made[4]]
 
-    grad_low = [out_grad[s] for s in each]
-    norm = ([a for a, _ in act_sums], [b for _, b in act_sums], gain_four, full_units)
-    down_parts = weight_grad(spot, grad_low, active, devices, groups, norm, False, last)
+    own_sums, other_sums = [a for a, _ in act_sums], [b for _, b in act_sums]
+    norm = (own_sums, other_sums, gain_four, full_units)
+    down_parts = weight_grad(spot, [flat_grads], active, devices, groups, norm, False, last)
     down_sum = ScatterSum(down_parts, groups)
     last = [down_parts[0]]
-    pre_low, third_terms, scaled, back_sums = [], [], [], []
-    gain_four_grad = 0.0
-    for s in each:
-        part, sums, gain_part = wide_back(
-            grad_low[s], down_full, active[s], *act_sums[s], gain_four, full_units, last
-        )
-        scaled.append(part)
-        gain_four_grad += gain_part
-        back_sums.append(mp_rows(sums, units))
-        last = [sums]
+    pre_low, third_terms = [], []
+    scaled, back_sums, gain_four_grad = wide_back(
+        flat_grads, down_full, active, own_sums, other_sums, gain_four, full_units, last
+    )
+    last = [back_sums[-1]]
+    back_sums = [mp_rows(sums, units) for sums in back_sums]
     last = [down_sum.mates(last)] + [other for _, other in back_sums]
     for s in each:
         low, terms = pre_back(
@@ -1333,7 +1380,7 @@
     last = [wide_terms[0][0]]
     for s in each:
         made = middle(
-            grad_low[s], *third_terms[s], hidden[s], gain_three, near_full, attended[s],
+            s, flat_grads, *third_terms[s], hidden[s], gain_three, near_full, attended[s],
             *att_sums[s], gain_two, model, last
         )
         grad_hidden.append(made[0])
@@ -1370,28 +1417,30 @@
             results = result(0, None, [out_parts[0], down_sum.out])
             last = [results]
         else:
-            first_terms = [mp_sum(first_sums[0].own(last), units)]
-            results = result(1, results, [first_terms[0][0]])
-            last = [out_sum.chips([results])]
+            first_terms = mp_sum(first_sums[0].own(last), units)
+            last = [first_terms[0]]
         away, kept, gain_part = first_back(
             order, made, first_low[s], heads_weight, gain_one, groups, last
         )
         gain_one_grad += gain_part
-        first_sums.append(ScatterSum((away, kept), groups))
         if s == 0:
+            first_sums.append(ScatterSum((away, kept), groups))
             last = [first_sums[0].mates([away])]
             last = [out_sum.mates(last)]
         else:
-            last = [away, in_sum.rows]
+            gain_one_sums = mp_rows(gain_one_grad, units)
+            got = exchange(away, "seq", groups, 1)
+            results = result(1, results, [away])
+            last = [out_sum.chips([results], PAUSE)]
+            near = add_halves(kept, got, span, last)
+            last = [near[0], in_sum.rows]
 
     heads_part = heads_grad(first_low, projected_grads, last)
     heads_rows = lax.psum_scatter(heads_part, "dp", scatter_dimension=0, tiled=True)
-    last = [first_sums[1].mates([heads_part])]
-    gain_one_sums = mp_rows(gain_one_grad, units)
-
-    def input_grad(s, into, after):
+
+    def input_grad(s, terms, into, after):
         return input_rows(
-            s, sequences, tokens[s], *first_terms[s], gain_one, grad_hidden[s], into, after
+            s, sequences, flat_tokens, terms, gain_one, grad_hidden[s], into, after
         )
 
     gain_rows = jnp.concatenate(
@@ -1405,17 +1454,33 @@
         ],
         axis=1,
     )
-    gain_rows = data_sum(gain_rows, devices, groups)
-
-    grad_input = input_grad(0, None, last)
-    first_terms.append(mp_sum(first_sums[1].own([grad_input, gain_rows]), units))
+    terms = []
+    last = [heads_part, gain_one_sums[1]]
+    for n, part in enumerate(near):
+        far = exchange(part, "seq", groups, 2)
+        column = n * (model // 2)
+        own = add(
+            [(kept, span, column), (got, span, column), (far, 0, 0)],
+            span,
+            last,
+            model // 2,
+            None if n == 0 else LONG_PAUSE,
+        )
+        terms.append(mp_sum(own, units))
+        if n == 0:
+            grad_input = input_grad(0, [first_terms], None, [own])
+            gain_rows = relay(gain_rows, [grad_input])
+            gain_rows = gain_rows + exchange(gain_rows, "seq", groups, 1)
+            gain_rows = axis_sum(gain_rows, "dp", devices)
+            last = [terms[0][1], gain_rows]
+    gain_rows = gain_rows + exchange(gain_rows, "seq", groups, 2)
     in_sum.chips()
     pieces = [
         lax.dynamic_slice_in_dim(heads_rows, jnp.bitwise_xor(place, n) * chunk, chunk, 0)
         for n in range(groups)
     ]
     pieces = pass_round(pieces, groups)
-    grad_input = input_grad(1, grad_input, [*last, *pieces[1:]])
+    grad_input = input_grad(1, terms, grad_input, [gain_rows])
     rows = jnp.stack(in_order(pieces, place)).astype(F32)
     grad_qkv_w = rows.reshape(groups, chunk, 3, share).transpose(2, 1, 0, 3)
     grad_qkv_w = grad_qkv_w.reshape(3, chunk, local_width)

time: 1010 us -> 954 us (0.945)
  waiting for transfers between devices: 278 us -> 241 us
  Pallas kernels: 588 us -> 556 us
    ppermute x57 -> x59, waiting for transfers between devices: 277 us -> 240 us  [exchange(): return lax.ppermute(array, axis, [(n, n ^ offset) for n in range(size)])]
    pallas_call x40 -> x41, Pallas kernels: 529 us -> 496 us  [call(): pl.pallas_call(run, grid_spec=pltpu.PrefetchScalarGridSpec(num_scalar_pre...]
    ppermute x57 -> x59, starting transfers between devices: 46.8 us -> 52 us  [exchange(): return lax.ppermute(array, axis, [(n, n ^ offset) for n in range(size)])]
    unnamed x124 -> x126, local copies, waits for them, and re-layouts: 26.9 us -> 31.6 us
  transfers between devices with their start and end apart: 64 -> 66, of which waited for: 26 -> 27; matrix products, arithmetic and copies ran while one was open for 5% -> 5% of each run, Pallas kernels for 57% -> 59%
where the time goes in v4:
time: 954 us; the launch traced here: 939 us
  Pallas kernels  556 us (58%)
  waiting for transfers between devices  241 us (25%)
  local copies, waits for them, and re-layouts  55.8 us (6%)
  starting transfers between devices  52.8 us (6%)
  other arithmetic  18.4 us (2%)
  between operations  15.4 us (2%)
    pallas_call x41, Pallas kernels, call(): pl.pallas_call(run, grid_spec=pltpu.PrefetchScalarGridSpec(num_scalar_pre...  496 us
    ppermute x59, waiting for transfers between devices, exchange(): return lax.ppermute(array, axis, [(n, n ^ offset) for n in range(size)])  240 us
    pallas_call x3, Pallas kernels, weight_grad(): pl.pallas_call(partial(weight_grad_kernel, sequences=sequences, devices=d...  59.4 us
    ppermute x59, starting transfers between devices, exchange(): return lax.ppermute(array, axis, [(n, n ^ offset) for n in range(size)])  52 us
    unnamed x126, local copies, waits for them, and re-layouts  31.6 us
  transfers between devices with their start and end apart: 66, of which 27 were waited for; matrix products, arithmetic and copies ran while one was open for 5% of the time, Pallas kernels for 59%

profile of v4, /device:TPU:0, one launch (start us, length us, event | category | flops | bytes accessed | tf_op | source)
XLA Modules:
  0.0 939.3 jit_solution(4031687866378730935)
XLA Ops:
  10.7 2.6 collective-permute-start.6
  13.4 6.2 collective-permute-done.6
  19.6 4.2 collective-permute-done.7
  25.0 4.8 slice_bitcast_fusion
  36.0 2.6 collective-permute-start.9
  38.6 4.7 collective-permute-done.9
  44.1 33.6 %collective-permute-done.3.refs_3_ = bf16[512,2048]{1,0:T(8,128)(2,1)S(1)} collective-permute-done((bf16[512,2048]{1,0:T(8,128)(2,1)}, bf16[512,2048]{1,0:T(8,128)(2,1)S(1)}, u32[]{:S(2)}, u32[]{:S(2)}) %collective-permute-start.3) | collective-permute-done | bytes 2097184 | tf_op jit(solution)/shard_map/ppermute | solution.py:1031
  98.5 18.6 %project.2 = (bf16[2048,2048]{1,0:T(8,128)(2,1)}, bf16[2048,768]{1,0:T(8,128)(2,1)}) custom-call(s32[1]{0:T(128)} %bitcast.1.refs_0_.place, bf16[512,2048]{1,0:T(8,128)(2,1)} %get-tuple-element.190.refs_1_, bf16[512,2048]{1,0:T(8,128)(2,1)} %collective-permute-done.2.refs_2_, bf16[512,2048]{1,0:T(8,128)(2,1)} %copy-done.4, ...), custom_call_target="tpu_custom_call" | custom-call | flops 4026531840 | tf_op jit(solution)/shard_map/project/pallas_call | solution.py:493
  117.1 16.8 %attend.2 = (bf16[512,256]{1,0:T(8,128)(2,1)}, bf16[512,256]{1,0:T(8,128)(2,1)}, bf16[512,256]{1,0:T(8,128)(2,1)}, bf16[512,256]{1,0:T(8,128)(2,1)}, f32[4,2048]{1,0:T(4,128)}) custom-call(s32[2]{0:T(128)} %pad_add_fusion.1.refs_0_, bf16[2048,768]{1,0:T(8,128)(2,1)} %get-tuple-element.85.refs_1_), custom_call_target="tpu_custom_call" | custom-call | flops 7784628224 | tf_op jit(solution)/shard_map/attend/pallas_call | solution.py:493
  133.9 29.0 %collective-permute-done.1.refs_0_.refs_3_ = bf16[512,2048]{1,0:T(8,128)(2,1)} collective-permute-done((bf16[512,2048]{1,0:T(8,128)(2,1)}, bf16[512,2048]{1,0:T(8,128)(2,1)}, u32[]{:S(2)}, u32[]{:S(2)}) %collective-permute-start.1) | collective-permute-done | bytes 2097184 | tf_op jit(solution)/shard_map/ppermute | solution.py:1031
  162.9 3.9 relay.2.refs_11_
  172.6 18.8 %project.3 = (bf16[2048,2048]{1,0:T(8,128)(2,1)}, bf16[2048,768]{1,0:T(8,128)(2,1)}) custom-call(s32[1]{0:T(128)} %bitcast.1.refs_0_.place, bf16[512,2048]{1,0:T(8,128)(2,1)} %get-tuple-element.191.refs_1_, bf16[512,2048]{1,0:T(8,128)(2,1)} %collective-permute-done.refs_2_, bf16[512,2048]{1,0:T(8,128)(2,1)} %collective-permute-done.1.refs_0_.refs_3_, ...), custom_call_target="tpu_custom_call" | custom-call | flops 4026531840 | tf_op jit(solution)/shard_map/project/pallas_call | solution.py:493
  191.4 31.3 %attend.3 = (bf16[512,256]{1,0:T(8,128)(2,1)}, bf16[512,256]{1,0:T(8,128)(2,1)}, bf16[512,256]{1,0:T(8,128)(2,1)}, bf16[512,256]{1,0:T(8,128)(2,1)}, f32[4,2048]{1,0:T(4,128)}) custom-call(s32[2]{0:T(128)} %pad_add_fusion.refs_0_, bf16[2048,768]{1,0:T(8,128)(2,1)} %get-tuple-element.87.refs_1_), custom_call_target="tpu_custom_call" | custom-call | flops 7784628224 | tf_op jit(solution)/shard_map/attend/pallas_call | solution.py:493
  225.3 12.8 %collective-permute-done.12.refs_7_.refs_3_ = bf16[512,256]{1,0:T(8,128)(2,1)S(1)} collective-permute-done((bf16[512,256]{1,0:T(8,128)(2,1)}, bf16[512,256]{1,0:T(8,128)(2,1)S(1)}, u32[]{:S(2)}, u32[]{:S(2)}) %collective-permute-start.12) | collective-permute-done | bytes 262176 | tf_op jit(solution)/shard_map/ppermute | solution.py:1031
  238.1 10.9 %collective-permute-done.13.refs_8_.refs_4_ = bf16[512,256]{1,0:T(8,128)(2,1)S(1)} collective-permute-done((bf16[512,256]{1,0:T(8,128)(2,1)}, bf16[512,256]{1,0:T(8,128)(2,1)S(1)}, u32[]{:S(2)}, u32[]{:S(2)}) %collective-permute-start.13) | collective-permute-done | bytes 262176 | tf_op jit(solution)/shard_map/ppermute | solution.py:1031
  249.7 2.7 collect.2
  252.4 2.6 collect.3
  260.4 6.4 out_branch.2
  267.7 6.9 out_branch.3
  275.8 39.7 %collective-permute-done.20.refs_2_ = bf16[512,2048]{1,0:T(8,128)(2,1)S(1)} collective-permute-done((bf16[512,2048]{1,0:T(8,128)(2,1)}, bf16[512,2048]{1,0:T(8,128)(2,1)S(1)}, u32[]{:S(2)}, u32[]{:S(2)}) %collective-permute-start.20) | collective-permute-done | bytes 2097184 | tf_op jit(solution)/shard_map/ppermute | solution.py:1031
  316.9 23.3 %widen.2 = (f32[512,2048]{1,0:T(8,128)}, bf16[512,2048]{1,0:T(8,128)(2,1)}, bf16[512,4096]{1,0:T(8,128)(2,1)}, bf16[512,4096]{1,0:T(8,128)(2,1)}, f32[2,512]{1,0:T(2,128)}) custom-call(bf16[1024,2048]{1,0:T(8,128)(2,1)} %bitcast.66, bf16[512,2048]{1,0:T(8,128)(2,1)} %get-tuple-element.101.refs_5_.refs_1_, bf16[512,2048]{1,0:T(8,128)(2,1)} %copy-done.12, ...), custom_call_target="tpu_custom_call" | custom-call | flops 5798205952 | tf_op jit(solution)/shard_map/widen/pallas_call | solution.py:493
  340.2 18.7 %collective-permute-done.19.refs_2_ = bf16[512,2048]{1,0:T(8,128)(2,1)S(1)} collective-permute-done((bf16[512,2048]{1,0:T(8,128)(2,1)}, bf16[512,2048]{1,0:T(8,128)(2,1)S(1)}, u32[]{:S(2)}, u32[]{:S(2)}) %collective-permute-start.19) | collective-permute-done | bytes 2097184 | tf_op jit(solution)/shard_map/ppermute | solution.py:1031
  360.2 23.2 %widen.3 = (f32[512,2048]{1,0:T(8,128)}, bf16[512,2048]{1,0:T(8,128)(2,1)}, bf16[512,4096]{1,0:T(8,128)(2,1)}, bf16[512,4096]{1,0:T(8,128)(2,1)}, f32[2,512]{1,0:T(2,128)}) custom-call(bf16[1024,2048]{1,0:T(8,128)(2,1)} %bitcast.67, bf16[512,2048]{1,0:T(8,128)(2,1)} %get-tuple-element.102.refs_5_.refs_1_, bf16[512,2048]{1,0:T(8,128)(2,1)} %copy-done.11, ...), custom_call_target="tpu_custom_call" | custom-call | flops 5798205952 | tf_op jit(solution)/shard_map/widen/pallas_call | solution.py:493
  388.2 26.0 %weight_grad.3 = (bf16[1024,4096]{1,0:T(8,128)(2,1)}, bf16[1024,4096]{1,0:T(8,128)(2,1)}) custom-call(s32[1]{0:T(128)} %bitcast.1.refs_0_.place, bf16[1024,2048]{1,0:T(8,128)(2,1)} %bitcast.70, bf16[1024,2048]{1,0:T(8,128)(2,1)} %bitcast.71, bf16[512,4096]{1,0:T(8,128)(2,1)} %get-tuple-element.106.refs_2_.refs_3_.refs_1_.refs_0_, ...), custom_call_target="tpu_custom_call" | custom-call | flops 6227702784 | tf_op jit(solution)/shard_map/weight_grad/pallas_call | solution.py:453
  414.2 27.4 %wide_back.1 = (bf16[512,4096]{1,0:T(8,128)(2,1)}, bf16[512,4096]{1,0:T(8,128)(2,1)}, f32[2,512]{1,0:T(2,128)}, f32[2,512]{1,0:T(2,128)}, f32[1,4096]{1,0:T(1,128)}) custom-call(bf16[1024,2048]{1,0:T(8,128)(2,1)} %bitcast.72, bf16[4096,2048]{1,0:T(8,128)(2,1)} %all-gather.8.cloned.1.call-done.refs_1_.refs_4_, f32[1,4096]{1,0:T(1,128)} %reshape.283.refs_8_.refs_2_.refs_3_, ...), custom_call_target="tpu_custom_call" | custom-call | flops 7516192768 | tf_op jit(solution)/shard_map/wide_back/pallas_call | solution.py:493
  441.7 6.1 add.192.refs_8_
  454.9 19.6 %pre_back.2 = (bf16[512,4096]{1,0:T(8,128)(2,1)}, bf16[512,2048]{1,0:T(8,128)(2,1)}) custom-call(bf16[512,4096]{1,0:T(8,128)(2,1)} %get-tuple-element.111.refs_0_, bf16[512,4096]{1,0:T(8,128)(2,1)} %get-tuple-element.106.refs_2_.refs_3_.refs_1_.refs_0_, bf16[512,4096]{1,0:T(8,128)(2,1)} %get-tuple-element.112.refs_2_, ...), custom_call_target="tpu_custom_call" | custom-call | flops 4939212288 | tf_op jit(solution)/shard_map/pre_back/pallas_call | solution.py:493
  475.6 19.6 %pre_back.3 = (bf16[512,4096]{1,0:T(8,128)(2,1)}, bf16[512,2048]{1,0:T(8,128)(2,1)}) custom-call(bf16[512,4096]{1,0:T(8,128)(2,1)} %get-tuple-element.108.refs_0_, bf16[512,4096]{1,0:T(8,128)(2,1)} %get-tuple-element.104.refs_3_.refs_4_.refs_1_.refs_0_, bf16[512,4096]{1,0:T(8,128)(2,1)} %get-tuple-element.109.refs_2_, ...), custom_call_target="tpu_custom_call" | custom-call | flops 4939212288 | tf_op jit(solution)/shard_map/pre_back/pallas_call | solution.py:493
  496.2 16.2 %narrow.2.refs_10_.refs_0_ = bf16[512,2048]{1,0:T(8,128)(2,1)} custom-call(bf16[512,4096]{1,0:T(8,128)(2,1)} %get-tuple-element.106.refs_2_.refs_3_.refs_1_.refs_0_, f32[2,512]{1,0:T(2,128)} %get-tuple-element.103.refs_5_.refs_4_.refs_3_.refs_1_, f32[2,512]{1,0:T(2,128)} %copy-done.23, f32[1,4096]{1,0:T(1,128)} %reshape.283.refs_8_.refs_2_.refs_3_, ...), custom_call_target="tpu_custom_call" | custom-call | flops 3972844800 | tf_op jit(solution)/shard_map/narrow/pallas_call | solution.py:493
  512.5 11.0 %collective-permute-done.27.refs_2_ = bf16[512,2048]{1,0:T(8,128)(2,1)} collective-permute-done((bf16[512,2048]{1,0:T(8,128)(2,1)}, bf16[512,2048]{1,0:T(8,128)(2,1)}, u32[]{:S(2)}, u32[]{:S(2)}) %collective-permute-start.27) | collective-permute-done | bytes 2097184 | tf_op jit(solution)/shard_map/ppermute | solution.py:1031
  523.4 12.8 %middle.2 = (f32[512,2048]{1,0:T(8,128)}, bf16[512,2048]{1,0:T(8,128)(2,1)}, f32[512,1024]{1,0:T(8,128)}, f32[2,512]{1,0:T(2,128)}, f32[1,2048]{1,0:T(1,128)}, /*index=5*/f32[1,1024]{1,0:T(1,128)}) custom-call(bf16[1024,2048]{1,0:T(8,128)(2,1)} %bitcast.73, bf16[512,2048]{1,0:T(8,128)(2,1)} %get-tuple-element.115.refs_8_.refs_1_, ...), custom_call_target="tpu_custom_call" | custom-call | flops 3221225472 | tf_op jit(solution)/shard_map/middle/pallas_call | solution.py:493
  536.2 23.7 %weight_grad.4 = (bf16[1024,4096]{1,0:T(8,128)(2,1)}, bf16[1024,4096]{1,0:T(8,128)(2,1)}) custom-call(s32[1]{0:T(128)} %bitcast.1.refs_0_.place, bf16[512,2048]{1,0:T(8,128)(2,1)} %get-tuple-element.121.refs_0_, bf16[512,2048]{1,0:T(8,128)(2,1)} %get-tuple-element.122.refs_1_, bf16[512,4096]{1,0:T(8,128)(2,1)} %get-tuple-element.123.refs_2_, ...), custom_call_target="tpu_custom_call" | custom-call | flops 6227702784 | tf_op jit(solution)/shard_map/weight_grad/pallas_call | solution.py:453
  560.0 6.3 collective-permute-done.26.refs_4_.refs_2_
  569.6 7.3 add.193.refs_7_
  581.8 4.8 share_out.2
  588.5 12.7 %middle.3 = (f32[512,2048]{1,0:T(8,128)}, bf16[512,2048]{1,0:T(8,128)(2,1)}, f32[512,1024]{1,0:T(8,128)}, f32[2,512]{1,0:T(2,128)}, f32[1,2048]{1,0:T(1,128)}, /*index=5*/f32[1,1024]{1,0:T(1,128)}) custom-call(bf16[1024,2048]{1,0:T(8,128)(2,1)} %bitcast.74, bf16[512,2048]{1,0:T(8,128)(2,1)} %get-tuple-element.116.refs_5_.refs_1_, ...), custom_call_target="tpu_custom_call" | custom-call | flops 3221225472 | tf_op jit(solution)/shard_map/middle/pallas_call | solution.py:493
  601.2 16.1 %narrow.3.refs_2_.refs_0_ = bf16[512,2048]{1,0:T(8,128)(2,1)} custom-call(bf16[512,4096]{1,0:T(8,128)(2,1)} %get-tuple-element.104.refs_3_.refs_4_.refs_1_.refs_0_, f32[2,512]{1,0:T(2,128)} %get-tuple-element.105.refs_5_.refs_9_.refs_6_.refs_3_.refs_1_, f32[2,512]{1,0:T(2,128)} %copy-done.22, f32[1,4096]{1,0:T(1,128)} %reshape.283.refs_8_.refs_2_.refs_3_, ...), custom_call_target="tpu_custom_call" | custom-call | flops 3972844800 | tf_op jit(solution)/shard_map/narrow/pallas_call | solution.py:493
  617.7 11.3 %add.194.refs_7_ = bf16[1024,4096]{1,0:T(8,128)(2,1)} custom-call(bf16[1024,4096]{1,0:T(8,128)(2,1)} %get-tuple-element.136.refs_0_, bf16[1024,4096]{1,0:T(8,128)(2,1)} %collective-permute-done.36.refs_1_, bf16[512,2048]{1,0:T(8,128)(2,1)} %narrow.3.refs_2_.refs_0_), custom_call_target="tpu_custom_call" | custom-call | flops 1572864000 | tf_op jit(solution)/shard_map/add/pallas_call | solution.py:493
  629.7 4.1 share_out.3
  636.4 26.2 %attend_back.2.refs_4_.refs_1_.refs_0_ = bf16[2048,768]{1,0:T(8,128)(2,1)} custom-call(s32[2]{0:T(128)} %pad_add_fusion.1.refs_0_, bf16[2048,768]{1,0:T(8,128)(2,1)} %get-tuple-element.85.refs_1_, bf16[512,256]{1,0:T(8,128)(2,1)} %get-tuple-element.126.refs_10_.refs_2_, bf16[512,256]{1,0:T(8,128)(2,1)} %copy-done.49, bf16[512,256]{1,0:T(8,128)(2,1)} %copy-done.50, ...), custom_call_target="tpu_custom_call" | custom-call | flops 281857228800 | tf_op jit(solution)/shard_map/attend_back/pallas_call | solution.py:493
  662.6 9.7 %weight_grad.5 = (bf16[1024,1024]{1,0:T(8,128)(2,1)}, bf16[1024,1024]{1,0:T(8,128)(2,1)}) custom-call(s32[1]{0:T(128)} %bitcast.1.refs_0_.place, bf16[512,2048]{1,0:T(8,128)(2,1)} %get-tuple-element.128.refs_0_, bf16[512,2048]{1,0:T(8,128)(2,1)} %get-tuple-element.129.refs_1_, bf16[512,1024]{1,0:T(8,128)(2,1)} %get-tuple-element.130.refs_2_, ...), custom_call_target="tpu_custom_call" | custom-call | flops 1556925696 | tf_op jit(solution)/shard_map/weight_grad/pallas_call | solution.py:453
  672.3 3.7 convert_bitcast_fusion.2
  676.0 5.3 result.2.refs_5_.refs_3_
  681.3 16.8 %first_back.2 = (bf16[1024,2048]{1,0:T(8,128)(2,1)}, bf16[1024,2048]{1,0:T(8,128)(2,1)}, f32[1,2048]{1,0:T(1,128)}) custom-call(s32[4]{0:T(128)} %broadcast_xor_fusion.refs_0_, bf16[2048,768]{1,0:T(8,128)(2,1)} %attend_back.2.refs_4_.refs_1_.refs_0_, bf16[2048,2048]{1,0:T(8,128)(2,1)} %get-tuple-element.143.refs_2_, ...), custom_call_target="tpu_custom_call" | custom-call | flops 3623878656 | tf_op jit(solution)/shard_map/first_back/pallas_call | solution.py:493
  698.7 9.8 %collective-permute-done.41.refs_1_ = bf16[1024,2048]{1,0:T(8,128)(2,1)S(1)} collective-permute-done((bf16[1024,2048]{1,0:T(8,128)(2,1)}, bf16[1024,2048]{1,0:T(8,128)(2,1)S(1)}, u32[]{:S(2)}, u32[]{:S(2)}) %collective-permute-start.41) | collective-permute-done | bytes 4194336 | tf_op jit(solution)/shard_map/ppermute | solution.py:1031
  710.5 4.5 add.195.refs_2_
  717.7 3.6 add.196.refs_15_
  722.5 45.0 %attend_back.3.refs_3_.refs_1_ = bf16[2048,768]{1,0:T(8,128)(2,1)} custom-call(s32[2]{0:T(128)} %pad_add_fusion.refs_0_, bf16[2048,768]{1,0:T(8,128)(2,1)} %get-tuple-element.87.refs_1_, bf16[512,256]{1,0:T(8,128)(2,1)} %get-tuple-element.137.refs_15_.refs_2_, bf16[512,256]{1,0:T(8,128)(2,1)} %collective-permute-done.37.refs_5_.refs_3_, ...), custom_call_target="tpu_custom_call" | custom-call | flops 11274289152 | tf_op jit(solution)/shard_map/attend_back/pallas_call | solution.py:493
  768.8 4.9 add.197.refs_5_.refs_3_
  773.7 16.8 %first_back.3 = (bf16[1024,2048]{1,0:T(8,128)(2,1)}, bf16[1024,2048]{1,0:T(8,128)(2,1)}, f32[1,2048]{1,0:T(1,128)}) custom-call(s32[4]{0:T(128)} %broadcast_xor_fusion.refs_0_, bf16[2048,768]{1,0:T(8,128)(2,1)} %attend_back.3.refs_3_.refs_1_, bf16[2048,2048]{1,0:T(8,128)(2,1)} %get-tuple-element.146.refs_2_.refs_3_, ...), custom_call_target="tpu_custom_call" | custom-call | flops 3623878656 | tf_op jit(solution)/shard_map/first_back/pallas_call | solution.py:493
  791.8 5.4 result.3.refs_3_
  798.2 3.9 add.198.refs_2_
  802.8 4.2 add_halves.1
  808.1 21.0 %heads_grad.1.refs_3_ = bf16[2048,768]{1,0:T(8,128)(2,1)} custom-call(bf16[2048,768]{1,0:T(8,128)(2,1)} %attend_back.2.refs_4_.refs_1_.refs_0_, bf16[2048,768]{1,0:T(8,128)(2,1)} %attend_back.3.refs_3_.refs_1_, bf16[2048,2048]{1,0:T(8,128)(2,1)} %get-tuple-element.143.refs_2_, bf16[2048,2048]{1,0:T(8,128)(2,1)} %get-tuple-element.146.refs_2_.refs_3_, ...), custom_call_target="tpu_custom_call" | custom-call | flops 4831838208 | tf_op jit(solution)/shard_map/heads_grad/pallas_call | solution.py:493
  832.7 18.0 %collective-permute-done.46.refs_4_ = f32[1,2048]{1,0:T(1,128)S(1)} collective-permute-done((f32[1,2048]{1,0:T(1,128)S(1)}, f32[1,2048]{1,0:T(1,128)S(1)}, u32[]{:S(2)}, u32[]{:S(2)}) %collective-permute-start.46) | collective-permute-done | bytes 8224 | tf_op jit(solution)/shard_map/ppermute | solution.py:1031
  852.3 3.9 add.199.refs_5_.refs_3_
  860.6 7.4 input_grad.2.refs_1_.refs_7_
  871.6 5.4 collective-permute-done.51
  879.1 3.0 copy.111
  882.1 3.6 collective-permute-done.52
  893.2 3.9 add.200.refs_5_
  902.1 14.5 %collective-permute-done.58 = bf16[128,4096]{1,0:T(8,128)(2,1)} collective-permute-done((bf16[128,4096]{1,0:T(8,128)(2,1)}, bf16[128,4096]{1,0:T(8,128)(2,1)}, u32[]{:S(2)}, u32[]{:S(2)}) %collective-permute-start.58) | collective-permute-done | bytes 1048608 | tf_op jit(solution)/shard_map/ppermute | solution.py:1031
  916.5 2.8 convert_add_fusion
  922.0 7.3 input_grad.3
  (343 shorter events, 124.1 us)
Async XLA Ops:
  7.2 91.3 %all-gather.4.cloned.1.call-start = ((), (), s32[]{:S(2)}) async-start(), calls=%async_computation.4 | async-start | bytes 3932160 | tf_op jit(solution)/shard_map/all_gather | solution.py:1282
  10.2 3.2 collective-permute-start.5
  10.7 8.9 collective-permute-start.6
  13.3 10.5 %collective-permute-start.7 = (bf16[144,768]{1,0:T(8,128)(2,1)S(1)}, bf16[144,768]{1,0:T(8,128)(2,1)S(1)}, u32[]{:S(2)}, u32[]{:S(2)}) collective-permute-start(bf16[144,768]{1,0:T(8,128)(2,1)S(1)} %get-tuple-element.221), channel_id=1, source_target_pairs={{0,6},{2,4},{4,2},{6,0},{1,7},{3,5},{5,3},{7,1},{8,14},{10,12},{12... | collective-permute-start | bytes 663560 | tf_op jit(solution)/shard_map/ppermute | solution.py:1031
  25.0 234.8 %all-gather.6.cloned.1.call-start = ((), (), s32[]{:S(2)}) async-start(), calls=%async_computation.5 | async-start | bytes 22282240 | tf_op jit(solution)/shard_map/all_gather | solution.py:1295
  29.8 47.9 %collective-permute-start.3 = (bf16[512,2048]{1,0:T(8,128)(2,1)}, bf16[512,2048]{1,0:T(8,128)(2,1)S(1)}, u32[]{:S(2)}, u32[]{:S(2)}) collective-permute-start(bf16[512,2048]{1,0:T(8,128)(2,1)} %get-tuple-element.190.refs_1_), channel_id=1, source_target_pairs={{0,4},{2,6},{4,0},{6,2},{1,5},{3,7},{5,1},{7,3},{8,12},{10,14},{12... | collective-permute-start | bytes 6291464 | tf_op jit(solution)/shard_map/ppermute | solution.py:1031
  31.9 4.0 collective-permute-start.8
  36.0 7.3 collective-permute-start.9
  81.5 332.7 %all-gather.8.cloned.1.call-start = ((), (), s32[]{:S(2)}) async-start(), calls=%async_computation.6 | async-start | bytes 17825792 | tf_op jit(solution)/shard_map/all_gather | solution.py:1298
  82.2 590.1 %reduce-scatter.5.cloned.1.call-start = ((), (), s32[]{:S(2)}) async-start(), calls=%async_computation.7 | async-start | bytes 5242880 | tf_op jit(solution)/shard_map/reduce_scatter | solution.py:1178
  82.5 16.0 %collective-permute-start.2 = (bf16[512,2048]{1,0:T(8,128)(2,1)}, bf16[512,2048]{1,0:T(8,128)(2,1)}, u32[]{:S(2)}, u32[]{:S(2)}) collective-permute-start(bf16[512,2048]{1,0:T(8,128)(2,1)} %get-tuple-element.190.refs_1_), channel_id=1, source_target_pairs={{0,2},{2,0},{4,6},{6,4},{1,3},{3,1},{5,7},{7,5},{8,10},{10,8},{12,... | collective-permute-start | bytes 6291464 | tf_op jit(solution)/shard_map/ppermute | solution.py:1031
  83.1 15.4 %collective-permute-start.4 = (bf16[512,2048]{1,0:T(8,128)(2,1)S(1)}, bf16[512,2048]{1,0:T(8,128)(2,1)}, u32[]{:S(2)}, u32[]{:S(2)}) collective-permute-start(bf16[512,2048]{1,0:T(8,128)(2,1)S(1)} %copy-done.5), channel_id=1, source_target_pairs={{0,2},{2,0},{4,6},{6,4},{1,3},{3,1},{5,7},{7,5},{8,10},{10,8},{12,... | collective-permute-start | bytes 6291464 | tf_op jit(solution)/shard_map/ppermute | solution.py:1031
  83.1 79.9 %collective-permute-start.1 = (bf16[512,2048]{1,0:T(8,128)(2,1)}, bf16[512,2048]{1,0:T(8,128)(2,1)}, u32[]{:S(2)}, u32[]{:S(2)}) collective-permute-start(bf16[512,2048]{1,0:T(8,128)(2,1)} %get-tuple-element.191.refs_1_), channel_id=1, source_target_pairs={{0,4},{2,6},{4,0},{6,2},{1,5},{3,7},{5,1},{7,3},{8,12},{10,14},{12... | collective-permute-start | bytes 6291464 | tf_op jit(solution)/shard_map/ppermute | solution.py:1031
  84.8 86.2 %collective-permute-start = (bf16[512,2048]{1,0:T(8,128)(2,1)}, bf16[512,2048]{1,0:T(8,128)(2,1)}, u32[]{:S(2)}, u32[]{:S(2)}) collective-permute-start(bf16[512,2048]{1,0:T(8,128)(2,1)} %get-tuple-element.191.refs_1_), channel_id=1, source_target_pairs={{0,2},{2,0},{4,6},{6,4},{1,3},{3,1},{5,7},{7,5},{8,10},{10,8},{12,... | collective-permute-start | bytes 6291464 | tf_op jit(solution)/shard_map/ppermute | solution.py:1031
  166.8 4.5 collective-permute-start.10
  168.0 57.1 %collective-permute-start.14 = (bf16[512,256]{1,0:T(8,128)(2,1)S(1)}, bf16[512,256]{1,0:T(8,128)(2,1)S(1)}, u32[]{:S(2)}, u32[]{:S(2)}) collective-permute-start(bf16[512,256]{1,0:T(8,128)(2,1)S(1)} %copy-done.46), channel_id=1, source_target_pairs={{0,2},{2,0},{4,6},{6,4},{1,3},{3,1},{5,7},{7,5},{8,10},{10,8},{12,... | collective-permute-start | bytes 786440 | tf_op jit(solution)/shard_map/ppermute | solution.py:1031
  168.5 56.7 %collective-permute-start.15 = (bf16[512,256]{1,0:T(8,128)(2,1)S(1)}, bf16[512,256]{1,0:T(8,128)(2,1)S(1)}, u32[]{:S(2)}, u32[]{:S(2)}) collective-permute-start(bf16[512,256]{1,0:T(8,128)(2,1)S(1)} %copy-done.47), channel_id=1, source_target_pairs={{0,4},{2,6},{4,0},{6,2},{1,5},{3,7},{5,1},{7,3},{8,12},{10,14},{12... | collective-permute-start | bytes 786440 | tf_op jit(solution)/shard_map/ppermute | solution.py:1031
  171.0 54.2 %collective-permute-start.16 = (bf16[512,256]{1,0:T(8,128)(2,1)S(1)}, bf16[512,256]{1,0:T(8,128)(2,1)S(1)}, u32[]{:S(2)}, u32[]{:S(2)}) collective-permute-start(bf16[512,256]{1,0:T(8,128)(2,1)S(1)} %copy-done.48), channel_id=1, source_target_pairs={{0,6},{2,4},{4,2},{6,0},{1,7},{3,5},{5,3},{7,1},{8,14},{10,12},{12... | collective-permute-start | bytes 786440 | tf_op jit(solution)/shard_map/ppermute | solution.py:1031
  223.0 15.1 %collective-permute-start.12 = (bf16[512,256]{1,0:T(8,128)(2,1)}, bf16[512,256]{1,0:T(8,128)(2,1)S(1)}, u32[]{:S(2)}, u32[]{:S(2)}) collective-permute-start(bf16[512,256]{1,0:T(8,128)(2,1)} %get-tuple-element.90.refs_8_), channel_id=1, source_target_pairs={{0,4},{2,6},{4,0},{6,2},{1,5},{3,7},{5,1},{7,3},{8,12},{10,14},{12... | collective-permute-start | bytes 786440 | tf_op jit(solution)/shard_map/ppermute | solution.py:1031
  225.1 23.9 %collective-permute-start.13 = (bf16[512,256]{1,0:T(8,128)(2,1)}, bf16[512,256]{1,0:T(8,128)(2,1)S(1)}, u32[]{:S(2)}, u32[]{:S(2)}) collective-permute-start(bf16[512,256]{1,0:T(8,128)(2,1)} %get-tuple-element.91.refs_9_), channel_id=1, source_target_pairs={{0,6},{2,4},{4,2},{6,0},{1,7},{3,5},{5,3},{7,1},{8,14},{10,12},{12... | collective-permute-start | bytes 786440 | tf_op jit(solution)/shard_map/ppermute | solution.py:1031
  255.0 3.8 collective-permute-start.17
  256.2 3.6 collective-permute-start.18
  266.8 48.8 %collective-permute-start.20 = (bf16[512,2048]{1,0:T(8,128)(2,1)}, bf16[512,2048]{1,0:T(8,128)(2,1)S(1)}, u32[]{:S(2)}, u32[]{:S(2)}) collective-permute-start(bf16[512,2048]{1,0:T(8,128)(2,1)} %get-tuple-element.101.refs_5_.refs_1_), channel_id=1, source_target_pairs={{0,1},{1,0},{2,3},{3,2},{4,5},{5,4},{6,7},{7,6},{8,9},{9,8},{10,11... | collective-permute-start | bytes 6291464 | tf_op jit(solution)/shard_map/ppermute | solution.py:1031
  274.6 84.3 %collective-permute-start.19 = (bf16[512,2048]{1,0:T(8,128)(2,1)}, bf16[512,2048]{1,0:T(8,128)(2,1)S(1)}, u32[]{:S(2)}, u32[]{:S(2)}) collective-permute-start(bf16[512,2048]{1,0:T(8,128)(2,1)} %get-tuple-element.102.refs_5_.refs_1_), channel_id=1, source_target_pairs={{0,1},{1,0},{2,3},{3,2},{4,5},{5,4},{6,7},{7,6},{8,9},{9,8},{10,11... | collective-permute-start | bytes 6291464 | tf_op jit(solution)/shard_map/ppermute | solution.py:1031
  383.4 3.8 collective-permute-start.21
  384.0 3.6 collective-permute-start.22
  414.2 27.5 %collective-permute-start.25 = (bf16[1024,4096]{1,0:T(8,128)(2,1)}, bf16[1024,4096]{1,0:T(8,128)(2,1)}, u32[]{:S(2)}, u32[]{:S(2)}) collective-permute-start(bf16[1024,4096]{1,0:T(8,128)(2,1)} %get-tuple-element.107.refs_9_), channel_id=1, source_target_pairs={{0,2},{2,0},{4,6},{6,4},{1,3},{3,1},{5,7},{7,5},{8,10},{10,8},{12,... | collective-permute-start | bytes 25165832 | tf_op jit(solution)/shard_map/ppermute | solution.py:1031
  447.8 118.5 %collective-permute-start.29 = (bf16[512,4096]{1,0:T(8,128)(2,1)}, bf16[512,4096]{1,0:T(8,128)(2,1)S(1)}, u32[]{:S(2)}, u32[]{:S(2)}) collective-permute-start(bf16[512,4096]{1,0:T(8,128)(2,1)} %add.192.refs_8_), channel_id=1, source_target_pairs={{0,4},{2,6},{4,0},{6,2},{1,5},{3,7},{5,1},{7,3},{8,12},{10,14},{12... | collective-permute-start | bytes 12582920 | tf_op jit(solution)/shard_map/ppermute | solution.py:1031
  449.7 3.6 collective-permute-start.23
  450.7 3.6 collective-permute-start.24
  474.5 48.9 %collective-permute-start.27 = (bf16[512,2048]{1,0:T(8,128)(2,1)}, bf16[512,2048]{1,0:T(8,128)(2,1)}, u32[]{:S(2)}, u32[]{:S(2)}) collective-permute-start(bf16[512,2048]{1,0:T(8,128)(2,1)} %get-tuple-element.115.refs_8_.refs_1_), channel_id=1, source_target_pairs={{0,1},{1,0},{2,3},{3,2},{4,5},{5,4},{6,7},{7,6},{8,9},{9,8},{10,11... | collective-permute-start | bytes 6291464 | tf_op jit(solution)/shard_map/ppermute | solution.py:1031
  495.1 71.1 %collective-permute-start.26 = (bf16[512,2048]{1,0:T(8,128)(2,1)}, bf16[512,2048]{1,0:T(8,128)(2,1)S(1)}, u32[]{:S(2)}, u32[]{:S(2)}) collective-permute-start(bf16[512,2048]{1,0:T(8,128)(2,1)} %get-tuple-element.116.refs_5_.refs_1_), channel_id=1, source_target_pairs={{0,1},{1,0},{2,3},{3,2},{4,5},{5,4},{6,7},{7,6},{8,9},{9,8},{10,11... | collective-permute-start | bytes 6291464 | tf_op jit(solution)/shard_map/ppermute | solution.py:1031
  560.0 57.3 %collective-permute-start.36 = (bf16[1024,4096]{1,0:T(8,128)(2,1)}, bf16[1024,4096]{1,0:T(8,128)(2,1)}, u32[]{:S(2)}, u32[]{:S(2)}) collective-permute-start(bf16[1024,4096]{1,0:T(8,128)(2,1)} %get-tuple-element.125.refs_3_), channel_id=1, source_target_pairs={{0,2},{2,0},{4,6},{6,4},{1,3},{3,1},{5,7},{7,5},{8,10},{10,8},{12,... | collective-permute-start | bytes 25165832 | tf_op jit(solution)/shard_map/ppermute | solution.py:1031
  576.9 231.2 %reduce-scatter.7.cloned.1.call-start = ((), (), s32[]{:S(2)}) async-start(), calls=%async_computation.8 | async-start | bytes 10485760 | tf_op jit(solution)/shard_map/reduce_scatter | solution.py:1160
  577.5 3.7 collective-permute-start.28
  579.1 96.9 %collective-permute-start.31 = (bf16[512,2048]{1,0:T(8,128)(2,1)}, bf16[512,2048]{1,0:T(8,128)(2,1)}, u32[]{:S(2)}, u32[]{:S(2)}) collective-permute-start(bf16[512,2048]{1,0:T(8,128)(2,1)} %narrow.2.refs_10_.refs_0_), channel_id=1, source_target_pairs={{0,1},{1,0},{2,3},{3,2},{4,5},{5,4},{6,7},{7,6},{8,9},{9,8},{10,11... | collective-permute-start | bytes 6291464 | tf_op jit(solution)/shard_map/ppermute | solution.py:1031
  586.6 47.2 %collective-permute-start.32 = (bf16[512,256]{1,0:T(8,128)(2,1)}, bf16[512,256]{1,0:T(8,128)(2,1)S(1)}, u32[]{:S(2)}, u32[]{:S(2)}) collective-permute-start(bf16[512,256]{1,0:T(8,128)(2,1)} %get-tuple-element.132), channel_id=1, source_target_pairs={{0,2},{2,0},{4,6},{6,4},{1,3},{3,1},{5,7},{7,5},{8,10},{10,8},{12,... | collective-permute-start | bytes 786440 | tf_op jit(solution)/shard_map/ppermute | solution.py:1031
  586.6 47.6 %collective-permute-start.33 = (bf16[512,256]{1,0:T(8,128)(2,1)}, bf16[512,256]{1,0:T(8,128)(2,1)S(1)}, u32[]{:S(2)}, u32[]{:S(2)}) collective-permute-start(bf16[512,256]{1,0:T(8,128)(2,1)} %get-tuple-element.133), channel_id=1, source_target_pairs={{0,4},{2,6},{4,0},{6,2},{1,5},{3,7},{5,1},{7,3},{8,12},{10,14},{12... | collective-permute-start | bytes 786440 | tf_op jit(solution)/shard_map/ppermute | solution.py:1031
  586.6 49.1 %collective-permute-start.34 = (bf16[512,256]{1,0:T(8,128)(2,1)}, bf16[512,256]{1,0:T(8,128)(2,1)S(1)}, u32[]{:S(2)}, u32[]{:S(2)}) collective-permute-start(bf16[512,256]{1,0:T(8,128)(2,1)} %get-tuple-element.134), channel_id=1, source_target_pairs={{0,6},{2,4},{4,2},{6,0},{1,7},{3,5},{5,3},{7,1},{8,14},{10,12},{12... | collective-permute-start | bytes 786440 | tf_op jit(solution)/shard_map/ppermute | solution.py:1031
  617.3 11.8 %collective-permute-start.35 = (f32[2,512]{1,0:T(2,128)S(1)}, f32[2,512]{1,0:T(2,128)S(1)}, u32[]{:S(2)}, u32[]{:S(2)}) collective-permute-start(f32[2,512]{1,0:T(2,128)S(1)} %copy-done.25), channel_id=1, source_target_pairs={{0,1},{1,0},{2,3},{3,2},{4,5},{5,4},{6,7},{7,6},{8,9},{9,8},{10,11... | collective-permute-start | bytes 12296 | tf_op jit(solution)/shard_map/ppermute | solution.py:1031
  629.1 258.0 %reduce-scatter.11.cloned.1.call-start = ((), (), s32[]{:S(2)}) async-start(), calls=%async_computation.10 | async-start | bytes 1310720 | tf_op jit(solution)/shard_map/reduce_scatter | solution.py:1178
  633.8 28.8 %collective-permute-start.37 = (bf16[512,256]{1,0:T(8,128)(2,1)}, bf16[512,256]{1,0:T(8,128)(2,1)}, u32[]{:S(2)}, u32[]{:S(2)}) collective-permute-start(bf16[512,256]{1,0:T(8,128)(2,1)} %get-tuple-element.138), channel_id=1, source_target_pairs={{0,2},{2,0},{4,6},{6,4},{1,3},{3,1},{5,7},{7,5},{8,10},{10,8},{12,... | collective-permute-start | bytes 786440 | tf_op jit(solution)/shard_map/ppermute | solution.py:1031
  633.8 28.8 %collective-permute-start.38 = (bf16[512,256]{1,0:T(8,128)(2,1)}, bf16[512,256]{1,0:T(8,128)(2,1)}, u32[]{:S(2)}, u32[]{:S(2)}) collective-permute-start(bf16[512,256]{1,0:T(8,128)(2,1)} %get-tuple-element.139), channel_id=1, source_target_pairs={{0,4},{2,6},{4,0},{6,2},{1,5},{3,7},{5,1},{7,3},{8,12},{10,14},{12... | collective-permute-start | bytes 786440 | tf_op jit(solution)/shard_map/ppermute | solution.py:1031
  634.2 28.4 %collective-permute-start.39 = (bf16[512,256]{1,0:T(8,128)(2,1)}, bf16[512,256]{1,0:T(8,128)(2,1)}, u32[]{:S(2)}, u32[]{:S(2)}) collective-permute-start(bf16[512,256]{1,0:T(8,128)(2,1)} %get-tuple-element.140), channel_id=1, source_target_pairs={{0,6},{2,4},{4,2},{6,0},{1,7},{3,5},{5,3},{7,1},{8,14},{10,12},{12... | collective-permute-start | bytes 786440 | tf_op jit(solution)/shard_map/ppermute | solution.py:1031
  698.1 10.4 %collective-permute-start.41 = (bf16[1024,2048]{1,0:T(8,128)(2,1)}, bf16[1024,2048]{1,0:T(8,128)(2,1)S(1)}, u32[]{:S(2)}, u32[]{:S(2)}) collective-permute-start(bf16[1024,2048]{1,0:T(8,128)(2,1)} %get-tuple-element.145.refs_2_), channel_id=1, source_target_pairs={{0,2},{2,0},{4,6},{6,4},{1,3},{3,1},{5,7},{7,5},{8,10},{10,8},{12,... | collective-permute-start | bytes 12582920 | tf_op jit(solution)/shard_map/ppermute | solution.py:1031
  698.5 19.2 %collective-permute-start.40 = (bf16[1024,1024]{1,0:T(8,128)(2,1)}, bf16[1024,1024]{1,0:T(8,128)(2,1)}, u32[]{:S(2)}, u32[]{:S(2)}) collective-permute-start(bf16[1024,1024]{1,0:T(8,128)(2,1)} %get-tuple-element.141.refs_3_), channel_id=1, source_target_pairs={{0,2},{2,0},{4,6},{6,4},{1,3},{3,1},{5,7},{7,5},{8,10},{10,8},{12,... | collective-permute-start | bytes 6291464 | tf_op jit(solution)/shard_map/ppermute | solution.py:1031
  715.0 52.5 %collective-permute-start.42 = (bf16[512,2048]{1,0:T(8,128)(2,1)}, bf16[512,2048]{1,0:T(8,128)(2,1)S(1)}, u32[]{:S(2)}, u32[]{:S(2)}) collective-permute-start(bf16[512,2048]{1,0:T(8,128)(2,1)} %add.195.refs_2_), channel_id=1, source_target_pairs={{0,4},{2,6},{4,0},{6,2},{1,5},{3,7},{5,1},{7,3},{8,12},{10,14},{12... | collective-permute-start | bytes 6291464 | tf_op jit(solution)/shard_map/ppermute | solution.py:1031
  716.1 74.5 %collective-permute-start.30 = (bf16[512,2048]{1,0:T(8,128)(2,1)S(1)}, bf16[512,2048]{1,0:T(8,128)(2,1)S(1)}, u32[]{:S(2)}, u32[]{:S(2)}) collective-permute-start(bf16[512,2048]{1,0:T(8,128)(2,1)S(1)} %copy-done), channel_id=1, source_target_pairs={{0,1},{1,0},{2,3},{3,2},{4,5},{5,4},{6,7},{7,6},{8,9},{9,8},{10,11... | collective-permute-start | bytes 6291464 | tf_op jit(solution)/shard_map/ppermute | solution.py:1031
  721.3 75.9 %collective-permute-start.44 = (bf16[512,1024]{1,0:T(8,128)(2,1)}, bf16[512,1024]{1,0:T(8,128)(2,1)S(1)}, u32[]{:S(2)}, u32[]{:S(2)}) collective-permute-start(bf16[512,1024]{1,0:T(8,128)(2,1)} %add.196.refs_15_), channel_id=1, source_target_pairs={{0,4},{2,6},{4,0},{6,2},{1,5},{3,7},{5,1},{7,3},{8,12},{10,14},{12... | collective-permute-start | bytes 3145736 | tf_op jit(solution)/shard_map/ppermute | solution.py:1031
  790.5 12.3 %collective-permute-start.43 = (bf16[1024,2048]{1,0:T(8,128)(2,1)}, bf16[1024,2048]{1,0:T(8,128)(2,1)}, u32[]{:S(2)}, u32[]{:S(2)}) collective-permute-start(bf16[1024,2048]{1,0:T(8,128)(2,1)} %get-tuple-element.147.refs_4_), channel_id=1, source_target_pairs={{0,2},{2,0},{4,6},{6,4},{1,3},{3,1},{5,7},{7,5},{8,10},{10,8},{12,... | collective-permute-start | bytes 12582920 | tf_op jit(solution)/shard_map/ppermute | solution.py:1031
  802.1 96.7 %reduce-scatter.9.cloned.1.call-start = ((), (), s32[]{:S(2)}) async-start(), calls=%async_computation.9 | async-start | bytes 3932160 | tf_op jit(solution)/shard_map/reduce_scatter | solution.py:1439
  802.5 58.1 %collective-permute-start.49 = (bf16[512,2048]{1,0:T(8,128)(2,1)S(1)}, bf16[512,2048]{1,0:T(8,128)(2,1)}, u32[]{:S(2)}, u32[]{:S(2)}) collective-permute-start(bf16[512,2048]{1,0:T(8,128)(2,1)S(1)} %copy-done.1), channel_id=1, source_target_pairs={{0,1},{1,0},{2,3},{3,2},{4,5},{5,4},{6,7},{7,6},{8,9},{9,8},{10,11... | collective-permute-start | bytes 6291464 | tf_op jit(solution)/shard_map/ppermute | solution.py:1031
  807.0 43.7 %collective-permute-start.45 = (bf16[512,1024]{1,0:T(8,128)(2,1)}, bf16[512,1024]{1,0:T(8,128)(2,1)S(1)}, u32[]{:S(2)}, u32[]{:S(2)}) collective-permute-start(bf16[512,1024]{1,0:T(8,128)(2,1)} %get-tuple-element.150.refs_4_), channel_id=1, source_target_pairs={{0,4},{2,6},{4,0},{6,2},{1,5},{3,7},{5,1},{7,3},{8,12},{10,14},{12... | collective-permute-start | bytes 3145736 | tf_op jit(solution)/shard_map/ppermute | solution.py:1031
  829.9 20.8 %collective-permute-start.46 = (f32[1,2048]{1,0:T(1,128)S(1)}, f32[1,2048]{1,0:T(1,128)S(1)}, u32[]{:S(2)}, u32[]{:S(2)}) collective-permute-start(f32[1,2048]{1,0:T(1,128)S(1)} %add.141), channel_id=1, source_target_pairs={{0,1},{1,0},{2,3},{3,2},{4,5},{5,4},{6,7},{7,6},{8,9},{9,8},{10,11... | collective-permute-start | bytes 24584 | tf_op jit(solution)/shard_map/ppermute | solution.py:1031
  831.4 61.8 %collective-permute-start.48 = (bf16[512,1024]{1,0:T(8,128)(2,1)}, bf16[512,1024]{1,0:T(8,128)(2,1)}, u32[]{:S(2)}, u32[]{:S(2)}) collective-permute-start(bf16[512,1024]{1,0:T(8,128)(2,1)} %get-tuple-element.153), channel_id=1, source_target_pairs={{0,4},{2,6},{4,0},{6,2},{1,5},{3,7},{5,1},{7,3},{8,12},{10,14},{12... | collective-permute-start | bytes 3145736 | tf_op jit(solution)/shard_map/ppermute | solution.py:1031
  856.1 37.1 %collective-permute-start.47 = (bf16[512,1024]{1,0:T(8,128)(2,1)}, bf16[512,1024]{1,0:T(8,128)(2,1)}, u32[]{:S(2)}, u32[]{:S(2)}) collective-permute-start(bf16[512,1024]{1,0:T(8,128)(2,1)} %add.199.refs_5_.refs_3_), channel_id=1, source_target_pairs={{0,1},{1,0},{2,3},{3,2},{4,5},{5,4},{6,7},{7,6},{8,9},{9,8},{10,11... | collective-permute-start | bytes 3145736 | tf_op jit(solution)/shard_map/ppermute | solution.py:1031
  871.6 5.4 collective-permute-start.51
  877.0 8.8 collective-permute-start.52
  885.8 5.1 collective-permute-start.54
  890.1 26.4 %collective-permute-start.58 = (bf16[128,4096]{1,0:T(8,128)(2,1)}, bf16[128,4096]{1,0:T(8,128)(2,1)}, u32[]{:S(2)}, u32[]{:S(2)}) collective-permute-start(bf16[128,4096]{1,0:T(8,128)(2,1)} %slice.147), channel_id=1, source_target_pairs={{0,4},{2,6},{4,0},{6,2},{1,5},{3,7},{5,1},{7,3},{8,12},{10,14},{12... | collective-permute-start | bytes 3145736 | tf_op jit(solution)/shard_map/ppermute | solution.py:1031
  897.1 23.9 %collective-permute-start.53 = (bf16[512,1024]{1,0:T(8,128)(2,1)}, bf16[512,1024]{1,0:T(8,128)(2,1)S(1)}, u32[]{:S(2)}, u32[]{:S(2)}) collective-permute-start(bf16[512,1024]{1,0:T(8,128)(2,1)} %add.200.refs_5_), channel_id=1, source_target_pairs={{0,1},{1,0},{2,3},{3,2},{4,5},{5,4},{6,7},{7,6},{8,9},{9,8},{10,11... | collective-permute-start | bytes 3145736 | tf_op jit(solution)/shard_map/ppermute | solution.py:1031
  900.1 29.2 %collective-permute-start.55 = (bf16[128,768]{1,0:T(8,128)(2,1)S(1)}, bf16[128,768]{1,0:T(8,128)(2,1)S(1)}, u32[]{:S(2)}, u32[]{:S(2)}) collective-permute-start(bf16[128,768]{1,0:T(8,128)(2,1)S(1)} %get-tuple-element.209), channel_id=1, source_target_pairs={{0,2},{2,0},{4,6},{6,4},{1,3},{3,1},{5,7},{7,5},{8,10},{10,8},{12,... | collective-permute-start | bytes 589832 | tf_op jit(solution)/shard_map/ppermute | solution.py:1031
  900.2 29.1 %collective-permute-start.56 = (bf16[128,768]{1,0:T(8,128)(2,1)S(1)}, bf16[128,768]{1,0:T(8,128)(2,1)S(1)}, u32[]{:S(2)}, u32[]{:S(2)}) collective-permute-start(bf16[128,768]{1,0:T(8,128)(2,1)S(1)} %get-tuple-element.208), channel_id=1, source_target_pairs={{0,4},{2,6},{4,0},{6,2},{1,5},{3,7},{5,1},{7,3},{8,12},{10,14},{12... | collective-permute-start | bytes 589832 | tf_op jit(solution)/shard_map/ppermute | solution.py:1031
  901.3 28.1 %collective-permute-start.57 = (bf16[128,768]{1,0:T(8,128)(2,1)S(1)}, bf16[128,768]{1,0:T(8,128)(2,1)S(1)}, u32[]{:S(2)}, u32[]{:S(2)}) collective-permute-start(bf16[128,768]{1,0:T(8,128)(2,1)S(1)} %get-tuple-element.207), channel_id=1, source_target_pairs={{0,6},{2,4},{4,2},{6,0},{1,7},{3,5},{5,3},{7,1},{8,14},{10,12},{12... | collective-permute-start | bytes 589832 | tf_op jit(solution)/shard_map/ppermute | solution.py:1031
  (62 other events, 408.6 us)
Sparse Core Ops, SparseCore 0:
  25.1 66.3 all-gather.3
  93.6 160.1 all-gather.5
  256.0 131.7 all-gather.7
  577.0 76.6 reduce-scatter.4
  656.0 144.9 reduce-scatter.6
  803.9 27.8 reduce-scatter.10
  834.1 60.6 reduce-scatter.8

commit v5 on v4

--- a/solution.py
+++ b/solution.py
@@ -20,7 +20,7 @@
 KERNEL_RATE = 0.25e9
 BACK_WEIGHT = 25
 PAUSE = 300
-LONG_PAUSE = 200
+LONG_PAUSE = 160
 
 
 def lasting(us):
@@ -310,23 +310,11 @@
 
 
 def heads_grad_kernel(*refs, sequences):
-    grads, lows, out, turned_grads = (
-        refs[:sequences],
-        refs[sequences : 2 * sequences],
-        refs[2 * sequences],
-        refs[2 * sequences + 1],
-    )
-    count = grads[0].shape[0]
-
-    @pl.when(pl.program_id(0) == 0)
-    def _():
-        for s in range(sequences):
-            turned_grads[:, s * count : (s + 1) * count] = grads[s][...].T
-
-    total = dot(turned_grads[:, :count], lows[0][...], 1, 0)
+    grads, lows, out = refs[:sequences], refs[sequences : 2 * sequences], refs[2 * sequences]
+    total = dot(lows[0][...].T, grads[0][...], 1, 0)
     for s in range(1, sequences):
-        total += dot(turned_grads[:, s * count : (s + 1) * count], lows[s][...], 1, 0)
-    out[...] = total.T.astype(BF16)
+        total += dot(lows[s][...].T, grads[s][...], 1, 0)
+    out[...] = total.astype(BF16)
 
 
 def heads_grad(lows, grads, after=()):
@@ -341,7 +329,7 @@
         [(grad, (count, width), None) for grad in grads]
         + [(low, (count, tile), lambda n: (0, n)) for low in lows],
         [((model, width), BF16, (tile, width), lambda n: (n, 0))],
-        [pltpu.VMEM((width, sequences * count), BF16)],
+        [],
         3e-9 * sequences * count * model * width,
         after,
     )[0]
@@ -476,8 +464,8 @@
 
 
 def call(kernel, name, grid, ins, outs, scratch, us, after=(), scalars=None, into=None):
-    if into is not None:
-        after = [into, *after]
+    into = into or []
+    after = [*into, *after]
     extra = len(after)
     first = 0 if scalars is None else 1
     count = first + len(ins)
@@ -501,7 +489,7 @@
             scratch_shapes=scratch,
         ),
         out_shape=[jax.ShapeDtypeStruct(shape, dtype) for shape, dtype, _, _ in outs],
-        input_output_aliases={} if into is None else {count: 0},
+        input_output_aliases={count + n: n for n in range(len(into))},
         compiler_params=params(),
         cost_estimate=lasting(us),
         name=name,
@@ -578,30 +566,38 @@
     branch[...] = dot(low, weight[...], 1, 1).astype(BF16)
 
 
-def out_branch(mixed, own, other, gain, near_full, full, after=()):
+def out_branch(mixed, own, other, gain, near_full, full, parts=1, after=()):
     span, width = mixed.shape
     model = near_full.shape[0]
     place = near_full.shape[1] // width - 1
-    rows = min(256, span)
-    return call(
-        partial(out_kernel, full=full),
-        "out_branch",
-        (span // rows,),
-        [
-            (mixed, (rows, width), lambda n: (n, 0)),
-            (own, (2, rows), lambda n: (0, n)),
-            (other, (2, rows), lambda n: (0, n)),
-            (gain, (1, width), None),
-            (near_full, (model, width), lambda n: (0, place)),
-        ],
-        [
-            ((span, width), BF16, (rows, width), lambda n: (n, 0)),
-            ((span, model), BF16, (rows, model), lambda n: (n, 0)),
-        ],
-        [],
-        6e-9 * span * width * model,
-        after,
-    )
+    rows = span // parts
+    made = [None]
+    branches = []
+    for n in range(parts):
+        made = call(
+            partial(out_kernel, full=full),
+            "out_branch",
+            (1,),
+            [
+                (mixed, (rows, width), lambda _, n=n: (n, 0)),
+                (own, (2, rows), lambda _, n=n: (0, n)),
+                (other, (2, rows), lambda _, n=n: (0, n)),
+                (gain, (1, width), None),
+                (near_full, (model, width), lambda _: (0, place)),
+            ],
+            [
+                ((span, width), BF16, (rows, width), lambda _, n=n: (n, 0)),
+                ((rows, model), BF16, (rows, model), None),
+            ],
+            [],
+            6e-9 * rows * width * model,
+            after,
+            None,
+            made[:1] if n else None,
+        )
+        branches.append(made[1])
+        after = [made[1]]
+    return made[0], branches
 
 
 def row_norm(block):
@@ -643,47 +639,61 @@
         sums[...] = jnp.concatenate([as_row(total[...]), as_row(squares[...])], axis=0)
 
 
-def widen(number, tokens, own, other, gain, weight, units, after=()):
-    span, model = own.shape
+def widen(number, part, parts, tokens, own, other, gain, weight, units, into=None, after=()):
+    rows, model = own.shape
+    span = rows * parts
     tile = 512
-    rows = (span, model)
-    across = (span, tile)
+    block = (rows, model)
+    across = (rows, tile)
+    here = lambda n: (part, 0)
+    tiled = lambda n: (part, n)
     return call(
         widen_kernel,
         "widen",
         (units // tile,),
         [
-            (tokens, rows, lambda n: (number, 0)),
-            (own, rows, None),
-            (other, rows, None),
+            (tokens, block, lambda n: (number * parts + part, 0)),
+            (own, block, None),
+            (other, block, None),
             (gain, (1, model), None),
             (weight, (model, tile), lambda n: (0, n)),
         ],
         [
-            (rows, F32, rows, None),
-            (rows, BF16, rows, None),
-            ((span, units), BF16, across, lambda n: (0, n)),
-            ((span, units), BF16, across, lambda n: (0, n)),
-            ((2, span), F32, (2, span), None),
+            ((span, model), F32, block, here),
+            ((span, model), BF16, block, here),
+            ((span, units), BF16, across, tiled),
+            ((span, units), BF16, across, tiled),
+            ((2, span), F32, (2, rows), lambda n: (0, part)),
         ],
-        [pltpu.VMEM((span, 128), F32)] * 2,
-        5.4e-9 * span * model * units,
-        after,
-    )
-
-
-def narrow_kernel(active, own, other, gain, weight, branch, total, columns, *, full):
+        [pltpu.VMEM((rows, 128), F32)] * 2,
+        5.4e-9 * rows * model * units,
+        after,
+        None,
+        into,
+    )
+
+
+def narrow_kernel(gain, weight, *refs, sequences, full):
+    active, refs = refs[:sequences], refs[sequences:]
+    own, refs = refs[:sequences], refs[sequences:]
+    other, refs = refs[:sequences], refs[sequences:]
+    branch, total, columns, low = refs
     step = pl.program_id(0)
+    span = active[0].shape[0]
 
     @pl.when(step == 0)
     def _():
-        mean, std = moments(own[...], other[...], full)
-        columns[0] = jnp.broadcast_to(as_column(mean), columns.shape[1:])
-        columns[1] = jnp.broadcast_to(as_column(std), columns.shape[1:])
+        for s in range(sequences):
+            mean, std = moments(own[s][...], other[s][...], full)
+            columns[2 * s] = jnp.broadcast_to(as_column(mean), columns.shape[1:])
+            columns[2 * s + 1] = jnp.broadcast_to(as_column(std), columns.shape[1:])
         total[...] = jnp.zeros_like(total)
 
-    low = normed_rows(active[...], columns[0, :, 0:1], columns[1, :, 0:1], gain[...]).astype(BF16)
-    total[...] += dot(low, weight[...], 1, 0)
+    for s in range(sequences):
+        low[s * span : (s + 1) * span, :] = normed_rows(
+            active[s][...], columns[2 * s, :, 0:1], columns[2 * s + 1, :, 0:1], gain[...]
+        ).astype(BF16)
+    total[...] += dot(low[...], weight[...], 1, 0)
 
     @pl.when(step == pl.num_programs(0) - 1)
     def _():
@@ -691,24 +701,29 @@
 
 
 def narrow(active, own, other, gain, weight, full, after=()):
-    span, units = active.shape
+    sequences = len(active)
+    span, units = active[0].shape
     model = weight.shape[1]
     tile = 512
     sums = (2, span)
+    rows = sequences * span
     return call(
-        partial(narrow_kernel, full=full),
+        partial(narrow_kernel, sequences=sequences, full=full),
         "narrow",
         (units // tile,),
         [
-            (active, (span, tile), lambda n: (0, n)),
-            (own, sums, None),
-            (other, sums, None),
             (gain, (1, tile), lambda n: (0, n)),
             (weight, (tile, model), lambda n: (n, 0)),
+        ]
+        + [(array, (span, tile), lambda n: (0, n)) for array in active]
+        + [(array, sums, None) for array in (*own, *other)],
+        [((rows, model), BF16, (rows, model), None)],
+        [
+            pltpu.VMEM((rows, model), F32),
+            pltpu.VMEM((2 * sequences, span, 128), F32),
+            pltpu.VMEM((rows, tile), BF16),
         ],
-        [((span, model), BF16, (span, model), None)],
-        [pltpu.VMEM((span, model), F32), pltpu.VMEM((2, span, 128), F32)],
-        3.7e-9 * span * model * units,
+        3.2e-9 * rows * model * units,
         after,
     )[0]
 
@@ -957,14 +972,18 @@
     )
 
 
-def first_back_kernel(order, grads, low, weight, gain, away, kept, gain_grad, total):
+def first_back_kernel(order, grads, low, weight, gain, *refs):
+    away, (kept, gain_grad, total) = refs[:4], refs[4:]
     step = pl.program_id(0)
     grad = dot(grads[...], weight[...], 1, 1)
     made = grad.astype(BF16)
-
-    @pl.when(step < 2)
-    def _():
-        away[...] = made
+    half = made.shape[1] // 2
+    for n in range(2):
+
+        @pl.when(step == n)
+        def _(n=n):
+            away[2 * n][...] = made[:, :half]
+            away[2 * n + 1][...] = made[:, half:]
 
     @pl.when(step >= 2)
     def _():
@@ -986,7 +1005,8 @@
     model = weight.shape[0]
     span = count // groups
     rows = (span, model)
-    return call(
+    half = (span, model // 2)
+    made = call(
         first_back_kernel,
         "first_back",
         (groups,),
@@ -996,8 +1016,8 @@
             (weight, (model, width), None),
             (gain, (1, model), None),
         ],
-        [
-            ((2 * span, model), BF16, rows, lambda n, p: (jnp.minimum(n, 1), 0)),
+        [(half, BF16, half, None)] * 4
+        + [
             ((2 * span, model), BF16, rows, lambda n, p: (jnp.maximum(n - 2, 0), 0)),
             ((1, model), F32, (1, model), None),
         ],
@@ -1006,6 +1026,7 @@
         after,
         order,
     )
+    return made[:4], made[4], made[5]
 
 
 def relay_kernel(array, out):
@@ -1057,49 +1078,89 @@
     )[0]
 
 
-def add_halves_kernel(first, second, left, right):
-    total = (first[...].astype(F32) + second[...].astype(F32)).astype(BF16)
-    half = total.shape[1] // 2
-    left[...] = total[:, :half]
-    right[...] = total[:, half:]
-
-
-def add_halves(first, second, rows, after=()):
-    width = first.shape[1]
+def add_halves_kernel(whole, left, right, *outs):
+    half = left.shape[1]
+    for n, (part, out) in enumerate(zip((left, right), outs)):
+        total = whole[:, n * half : (n + 1) * half].astype(F32) + part[...].astype(F32)
+        out[...] = total.astype(BF16)
+
+
+def add_halves(whole, left, right, after=()):
+    rows, width = left.shape
     tile = 128
-    block = (tile, width)
-    half = ((rows, width // 2), BF16, (tile, width // 2), lambda n: (n, 0))
+    half = (tile, width)
+    by_row = lambda n: (n, 0)
     return call(
         add_halves_kernel,
         "add_halves",
         (rows // tile,),
-        [(first, block, lambda n: (n, 0)), (second, block, lambda n: (n, 0))],
-        [half, half],
+        [(whole, (tile, 2 * width), by_row), (left, half, by_row), (right, half, by_row)],
+        [((rows, width), BF16, half, by_row)] * 2,
         [],
-        1.5e-6 * rows * width,
-        after,
-    )
-
-
-def result_kernel(own, other, hidden, out):
-    out[...] = (hidden[...] + (own[...].astype(F32) + other[...].astype(F32))).astype(BF16)
-
-
-def result_rows(number, count, own, other, hidden, into, after=()):
-    span, model = hidden.shape
+        3e-6 * rows * width,
+        after,
+    )
+
+
+def join_halves_kernel(whole, *refs):
+    pieces, out = refs[:-1], refs[-1]
+    half = pieces[0].shape[1]
+    for n in range(2):
+        at = slice(n * half, (n + 1) * half)
+        total = whole[:, at].astype(F32)
+        for piece in pieces[n::2]:
+            total += piece[...].astype(F32)
+        out[:, at] = total.astype(BF16)
+
+
+def join_halves(whole, got, far, after=()):
+    rows, width = far[0].shape
+    tile = 128
+    half = (tile, width)
+    below = rows // tile
+    return call(
+        join_halves_kernel,
+        "join_halves",
+        (rows // tile,),
+        [(whole, (tile, 2 * width), lambda n: (n + below, 0))]
+        + [(piece, half, lambda n: (n, 0)) for piece in (*got, *far)],
+        [((rows, 2 * width), BF16, (tile, 2 * width), lambda n: (n, 0))],
+        [],
+        3e-6 * rows * width,
+        after,
+    )[0]
+
+
+def result_kernel(own, other, *refs, tiles):
+    hidden, out = refs[:-1], refs[-1]
+    total = own[...].astype(F32) + other[...].astype(F32)
+    for s, part in enumerate(hidden):
+
+        @pl.when(pl.program_id(0) // tiles == s)
+        def _(part=part):
+            out[...] = (part[...] + total).astype(BF16)
+
+
+def result_rows(own, other, hidden, after=(), us=None):
+    span, model = hidden[0].shape
+    rows = own.shape[0]
     tile = min(128, span)
+    tiles = span // tile
     block = (tile, model)
+    by_row = lambda n: (n, 0)
     return call(
-        result_kernel,
+        partial(result_kernel, tiles=tiles),
         "result",
-        (span // tile,),
-        [(array, block, lambda n: (n, 0)) for array in (own, other, hidden)],
-        [((count, span, model), BF16, (None, *block), lambda n: (number, n, 0))],
+        (rows // tile,),
+        [(own, block, by_row), (other, block, by_row)]
+        + [
+            (array, block, lambda n, s=s: (jnp.clip(n - s * tiles, 0, tiles - 1), 0))
+            for s, array in enumerate(hidden)
+        ],
+        [((rows, model), BF16, block, by_row)],
         [],
-        1.5e-6 * span * model,
-        after,
-        None,
-        into,
+        us or 1.5e-6 * rows * model,
+        after,
     )[0]
 
 
@@ -1142,7 +1203,7 @@
         2e-6 * span * model,
         after,
         None,
-        into,
+        None if into is None else [into],
     )[0]
 
 
@@ -1192,11 +1253,7 @@
 
 
 def axis_sum(array, axis, size):
-    offset = 1
-    while offset < size:
-        array = array + exchange(array, axis, size, offset)
-        offset *= 2
-    return array
+    return sum([exchange(array, axis, size, offset) for offset in range(1, size)], array)
 
 
 def in_order(pieces, place):
@@ -1327,16 +1384,22 @@
         last = [sums]
     last = [other for _, other in att_sums]
     for s in each:
-        low, terms = out_branch(attended[s], *att_sums[s], gain_two, near_full, model, last)
+        parts = 2 if s == sequences - 1 else 1
+        low, terms = out_branch(attended[s], *att_sums[s], gain_two, near_full, model, parts, last)
         inner.append(low)
-        branch.append(mp_sum(terms, units))
-        last = [terms]
+        branch.append([mp_sum(part, units) for part in terms])
+        last = [terms[-1]]
 
     flat_tokens = tokens.reshape(sequences * span, model)
     flat_grads = out_grad.reshape(sequences * span, model)
     hidden, third_low, active, slope, act_sums = [], [], [], [], []
     for s in each:
-        made = widen(s, flat_tokens, *branch[s], gain_three, near_full, ffn_width, last)
+        made = None
+        for n, part in enumerate(branch[s]):
+            made = widen(
+                s, n, len(branch[s]), flat_tokens, *part, gain_three, near_full, ffn_width, made, last
+            )
+            last = [made[4]]
         hidden.append(made[0])
         third_low.append(made[1])
         active.append(made[2])
@@ -1365,19 +1428,14 @@
         third_terms.append(mp_sum(terms, units))
         last = [terms]
 
-    def finish(s, after):
-        terms = narrow(active[s], *act_sums[s], gain_four, down_full, full_units, after)
-        return mp_sum(terms, units)
-
-    def result(s, into, after):
-        return result_rows(s, sequences, *wide_terms[s], hidden[s], into, after)
-
     gain_three_grad, gain_two_grad, gain_one_grad = 0.0, 0.0, 0.0
     order = jnp.bitwise_xor(place, jnp.array([3, 1, 2, 0], jnp.int32))
-    first_sums = []
     grad_hidden, hidden_low, grads, projected_grads = [], [], [], []
-    wide_terms = [finish(0, last)]
-    last = [wide_terms[0][0]]
+    wide_terms = narrow(
+        active, own_sums, other_sums, gain_four, down_full, full_units, last
+    )
+    last = [wide_terms]
+    wide_terms = mp_sum(wide_terms, units)
     for s in each:
         made = middle(
             s, flat_grads, *third_terms[s], hidden[s], gain_three, near_full, attended[s],
@@ -1394,8 +1452,7 @@
             in_sum = ScatterSum(in_parts, groups, Z_FIRST)
             last = [down_sum.chips([in_parts[0], third_terms[1][1]])]
         else:
-            wide_terms.append(finish(s, [made[3]]))
-            last = [in_sum.mates([wide_terms[s][0]])]
+            last = [in_sum.mates([made[3]])]
         parts = share_out(
             spot, made[2], attended[s], *att_sums[s], *mp_rows(made[3], units), model, groups,
             last,
@@ -1414,25 +1471,24 @@
                 spot, hidden_low, inner, devices, groups, None, False, last + grads[1][1:]
             )
             out_sum = ScatterSum(out_parts, groups)
-            results = result(0, None, [out_parts[0], down_sum.out])
-            last = [results]
+            last = [out_sum.mates([out_parts[0], down_sum.out])]
         else:
-            first_terms = mp_sum(first_sums[0].own(last), units)
+            first_terms = mp_sum(join_halves(kept, got[2:], far, last), units)
             last = [first_terms[0]]
         away, kept, gain_part = first_back(
             order, made, first_low[s], heads_weight, gain_one, groups, last
         )
         gain_one_grad += gain_part
+        got = [exchange(piece, "seq", groups, 1) for piece in away]
         if s == 0:
-            first_sums.append(ScatterSum((away, kept), groups))
-            last = [first_sums[0].mates([away])]
-            last = [out_sum.mates(last)]
+            last = [out_sum.chips([kept])]
+            near = add_halves(kept, *got[:2], last)
+            far = [exchange(piece, "seq", groups, 2) for piece in near]
+            last = [near[0]]
         else:
             gain_one_sums = mp_rows(gain_one_grad, units)
-            got = exchange(away, "seq", groups, 1)
-            results = result(1, results, [away])
-            last = [out_sum.chips([results], PAUSE)]
-            near = add_halves(kept, got, span, last)
+            results = result_rows(*wide_terms, hidden, [kept], PAUSE)
+            near = add_halves(kept, *got[:2], [results])
             last = [near[0], in_sum.rows]
 
     heads_part = heads_grad(first_low, projected_grads, last)
@@ -1460,7 +1516,7 @@
         far = exchange(part, "seq", groups, 2)
         column = n * (model // 2)
         own = add(
-            [(kept, span, column), (got, span, column), (far, 0, 0)],
+            [(kept, span, column), (got[2 + n], 0, 0), (far, 0, 0)],
             span,
             last,
             model // 2,
@@ -1468,12 +1524,11 @@
         )
         terms.append(mp_sum(own, units))
         if n == 0:
-            grad_input = input_grad(0, [first_terms], None, [own])
-            gain_rows = relay(gain_rows, [grad_input])
-            gain_rows = gain_rows + exchange(gain_rows, "seq", groups, 1)
+            gain_rows = relay(gain_rows, [own])
+            grad_input = input_grad(0, [first_terms], None, [gain_rows])
             gain_rows = axis_sum(gain_rows, "dp", devices)
             last = [terms[0][1], gain_rows]
-    gain_rows = gain_rows + exchange(gain_rows, "seq", groups, 2)
+    gain_rows = axis_sum(relay(gain_rows, [own]), "seq", groups)
     in_sum.chips()
     pieces = [
         lax.dynamic_slice_in_dim(heads_rows, jnp.bitwise_xor(place, n) * chunk, chunk, 0)
@@ -1487,7 +1542,7 @@
     gain_sums = lax.dynamic_index_in_dim(gain_rows, number, 0, False)
     one, three, two, four = [gain_sums[cuts[n] : cuts[n + 1]] for n in range(4)]
     return (
-        results,
+        results.reshape(sequences, span, model),
         grad_input,
         grad_qkv_w,
         out_sum.out.T,

time: 954 us -> 915 us (0.959)
  waiting for transfers between devices: 241 us -> 181 us
  Pallas kernels: 556 us -> 578 us
  starting transfers between devices: 52.8 us -> 64.9 us
    ppermute x59 -> x69, waiting for transfers between devices: 240 us -> 172 us  [exchange(): return lax.ppermute(array, axis, [(n, n ^ offset) for n in range(size)])]
    pallas_call x41 -> x42, Pallas kernels: 496 us -> 518 us  [call(): pl.pallas_call(run, grid_spec=pltpu.PrefetchScalarGridSpec(num_scalar_pre...]
    ppermute x59 -> x69, starting transfers between devices: 52 us -> 64.2 us  [exchange(): return lax.ppermute(array, axis, [(n, n ^ offset) for n in range(size)])]
    unnamed x126 -> x131, local copies, waits for them, and re-layouts: 31.6 us -> 30.4 us
  transfers between devices with their start and end apart: 66 -> 76, of which waited for: 27 -> 25; matrix products, arithmetic and copies ran while one was open for 5% -> 5% of each run, Pallas kernels for 59% -> 63%
where the time goes in v5:
time: 915 us; the launch traced here: 908 us
  Pallas kernels  578 us (63%)
  waiting for transfers between devices  181 us (20%)
  starting transfers between devices  64.9 us (7%)
  local copies, waits for them, and re-layouts  53.7 us (6%)
  other arithmetic  15.6 us (2%)
  between operations  15.2 us (2%)
    pallas_call x42, Pallas kernels, call(): pl.pallas_call(run, grid_spec=pltpu.PrefetchScalarGridSpec(num_scalar_pre...  518 us
    ppermute x69, waiting for transfers between devices, exchange(): return lax.ppermute(array, axis, [(n, n ^ offset) for n in range(size)])  172 us
    ppermute x69, starting transfers between devices, exchange(): return lax.ppermute(array, axis, [(n, n ^ offset) for n in range(size)])  64.2 us
    pallas_call x3, Pallas kernels, weight_grad(): pl.pallas_call(partial(weight_grad_kernel, sequences=sequences, devices=d...  59.2 us
    unnamed x131, local copies, waits for them, and re-layouts  30.4 us
  transfers between devices with their start and end apart: 76, of which 25 were waited for; matrix products, arithmetic and copies ran while one was open for 5% of the time, Pallas kernels for 63%

profile of v5, /device:TPU:0, one launch (start us, length us, event | category | flops | bytes accessed | tf_op | source)
XLA Modules:
  0.0 908.0 jit_solution(16845893803360114577)
XLA Ops:
  10.2 2.5 collective-permute-start.2
  13.4 5.1 collective-permute-done.2
  18.5 4.9 collective-permute-done.1
  24.6 4.8 slice_bitcast_fusion
  33.9 2.6 collective-permute-start.4
  36.7 6.2 collective-permute-done.4
  43.8 34.1 %collective-permute-done.7.refs_3_ = bf16[512,2048]{1,0:T(8,128)(2,1)S(1)} collective-permute-done((bf16[512,2048]{1,0:T(8,128)(2,1)}, bf16[512,2048]{1,0:T(8,128)(2,1)S(1)}, u32[]{:S(2)}, u32[]{:S(2)}) %collective-permute-start.7) | collective-permute-done | bytes 2097184 | tf_op jit(solution)/shard_map/ppermute | solution.py:1052
  79.1 2.4 pack.1
  98.7 19.0 %project.2 = (bf16[2048,2048]{1,0:T(8,128)(2,1)}, bf16[2048,768]{1,0:T(8,128)(2,1)}) custom-call(s32[1]{0:T(128)} %bitcast.14.refs_0_.place, bf16[512,2048]{1,0:T(8,128)(2,1)} %get-tuple-element.221.refs_1_, bf16[512,2048]{1,0:T(8,128)(2,1)} %collective-permute-done.6.refs_2_, bf16[512,2048]{1,0:T(8,128)(2,1)} %copy-done.1, ...), custom_call_target="tpu_custom_call" | custom-call | flops 4026531840 | tf_op jit(solution)/shard_map/project/pallas_call | solution.py:481
  117.7 24.1 %attend.2 = (bf16[512,256]{1,0:T(8,128)(2,1)}, bf16[512,256]{1,0:T(8,128)(2,1)}, bf16[512,256]{1,0:T(8,128)(2,1)}, bf16[512,256]{1,0:T(8,128)(2,1)}, f32[4,2048]{1,0:T(4,128)}) custom-call(s32[2]{0:T(128)} %pad_add_fusion.refs_0_, bf16[2048,768]{1,0:T(8,128)(2,1)} %get-tuple-element.100.refs_1_), custom_call_target="tpu_custom_call" | custom-call | flops 7784628224 | tf_op jit(solution)/shard_map/attend/pallas_call | solution.py:481
  141.8 20.7 %collective-permute-done.13.refs_0_.refs_3_ = bf16[512,2048]{1,0:T(8,128)(2,1)} collective-permute-done((bf16[512,2048]{1,0:T(8,128)(2,1)}, bf16[512,2048]{1,0:T(8,128)(2,1)}, u32[]{:S(2)}, u32[]{:S(2)}) %collective-permute-start.13) | collective-permute-done | bytes 2097184 | tf_op jit(solution)/shard_map/ppermute | solution.py:1052
  162.5 3.9 relay.3.refs_11_
  167.6 2.5 collective-permute-start.10
  172.5 18.7 %project.3 = (bf16[2048,2048]{1,0:T(8,128)(2,1)}, bf16[2048,768]{1,0:T(8,128)(2,1)}) custom-call(s32[1]{0:T(128)} %bitcast.14.refs_0_.place, bf16[512,2048]{1,0:T(8,128)(2,1)} %get-tuple-element.220.refs_1_, bf16[512,2048]{1,0:T(8,128)(2,1)} %collective-permute-done.12.refs_2_, bf16[512,2048]{1,0:T(8,128)(2,1)} %collective-permute-done.13.refs_0_.refs_3_, ...), custom_call_target="tpu_custom_call" | custom-call | flops 4026531840 | tf_op jit(solution)/shard_map/project/pallas_call | solution.py:481
  191.3 31.6 %attend.3 = (bf16[512,256]{1,0:T(8,128)(2,1)}, bf16[512,256]{1,0:T(8,128)(2,1)}, bf16[512,256]{1,0:T(8,128)(2,1)}, bf16[512,256]{1,0:T(8,128)(2,1)}, f32[4,2048]{1,0:T(4,128)}) custom-call(s32[2]{0:T(128)} %pad_add_fusion.1.refs_0_, bf16[2048,768]{1,0:T(8,128)(2,1)} %get-tuple-element.106.refs_1_), custom_call_target="tpu_custom_call" | custom-call | flops 7784628224 | tf_op jit(solution)/shard_map/attend/pallas_call | solution.py:481
  225.4 12.9 %collective-permute-done.16.refs_7_.refs_3_ = bf16[512,256]{1,0:T(8,128)(2,1)S(1)} collective-permute-done((bf16[512,256]{1,0:T(8,128)(2,1)}, bf16[512,256]{1,0:T(8,128)(2,1)S(1)}, u32[]{:S(2)}, u32[]{:S(2)}) %collective-permute-start.16) | collective-permute-done | bytes 262176 | tf_op jit(solution)/shard_map/ppermute | solution.py:1052
  238.3 10.6 %collective-permute-done.17.refs_8_.refs_4_ = bf16[512,256]{1,0:T(8,128)(2,1)S(1)} collective-permute-done((bf16[512,256]{1,0:T(8,128)(2,1)}, bf16[512,256]{1,0:T(8,128)(2,1)S(1)}, u32[]{:S(2)}, u32[]{:S(2)}) %collective-permute-start.17) | collective-permute-done | bytes 262176 | tf_op jit(solution)/shard_map/ppermute | solution.py:1052
  249.6 2.6 collect.2
  252.2 2.6 collect.3
  260.4 6.6 out_branch.3
  267.6 5.0 out_branch.4
  274.0 4.8 out_branch.5
  279.5 36.3 %collective-permute-done.20.refs_2_ = bf16[512,2048]{1,0:T(8,128)(2,1)S(1)} collective-permute-done((bf16[512,2048]{1,0:T(8,128)(2,1)}, bf16[512,2048]{1,0:T(8,128)(2,1)S(1)}, u32[]{:S(2)}, u32[]{:S(2)}) %collective-permute-start.20) | collective-permute-done | bytes 2097184 | tf_op jit(solution)/shard_map/ppermute | solution.py:1052
  317.1 23.3 %widen.3 = (f32[512,2048]{1,0:T(8,128)}, bf16[512,2048]{1,0:T(8,128)(2,1)}, bf16[512,4096]{1,0:T(8,128)(2,1)}, bf16[512,4096]{1,0:T(8,128)(2,1)}, f32[2,512]{1,0:T(2,128)}) custom-call(bf16[1024,2048]{1,0:T(8,128)(2,1)} %bitcast.67, bf16[512,2048]{1,0:T(8,128)(2,1)} %get-tuple-element.115.refs_5_.refs_1_, bf16[512,2048]{1,0:T(8,128)(2,1)} %copy-done.6, ...), custom_call_target="tpu_custom_call" | custom-call | flops 5798205952 | tf_op jit(solution)/shard_map/widen/pallas_call | solution.py:481
  341.4 15.9 %widen.4 = (f32[512,2048]{1,0:T(8,128)}, bf16[512,2048]{1,0:T(8,128)(2,1)}, bf16[512,4096]{1,0:T(8,128)(2,1)}, bf16[512,4096]{1,0:T(8,128)(2,1)}, f32[2,512]{1,0:T(2,128)}) custom-call(bf16[1024,2048]{1,0:T(8,128)(2,1)} %bitcast.68, bf16[256,2048]{1,0:T(8,128)(2,1)} %get-tuple-element.118.refs_6_.refs_1_, bf16[256,2048]{1,0:T(8,128)(2,1)} %copy-done.15, ...), custom_call_target="tpu_custom_call" | custom-call | flops 2899102976 | tf_op jit(solution)/shard_map/widen/pallas_call | solution.py:481
  359.9 16.3 %widen.5 = (f32[512,2048]{1,0:T(8,128)}, bf16[512,2048]{1,0:T(8,128)(2,1)}, bf16[512,4096]{1,0:T(8,128)(2,1)}, bf16[512,4096]{1,0:T(8,128)(2,1)}, f32[2,512]{1,0:T(2,128)}) custom-call(bf16[1024,2048]{1,0:T(8,128)(2,1)} %bitcast.69, ...), custom_call_target="tpu_custom_call", output_to_operand_aliasing={{0}: (5, {}), {1}: (6, {}), {2}: (7, {}), {3}: (8, {}), {4}... | custom-call | flops 2899102976 | tf_op jit(solution)/shard_map/widen/pallas_call | solution.py:481
  381.1 25.8 %weight_grad.3 = (bf16[1024,4096]{1,0:T(8,128)(2,1)}, bf16[1024,4096]{1,0:T(8,128)(2,1)}) custom-call(s32[1]{0:T(128)} %bitcast.14.refs_0_.place, bf16[1024,2048]{1,0:T(8,128)(2,1)} %bitcast.72, bf16[1024,2048]{1,0:T(8,128)(2,1)} %bitcast.73, bf16[512,4096]{1,0:T(8,128)(2,1)} %get-tuple-element.120.refs_2_.refs_3_.refs_1_, ...), custom_call_target="tpu_custom_call" | custom-call | flops 6227702784 | tf_op jit(solution)/shard_map/weight_grad/pallas_call | solution.py:441
  407.0 27.4 %wide_back.1 = (bf16[512,4096]{1,0:T(8,128)(2,1)}, bf16[512,4096]{1,0:T(8,128)(2,1)}, f32[2,512]{1,0:T(2,128)}, f32[2,512]{1,0:T(2,128)}, f32[1,4096]{1,0:T(1,128)}) custom-call(bf16[1024,2048]{1,0:T(8,128)(2,1)} %bitcast.74, bf16[4096,2048]{1,0:T(8,128)(2,1)} %all-gather.4.cloned.1.call-done.refs_1_, f32[1,4096]{1,0:T(1,128)} %reshape.280.refs_8_.refs_2_.refs_0_, ...), custom_call_target="tpu_custom_call" | custom-call | flops 7516192768 | tf_op jit(solution)/shard_map/wide_back/pallas_call | solution.py:481
  434.4 6.0 add.207.refs_8_
  447.8 19.6 %pre_back.2 = (bf16[512,4096]{1,0:T(8,128)(2,1)}, bf16[512,2048]{1,0:T(8,128)(2,1)}) custom-call(bf16[512,4096]{1,0:T(8,128)(2,1)} %get-tuple-element.133.refs_0_, bf16[512,4096]{1,0:T(8,128)(2,1)} %get-tuple-element.120.refs_2_.refs_3_.refs_1_, bf16[512,4096]{1,0:T(8,128)(2,1)} %get-tuple-element.134.refs_2_, ...), custom_call_target="tpu_custom_call" | custom-call | flops 4939212288 | tf_op jit(solution)/shard_map/pre_back/pallas_call | solution.py:481
  468.2 20.0 %pre_back.3 = (bf16[512,4096]{1,0:T(8,128)(2,1)}, bf16[512,2048]{1,0:T(8,128)(2,1)}) custom-call(bf16[512,4096]{1,0:T(8,128)(2,1)} %get-tuple-element.130.refs_0_, bf16[512,4096]{1,0:T(8,128)(2,1)} %get-tuple-element.127.refs_3_.refs_4_.refs_1_, bf16[512,4096]{1,0:T(8,128)(2,1)} %get-tuple-element.131.refs_2_, ...), custom_call_target="tpu_custom_call" | custom-call | flops 4939212288 | tf_op jit(solution)/shard_map/pre_back/pallas_call | solution.py:481
  489.6 25.5 %narrow.1.refs_10_.refs_0_ = bf16[1024,2048]{1,0:T(8,128)(2,1)} custom-call(f32[1,4096]{1,0:T(1,128)} %reshape.280.refs_8_.refs_2_.refs_0_, bf16[4096,2048]{1,0:T(8,128)(2,1)} %all-gather.4.cloned.1.call-done.refs_1_, bf16[512,4096]{1,0:T(8,128)(2,1)} %get-tuple-element.120.refs_2_.refs_3_.refs_1_, ...), custom_call_target="tpu_custom_call" | custom-call | flops 6871947776 | tf_op jit(solution)/shard_map/narrow/pallas_call | solution.py:481
  516.4 13.0 %middle.2 = (f32[512,2048]{1,0:T(8,128)}, bf16[512,2048]{1,0:T(8,128)(2,1)}, f32[512,1024]{1,0:T(8,128)}, f32[2,512]{1,0:T(2,128)}, f32[1,2048]{1,0:T(1,128)}, /*index=5*/f32[1,1024]{1,0:T(1,128)}) custom-call(bf16[1024,2048]{1,0:T(8,128)(2,1)} %bitcast.75, bf16[512,2048]{1,0:T(8,128)(2,1)} %get-tuple-element.137.refs_8_.refs_1_, ...), custom_call_target="tpu_custom_call" | custom-call | flops 3221225472 | tf_op jit(solution)/shard_map/middle/pallas_call | solution.py:481
  529.4 23.8 %weight_grad.4 = (bf16[1024,4096]{1,0:T(8,128)(2,1)}, bf16[1024,4096]{1,0:T(8,128)(2,1)}) custom-call(s32[1]{0:T(128)} %bitcast.14.refs_0_.place, bf16[512,2048]{1,0:T(8,128)(2,1)} %get-tuple-element.143.refs_0_, bf16[512,2048]{1,0:T(8,128)(2,1)} %get-tuple-element.144.refs_1_, bf16[512,4096]{1,0:T(8,128)(2,1)} %get-tuple-element.145.refs_2_, ...), custom_call_target="tpu_custom_call" | custom-call | flops 6227702784 | tf_op jit(solution)/shard_map/weight_grad/pallas_call | solution.py:441
  553.2 6.0 collective-permute-done.29.refs_4_.refs_2_
  562.6 7.2 add.208.refs_7_
  571.2 2.9 collective-permute-done.31.refs_6_
  574.7 4.1 share_out.2
  580.6 12.6 %middle.3 = (f32[512,2048]{1,0:T(8,128)}, bf16[512,2048]{1,0:T(8,128)(2,1)}, f32[512,1024]{1,0:T(8,128)}, f32[2,512]{1,0:T(2,128)}, f32[1,2048]{1,0:T(1,128)}, /*index=5*/f32[1,1024]{1,0:T(1,128)}) custom-call(bf16[1024,2048]{1,0:T(8,128)(2,1)} %bitcast.76, bf16[512,2048]{1,0:T(8,128)(2,1)} %get-tuple-element.138.refs_8_.refs_1_, ...), custom_call_target="tpu_custom_call" | custom-call | flops 3221225472 | tf_op jit(solution)/shard_map/middle/pallas_call | solution.py:481
  594.0 11.3 %add.209.refs_7_ = bf16[1024,4096]{1,0:T(8,128)(2,1)} custom-call(bf16[1024,4096]{1,0:T(8,128)(2,1)} %get-tuple-element.151.refs_0_, bf16[1024,4096]{1,0:T(8,128)(2,1)} %collective-permute-done.34.refs_1_, f32[2,512]{1,0:T(2,128)} %get-tuple-element.150.refs_2_.refs_5_), custom_call_target="tpu_custom_call" | custom-call | flops 1572864000 | tf_op jit(solution)/shard_map/add/pallas_call | solution.py:481
  606.0 4.1 share_out.3
  612.8 35.1 %attend_back.2.refs_4_.refs_1_.refs_0_ = bf16[2048,768]{1,0:T(8,128)(2,1)} custom-call(s32[2]{0:T(128)} %pad_add_fusion.refs_0_, bf16[2048,768]{1,0:T(8,128)(2,1)} %get-tuple-element.100.refs_1_, bf16[512,256]{1,0:T(8,128)(2,1)} %get-tuple-element.148.refs_10_.refs_2_, bf16[512,256]{1,0:T(8,128)(2,1)} %copy-done.51, bf16[512,256]{1,0:T(8,128)(2,1)} %copy-done.52, ...), custom_call_target="tpu_custom_call" | custom-call | flops 281857228800 | tf_op jit(solution)/shard_map/attend_back/pallas_call | solution.py:481
  647.9 9.5 %weight_grad.5 = (bf16[1024,1024]{1,0:T(8,128)(2,1)}, bf16[1024,1024]{1,0:T(8,128)(2,1)}) custom-call(s32[1]{0:T(128)} %bitcast.14.refs_0_.place, bf16[512,2048]{1,0:T(8,128)(2,1)} %get-tuple-element.160.refs_0_, bf16[512,2048]{1,0:T(8,128)(2,1)} %get-tuple-element.161.refs_1_, bf16[512,1024]{1,0:T(8,128)(2,1)} %get-tuple-element.162.refs_2_, ...), custom_call_target="tpu_custom_call" | custom-call | flops 1556925696 | tf_op jit(solution)/shard_map/weight_grad/pallas_call | solution.py:441
  659.5 3.0 convert_bitcast_fusion.2
  662.6 3.6 add.210.refs_5_
  666.6 17.4 %first_back.2 = (bf16[512,1024]{1,0:T(8,128)(2,1)}, bf16[512,1024]{1,0:T(8,128)(2,1)}, bf16[512,1024]{1,0:T(8,128)(2,1)}, bf16[512,1024]{1,0:T(8,128)(2,1)}, bf1...) custom-call(s32[4]{0:T(128)} %broadcast_xor_fusion.refs_0_, bf16[2048,768]{1,0:T(8,128)(2,1)} %attend_back.2.refs_4_.refs_1_.refs_0_, ...), custom_call_target="tpu_custom_call" | custom-call | flops 3623878656 | tf_op jit(solution)/shard_map/first_back/pallas_call | solution.py:481
  684.6 6.8 collective-permute-done.44.refs_2_
  692.4 3.9 add.211.refs_3_
  697.2 4.2 add_halves.2
  703.5 45.6 %attend_back.3.refs_5_.refs_1_ = bf16[2048,768]{1,0:T(8,128)(2,1)} custom-call(s32[2]{0:T(128)} %pad_add_fusion.1.refs_0_, bf16[2048,768]{1,0:T(8,128)(2,1)} %get-tuple-element.106.refs_1_, bf16[512,256]{1,0:T(8,128)(2,1)} %get-tuple-element.152.refs_15_.refs_2_, bf16[512,256]{1,0:T(8,128)(2,1)} %collective-permute-done.35.refs_5_.refs_3_, ...), custom_call_target="tpu_custom_call" | custom-call | flops 11274289152 | tf_op jit(solution)/shard_map/attend_back/pallas_call | solution.py:481
  750.1 5.0 join_halves.1.refs_5_.refs_3_
  756.0 17.5 %first_back.3 = (bf16[512,1024]{1,0:T(8,128)(2,1)}, bf16[512,1024]{1,0:T(8,128)(2,1)}, bf16[512,1024]{1,0:T(8,128)(2,1)}, bf16[512,1024]{1,0:T(8,128)(2,1)}, bf1...) custom-call(s32[4]{0:T(128)} %broadcast_xor_fusion.refs_0_, bf16[2048,768]{1,0:T(8,128)(2,1)} %attend_back.3.refs_5_.refs_1_, ...), custom_call_target="tpu_custom_call" | custom-call | flops 3623878656 | tf_op jit(solution)/shard_map/first_back/pallas_call | solution.py:481
  774.1 10.2 %result.1.refs_3_ = bf16[1024,2048]{1,0:T(8,128)(2,1)} custom-call(bf16[1024,2048]{1,0:T(8,128)(2,1)} %narrow.1.refs_10_.refs_0_, bf16[1024,2048]{1,0:T(8,128)(2,1)} %collective-permute-done.28.refs_1_, f32[512,2048]{1,0:T(8,128)} %get-tuple-element.139.refs_3_.refs_2_, f32[512,2048]{1,0:T(8,128)} %get-tuple-element.140.refs_3_, ...), custom_call_target="tpu_custom_call" | custom-call | flops 74999996416 | tf_op jit(solution)/shard_map/result/pallas_call | solution.py:481
  786.3 4.2 add_halves.3
  790.9 18.9 %heads_grad.1.refs_3_ = bf16[2048,768]{1,0:T(8,128)(2,1)} custom-call(bf16[2048,768]{1,0:T(8,128)(2,1)} %attend_back.2.refs_4_.refs_1_.refs_0_, bf16[2048,768]{1,0:T(8,128)(2,1)} %attend_back.3.refs_5_.refs_1_, bf16[2048,2048]{1,0:T(8,128)(2,1)} %get-tuple-element.159.refs_2_, bf16[2048,2048]{1,0:T(8,128)(2,1)} %get-tuple-element.170.refs_2_.refs_3_, ...), custom_call_target="tpu_custom_call" | custom-call | flops 4831838208 | tf_op jit(solution)/shard_map/heads_grad/pallas_call | solution.py:481
  811.7 2.5 collective-permute-done.53.refs_4_
  816.8 3.9 add.212.refs_1_.refs_3_
  831.7 7.3 collective-permute-start.58
  839.0 4.0 collective-permute-start.59
  843.0 7.3 input_grad.2.refs_7_
  852.4 3.9 add.213.refs_1_.refs_5_
  860.4 14.2 %collective-permute-done.68 = bf16[128,4096]{1,0:T(8,128)(2,1)S(1)} collective-permute-done((bf16[128,4096]{1,0:T(8,128)(2,1)S(1)}, bf16[128,4096]{1,0:T(8,128)(2,1)S(1)}, u32[]{:S(2)}, u32[]{:S(2)}) %collective-permute-start.68) | collective-permute-done | bytes 1048608 | tf_op jit(solution)/shard_map/ppermute | solution.py:1052
  876.2 8.3 reduce-scatter.9.cloned.1.call-done
  891.0 7.2 input_grad.3
  (366 shorter events, 120.1 us)
Async XLA Ops:
  7.2 91.5 %all-gather.6.cloned.1.call-start = ((), (), s32[]{:S(2)}) async-start(), calls=%async_computation.5 | async-start | bytes 3932160 | tf_op jit(solution)/shard_map/all_gather | solution.py:1339
  10.2 8.3 collective-permute-start.2
  12.7 5.8 collective-permute-start
  13.4 10.1 %collective-permute-start.1 = (bf16[144,768]{1,0:T(8,128)(2,1)S(1)}, bf16[144,768]{1,0:T(8,128)(2,1)S(1)}, u32[]{:S(2)}, u32[]{:S(2)}) collective-permute-start(bf16[144,768]{1,0:T(8,128)(2,1)S(1)} %get-tuple-element.250), channel_id=1, source_target_pairs={{0,4},{2,6},{4,0},{6,2},{1,5},{3,7},{5,1},{7,3},{8,12},{10,14},{12... | collective-permute-start | bytes 663560 | tf_op jit(solution)/shard_map/ppermute | solution.py:1052
  24.6 235.3 %all-gather.8.cloned.1.call-start = ((), (), s32[]{:S(2)}) async-start(), calls=%async_computation.6 | async-start | bytes 22282240 | tf_op jit(solution)/shard_map/all_gather | solution.py:1352
  29.4 48.4 %collective-permute-start.7 = (bf16[512,2048]{1,0:T(8,128)(2,1)}, bf16[512,2048]{1,0:T(8,128)(2,1)S(1)}, u32[]{:S(2)}, u32[]{:S(2)}) collective-permute-start(bf16[512,2048]{1,0:T(8,128)(2,1)} %get-tuple-element.221.refs_1_), channel_id=1, source_target_pairs={{0,4},{2,6},{4,0},{6,2},{1,5},{3,7},{5,1},{7,3},{8,12},{10,14},{12... | collective-permute-start | bytes 6291464 | tf_op jit(solution)/shard_map/ppermute | solution.py:1052
  33.9 9.0 collective-permute-start.4
  36.4 6.5 collective-permute-start.5
  81.6 325.3 %all-gather.4.cloned.1.call-start = ((), (), s32[]{:S(2)}) async-start(), calls=%async_computation.4 | async-start | bytes 17825792 | tf_op jit(solution)/shard_map/all_gather | solution.py:1355
  82.4 577.2 %reduce-scatter.5.cloned.1.call-start = ((), (), s32[]{:S(2)}) async-start(), calls=%async_computation.7 | async-start | bytes 5242880 | tf_op jit(solution)/shard_map/reduce_scatter | solution.py:1239
  82.6 16.1 %collective-permute-start.6 = (bf16[512,2048]{1,0:T(8,128)(2,1)}, bf16[512,2048]{1,0:T(8,128)(2,1)}, u32[]{:S(2)}, u32[]{:S(2)}) collective-permute-start(bf16[512,2048]{1,0:T(8,128)(2,1)} %get-tuple-element.221.refs_1_), channel_id=1, source_target_pairs={{0,2},{2,0},{4,6},{6,4},{1,3},{3,1},{5,7},{7,5},{8,10},{10,8},{12,... | collective-permute-start | bytes 6291464 | tf_op jit(solution)/shard_map/ppermute | solution.py:1052
  83.2 15.5 %collective-permute-start.8 = (bf16[512,2048]{1,0:T(8,128)(2,1)S(1)}, bf16[512,2048]{1,0:T(8,128)(2,1)}, u32[]{:S(2)}, u32[]{:S(2)}) collective-permute-start(bf16[512,2048]{1,0:T(8,128)(2,1)S(1)} %copy-done.2), channel_id=1, source_target_pairs={{0,2},{2,0},{4,6},{6,4},{1,3},{3,1},{5,7},{7,5},{8,10},{10,8},{12,... | collective-permute-start | bytes 6291464 | tf_op jit(solution)/shard_map/ppermute | solution.py:1052
  83.2 79.3 %collective-permute-start.13 = (bf16[512,2048]{1,0:T(8,128)(2,1)}, bf16[512,2048]{1,0:T(8,128)(2,1)}, u32[]{:S(2)}, u32[]{:S(2)}) collective-permute-start(bf16[512,2048]{1,0:T(8,128)(2,1)} %get-tuple-element.220.refs_1_), channel_id=1, source_target_pairs={{0,4},{2,6},{4,0},{6,2},{1,5},{3,7},{5,1},{7,3},{8,12},{10,14},{12... | collective-permute-start | bytes 6291464 | tf_op jit(solution)/shard_map/ppermute | solution.py:1052
  84.9 85.5 %collective-permute-start.12 = (bf16[512,2048]{1,0:T(8,128)(2,1)}, bf16[512,2048]{1,0:T(8,128)(2,1)}, u32[]{:S(2)}, u32[]{:S(2)}) collective-permute-start(bf16[512,2048]{1,0:T(8,128)(2,1)} %get-tuple-element.220.refs_1_), channel_id=1, source_target_pairs={{0,2},{2,0},{4,6},{6,4},{1,3},{3,1},{5,7},{7,5},{8,10},{10,8},{12,... | collective-permute-start | bytes 6291464 | tf_op jit(solution)/shard_map/ppermute | solution.py:1052
  167.6 57.7 %collective-permute-start.10 = (bf16[512,256]{1,0:T(8,128)(2,1)S(1)}, bf16[512,256]{1,0:T(8,128)(2,1)S(1)}, u32[]{:S(2)}, u32[]{:S(2)}) collective-permute-start(bf16[512,256]{1,0:T(8,128)(2,1)S(1)} %copy-done.49), channel_id=1, source_target_pairs={{0,4},{2,6},{4,0},{6,2},{1,5},{3,7},{5,1},{7,3},{8,12},{10,14},{12... | collective-permute-start | bytes 786440 | tf_op jit(solution)/shard_map/ppermute | solution.py:1052
  170.1 55.2 %collective-permute-start.11 = (bf16[512,256]{1,0:T(8,128)(2,1)S(1)}, bf16[512,256]{1,0:T(8,128)(2,1)S(1)}, u32[]{:S(2)}, u32[]{:S(2)}) collective-permute-start(bf16[512,256]{1,0:T(8,128)(2,1)S(1)} %copy-done.50), channel_id=1, source_target_pairs={{0,6},{2,4},{4,2},{6,0},{1,7},{3,5},{5,3},{7,1},{8,14},{10,12},{12... | collective-permute-start | bytes 786440 | tf_op jit(solution)/shard_map/ppermute | solution.py:1052
  170.3 55.1 %collective-permute-start.9 = (bf16[512,256]{1,0:T(8,128)(2,1)S(1)}, bf16[512,256]{1,0:T(8,128)(2,1)S(1)}, u32[]{:S(2)}, u32[]{:S(2)}) collective-permute-start(bf16[512,256]{1,0:T(8,128)(2,1)S(1)} %copy-done.48), channel_id=1, source_target_pairs={{0,2},{2,0},{4,6},{6,4},{1,3},{3,1},{5,7},{7,5},{8,10},{10,8},{12,... | collective-permute-start | bytes 786440 | tf_op jit(solution)/shard_map/ppermute | solution.py:1052
  223.0 15.2 %collective-permute-start.16 = (bf16[512,256]{1,0:T(8,128)(2,1)}, bf16[512,256]{1,0:T(8,128)(2,1)S(1)}, u32[]{:S(2)}, u32[]{:S(2)}) collective-permute-start(bf16[512,256]{1,0:T(8,128)(2,1)} %get-tuple-element.109.refs_8_), channel_id=1, source_target_pairs={{0,4},{2,6},{4,0},{6,2},{1,5},{3,7},{5,1},{7,3},{8,12},{10,14},{12... | collective-permute-start | bytes 786440 | tf_op jit(solution)/shard_map/ppermute | solution.py:1052
  225.3 23.5 %collective-permute-start.17 = (bf16[512,256]{1,0:T(8,128)(2,1)}, bf16[512,256]{1,0:T(8,128)(2,1)S(1)}, u32[]{:S(2)}, u32[]{:S(2)}) collective-permute-start(bf16[512,256]{1,0:T(8,128)(2,1)} %get-tuple-element.110.refs_9_), channel_id=1, source_target_pairs={{0,6},{2,4},{4,2},{6,0},{1,7},{3,5},{5,3},{7,1},{8,14},{10,12},{12... | collective-permute-start | bytes 786440 | tf_op jit(solution)/shard_map/ppermute | solution.py:1052
  267.0 48.8 %collective-permute-start.20 = (bf16[512,2048]{1,0:T(8,128)(2,1)}, bf16[512,2048]{1,0:T(8,128)(2,1)S(1)}, u32[]{:S(2)}, u32[]{:S(2)}) collective-permute-start(bf16[512,2048]{1,0:T(8,128)(2,1)} %get-tuple-element.115.refs_5_.refs_1_), channel_id=1, source_target_pairs={{0,1},{1,0},{2,3},{3,2},{4,5},{5,4},{6,7},{7,6},{8,9},{9,8},{10,11... | collective-permute-start | bytes 6291464 | tf_op jit(solution)/shard_map/ppermute | solution.py:1052
  272.6 67.8 %collective-permute-start.22 = (bf16[256,2048]{1,0:T(8,128)(2,1)}, bf16[256,2048]{1,0:T(8,128)(2,1)S(1)}, u32[]{:S(2)}, u32[]{:S(2)}) collective-permute-start(bf16[256,2048]{1,0:T(8,128)(2,1)} %get-tuple-element.118.refs_6_.refs_1_), channel_id=1, source_target_pairs={{0,1},{1,0},{2,3},{3,2},{4,5},{5,4},{6,7},{7,6},{8,9},{9,8},{10,11... | collective-permute-start | bytes 3145736 | tf_op jit(solution)/shard_map/ppermute | solution.py:1052
  278.9 80.1 %collective-permute-start.21 = (bf16[256,2048]{1,0:T(8,128)(2,1)}, bf16[256,2048]{1,0:T(8,128)(2,1)S(1)}, u32[]{:S(2)}, u32[]{:S(2)}) collective-permute-start(bf16[256,2048]{1,0:T(8,128)(2,1)} %get-tuple-element.119.refs_5_.refs_1_), channel_id=1, source_target_pairs={{0,1},{1,0},{2,3},{3,2},{4,5},{5,4},{6,7},{7,6},{8,9},{9,8},{10,11... | collective-permute-start | bytes 3145736 | tf_op jit(solution)/shard_map/ppermute | solution.py:1052
  406.9 27.5 %collective-permute-start.27 = (bf16[1024,4096]{1,0:T(8,128)(2,1)}, bf16[1024,4096]{1,0:T(8,128)(2,1)}, u32[]{:S(2)}, u32[]{:S(2)}) collective-permute-start(bf16[1024,4096]{1,0:T(8,128)(2,1)} %get-tuple-element.129.refs_9_), channel_id=1, source_target_pairs={{0,2},{2,0},{4,6},{6,4},{1,3},{3,1},{5,7},{7,5},{8,10},{10,8},{12,... | collective-permute-start | bytes 25165832 | tf_op jit(solution)/shard_map/ppermute | solution.py:1052
  440.5 118.8 %collective-permute-start.32 = (bf16[512,4096]{1,0:T(8,128)(2,1)}, bf16[512,4096]{1,0:T(8,128)(2,1)S(1)}, u32[]{:S(2)}, u32[]{:S(2)}) collective-permute-start(bf16[512,4096]{1,0:T(8,128)(2,1)} %add.207.refs_8_), channel_id=1, source_target_pairs={{0,4},{2,6},{4,0},{6,2},{1,5},{3,7},{5,1},{7,3},{8,12},{10,14},{12... | collective-permute-start | bytes 12582920 | tf_op jit(solution)/shard_map/ppermute | solution.py:1052
  467.4 48.9 %collective-permute-start.30 = (bf16[512,2048]{1,0:T(8,128)(2,1)}, bf16[512,2048]{1,0:T(8,128)(2,1)}, u32[]{:S(2)}, u32[]{:S(2)}) collective-permute-start(bf16[512,2048]{1,0:T(8,128)(2,1)} %get-tuple-element.137.refs_8_.refs_1_), channel_id=1, source_target_pairs={{0,1},{1,0},{2,3},{3,2},{4,5},{5,4},{6,7},{7,6},{8,9},{9,8},{10,11... | collective-permute-start | bytes 6291464 | tf_op jit(solution)/shard_map/ppermute | solution.py:1052
  488.2 71.0 %collective-permute-start.29 = (bf16[512,2048]{1,0:T(8,128)(2,1)}, bf16[512,2048]{1,0:T(8,128)(2,1)S(1)}, u32[]{:S(2)}, u32[]{:S(2)}) collective-permute-start(bf16[512,2048]{1,0:T(8,128)(2,1)} %get-tuple-element.138.refs_8_.refs_1_), channel_id=1, source_target_pairs={{0,1},{1,0},{2,3},{3,2},{4,5},{5,4},{6,7},{7,6},{8,9},{9,8},{10,11... | collective-permute-start | bytes 6291464 | tf_op jit(solution)/shard_map/ppermute | solution.py:1052
  553.2 40.8 %collective-permute-start.34 = (bf16[1024,4096]{1,0:T(8,128)(2,1)}, bf16[1024,4096]{1,0:T(8,128)(2,1)}, u32[]{:S(2)}, u32[]{:S(2)}) collective-permute-start(bf16[1024,4096]{1,0:T(8,128)(2,1)} %get-tuple-element.147.refs_3_), channel_id=1, source_target_pairs={{0,2},{2,0},{4,6},{6,4},{1,3},{3,1},{5,7},{7,5},{8,10},{10,8},{12,... | collective-permute-start | bytes 25165832 | tf_op jit(solution)/shard_map/ppermute | solution.py:1052
  569.8 221.0 %reduce-scatter.7.cloned.1.call-start = ((), (), s32[]{:S(2)}) async-start(), calls=%async_computation.8 | async-start | bytes 10485760 | tf_op jit(solution)/shard_map/reduce_scatter | solution.py:1221
  578.8 31.8 %collective-permute-start.38 = (bf16[512,256]{1,0:T(8,128)(2,1)}, bf16[512,256]{1,0:T(8,128)(2,1)S(1)}, u32[]{:S(2)}, u32[]{:S(2)}) collective-permute-start(bf16[512,256]{1,0:T(8,128)(2,1)} %get-tuple-element.156), channel_id=1, source_target_pairs={{0,2},{2,0},{4,6},{6,4},{1,3},{3,1},{5,7},{7,5},{8,10},{10,8},{12,... | collective-permute-start | bytes 786440 | tf_op jit(solution)/shard_map/ppermute | solution.py:1052
  578.8 33.2 %collective-permute-start.39 = (bf16[512,256]{1,0:T(8,128)(2,1)}, bf16[512,256]{1,0:T(8,128)(2,1)S(1)}, u32[]{:S(2)}, u32[]{:S(2)}) collective-permute-start(bf16[512,256]{1,0:T(8,128)(2,1)} %get-tuple-element.157), channel_id=1, source_target_pairs={{0,4},{2,6},{4,0},{6,2},{1,5},{3,7},{5,1},{7,3},{8,12},{10,14},{12... | collective-permute-start | bytes 786440 | tf_op jit(solution)/shard_map/ppermute | solution.py:1052
  579.1 32.8 %collective-permute-start.40 = (bf16[512,256]{1,0:T(8,128)(2,1)}, bf16[512,256]{1,0:T(8,128)(2,1)S(1)}, u32[]{:S(2)}, u32[]{:S(2)}) collective-permute-start(bf16[512,256]{1,0:T(8,128)(2,1)} %get-tuple-element.158), channel_id=1, source_target_pairs={{0,6},{2,4},{4,2},{6,0},{1,7},{3,5},{5,3},{7,1},{8,14},{10,12},{12... | collective-permute-start | bytes 786440 | tf_op jit(solution)/shard_map/ppermute | solution.py:1052
  593.2 12.2 %collective-permute-start.33 = (f32[2,512]{1,0:T(2,128)}, f32[2,512]{1,0:T(2,128)S(1)}, u32[]{:S(2)}, u32[]{:S(2)}) collective-permute-start(f32[2,512]{1,0:T(2,128)} %get-tuple-element.150.refs_2_.refs_5_), channel_id=1, source_target_pairs={{0,1},{1,0},{2,3},{3,2},{4,5},{5,4},{6,7},{7,6},{8,9},{9,8},{10,11... | collective-permute-start | bytes 12296 | tf_op jit(solution)/shard_map/ppermute | solution.py:1052
  605.3 224.2 %reduce-scatter.11.cloned.1.call-start = ((), (), s32[]{:S(2)}) async-start(), calls=%async_computation.10 | async-start | bytes 1310720 | tf_op jit(solution)/shard_map/reduce_scatter | solution.py:1239
  610.1 37.8 %collective-permute-start.35 = (bf16[512,256]{1,0:T(8,128)(2,1)}, bf16[512,256]{1,0:T(8,128)(2,1)}, u32[]{:S(2)}, u32[]{:S(2)}) collective-permute-start(bf16[512,256]{1,0:T(8,128)(2,1)} %get-tuple-element.153), channel_id=1, source_target_pairs={{0,2},{2,0},{4,6},{6,4},{1,3},{3,1},{5,7},{7,5},{8,10},{10,8},{12,... | collective-permute-start | bytes 786440 | tf_op jit(solution)/shard_map/ppermute | solution.py:1052
  610.1 37.8 %collective-permute-start.36 = (bf16[512,256]{1,0:T(8,128)(2,1)}, bf16[512,256]{1,0:T(8,128)(2,1)}, u32[]{:S(2)}, u32[]{:S(2)}) collective-permute-start(bf16[512,256]{1,0:T(8,128)(2,1)} %get-tuple-element.154), channel_id=1, source_target_pairs={{0,4},{2,6},{4,0},{6,2},{1,5},{3,7},{5,1},{7,3},{8,12},{10,14},{12... | collective-permute-start | bytes 786440 | tf_op jit(solution)/shard_map/ppermute | solution.py:1052
  610.6 37.3 %collective-permute-start.37 = (bf16[512,256]{1,0:T(8,128)(2,1)}, bf16[512,256]{1,0:T(8,128)(2,1)}, u32[]{:S(2)}, u32[]{:S(2)}) collective-permute-start(bf16[512,256]{1,0:T(8,128)(2,1)} %get-tuple-element.155), channel_id=1, source_target_pairs={{0,6},{2,4},{4,2},{6,0},{1,7},{3,5},{5,3},{7,1},{8,14},{10,12},{12... | collective-permute-start | bytes 786440 | tf_op jit(solution)/shard_map/ppermute | solution.py:1052
  657.7 116.3 %collective-permute-start.28 = (bf16[1024,2048]{1,0:T(8,128)(2,1)}, bf16[1024,2048]{1,0:T(8,128)(2,1)}, u32[]{:S(2)}, u32[]{:S(2)}) collective-permute-start(bf16[1024,2048]{1,0:T(8,128)(2,1)} %narrow.1.refs_10_.refs_0_), channel_id=1, source_target_pairs={{0,1},{1,0},{2,3},{3,2},{4,5},{5,4},{6,7},{7,6},{8,9},{9,8},{10,11... | collective-permute-start | bytes 12582920 | tf_op jit(solution)/shard_map/ppermute | solution.py:1052
  666.2 25.2 %collective-permute-start.44 = (bf16[512,1024]{1,0:T(8,128)(2,1)}, bf16[512,1024]{1,0:T(8,128)(2,1)S(1)}, u32[]{:S(2)}, u32[]{:S(2)}) collective-permute-start(bf16[512,1024]{1,0:T(8,128)(2,1)} %add.210.refs_5_), channel_id=1, source_target_pairs={{0,4},{2,6},{4,0},{6,2},{1,5},{3,7},{5,1},{7,3},{8,12},{10,14},{12... | collective-permute-start | bytes 3145736 | tf_op jit(solution)/shard_map/ppermute | solution.py:1052
  684.0 12.2 %collective-permute-start.42 = (bf16[512,1024]{1,0:T(8,128)(2,1)}, bf16[512,1024]{1,0:T(8,128)(2,1)S(1)}, u32[]{:S(2)}, u32[]{:S(2)}) collective-permute-start(bf16[512,1024]{1,0:T(8,128)(2,1)} %get-tuple-element.167), channel_id=1, source_target_pairs={{0,2},{2,0},{4,6},{6,4},{1,3},{3,1},{5,7},{7,5},{8,10},{10,8},{12,... | collective-permute-start | bytes 3145736 | tf_op jit(solution)/shard_map/ppermute | solution.py:1052
  684.0 12.2 %collective-permute-start.43 = (bf16[512,1024]{1,0:T(8,128)(2,1)}, bf16[512,1024]{1,0:T(8,128)(2,1)}, u32[]{:S(2)}, u32[]{:S(2)}) collective-permute-start(bf16[512,1024]{1,0:T(8,128)(2,1)} %get-tuple-element.168), channel_id=1, source_target_pairs={{0,2},{2,0},{4,6},{6,4},{1,3},{3,1},{5,7},{7,5},{8,10},{10,8},{12,... | collective-permute-start | bytes 3145736 | tf_op jit(solution)/shard_map/ppermute | solution.py:1052
  684.6 64.5 %collective-permute-start.45 = (bf16[512,1024]{1,0:T(8,128)(2,1)}, bf16[512,1024]{1,0:T(8,128)(2,1)}, u32[]{:S(2)}, u32[]{:S(2)}) collective-permute-start(bf16[512,1024]{1,0:T(8,128)(2,1)} %get-tuple-element.171), channel_id=1, source_target_pairs={{0,2},{2,0},{4,6},{6,4},{1,3},{3,1},{5,7},{7,5},{8,10},{10,8},{12,... | collective-permute-start | bytes 3145736 | tf_op jit(solution)/shard_map/ppermute | solution.py:1052
  691.4 57.7 %collective-permute-start.46 = (bf16[512,1024]{1,0:T(8,128)(2,1)}, bf16[512,1024]{1,0:T(8,128)(2,1)}, u32[]{:S(2)}, u32[]{:S(2)}) collective-permute-start(bf16[512,1024]{1,0:T(8,128)(2,1)} %get-tuple-element.172), channel_id=1, source_target_pairs={{0,2},{2,0},{4,6},{6,4},{1,3},{3,1},{5,7},{7,5},{8,10},{10,8},{12,... | collective-permute-start | bytes 3145736 | tf_op jit(solution)/shard_map/ppermute | solution.py:1052
  701.4 47.7 %collective-permute-start.47 = (bf16[512,1024]{1,0:T(8,128)(2,1)}, bf16[512,1024]{1,0:T(8,128)(2,1)S(1)}, u32[]{:S(2)}, u32[]{:S(2)}) collective-permute-start(bf16[512,1024]{1,0:T(8,128)(2,1)} %get-tuple-element.169.refs_15_), channel_id=1, source_target_pairs={{0,4},{2,6},{4,0},{6,2},{1,5},{3,7},{5,1},{7,3},{8,12},{10,14},{12... | collective-permute-start | bytes 3145736 | tf_op jit(solution)/shard_map/ppermute | solution.py:1052
  701.9 47.2 %collective-permute-start.48 = (bf16[512,1024]{1,0:T(8,128)(2,1)}, bf16[512,1024]{1,0:T(8,128)(2,1)}, u32[]{:S(2)}, u32[]{:S(2)}) collective-permute-start(bf16[512,1024]{1,0:T(8,128)(2,1)} %get-tuple-element.173), channel_id=1, source_target_pairs={{0,4},{2,6},{4,0},{6,2},{1,5},{3,7},{5,1},{7,3},{8,12},{10,14},{12... | collective-permute-start | bytes 3145736 | tf_op jit(solution)/shard_map/ppermute | solution.py:1052
  703.4 181.1 %reduce-scatter.9.cloned.1.call-start = ((), (), s32[]{:S(2)}) async-start(), calls=%async_computation.9 | async-start | bytes 3932160 | tf_op jit(solution)/shard_map/reduce_scatter | solution.py:1495
  755.0 76.6 %collective-permute-start.61 = (bf16[512,2048]{1,0:T(8,128)(2,1)}, bf16[512,2048]{1,0:T(8,128)(2,1)}, u32[]{:S(2)}, u32[]{:S(2)}) collective-permute-start(bf16[512,2048]{1,0:T(8,128)(2,1)} %join_halves.1.refs_5_.refs_3_), channel_id=1, source_target_pairs={{0,1},{1,0},{2,3},{3,2},{4,5},{5,4},{6,7},{7,6},{8,9},{9,8},{10,11... | collective-permute-start | bytes 6291464 | tf_op jit(solution)/shard_map/ppermute | solution.py:1052
  773.5 10.8 %collective-permute-start.50 = (bf16[512,1024]{1,0:T(8,128)(2,1)}, bf16[512,1024]{1,0:T(8,128)(2,1)S(1)}, u32[]{:S(2)}, u32[]{:S(2)}) collective-permute-start(bf16[512,1024]{1,0:T(8,128)(2,1)} %get-tuple-element.177), channel_id=1, source_target_pairs={{0,2},{2,0},{4,6},{6,4},{1,3},{3,1},{5,7},{7,5},{8,10},{10,8},{12,... | collective-permute-start | bytes 3145736 | tf_op jit(solution)/shard_map/ppermute | solution.py:1052
  773.5 10.8 %collective-permute-start.51 = (bf16[512,1024]{1,0:T(8,128)(2,1)}, bf16[512,1024]{1,0:T(8,128)(2,1)S(1)}, u32[]{:S(2)}, u32[]{:S(2)}) collective-permute-start(bf16[512,1024]{1,0:T(8,128)(2,1)} %get-tuple-element.178), channel_id=1, source_target_pairs={{0,2},{2,0},{4,6},{6,4},{1,3},{3,1},{5,7},{7,5},{8,10},{10,8},{12,... | collective-permute-start | bytes 3145736 | tf_op jit(solution)/shard_map/ppermute | solution.py:1052
  774.0 41.8 %collective-permute-start.49 = (bf16[512,1024]{1,0:T(8,128)(2,1)}, bf16[512,1024]{1,0:T(8,128)(2,1)S(1)}, u32[]{:S(2)}, u32[]{:S(2)}) collective-permute-start(bf16[512,1024]{1,0:T(8,128)(2,1)} %get-tuple-element.176), channel_id=1, source_target_pairs={{0,2},{2,0},{4,6},{6,4},{1,3},{3,1},{5,7},{7,5},{8,10},{10,8},{12,... | collective-permute-start | bytes 3145736 | tf_op jit(solution)/shard_map/ppermute | solution.py:1052
  790.4 25.9 %collective-permute-start.52 = (bf16[512,1024]{1,0:T(8,128)(2,1)}, bf16[512,1024]{1,0:T(8,128)(2,1)}, u32[]{:S(2)}, u32[]{:S(2)}) collective-permute-start(bf16[512,1024]{1,0:T(8,128)(2,1)} %get-tuple-element.179.refs_4_), channel_id=1, source_target_pairs={{0,4},{2,6},{4,0},{6,2},{1,5},{3,7},{5,1},{7,3},{8,12},{10,14},{12... | collective-permute-start | bytes 3145736 | tf_op jit(solution)/shard_map/ppermute | solution.py:1052
  811.7 40.7 %collective-permute-start.55 = (bf16[512,1024]{1,0:T(8,128)(2,1)}, bf16[512,1024]{1,0:T(8,128)(2,1)}, u32[]{:S(2)}, u32[]{:S(2)}) collective-permute-start(bf16[512,1024]{1,0:T(8,128)(2,1)} %get-tuple-element.182), channel_id=1, source_target_pairs={{0,2},{2,0},{4,6},{6,4},{1,3},{3,1},{5,7},{7,5},{8,10},{10,8},{12,... | collective-permute-start | bytes 3145736 | tf_op jit(solution)/shard_map/ppermute | solution.py:1052
  814.2 38.2 %collective-permute-start.56 = (bf16[512,1024]{1,0:T(8,128)(2,1)}, bf16[512,1024]{1,0:T(8,128)(2,1)}, u32[]{:S(2)}, u32[]{:S(2)}) collective-permute-start(bf16[512,1024]{1,0:T(8,128)(2,1)} %get-tuple-element.183), channel_id=1, source_target_pairs={{0,4},{2,6},{4,0},{6,2},{1,5},{3,7},{5,1},{7,3},{8,12},{10,14},{12... | collective-permute-start | bytes 3145736 | tf_op jit(solution)/shard_map/ppermute | solution.py:1052
  820.7 31.7 %collective-permute-start.54 = (bf16[512,1024]{1,0:T(8,128)(2,1)}, bf16[512,1024]{1,0:T(8,128)(2,1)}, u32[]{:S(2)}, u32[]{:S(2)}) collective-permute-start(bf16[512,1024]{1,0:T(8,128)(2,1)} %add.212.refs_1_.refs_3_), channel_id=1, source_target_pairs={{0,1},{1,0},{2,3},{3,2},{4,5},{5,4},{6,7},{7,6},{8,9},{9,8},{10,11... | collective-permute-start | bytes 3145736 | tf_op jit(solution)/shard_map/ppermute | solution.py:1052
  828.6 10.3 %collective-permute-start.57 = (f32[16,576]{1,0:T(8,128)}, f32[16,576]{1,0:T(8,128)S(1)}, u32[]{:S(2)}, u32[]{:S(2)}) collective-permute-start(f32[16,576]{1,0:T(8,128)} %relay.4.refs_5_), channel_id=1, source_target_pairs={{0,8},{8,0},{16,24},{24,16},{1,9},{9,1},{17,25},{25,17},{2,10},{10... | collective-permute-start | bytes 110600 | tf_op jit(solution)/shard_map/ppermute | solution.py:1052
  831.7 18.7 %collective-permute-start.58 = (f32[16,576]{1,0:T(8,128)S(1)}, f32[16,576]{1,0:T(8,128)S(1)}, u32[]{:S(2)}, u32[]{:S(2)}) collective-permute-start(f32[16,576]{1,0:T(8,128)S(1)} %copy-done.16), channel_id=1, source_target_pairs={{0,16},{8,24},{16,0},{24,8},{1,17},{9,25},{17,1},{25,9},{2,18},{10... | collective-permute-start | bytes 110600 | tf_op jit(solution)/shard_map/ppermute | solution.py:1052
  839.0 12.8 %collective-permute-start.59 = (f32[16,576]{1,0:T(8,128)S(1)}, f32[16,576]{1,0:T(8,128)S(1)}, u32[]{:S(2)}, u32[]{:S(2)}) collective-permute-start(f32[16,576]{1,0:T(8,128)S(1)} %copy-done.16), channel_id=1, source_target_pairs={{0,24},{8,16},{16,8},{24,0},{1,25},{9,17},{17,9},{25,1},{2,26},{10... | collective-permute-start | bytes 110600 | tf_op jit(solution)/shard_map/ppermute | solution.py:1052
  850.4 24.3 %collective-permute-start.68 = (bf16[128,4096]{1,0:T(8,128)(2,1)S(1)}, bf16[128,4096]{1,0:T(8,128)(2,1)S(1)}, u32[]{:S(2)}, u32[]{:S(2)}) collective-permute-start(bf16[128,4096]{1,0:T(8,128)(2,1)S(1)} %slice.147), channel_id=1, source_target_pairs={{0,4},{2,6},{4,0},{6,2},{1,5},{3,7},{5,1},{7,3},{8,12},{10,14},{12... | collective-permute-start | bytes 3145736 | tf_op jit(solution)/shard_map/ppermute | solution.py:1052
  857.7 28.2 %collective-permute-start.62 = (f32[16,576]{1,0:T(8,128)}, f32[16,576]{1,0:T(8,128)S(1)}, u32[]{:S(2)}, u32[]{:S(2)}) collective-permute-start(f32[16,576]{1,0:T(8,128)} %relay.5), channel_id=1, source_target_pairs={{0,2},{2,0},{4,6},{6,4},{1,3},{3,1},{5,7},{7,5},{8,10},{10,8},{12,... | collective-permute-start | bytes 110600 | tf_op jit(solution)/shard_map/ppermute | solution.py:1052
  857.7 29.7 %collective-permute-start.63 = (f32[16,576]{1,0:T(8,128)}, f32[16,576]{1,0:T(8,128)S(1)}, u32[]{:S(2)}, u32[]{:S(2)}) collective-permute-start(f32[16,576]{1,0:T(8,128)} %relay.5), channel_id=1, source_target_pairs={{0,4},{2,6},{4,0},{6,2},{1,5},{3,7},{5,1},{7,3},{8,12},{10,14},{12... | collective-permute-start | bytes 110600 | tf_op jit(solution)/shard_map/ppermute | solution.py:1052
  858.3 29.4 %collective-permute-start.64 = (f32[16,576]{1,0:T(8,128)}, f32[16,576]{1,0:T(8,128)S(1)}, u32[]{:S(2)}, u32[]{:S(2)}) collective-permute-start(f32[16,576]{1,0:T(8,128)} %relay.5), channel_id=1, source_target_pairs={{0,6},{2,4},{4,2},{6,0},{1,7},{3,5},{5,3},{7,1},{8,14},{10,12},{12... | collective-permute-start | bytes 110600 | tf_op jit(solution)/shard_map/ppermute | solution.py:1052
  859.6 30.5 %collective-permute-start.60 = (bf16[512,1024]{1,0:T(8,128)(2,1)}, bf16[512,1024]{1,0:T(8,128)(2,1)S(1)}, u32[]{:S(2)}, u32[]{:S(2)}) collective-permute-start(bf16[512,1024]{1,0:T(8,128)(2,1)} %add.213.refs_1_.refs_5_), channel_id=1, source_target_pairs={{0,1},{1,0},{2,3},{3,2},{4,5},{5,4},{6,7},{7,6},{8,9},{9,8},{10,11... | collective-permute-start | bytes 3145736 | tf_op jit(solution)/shard_map/ppermute | solution.py:1052
  885.8 12.5 %collective-permute-start.65 = (bf16[128,768]{1,0:T(8,128)(2,1)S(1)}, bf16[128,768]{1,0:T(8,128)(2,1)S(1)}, u32[]{:S(2)}, u32[]{:S(2)}) collective-permute-start(bf16[128,768]{1,0:T(8,128)(2,1)S(1)} %get-tuple-element.239), channel_id=1, source_target_pairs={{0,2},{2,0},{4,6},{6,4},{1,3},{3,1},{5,7},{7,5},{8,10},{10,8},{12,... | collective-permute-start | bytes 589832 | tf_op jit(solution)/shard_map/ppermute | solution.py:1052
  885.9 12.4 %collective-permute-start.66 = (bf16[128,768]{1,0:T(8,128)(2,1)S(1)}, bf16[128,768]{1,0:T(8,128)(2,1)S(1)}, u32[]{:S(2)}, u32[]{:S(2)}) collective-permute-start(bf16[128,768]{1,0:T(8,128)(2,1)S(1)} %get-tuple-element.238), channel_id=1, source_target_pairs={{0,4},{2,6},{4,0},{6,2},{1,5},{3,7},{5,1},{7,3},{8,12},{10,14},{12... | collective-permute-start | bytes 589832 | tf_op jit(solution)/shard_map/ppermute | solution.py:1052
  887.4 10.8 %collective-permute-start.67 = (bf16[128,768]{1,0:T(8,128)(2,1)S(1)}, bf16[128,768]{1,0:T(8,128)(2,1)S(1)}, u32[]{:S(2)}, u32[]{:S(2)}) collective-permute-start(bf16[128,768]{1,0:T(8,128)(2,1)S(1)} %get-tuple-element.237), channel_id=1, source_target_pairs={{0,6},{2,4},{4,2},{6,0},{1,7},{3,5},{5,3},{7,1},{8,14},{10,12},{12... | collective-permute-start | bytes 589832 | tf_op jit(solution)/shard_map/ppermute | solution.py:1052
  (74 other events, 368.2 us)
Sparse Core Ops, SparseCore 0:
  24.7 67.1 all-gather.5
  94.1 159.8 all-gather.7
  256.1 131.8 all-gather.3
  570.0 73.2 reduce-scatter.4
  645.6 144.9 reduce-scatter.6
  792.8 27.8 reduce-scatter.10
  823.0 61.4 reduce-scatter.8

commit v6 on v5

--- a/solution.py
+++ b/solution.py
@@ -15,11 +15,11 @@
 LOG2_E = 1.4426950408889634
 SCORE_SCALE = 0.125
 VMEM = 56 * 2**20
-Z_FIRST = True
 BF16 = jnp.bfloat16
 KERNEL_RATE = 0.25e9
 BACK_WEIGHT = 25
 PAUSE = 300
+MIDDLE_PAUSE = 450
 LONG_PAUSE = 160
 
 
@@ -938,7 +938,9 @@
         out[...] = (std * (scaled[:, pl.ds(at, share)] - first - normal * second)).astype(BF16)
 
 
-def share_out(place, scaled, mixed, own, other, own_back, other_back, full, groups, after=()):
+def share_out(
+    place, scaled, mixed, own, other, own_back, other_back, full, groups, after=(), us=None
+):
     span, width = scaled.shape
     share = width // groups
     if share % 128:
@@ -966,7 +968,7 @@
         ],
         [((span, share), BF16, (span, share), None)] * groups,
         [],
-        7.6e-6 * span * width,
+        us or 7.6e-6 * span * width,
         after,
         place,
     )
@@ -1236,7 +1238,8 @@
             self.out = self.rows[half:].astype(F32) + far.astype(F32)
             return self.out
         own = self.own(after, us)
-        self.out = lax.psum_scatter(own, "dp", scatter_dimension=0, tiled=True).astype(F32)
+        self.raw = lax.psum_scatter(own, "dp", scatter_dimension=0, tiled=True)
+        self.out = self.raw.astype(F32)
         return own
 
 
@@ -1336,6 +1339,7 @@
     ]
     pieces = in_order(pass_round(pieces, groups), place)
     rows = jnp.concatenate([piece[:chunk] for piece in pieces], axis=0)
+    rows = relay(rows, [blocks[s][0] for s in each])
     heads_weight = lax.all_gather(rows, "dp", axis=0, tiled=True)
 
     flat = jnp.stack([piece[chunk:].reshape(-1)[: cuts[4]] for piece in pieces]).reshape(1, -1)
@@ -1409,8 +1413,8 @@
 
     own_sums, other_sums = [a for a, _ in act_sums], [b for _, b in act_sums]
     norm = (own_sums, other_sums, gain_four, full_units)
-    down_parts = weight_grad(spot, [flat_grads], active, devices, groups, norm, False, last)
-    down_sum = ScatterSum(down_parts, groups)
+    down_parts = weight_grad(spot, [flat_grads], active, devices, groups, norm, True, last)
+    down_sum = ScatterSum(down_parts, groups, True)
     last = [down_parts[0]]
     pre_low, third_terms = [], []
     scaled, back_sums, gain_four_grad = wide_back(
@@ -1447,18 +1451,22 @@
         gain_two_grad += made[5]
         if s == 0:
             in_parts = weight_grad(
-                spot, third_low, pre_low, devices, groups, None, Z_FIRST, [made[3]]
+                spot, third_low, pre_low, devices, groups, None, False, [made[3]]
             )
-            in_sum = ScatterSum(in_parts, groups, Z_FIRST)
-            last = [down_sum.chips([in_parts[0], third_terms[1][1]])]
+            in_sum = ScatterSum(in_parts, groups)
+            last = [in_parts[0], third_terms[1][1]]
         else:
             last = [in_sum.mates([made[3]])]
         parts = share_out(
             spot, made[2], attended[s], *att_sums[s], *mp_rows(made[3], units), model, groups,
-            last,
+            last, MIDDLE_PAUSE if s == 0 else None,
         )
         last = [parts[0]]
         grads.append(pass_round(parts, groups))
+    last += [down_sum.rows]
+    out_parts = weight_grad(spot, hidden_low, inner, devices, groups, None, True, last)
+    out_sum = ScatterSum(out_parts, groups, True)
+    last = [out_parts[0], *grads[1][1:]]
     for s in each:
         made = attend_back(
             metas[s], projected[s], grads[s], mixed[s], logs[s], tables, last,
@@ -1467,11 +1475,7 @@
         projected_grads.append(made)
         last = [made]
         if s == 0:
-            out_parts = weight_grad(
-                spot, hidden_low, inner, devices, groups, None, False, last + grads[1][1:]
-            )
-            out_sum = ScatterSum(out_parts, groups)
-            last = [out_sum.mates([out_parts[0], down_sum.out])]
+            last = [out_sum.mates(last)]
         else:
             first_terms = mp_sum(join_halves(kept, got[2:], far, last), units)
             last = [first_terms[0]]
@@ -1481,15 +1485,14 @@
         gain_one_grad += gain_part
         got = [exchange(piece, "seq", groups, 1) for piece in away]
         if s == 0:
-            last = [out_sum.chips([kept])]
-            near = add_halves(kept, *got[:2], last)
+            near = add_halves(kept, *got[:2], [kept])
             far = [exchange(piece, "seq", groups, 2) for piece in near]
-            last = [near[0]]
+            last = [in_sum.chips([near[0]])]
         else:
             gain_one_sums = mp_rows(gain_one_grad, units)
             results = result_rows(*wide_terms, hidden, [kept], PAUSE)
             near = add_halves(kept, *got[:2], [results])
-            last = [near[0], in_sum.rows]
+            last = [near[0], in_sum.raw, out_sum.rows]
 
     heads_part = heads_grad(first_low, projected_grads, last)
     heads_rows = lax.psum_scatter(heads_part, "dp", scatter_dimension=0, tiled=True)
@@ -1527,9 +1530,10 @@
             gain_rows = relay(gain_rows, [own])
             grad_input = input_grad(0, [first_terms], None, [gain_rows])
             gain_rows = axis_sum(gain_rows, "dp", devices)
-            last = [terms[0][1], gain_rows]
+            last = [terms[0][1], gain_rows, grad_input]
     gain_rows = axis_sum(relay(gain_rows, [own]), "seq", groups)
-    in_sum.chips()
+    down_sum.chips()
+    out_sum.chips()
     pieces = [
         lax.dynamic_slice_in_dim(heads_rows, jnp.bitwise_xor(place, n) * chunk, chunk, 0)
         for n in range(groups)

time: 915 us -> 909 us (level)
  Pallas kernels: 578 us -> 597 us
  waiting for transfers between devices: 181 us -> 162 us
    pallas_call x42, Pallas kernels: 518 us -> 538 us  [call(): pl.pallas_call(run, grid_spec=pltpu.PrefetchScalarGridSpec(num_scalar_pre...]
    ppermute x69, waiting for transfers between devices: 172 us -> 161 us  [exchange(): return lax.ppermute(array, axis, [(n, n ^ offset) for n in range(size)])]
  transfers between devices with their start and end apart: 76 -> 76, of which waited for: 25 -> 25; matrix products, arithmetic and copies ran while one was open for 5% -> 5% of each run, Pallas kernels for 63% -> 65%
where the time goes in v6:
time: 909 us; the launch traced here: 903 us
  Pallas kernels  597 us (66%)
  waiting for transfers between devices  162 us (18%)
  starting transfers between devices  59.8 us (7%)
  local copies, waits for them, and re-layouts  53.7 us (6%)
  other arithmetic  15.3 us (2%)
  between operations  15.2 us (2%)
    pallas_call x42, Pallas kernels, call(): pl.pallas_call(run, grid_spec=pltpu.PrefetchScalarGridSpec(num_scalar_pre...  538 us
    ppermute x69, waiting for transfers between devices, exchange(): return lax.ppermute(array, axis, [(n, n ^ offset) for n in range(size)])  161 us
    pallas_call x3, Pallas kernels, weight_grad(): pl.pallas_call(partial(weight_grad_kernel, sequences=sequences, devices=d...  59.6 us
    ppermute x69, starting transfers between devices, exchange(): return lax.ppermute(array, axis, [(n, n ^ offset) for n in range(size)])  59.3 us
    unnamed x131, local copies, waits for them, and re-layouts  30.4 us
  transfers between devices with their start and end apart: 76, of which 25 were waited for; matrix products, arithmetic and copies ran while one was open for 5% of the time, Pallas kernels for 65%

profile of v6, /device:TPU:0, one launch (start us, length us, event | category | flops | bytes accessed | tf_op | source)
XLA Modules:
  0.0 902.8 jit_solution(62834882556210762)
XLA Ops:
  12.7 2.6 collective-permute-start.1
  15.3 4.8 slice_bitcast_fusion
  21.5 4.2 collective-permute-done.2
  26.9 3.4 relay.4
  32.5 2.6 collective-permute-start.4
  37.8 3.1 collective-permute-done.5
  41.7 36.5 %collective-permute-done.7.refs_3_ = bf16[512,2048]{1,0:T(8,128)(2,1)} collective-permute-done((bf16[512,2048]{1,0:T(8,128)(2,1)S(1)}, bf16[512,2048]{1,0:T(8,128)(2,1)}, u32[]{:S(2)}, u32[]{:S(2)}) %collective-permute-start.7) | collective-permute-done | bytes 2097184 | tf_op jit(solution)/shard_map/ppermute | solution.py:1054
  78.2 2.4 pack.1
  84.0 2.4 power_multiply_fusion.1
  97.5 18.3 %project.2 = (bf16[2048,2048]{1,0:T(8,128)(2,1)}, bf16[2048,768]{1,0:T(8,128)(2,1)}) custom-call(s32[1]{0:T(128)} %bitcast.14.refs_0_.place, bf16[512,2048]{1,0:T(8,128)(2,1)} %get-tuple-element.221.refs_1_, bf16[512,2048]{1,0:T(8,128)(2,1)} %collective-permute-done.6.refs_2_, bf16[512,2048]{1,0:T(8,128)(2,1)} %collective-permute-done.7.refs_3_, ...), custom_call_target="tpu_custom_call" | custom-call | flops 4026531840 | tf_op jit(solution)/shard_map/project/pallas_call | solution.py:481
  115.8 31.1 %attend.2 = (bf16[512,256]{1,0:T(8,128)(2,1)}, bf16[512,256]{1,0:T(8,128)(2,1)}, bf16[512,256]{1,0:T(8,128)(2,1)}, bf16[512,256]{1,0:T(8,128)(2,1)}, f32[4,2048]{1,0:T(4,128)}) custom-call(s32[2]{0:T(128)} %pad_add_fusion.refs_0_, bf16[2048,768]{1,0:T(8,128)(2,1)} %get-tuple-element.100.refs_1_), custom_call_target="tpu_custom_call" | custom-call | flops 7784628224 | tf_op jit(solution)/shard_map/attend/pallas_call | solution.py:481
  147.0 9.5 %collective-permute-done.13.refs_0_.refs_3_ = bf16[512,2048]{1,0:T(8,128)(2,1)} collective-permute-done((bf16[512,2048]{1,0:T(8,128)(2,1)S(1)}, bf16[512,2048]{1,0:T(8,128)(2,1)}, u32[]{:S(2)}, u32[]{:S(2)}) %collective-permute-start.13) | collective-permute-done | bytes 2097184 | tf_op jit(solution)/shard_map/ppermute | solution.py:1054
  156.4 4.0 relay.5.refs_11_
  162.2 2.5 collective-permute-start.10
  166.1 18.6 %project.3 = (bf16[2048,2048]{1,0:T(8,128)(2,1)}, bf16[2048,768]{1,0:T(8,128)(2,1)}) custom-call(s32[1]{0:T(128)} %bitcast.14.refs_0_.place, bf16[512,2048]{1,0:T(8,128)(2,1)} %get-tuple-element.220.refs_2_.refs_1_, bf16[512,2048]{1,0:T(8,128)(2,1)} %collective-permute-done.12.refs_2_, bf16[512,2048]{1,0:T(8,128)(2,1)} %collective-permute-done.13.refs_0_.refs_3_, ...), custom_call_target="tpu_custom_call" | custom-call | flops 4026531840 | tf_op jit(solution)/shard_map/project/pallas_call | solution.py:481
  184.7 31.7 %attend.3 = (bf16[512,256]{1,0:T(8,128)(2,1)}, bf16[512,256]{1,0:T(8,128)(2,1)}, bf16[512,256]{1,0:T(8,128)(2,1)}, bf16[512,256]{1,0:T(8,128)(2,1)}, f32[4,2048]{1,0:T(4,128)}) custom-call(s32[2]{0:T(128)} %pad_add_fusion.1.refs_0_, bf16[2048,768]{1,0:T(8,128)(2,1)} %get-tuple-element.106.refs_1_), custom_call_target="tpu_custom_call" | custom-call | flops 7784628224 | tf_op jit(solution)/shard_map/attend/pallas_call | solution.py:481
  216.6 3.2 collective-permute-start.16
  220.0 12.8 %collective-permute-done.16.refs_7_.refs_3_ = bf16[512,256]{1,0:T(8,128)(2,1)S(1)} collective-permute-done((bf16[512,256]{1,0:T(8,128)(2,1)}, bf16[512,256]{1,0:T(8,128)(2,1)S(1)}, u32[]{:S(2)}, u32[]{:S(2)}) %collective-permute-start.16) | collective-permute-done | bytes 262176 | tf_op jit(solution)/shard_map/ppermute | solution.py:1054
  232.8 10.9 %collective-permute-done.17.refs_8_.refs_4_ = bf16[512,256]{1,0:T(8,128)(2,1)S(1)} collective-permute-done((bf16[512,256]{1,0:T(8,128)(2,1)}, bf16[512,256]{1,0:T(8,128)(2,1)S(1)}, u32[]{:S(2)}, u32[]{:S(2)}) %collective-permute-start.17) | collective-permute-done | bytes 262176 | tf_op jit(solution)/shard_map/ppermute | solution.py:1054
  244.3 2.6 collect.2
  247.4 2.7 collect.3
  254.5 6.6 out_branch.3
  262.6 5.4 out_branch.4
  268.2 4.8 out_branch.5
  274.9 35.0 %collective-permute-done.20.refs_2_ = bf16[512,2048]{1,0:T(8,128)(2,1)S(1)} collective-permute-done((bf16[512,2048]{1,0:T(8,128)(2,1)}, bf16[512,2048]{1,0:T(8,128)(2,1)S(1)}, u32[]{:S(2)}, u32[]{:S(2)}) %collective-permute-start.20) | collective-permute-done | bytes 2097184 | tf_op jit(solution)/shard_map/ppermute | solution.py:1054
  311.2 23.4 %widen.3 = (f32[512,2048]{1,0:T(8,128)}, bf16[512,2048]{1,0:T(8,128)(2,1)}, bf16[512,4096]{1,0:T(8,128)(2,1)}, bf16[512,4096]{1,0:T(8,128)(2,1)}, f32[2,512]{1,0:T(2,128)}) custom-call(bf16[1024,2048]{1,0:T(8,128)(2,1)} %bitcast.67, bf16[512,2048]{1,0:T(8,128)(2,1)} %get-tuple-element.115.refs_5_.refs_1_, bf16[512,2048]{1,0:T(8,128)(2,1)} %copy-done.8, ...), custom_call_target="tpu_custom_call" | custom-call | flops 5798205952 | tf_op jit(solution)/shard_map/widen/pallas_call | solution.py:481
  337.2 15.9 %widen.4 = (f32[512,2048]{1,0:T(8,128)}, bf16[512,2048]{1,0:T(8,128)(2,1)}, bf16[512,4096]{1,0:T(8,128)(2,1)}, bf16[512,4096]{1,0:T(8,128)(2,1)}, f32[2,512]{1,0:T(2,128)}) custom-call(bf16[1024,2048]{1,0:T(8,128)(2,1)} %bitcast.68, bf16[256,2048]{1,0:T(8,128)(2,1)} %get-tuple-element.118.refs_6_.refs_1_, bf16[256,2048]{1,0:T(8,128)(2,1)} %copy-done.19, ...), custom_call_target="tpu_custom_call" | custom-call | flops 2899102976 | tf_op jit(solution)/shard_map/widen/pallas_call | solution.py:481
  355.4 16.4 %widen.5 = (f32[512,2048]{1,0:T(8,128)}, bf16[512,2048]{1,0:T(8,128)(2,1)}, bf16[512,4096]{1,0:T(8,128)(2,1)}, bf16[512,4096]{1,0:T(8,128)(2,1)}, f32[2,512]{1,0:T(2,128)}) custom-call(bf16[1024,2048]{1,0:T(8,128)(2,1)} %bitcast.69, ...), custom_call_target="tpu_custom_call", output_to_operand_aliasing={{0}: (5, {}), {1}: (6, {}), {2}: (7, {}), {3}: (8, {}), {4}... | custom-call | flops 2899102976 | tf_op jit(solution)/shard_map/widen/pallas_call | solution.py:481
  376.1 25.8 %weight_grad.3 = (bf16[1024,4096]{1,0:T(8,128)(2,1)}, bf16[1024,4096]{1,0:T(8,128)(2,1)}) custom-call(s32[1]{0:T(128)} %bitcast.14.refs_0_.place, bf16[1024,2048]{1,0:T(8,128)(2,1)} %bitcast.72, bf16[1024,2048]{1,0:T(8,128)(2,1)} %bitcast.73, bf16[512,4096]{1,0:T(8,128)(2,1)} %get-tuple-element.120.refs_2_.refs_3_.refs_1_, ...), custom_call_target="tpu_custom_call" | custom-call | flops 6227702784 | tf_op jit(solution)/shard_map/weight_grad/pallas_call | solution.py:441
  402.0 27.4 %wide_back.1 = (bf16[512,4096]{1,0:T(8,128)(2,1)}, bf16[512,4096]{1,0:T(8,128)(2,1)}, f32[2,512]{1,0:T(2,128)}, f32[2,512]{1,0:T(2,128)}, f32[1,4096]{1,0:T(1,128)}) custom-call(bf16[1024,2048]{1,0:T(8,128)(2,1)} %bitcast.74, bf16[4096,2048]{1,0:T(8,128)(2,1)} %all-gather.4.cloned.1.call-done.refs_1_, f32[1,4096]{1,0:T(1,128)} %reshape.280.refs_8_.refs_2_.refs_0_, ...), custom_call_target="tpu_custom_call" | custom-call | flops 7516192768 | tf_op jit(solution)/shard_map/wide_back/pallas_call | solution.py:481
  429.4 11.3 %add.211.refs_8_ = bf16[1024,4096]{1,0:T(8,128)(2,1)} custom-call(bf16[1024,4096]{1,0:T(8,128)(2,1)} %get-tuple-element.136.refs_0_, bf16[1024,4096]{1,0:T(8,128)(2,1)} %collective-permute-done.27.refs_1_, f32[2,512]{1,0:T(2,128)} %get-tuple-element.132.refs_2_.refs_5_), custom_call_target="tpu_custom_call" | custom-call | flops 1572864000 | tf_op jit(solution)/shard_map/add/pallas_call | solution.py:481
  446.0 20.2 %pre_back.2 = (bf16[512,4096]{1,0:T(8,128)(2,1)}, bf16[512,2048]{1,0:T(8,128)(2,1)}) custom-call(bf16[512,4096]{1,0:T(8,128)(2,1)} %get-tuple-element.133.refs_0_, bf16[512,4096]{1,0:T(8,128)(2,1)} %get-tuple-element.120.refs_2_.refs_3_.refs_1_, bf16[512,4096]{1,0:T(8,128)(2,1)} %get-tuple-element.134.refs_2_, ...), custom_call_target="tpu_custom_call" | custom-call | flops 4939212288 | tf_op jit(solution)/shard_map/pre_back/pallas_call | solution.py:481
  467.7 19.7 %pre_back.3 = (bf16[512,4096]{1,0:T(8,128)(2,1)}, bf16[512,2048]{1,0:T(8,128)(2,1)}) custom-call(bf16[512,4096]{1,0:T(8,128)(2,1)} %get-tuple-element.130.refs_0_, bf16[512,4096]{1,0:T(8,128)(2,1)} %get-tuple-element.127.refs_3_.refs_4_.refs_1_, bf16[512,4096]{1,0:T(8,128)(2,1)} %get-tuple-element.131.refs_2_, ...), custom_call_target="tpu_custom_call" | custom-call | flops 4939212288 | tf_op jit(solution)/shard_map/pre_back/pallas_call | solution.py:481
  488.0 25.4 %narrow.1.refs_10_.refs_0_ = bf16[1024,2048]{1,0:T(8,128)(2,1)} custom-call(f32[1,4096]{1,0:T(1,128)} %reshape.280.refs_8_.refs_2_.refs_0_, bf16[4096,2048]{1,0:T(8,128)(2,1)} %all-gather.4.cloned.1.call-done.refs_1_, bf16[512,4096]{1,0:T(8,128)(2,1)} %get-tuple-element.120.refs_2_.refs_3_.refs_1_, ...), custom_call_target="tpu_custom_call" | custom-call | flops 6871947776 | tf_op jit(solution)/shard_map/narrow/pallas_call | solution.py:481
  516.4 13.0 %middle.2 = (f32[512,2048]{1,0:T(8,128)}, bf16[512,2048]{1,0:T(8,128)(2,1)}, f32[512,1024]{1,0:T(8,128)}, f32[2,512]{1,0:T(2,128)}, f32[1,2048]{1,0:T(1,128)}, /*index=5*/f32[1,1024]{1,0:T(1,128)}) custom-call(bf16[1024,2048]{1,0:T(8,128)(2,1)} %bitcast.75, bf16[512,2048]{1,0:T(8,128)(2,1)} %get-tuple-element.137.refs_8_.refs_1_, ...), custom_call_target="tpu_custom_call" | custom-call | flops 3221225472 | tf_op jit(solution)/shard_map/middle/pallas_call | solution.py:481
  531.0 24.1 %weight_grad.4 = (bf16[1024,4096]{1,0:T(8,128)(2,1)}, bf16[1024,4096]{1,0:T(8,128)(2,1)}) custom-call(s32[1]{0:T(128)} %bitcast.14.refs_0_.place, bf16[512,2048]{1,0:T(8,128)(2,1)} %get-tuple-element.143.refs_0_, bf16[512,2048]{1,0:T(8,128)(2,1)} %get-tuple-element.144.refs_1_, bf16[512,4096]{1,0:T(8,128)(2,1)} %get-tuple-element.145.refs_2_, ...), custom_call_target="tpu_custom_call" | custom-call | flops 6227702784 | tf_op jit(solution)/shard_map/weight_grad/pallas_call | solution.py:441
  555.1 2.6 collective-permute-done.29.refs_8_.refs_2_
  559.0 4.0 share_out.2
  563.1 12.6 %middle.3 = (f32[512,2048]{1,0:T(8,128)}, bf16[512,2048]{1,0:T(8,128)(2,1)}, f32[512,1024]{1,0:T(8,128)}, f32[2,512]{1,0:T(2,128)}, f32[1,2048]{1,0:T(1,128)}, /*index=5*/f32[1,1024]{1,0:T(1,128)}) custom-call(bf16[1024,2048]{1,0:T(8,128)(2,1)} %bitcast.76, bf16[512,2048]{1,0:T(8,128)(2,1)} %get-tuple-element.138.refs_8_.refs_1_, ...), custom_call_target="tpu_custom_call" | custom-call | flops 3221225472 | tf_op jit(solution)/shard_map/middle/pallas_call | solution.py:481
  578.9 6.0 add.212.refs_7_
  585.5 4.1 share_out.3
  591.8 9.7 %weight_grad.5 = (bf16[1024,1024]{1,0:T(8,128)(2,1)}, bf16[1024,1024]{1,0:T(8,128)(2,1)}) custom-call(s32[1]{0:T(128)} %bitcast.14.refs_0_.place, bf16[512,2048]{1,0:T(8,128)(2,1)} %get-tuple-element.159.refs_0_, bf16[512,2048]{1,0:T(8,128)(2,1)} %get-tuple-element.160.refs_1_, bf16[512,1024]{1,0:T(8,128)(2,1)} %get-tuple-element.161.refs_2_, ...), custom_call_target="tpu_custom_call" | custom-call | flops 1556925696 | tf_op jit(solution)/shard_map/weight_grad/pallas_call | solution.py:441
  604.9 44.9 %attend_back.2.refs_2_.refs_1_.refs_0_ = bf16[2048,768]{1,0:T(8,128)(2,1)} custom-call(s32[2]{0:T(128)} %pad_add_fusion.refs_0_, bf16[2048,768]{1,0:T(8,128)(2,1)} %get-tuple-element.100.refs_1_, bf16[512,256]{1,0:T(8,128)(2,1)} %get-tuple-element.148.refs_10_.refs_2_, bf16[512,256]{1,0:T(8,128)(2,1)} %copy-done.48, bf16[512,256]{1,0:T(8,128)(2,1)} %copy-done.50, ...), custom_call_target="tpu_custom_call" | custom-call | flops 281857228800 | tf_op jit(solution)/shard_map/attend_back/pallas_call | solution.py:481
  649.9 6.2 add.213.refs_5_
  657.2 17.9 %first_back.2 = (bf16[512,1024]{1,0:T(8,128)(2,1)}, bf16[512,1024]{1,0:T(8,128)(2,1)}, bf16[512,1024]{1,0:T(8,128)(2,1)}, bf16[512,1024]{1,0:T(8,128)(2,1)}, bf1...) custom-call(s32[4]{0:T(128)} %broadcast_xor_fusion.refs_0_, bf16[2048,768]{1,0:T(8,128)(2,1)} %attend_back.2.refs_2_.refs_1_.refs_0_, ...), custom_call_target="tpu_custom_call" | custom-call | flops 3623878656 | tf_op jit(solution)/shard_map/first_back/pallas_call | solution.py:481
  675.6 2.3 collective-permute-done.42.refs_1_
  680.4 4.2 add_halves.2
  685.7 9.6 %collective-permute-done.37.refs_2_ = bf16[512,4096]{1,0:T(8,128)(2,1)} collective-permute-done((bf16[512,4096]{1,0:T(8,128)(2,1)}, bf16[512,4096]{1,0:T(8,128)(2,1)}, u32[]{:S(2)}, u32[]{:S(2)}) %collective-permute-start.37) | collective-permute-done | bytes 4194336 | tf_op jit(solution)/shard_map/ppermute | solution.py:1054
  696.7 7.3 add.214.refs_15_
  704.0 44.9 %attend_back.3.refs_5_.refs_1_ = bf16[2048,768]{1,0:T(8,128)(2,1)} custom-call(s32[2]{0:T(128)} %pad_add_fusion.1.refs_0_, bf16[2048,768]{1,0:T(8,128)(2,1)} %get-tuple-element.106.refs_1_, bf16[512,256]{1,0:T(8,128)(2,1)} %get-tuple-element.152.refs_4_.refs_2_, bf16[512,256]{1,0:T(8,128)(2,1)} %copy-done.45, bf16[512,256]{1,0:T(8,128)(2,1)} %copy-done.46, ...), custom_call_target="tpu_custom_call" | custom-call | flops 11274289152 | tf_op jit(solution)/shard_map/attend_back/pallas_call | solution.py:481
  750.6 5.0 join_halves.1.refs_5_.refs_3_
  756.1 17.5 %first_back.3 = (bf16[512,1024]{1,0:T(8,128)(2,1)}, bf16[512,1024]{1,0:T(8,128)(2,1)}, bf16[512,1024]{1,0:T(8,128)(2,1)}, bf16[512,1024]{1,0:T(8,128)(2,1)}, bf1...) custom-call(s32[4]{0:T(128)} %broadcast_xor_fusion.refs_0_, bf16[2048,768]{1,0:T(8,128)(2,1)} %attend_back.3.refs_5_.refs_1_, ...), custom_call_target="tpu_custom_call" | custom-call | flops 3623878656 | tf_op jit(solution)/shard_map/first_back/pallas_call | solution.py:481
  774.2 10.3 %result.1.refs_3_ = bf16[1024,2048]{1,0:T(8,128)(2,1)} custom-call(bf16[1024,2048]{1,0:T(8,128)(2,1)} %narrow.1.refs_10_.refs_0_, bf16[1024,2048]{1,0:T(8,128)(2,1)} %collective-permute-done.28.refs_1_, f32[512,2048]{1,0:T(8,128)} %get-tuple-element.139.refs_3_.refs_2_, f32[512,2048]{1,0:T(8,128)} %get-tuple-element.140.refs_3_, ...), custom_call_target="tpu_custom_call" | custom-call | flops 74999996416 | tf_op jit(solution)/shard_map/result/pallas_call | solution.py:481
  786.4 4.2 add_halves.3
  791.3 18.8 %heads_grad.1.refs_3_ = bf16[2048,768]{1,0:T(8,128)(2,1)} custom-call(bf16[2048,768]{1,0:T(8,128)(2,1)} %attend_back.2.refs_2_.refs_1_.refs_0_, bf16[2048,768]{1,0:T(8,128)(2,1)} %attend_back.3.refs_5_.refs_1_, bf16[2048,2048]{1,0:T(8,128)(2,1)} %get-tuple-element.164.refs_2_, bf16[2048,2048]{1,0:T(8,128)(2,1)} %get-tuple-element.170.refs_2_.refs_3_, ...), custom_call_target="tpu_custom_call" | custom-call | flops 4831838208 | tf_op jit(solution)/shard_map/heads_grad/pallas_call | solution.py:481
  812.5 2.1 collective-permute-done.52.refs_4_
  817.9 3.9 add.215.refs_1_.refs_3_
  828.9 3.8 collective-permute-start.58
  832.9 3.2 collective-permute-done.58
  836.1 7.4 input_grad.2.refs_5_.refs_7_
  846.6 3.9 add.216.refs_1_.refs_5_
  851.9 17.2 %collective-permute-done.68 = bf16[128,4096]{1,0:T(8,128)(2,1)S(1)} collective-permute-done((bf16[128,4096]{1,0:T(8,128)(2,1)S(1)}, bf16[128,4096]{1,0:T(8,128)(2,1)S(1)}, u32[]{:S(2)}, u32[]{:S(2)}) %collective-permute-start.68) | collective-permute-done | bytes 1048608 | tf_op jit(solution)/shard_map/ppermute | solution.py:1054
  870.6 3.0 copy.116
  885.8 7.2 input_grad.3
  (367 shorter events, 119.3 us)
Async XLA Ops:
  7.2 90.3 %all-gather.6.cloned.1.call-start = ((), (), s32[]{:S(2)}) async-start(), calls=%async_computation.5 | async-start | bytes 3932160 | tf_op jit(solution)/shard_map/all_gather | solution.py:1343
  12.1 8.0 collective-permute-start
  12.7 8.9 collective-permute-start.1
  15.3 10.5 %collective-permute-start.2 = (bf16[144,768]{1,0:T(8,128)(2,1)S(1)}, bf16[144,768]{1,0:T(8,128)(2,1)S(1)}, u32[]{:S(2)}, u32[]{:S(2)}) collective-permute-start(bf16[144,768]{1,0:T(8,128)(2,1)S(1)} %get-tuple-element.249), channel_id=1, source_target_pairs={{0,6},{2,4},{4,2},{6,0},{1,7},{3,5},{5,3},{7,1},{8,14},{10,12},{12... | collective-permute-start | bytes 663560 | tf_op jit(solution)/shard_map/ppermute | solution.py:1054
  30.3 223.6 %all-gather.8.cloned.1.call-start = ((), (), s32[]{:S(2)}) async-start(), calls=%async_computation.6 | async-start | bytes 22282240 | tf_op jit(solution)/shard_map/all_gather | solution.py:1356
  30.4 47.8 %collective-permute-start.7 = (bf16[512,2048]{1,0:T(8,128)(2,1)S(1)}, bf16[512,2048]{1,0:T(8,128)(2,1)}, u32[]{:S(2)}, u32[]{:S(2)}) collective-permute-start(bf16[512,2048]{1,0:T(8,128)(2,1)S(1)} %copy-done.1), channel_id=1, source_target_pairs={{0,4},{2,6},{4,0},{6,2},{1,5},{3,7},{5,1},{7,3},{8,12},{10,14},{12... | collective-permute-start | bytes 6291464 | tf_op jit(solution)/shard_map/ppermute | solution.py:1054
  32.5 5.3 collective-permute-start.4
  35.1 5.8 collective-permute-start.5
  80.7 321.3 %all-gather.4.cloned.1.call-start = ((), (), s32[]{:S(2)}) async-start(), calls=%async_computation.4 | async-start | bytes 17825792 | tf_op jit(solution)/shard_map/all_gather | solution.py:1359
  81.4 510.4 %reduce-scatter.5.cloned.1.call-start = ((), (), s32[]{:S(2)}) async-start(), calls=%async_computation.7 | async-start | bytes 10485760 | tf_op jit(solution)/shard_map/reduce_scatter | solution.py:1223
  81.6 15.8 %collective-permute-start.6 = (bf16[512,2048]{1,0:T(8,128)(2,1)}, bf16[512,2048]{1,0:T(8,128)(2,1)}, u32[]{:S(2)}, u32[]{:S(2)}) collective-permute-start(bf16[512,2048]{1,0:T(8,128)(2,1)} %get-tuple-element.221.refs_1_), channel_id=1, source_target_pairs={{0,2},{2,0},{4,6},{6,4},{1,3},{3,1},{5,7},{7,5},{8,10},{10,8},{12,... | collective-permute-start | bytes 6291464 | tf_op jit(solution)/shard_map/ppermute | solution.py:1054
  81.7 15.7 %collective-permute-start.8 = (bf16[512,2048]{1,0:T(8,128)(2,1)}, bf16[512,2048]{1,0:T(8,128)(2,1)}, u32[]{:S(2)}, u32[]{:S(2)}) collective-permute-start(bf16[512,2048]{1,0:T(8,128)(2,1)} %collective-permute-done.7.refs_3_), channel_id=1, source_target_pairs={{0,2},{2,0},{4,6},{6,4},{1,3},{3,1},{5,7},{7,5},{8,10},{10,8},{12,... | collective-permute-start | bytes 6291464 | tf_op jit(solution)/shard_map/ppermute | solution.py:1054
  82.2 74.2 %collective-permute-start.13 = (bf16[512,2048]{1,0:T(8,128)(2,1)S(1)}, bf16[512,2048]{1,0:T(8,128)(2,1)}, u32[]{:S(2)}, u32[]{:S(2)}) collective-permute-start(bf16[512,2048]{1,0:T(8,128)(2,1)S(1)} %copy-done), channel_id=1, source_target_pairs={{0,4},{2,6},{4,0},{6,2},{1,5},{3,7},{5,1},{7,3},{8,12},{10,14},{12... | collective-permute-start | bytes 6291464 | tf_op jit(solution)/shard_map/ppermute | solution.py:1054
  84.0 80.7 %collective-permute-start.12 = (bf16[512,2048]{1,0:T(8,128)(2,1)S(1)}, bf16[512,2048]{1,0:T(8,128)(2,1)}, u32[]{:S(2)}, u32[]{:S(2)}) collective-permute-start(bf16[512,2048]{1,0:T(8,128)(2,1)S(1)} %copy-done), channel_id=1, source_target_pairs={{0,2},{2,0},{4,6},{6,4},{1,3},{3,1},{5,7},{7,5},{8,10},{10,8},{12,... | collective-permute-start | bytes 6291464 | tf_op jit(solution)/shard_map/ppermute | solution.py:1054
  161.7 58.2 %collective-permute-start.9 = (bf16[512,256]{1,0:T(8,128)(2,1)S(1)}, bf16[512,256]{1,0:T(8,128)(2,1)S(1)}, u32[]{:S(2)}, u32[]{:S(2)}) collective-permute-start(bf16[512,256]{1,0:T(8,128)(2,1)S(1)} %copy-done.42), channel_id=1, source_target_pairs={{0,2},{2,0},{4,6},{6,4},{1,3},{3,1},{5,7},{7,5},{8,10},{10,8},{12,... | collective-permute-start | bytes 786440 | tf_op jit(solution)/shard_map/ppermute | solution.py:1054
  162.2 57.8 %collective-permute-start.10 = (bf16[512,256]{1,0:T(8,128)(2,1)S(1)}, bf16[512,256]{1,0:T(8,128)(2,1)S(1)}, u32[]{:S(2)}, u32[]{:S(2)}) collective-permute-start(bf16[512,256]{1,0:T(8,128)(2,1)S(1)} %copy-done.43), channel_id=1, source_target_pairs={{0,4},{2,6},{4,0},{6,2},{1,5},{3,7},{5,1},{7,3},{8,12},{10,14},{12... | collective-permute-start | bytes 786440 | tf_op jit(solution)/shard_map/ppermute | solution.py:1054
  164.6 55.3 %collective-permute-start.11 = (bf16[512,256]{1,0:T(8,128)(2,1)S(1)}, bf16[512,256]{1,0:T(8,128)(2,1)S(1)}, u32[]{:S(2)}, u32[]{:S(2)}) collective-permute-start(bf16[512,256]{1,0:T(8,128)(2,1)S(1)} %copy-done.44), channel_id=1, source_target_pairs={{0,6},{2,4},{4,2},{6,0},{1,7},{3,5},{5,3},{7,1},{8,14},{10,12},{12... | collective-permute-start | bytes 786440 | tf_op jit(solution)/shard_map/ppermute | solution.py:1054
  216.6 16.2 %collective-permute-start.16 = (bf16[512,256]{1,0:T(8,128)(2,1)}, bf16[512,256]{1,0:T(8,128)(2,1)S(1)}, u32[]{:S(2)}, u32[]{:S(2)}) collective-permute-start(bf16[512,256]{1,0:T(8,128)(2,1)} %get-tuple-element.109.refs_8_), channel_id=1, source_target_pairs={{0,4},{2,6},{4,0},{6,2},{1,5},{3,7},{5,1},{7,3},{8,12},{10,14},{12... | collective-permute-start | bytes 786440 | tf_op jit(solution)/shard_map/ppermute | solution.py:1054
  219.8 23.8 %collective-permute-start.17 = (bf16[512,256]{1,0:T(8,128)(2,1)}, bf16[512,256]{1,0:T(8,128)(2,1)S(1)}, u32[]{:S(2)}, u32[]{:S(2)}) collective-permute-start(bf16[512,256]{1,0:T(8,128)(2,1)} %get-tuple-element.110.refs_9_), channel_id=1, source_target_pairs={{0,6},{2,4},{4,2},{6,0},{1,7},{3,5},{5,3},{7,1},{8,14},{10,12},{12... | collective-permute-start | bytes 786440 | tf_op jit(solution)/shard_map/ppermute | solution.py:1054
  247.0 5.7 collective-permute-start.18
  261.1 48.8 %collective-permute-start.20 = (bf16[512,2048]{1,0:T(8,128)(2,1)}, bf16[512,2048]{1,0:T(8,128)(2,1)S(1)}, u32[]{:S(2)}, u32[]{:S(2)}) collective-permute-start(bf16[512,2048]{1,0:T(8,128)(2,1)} %get-tuple-element.115.refs_5_.refs_1_), channel_id=1, source_target_pairs={{0,1},{1,0},{2,3},{3,2},{4,5},{5,4},{6,7},{7,6},{8,9},{9,8},{10,11... | collective-permute-start | bytes 6291464 | tf_op jit(solution)/shard_map/ppermute | solution.py:1054
  268.0 68.2 %collective-permute-start.22 = (bf16[256,2048]{1,0:T(8,128)(2,1)}, bf16[256,2048]{1,0:T(8,128)(2,1)S(1)}, u32[]{:S(2)}, u32[]{:S(2)}) collective-permute-start(bf16[256,2048]{1,0:T(8,128)(2,1)} %get-tuple-element.118.refs_6_.refs_1_), channel_id=1, source_target_pairs={{0,1},{1,0},{2,3},{3,2},{4,5},{5,4},{6,7},{7,6},{8,9},{9,8},{10,11... | collective-permute-start | bytes 3145736 | tf_op jit(solution)/shard_map/ppermute | solution.py:1054
  273.1 81.3 %collective-permute-start.21 = (bf16[256,2048]{1,0:T(8,128)(2,1)}, bf16[256,2048]{1,0:T(8,128)(2,1)S(1)}, u32[]{:S(2)}, u32[]{:S(2)}) collective-permute-start(bf16[256,2048]{1,0:T(8,128)(2,1)} %get-tuple-element.119.refs_5_.refs_1_), channel_id=1, source_target_pairs={{0,1},{1,0},{2,3},{3,2},{4,5},{5,4},{6,7},{7,6},{8,9},{9,8},{10,11... | collective-permute-start | bytes 3145736 | tf_op jit(solution)/shard_map/ppermute | solution.py:1054
  334.6 39.1 %collective-permute-start.23 = (f32[2,512]{1,0:T(2,128)}, f32[2,512]{1,0:T(2,128)S(1)}, u32[]{:S(2)}, u32[]{:S(2)}) collective-permute-start(f32[2,512]{1,0:T(2,128)} %get-tuple-element.121.refs_5_.refs_4_.refs_3_), channel_id=1, source_target_pairs={{0,1},{1,0},{2,3},{3,2},{4,5},{5,4},{6,7},{7,6},{8,9},{9,8},{10,11... | collective-permute-start | bytes 12296 | tf_op jit(solution)/shard_map/ppermute | solution.py:1054
  401.9 27.5 %collective-permute-start.27 = (bf16[1024,4096]{1,0:T(8,128)(2,1)}, bf16[1024,4096]{1,0:T(8,128)(2,1)}, u32[]{:S(2)}, u32[]{:S(2)}) collective-permute-start(bf16[1024,4096]{1,0:T(8,128)(2,1)} %get-tuple-element.129.refs_9_), channel_id=1, source_target_pairs={{0,2},{2,0},{4,6},{6,4},{1,3},{3,1},{5,7},{7,5},{8,10},{10,8},{12,... | collective-permute-start | bytes 25165832 | tf_op jit(solution)/shard_map/ppermute | solution.py:1054
  440.8 350.5 %reduce-scatter.9.cloned.1.call-start = ((), (), s32[]{:S(2)}) async-start(), calls=%async_computation.9 | async-start | bytes 2621440 | tf_op jit(solution)/shard_map/reduce_scatter | solution.py:1223
  466.3 48.8 %collective-permute-start.30 = (bf16[512,2048]{1,0:T(8,128)(2,1)}, bf16[512,2048]{1,0:T(8,128)(2,1)S(1)}, u32[]{:S(2)}, u32[]{:S(2)}) collective-permute-start(bf16[512,2048]{1,0:T(8,128)(2,1)} %get-tuple-element.137.refs_8_.refs_1_), channel_id=1, source_target_pairs={{0,1},{1,0},{2,3},{3,2},{4,5},{5,4},{6,7},{7,6},{8,9},{9,8},{10,11... | collective-permute-start | bytes 6291464 | tf_op jit(solution)/shard_map/ppermute | solution.py:1054
  487.5 70.2 %collective-permute-start.29 = (bf16[512,2048]{1,0:T(8,128)(2,1)}, bf16[512,2048]{1,0:T(8,128)(2,1)S(1)}, u32[]{:S(2)}, u32[]{:S(2)}) collective-permute-start(bf16[512,2048]{1,0:T(8,128)(2,1)} %get-tuple-element.138.refs_8_.refs_1_), channel_id=1, source_target_pairs={{0,1},{1,0},{2,3},{3,2},{4,5},{5,4},{6,7},{7,6},{8,9},{9,8},{10,11... | collective-permute-start | bytes 6291464 | tf_op jit(solution)/shard_map/ppermute | solution.py:1054
  529.5 28.3 %collective-permute-start.31 = (f32[2,512]{1,0:T(2,128)}, f32[2,512]{1,0:T(2,128)S(1)}, u32[]{:S(2)}, u32[]{:S(2)}) collective-permute-start(f32[2,512]{1,0:T(2,128)} %get-tuple-element.142.refs_4_.refs_5_), channel_id=1, source_target_pairs={{0,1},{1,0},{2,3},{3,2},{4,5},{5,4},{6,7},{7,6},{8,9},{9,8},{10,11... | collective-permute-start | bytes 12296 | tf_op jit(solution)/shard_map/ppermute | solution.py:1054
  555.1 23.9 %collective-permute-start.33 = (bf16[1024,4096]{1,0:T(8,128)(2,1)}, bf16[1024,4096]{1,0:T(8,128)(2,1)}, u32[]{:S(2)}, u32[]{:S(2)}) collective-permute-start(bf16[1024,4096]{1,0:T(8,128)(2,1)} %get-tuple-element.147.refs_7_), channel_id=1, source_target_pairs={{0,2},{2,0},{4,6},{6,4},{1,3},{3,1},{5,7},{7,5},{8,10},{10,8},{12,... | collective-permute-start | bytes 25165832 | tf_op jit(solution)/shard_map/ppermute | solution.py:1054
  563.1 28.7 %collective-permute-start.38 = (bf16[512,256]{1,0:T(8,128)(2,1)}, bf16[512,256]{1,0:T(8,128)(2,1)S(1)}, u32[]{:S(2)}, u32[]{:S(2)}) collective-permute-start(bf16[512,256]{1,0:T(8,128)(2,1)} %get-tuple-element.156), channel_id=1, source_target_pairs={{0,2},{2,0},{4,6},{6,4},{1,3},{3,1},{5,7},{7,5},{8,10},{10,8},{12,... | collective-permute-start | bytes 786440 | tf_op jit(solution)/shard_map/ppermute | solution.py:1054
  575.7 9.2 %collective-permute-start.32 = (f32[2,512]{1,0:T(2,128)}, f32[2,512]{1,0:T(2,128)S(1)}, u32[]{:S(2)}, u32[]{:S(2)}) collective-permute-start(f32[2,512]{1,0:T(2,128)} %get-tuple-element.150.refs_2_.refs_5_), channel_id=1, source_target_pairs={{0,1},{1,0},{2,3},{3,2},{4,5},{5,4},{6,7},{7,6},{8,9},{9,8},{10,11... | collective-permute-start | bytes 12296 | tf_op jit(solution)/shard_map/ppermute | solution.py:1054
  577.4 24.2 %collective-permute-start.39 = (bf16[512,256]{1,0:T(8,128)(2,1)S(1)}, bf16[512,256]{1,0:T(8,128)(2,1)S(1)}, u32[]{:S(2)}, u32[]{:S(2)}) collective-permute-start(bf16[512,256]{1,0:T(8,128)(2,1)S(1)} %copy-done.52), channel_id=1, source_target_pairs={{0,4},{2,6},{4,0},{6,2},{1,5},{3,7},{5,1},{7,3},{8,12},{10,14},{12... | collective-permute-start | bytes 786440 | tf_op jit(solution)/shard_map/ppermute | solution.py:1054
  578.9 24.0 %collective-permute-start.40 = (bf16[512,256]{1,0:T(8,128)(2,1)S(1)}, bf16[512,256]{1,0:T(8,128)(2,1)S(1)}, u32[]{:S(2)}, u32[]{:S(2)}) collective-permute-start(bf16[512,256]{1,0:T(8,128)(2,1)S(1)} %copy-done.49), channel_id=1, source_target_pairs={{0,6},{2,4},{4,2},{6,0},{1,7},{3,5},{5,3},{7,1},{8,14},{10,12},{12... | collective-permute-start | bytes 786440 | tf_op jit(solution)/shard_map/ppermute | solution.py:1054
  589.7 13.8 %collective-permute-start.34 = (bf16[512,256]{1,0:T(8,128)(2,1)}, bf16[512,256]{1,0:T(8,128)(2,1)S(1)}, u32[]{:S(2)}, u32[]{:S(2)}) collective-permute-start(bf16[512,256]{1,0:T(8,128)(2,1)} %get-tuple-element.153), channel_id=1, source_target_pairs={{0,2},{2,0},{4,6},{6,4},{1,3},{3,1},{5,7},{7,5},{8,10},{10,8},{12,... | collective-permute-start | bytes 786440 | tf_op jit(solution)/shard_map/ppermute | solution.py:1054
  590.2 13.2 %collective-permute-start.35 = (bf16[512,256]{1,0:T(8,128)(2,1)}, bf16[512,256]{1,0:T(8,128)(2,1)S(1)}, u32[]{:S(2)}, u32[]{:S(2)}) collective-permute-start(bf16[512,256]{1,0:T(8,128)(2,1)} %get-tuple-element.154), channel_id=1, source_target_pairs={{0,4},{2,6},{4,0},{6,2},{1,5},{3,7},{5,1},{7,3},{8,12},{10,14},{12... | collective-permute-start | bytes 786440 | tf_op jit(solution)/shard_map/ppermute | solution.py:1054
  591.8 11.7 %collective-permute-start.36 = (bf16[512,256]{1,0:T(8,128)(2,1)}, bf16[512,256]{1,0:T(8,128)(2,1)S(1)}, u32[]{:S(2)}, u32[]{:S(2)}) collective-permute-start(bf16[512,256]{1,0:T(8,128)(2,1)} %get-tuple-element.155), channel_id=1, source_target_pairs={{0,6},{2,4},{4,2},{6,0},{1,7},{3,5},{5,3},{7,1},{8,14},{10,12},{12... | collective-permute-start | bytes 786440 | tf_op jit(solution)/shard_map/ppermute | solution.py:1054
  601.6 93.7 %collective-permute-start.37 = (bf16[512,4096]{1,0:T(8,128)(2,1)}, bf16[512,4096]{1,0:T(8,128)(2,1)}, u32[]{:S(2)}, u32[]{:S(2)}) collective-permute-start(bf16[512,4096]{1,0:T(8,128)(2,1)} %add.212.refs_7_), channel_id=1, source_target_pairs={{0,4},{2,6},{4,0},{6,2},{1,5},{3,7},{5,1},{7,3},{8,12},{10,14},{12... | collective-permute-start | bytes 12582920 | tf_op jit(solution)/shard_map/ppermute | solution.py:1054
  602.9 47.0 %collective-permute-start.41 = (bf16[1024,1024]{1,0:T(8,128)(2,1)}, bf16[1024,1024]{1,0:T(8,128)(2,1)}, u32[]{:S(2)}, u32[]{:S(2)}) collective-permute-start(bf16[1024,1024]{1,0:T(8,128)(2,1)} %get-tuple-element.163.refs_15_), channel_id=1, source_target_pairs={{0,2},{2,0},{4,6},{6,4},{1,3},{3,1},{5,7},{7,5},{8,10},{10,8},{12,... | collective-permute-start | bytes 6291464 | tf_op jit(solution)/shard_map/ppermute | solution.py:1054
  656.1 135.2 %reduce-scatter.7.cloned.1.call-start = ((), (), s32[]{:S(2)}) async-start(), calls=%async_computation.8 | async-start | bytes 5242880 | tf_op jit(solution)/shard_map/reduce_scatter | solution.py:1241
  656.1 118.0 %collective-permute-start.28 = (bf16[1024,2048]{1,0:T(8,128)(2,1)}, bf16[1024,2048]{1,0:T(8,128)(2,1)}, u32[]{:S(2)}, u32[]{:S(2)}) collective-permute-start(bf16[1024,2048]{1,0:T(8,128)(2,1)} %narrow.1.refs_10_.refs_0_), channel_id=1, source_target_pairs={{0,1},{1,0},{2,3},{3,2},{4,5},{5,4},{6,7},{7,6},{8,9},{9,8},{10,11... | collective-permute-start | bytes 12582920 | tf_op jit(solution)/shard_map/ppermute | solution.py:1054
  675.6 73.3 %collective-permute-start.44 = (bf16[512,1024]{1,0:T(8,128)(2,1)}, bf16[512,1024]{1,0:T(8,128)(2,1)S(1)}, u32[]{:S(2)}, u32[]{:S(2)}) collective-permute-start(bf16[512,1024]{1,0:T(8,128)(2,1)} %get-tuple-element.171), channel_id=1, source_target_pairs={{0,2},{2,0},{4,6},{6,4},{1,3},{3,1},{5,7},{7,5},{8,10},{10,8},{12,... | collective-permute-start | bytes 3145736 | tf_op jit(solution)/shard_map/ppermute | solution.py:1054
  677.9 71.0 %collective-permute-start.45 = (bf16[512,1024]{1,0:T(8,128)(2,1)}, bf16[512,1024]{1,0:T(8,128)(2,1)S(1)}, u32[]{:S(2)}, u32[]{:S(2)}) collective-permute-start(bf16[512,1024]{1,0:T(8,128)(2,1)} %get-tuple-element.172), channel_id=1, source_target_pairs={{0,2},{2,0},{4,6},{6,4},{1,3},{3,1},{5,7},{7,5},{8,10},{10,8},{12,... | collective-permute-start | bytes 3145736 | tf_op jit(solution)/shard_map/ppermute | solution.py:1054
  684.6 64.3 %collective-permute-start.47 = (bf16[512,1024]{1,0:T(8,128)(2,1)}, bf16[512,1024]{1,0:T(8,128)(2,1)S(1)}, u32[]{:S(2)}, u32[]{:S(2)}) collective-permute-start(bf16[512,1024]{1,0:T(8,128)(2,1)} %get-tuple-element.173), channel_id=1, source_target_pairs={{0,4},{2,6},{4,0},{6,2},{1,5},{3,7},{5,1},{7,3},{8,12},{10,14},{12... | collective-permute-start | bytes 3145736 | tf_op jit(solution)/shard_map/ppermute | solution.py:1054
  695.3 53.6 %collective-permute-start.46 = (bf16[512,1024]{1,0:T(8,128)(2,1)}, bf16[512,1024]{1,0:T(8,128)(2,1)}, u32[]{:S(2)}, u32[]{:S(2)}) collective-permute-start(bf16[512,1024]{1,0:T(8,128)(2,1)} %get-tuple-element.169.refs_3_), channel_id=1, source_target_pairs={{0,4},{2,6},{4,0},{6,2},{1,5},{3,7},{5,1},{7,3},{8,12},{10,14},{12... | collective-permute-start | bytes 3145736 | tf_op jit(solution)/shard_map/ppermute | solution.py:1054
  704.0 175.5 %reduce-scatter.11.cloned.1.call-start = ((), (), s32[]{:S(2)}) async-start(), calls=%async_computation.10 | async-start | bytes 3932160 | tf_op jit(solution)/shard_map/reduce_scatter | solution.py:1498
  755.6 77.3 %collective-permute-start.59 = (bf16[512,2048]{1,0:T(8,128)(2,1)}, bf16[512,2048]{1,0:T(8,128)(2,1)}, u32[]{:S(2)}, u32[]{:S(2)}) collective-permute-start(bf16[512,2048]{1,0:T(8,128)(2,1)} %join_halves.1.refs_5_.refs_3_), channel_id=1, source_target_pairs={{0,1},{1,0},{2,3},{3,2},{4,5},{5,4},{6,7},{7,6},{8,9},{9,8},{10,11... | collective-permute-start | bytes 6291464 | tf_op jit(solution)/shard_map/ppermute | solution.py:1054
  773.6 42.4 %collective-permute-start.48 = (bf16[512,1024]{1,0:T(8,128)(2,1)}, bf16[512,1024]{1,0:T(8,128)(2,1)S(1)}, u32[]{:S(2)}, u32[]{:S(2)}) collective-permute-start(bf16[512,1024]{1,0:T(8,128)(2,1)} %get-tuple-element.176), channel_id=1, source_target_pairs={{0,2},{2,0},{4,6},{6,4},{1,3},{3,1},{5,7},{7,5},{8,10},{10,8},{12,... | collective-permute-start | bytes 3145736 | tf_op jit(solution)/shard_map/ppermute | solution.py:1054
  773.6 10.8 %collective-permute-start.49 = (bf16[512,1024]{1,0:T(8,128)(2,1)}, bf16[512,1024]{1,0:T(8,128)(2,1)S(1)}, u32[]{:S(2)}, u32[]{:S(2)}) collective-permute-start(bf16[512,1024]{1,0:T(8,128)(2,1)} %get-tuple-element.177), channel_id=1, source_target_pairs={{0,2},{2,0},{4,6},{6,4},{1,3},{3,1},{5,7},{7,5},{8,10},{10,8},{12,... | collective-permute-start | bytes 3145736 | tf_op jit(solution)/shard_map/ppermute | solution.py:1054
  774.1 10.3 %collective-permute-start.50 = (bf16[512,1024]{1,0:T(8,128)(2,1)}, bf16[512,1024]{1,0:T(8,128)(2,1)S(1)}, u32[]{:S(2)}, u32[]{:S(2)}) collective-permute-start(bf16[512,1024]{1,0:T(8,128)(2,1)} %get-tuple-element.178), channel_id=1, source_target_pairs={{0,2},{2,0},{4,6},{6,4},{1,3},{3,1},{5,7},{7,5},{8,10},{10,8},{12,... | collective-permute-start | bytes 3145736 | tf_op jit(solution)/shard_map/ppermute | solution.py:1054
  790.5 25.8 %collective-permute-start.51 = (bf16[512,1024]{1,0:T(8,128)(2,1)}, bf16[512,1024]{1,0:T(8,128)(2,1)S(1)}, u32[]{:S(2)}, u32[]{:S(2)}) collective-permute-start(bf16[512,1024]{1,0:T(8,128)(2,1)} %get-tuple-element.179.refs_4_), channel_id=1, source_target_pairs={{0,4},{2,6},{4,0},{6,2},{1,5},{3,7},{5,1},{7,3},{8,12},{10,14},{12... | collective-permute-start | bytes 3145736 | tf_op jit(solution)/shard_map/ppermute | solution.py:1054
  812.5 33.7 %collective-permute-start.54 = (bf16[512,1024]{1,0:T(8,128)(2,1)}, bf16[512,1024]{1,0:T(8,128)(2,1)}, u32[]{:S(2)}, u32[]{:S(2)}) collective-permute-start(bf16[512,1024]{1,0:T(8,128)(2,1)} %get-tuple-element.182), channel_id=1, source_target_pairs={{0,2},{2,0},{4,6},{6,4},{1,3},{3,1},{5,7},{7,5},{8,10},{10,8},{12,... | collective-permute-start | bytes 3145736 | tf_op jit(solution)/shard_map/ppermute | solution.py:1054
  814.6 31.6 %collective-permute-start.55 = (bf16[512,1024]{1,0:T(8,128)(2,1)}, bf16[512,1024]{1,0:T(8,128)(2,1)}, u32[]{:S(2)}, u32[]{:S(2)}) collective-permute-start(bf16[512,1024]{1,0:T(8,128)(2,1)} %get-tuple-element.183), channel_id=1, source_target_pairs={{0,4},{2,6},{4,0},{6,2},{1,5},{3,7},{5,1},{7,3},{8,12},{10,14},{12... | collective-permute-start | bytes 3145736 | tf_op jit(solution)/shard_map/ppermute | solution.py:1054
  821.8 24.8 %collective-permute-start.53 = (bf16[512,1024]{1,0:T(8,128)(2,1)}, bf16[512,1024]{1,0:T(8,128)(2,1)}, u32[]{:S(2)}, u32[]{:S(2)}) collective-permute-start(bf16[512,1024]{1,0:T(8,128)(2,1)} %add.215.refs_1_.refs_3_), channel_id=1, source_target_pairs={{0,1},{1,0},{2,3},{3,2},{4,5},{5,4},{6,7},{7,6},{8,9},{9,8},{10,11... | collective-permute-start | bytes 3145736 | tf_op jit(solution)/shard_map/ppermute | solution.py:1054
  828.9 7.2 collective-permute-start.58
  832.9 10.6 %collective-permute-start.57 = (f32[16,576]{1,0:T(8,128)S(1)}, f32[16,576]{1,0:T(8,128)S(1)}, u32[]{:S(2)}, u32[]{:S(2)}) collective-permute-start(f32[16,576]{1,0:T(8,128)S(1)} %copy-done.20), channel_id=1, source_target_pairs={{0,16},{8,24},{16,0},{24,8},{1,17},{9,25},{17,1},{25,9},{2,18},{10... | collective-permute-start | bytes 110600 | tf_op jit(solution)/shard_map/ppermute | solution.py:1054
  836.1 8.1 collective-permute-start.56
  843.5 25.5 %collective-permute-start.68 = (bf16[128,4096]{1,0:T(8,128)(2,1)S(1)}, bf16[128,4096]{1,0:T(8,128)(2,1)S(1)}, u32[]{:S(2)}, u32[]{:S(2)}) collective-permute-start(bf16[128,4096]{1,0:T(8,128)(2,1)S(1)} %slice.157), channel_id=1, source_target_pairs={{0,4},{2,6},{4,0},{6,2},{1,5},{3,7},{5,1},{7,3},{8,12},{10,14},{12... | collective-permute-start | bytes 3145736 | tf_op jit(solution)/shard_map/ppermute | solution.py:1054
  844.3 29.3 %collective-permute-start.67 = (bf16[128,1024]{1,0:T(8,128)(2,1)S(1)}, bf16[128,1024]{1,0:T(8,128)(2,1)S(1)}, u32[]{:S(2)}, u32[]{:S(2)}) collective-permute-start(bf16[128,1024]{1,0:T(8,128)(2,1)S(1)} %slice.155), channel_id=1, source_target_pairs={{0,4},{2,6},{4,0},{6,2},{1,5},{3,7},{5,1},{7,3},{8,12},{10,14},{12... | collective-permute-start | bytes 786440 | tf_op jit(solution)/shard_map/ppermute | solution.py:1054
  850.5 35.3 %collective-permute-start.60 = (bf16[512,1024]{1,0:T(8,128)(2,1)}, bf16[512,1024]{1,0:T(8,128)(2,1)}, u32[]{:S(2)}, u32[]{:S(2)}) collective-permute-start(bf16[512,1024]{1,0:T(8,128)(2,1)} %add.216.refs_1_.refs_5_), channel_id=1, source_target_pairs={{0,1},{1,0},{2,3},{3,2},{4,5},{5,4},{6,7},{7,6},{8,9},{9,8},{10,11... | collective-permute-start | bytes 3145736 | tf_op jit(solution)/shard_map/ppermute | solution.py:1054
  877.6 4.8 collective-permute-start.62
  880.7 12.3 %collective-permute-start.66 = (bf16[128,768]{1,0:T(8,128)(2,1)S(1)}, bf16[128,768]{1,0:T(8,128)(2,1)S(1)}, u32[]{:S(2)}, u32[]{:S(2)}) collective-permute-start(bf16[128,768]{1,0:T(8,128)(2,1)S(1)} %get-tuple-element.235), channel_id=1, source_target_pairs={{0,6},{2,4},{4,2},{6,0},{1,7},{3,5},{5,3},{7,1},{8,14},{10,12},{12... | collective-permute-start | bytes 589832 | tf_op jit(solution)/shard_map/ppermute | solution.py:1054
  881.2 11.8 %collective-permute-start.65 = (bf16[128,768]{1,0:T(8,128)(2,1)S(1)}, bf16[128,768]{1,0:T(8,128)(2,1)S(1)}, u32[]{:S(2)}, u32[]{:S(2)}) collective-permute-start(bf16[128,768]{1,0:T(8,128)(2,1)S(1)} %get-tuple-element.236), channel_id=1, source_target_pairs={{0,4},{2,6},{4,0},{6,2},{1,5},{3,7},{5,1},{7,3},{8,12},{10,14},{12... | collective-permute-start | bytes 589832 | tf_op jit(solution)/shard_map/ppermute | solution.py:1054
  882.4 10.6 %collective-permute-start.64 = (bf16[128,768]{1,0:T(8,128)(2,1)S(1)}, bf16[128,768]{1,0:T(8,128)(2,1)S(1)}, u32[]{:S(2)}, u32[]{:S(2)}) collective-permute-start(bf16[128,768]{1,0:T(8,128)(2,1)S(1)} %get-tuple-element.237), channel_id=1, source_target_pairs={{0,2},{2,0},{4,6},{6,4},{1,3},{3,1},{5,7},{7,5},{8,10},{10,8},{12,... | collective-permute-start | bytes 589832 | tf_op jit(solution)/shard_map/ppermute | solution.py:1054
  (74 other events, 356.2 us)
Sparse Core Ops, SparseCore 0:
  30.4 64.7 all-gather.5
  97.4 154.8 all-gather.7
  254.5 131.7 all-gather.3
  440.9 145.5 reduce-scatter.4
  656.2 44.5 reduce-scatter.8
  704.1 77.0 reduce-scatter.6
  810.3 64.1 reduce-scatter.10

commit v7 on v6

--- a/solution.py
+++ b/solution.py
@@ -642,7 +642,7 @@
 def widen(number, part, parts, tokens, own, other, gain, weight, units, into=None, after=()):
     rows, model = own.shape
     span = rows * parts
-    tile = 512
+    tile = min(1024, units)
     block = (rows, model)
     across = (rows, tile)
     here = lambda n: (part, 0)
@@ -704,7 +704,7 @@
     sequences = len(active)
     span, units = active[0].shape
     model = weight.shape[1]
-    tile = 512
+    tile = min(1024, units)
     sums = (2, span)
     rows = sequences * span
     return call(
@@ -776,7 +776,7 @@
     sequences = len(active)
     span, units = active[0].shape
     model = weight.shape[1]
-    tile = 512
+    tile = min(1024, units)
     sums = (2, span)
     across = (span, tile)
     tiled = lambda n: (0, n)
@@ -829,7 +829,7 @@
 def pre_back(scaled, active, slope, own, other, own_back, other_back, weight, full, after=()):
     span, units = active.shape
     model = weight.shape[0]
-    tile = 512
+    tile = min(1024, units)
     sums = (2, span)
     across = (span, tile)
     tiled = lambda n: (0, n)
@@ -1209,6 +1209,28 @@
     )[0]
 
 
+def finish_kernel(own, far, out):
+    out[...] = (own[...].astype(F32) + far[...].astype(F32)).T
+
+
+def finish_rows(rows, far, after=()):
+    chunk, width = far.shape
+    tile = min(512, width)
+    return call(
+        finish_kernel,
+        "finish",
+        (width // tile,),
+        [
+            (rows, (chunk, tile), lambda n: (1, n)),
+            (far, (chunk, tile), lambda n: (0, n)),
+        ],
+        [((width, chunk), F32, (tile, chunk), lambda n: (n, 0))],
+        [],
+        2e-6 * chunk * width,
+        after,
+    )[0]
+
+
 class ScatterSum:
     def __init__(self, parts, groups, z_first=False):
         away, self.kept = parts
@@ -1231,12 +1253,12 @@
         pieces = [(self.kept, half, 0), (self.got, half, 0), (self.far, 0, 0)]
         return add(pieces, half, after, None, us)
 
+    def finish(self, after=()):
+        half = self.rows.shape[0] // 2
+        far = exchange(self.rows[:half], "seq", self.groups, 2)
+        return finish_rows(self.rows, far, after)
+
     def chips(self, after=(), us=None):
-        if self.z_first:
-            half = self.rows.shape[0] // 2
-            far = exchange(self.rows[:half], "seq", self.groups, 2)
-            self.out = self.rows[half:].astype(F32) + far.astype(F32)
-            return self.out
         own = self.own(after, us)
         self.raw = lax.psum_scatter(own, "dp", scatter_dimension=0, tiled=True)
         self.out = self.raw.astype(F32)
@@ -1531,15 +1553,16 @@
             grad_input = input_grad(0, [first_terms], None, [gain_rows])
             gain_rows = axis_sum(gain_rows, "dp", devices)
             last = [terms[0][1], gain_rows, grad_input]
-    gain_rows = axis_sum(relay(gain_rows, [own]), "seq", groups)
-    down_sum.chips()
-    out_sum.chips()
+    gain_rows = relay(gain_rows, [own])
+    grad_down = down_sum.finish([gain_rows])
+    grad_out = out_sum.finish([grad_down])
+    gain_rows = axis_sum(gain_rows, "seq", groups)
     pieces = [
         lax.dynamic_slice_in_dim(heads_rows, jnp.bitwise_xor(place, n) * chunk, chunk, 0)
         for n in range(groups)
     ]
     pieces = pass_round(pieces, groups)
-    grad_input = input_grad(1, terms, grad_input, [gain_rows])
+    grad_input = input_grad(1, terms, grad_input, [gain_rows, grad_out])
     rows = jnp.stack(in_order(pieces, place)).astype(F32)
     grad_qkv_w = rows.reshape(groups, chunk, 3, share).transpose(2, 1, 0, 3)
     grad_qkv_w = grad_qkv_w.reshape(3, chunk, local_width)
@@ -1549,9 +1572,9 @@
         results.reshape(sequences, span, model),
         grad_input,
         grad_qkv_w,
-        out_sum.out.T,
+        grad_out,
         in_sum.out,
-        down_sum.out.T,
+        grad_down,
         one,
         two.reshape(gain_attn.shape),
         three,

time: 909 us -> 903 us (level)
    pallas_call x42 -> x44, Pallas kernels: 538 us -> 533 us  [call(): pl.pallas_call(run, grid_spec=pltpu.PrefetchScalarGridSpec(num_scalar_pre...]
  transfers between devices with their start and end apart: 76 -> 76, of which waited for: 25 -> 26; matrix products, arithmetic and copies ran while one was open for 5% -> 4% of each run, Pallas kernels for 65% -> 64%
where the time goes in v7:
time: 903 us; the launch traced here: 899 us
  Pallas kernels  593 us (66%)
  waiting for transfers between devices  162 us (18%)
  starting transfers between devices  64.1 us (7%)
  local copies, waits for them, and re-layouts  52 us (6%)
  between operations  15.2 us (2%)
  other arithmetic  13 us (1%)
    pallas_call x44, Pallas kernels, call(): pl.pallas_call(run, grid_spec=pltpu.PrefetchScalarGridSpec(num_scalar_pre...  533 us
    ppermute x69, waiting for transfers between devices, exchange(): return lax.ppermute(array, axis, [(n, n ^ offset) for n in range(size)])  160 us
    ppermute x69, starting transfers between devices, exchange(): return lax.ppermute(array, axis, [(n, n ^ offset) for n in range(size)])  63.6 us
    pallas_call x3, Pallas kernels, weight_grad(): pl.pallas_call(partial(weight_grad_kernel, sequences=sequences, devices=d...  59.5 us
    unnamed x131, local copies, waits for them, and re-layouts  27.7 us
  transfers between devices with their start and end apart: 76, of which 26 were waited for; matrix products, arithmetic and copies ran while one was open for 4% of the time, Pallas kernels for 64%

profile of v7, /device:TPU:0, one launch (start us, length us, event | category | flops | bytes accessed | tf_op | source)
XLA Modules:
  0.0 899.2 jit_solution(10821862750984397244)
XLA Ops:
  12.7 2.6 collective-permute-start.1
  15.3 4.8 slice_bitcast_fusion
  21.5 4.2 collective-permute-done.2
  26.9 3.3 relay.4
  32.3 2.6 collective-permute-start.4
  37.6 3.1 collective-permute-done.5
  41.5 36.7 %collective-permute-done.7.refs_3_ = bf16[512,2048]{1,0:T(8,128)(2,1)} collective-permute-done((bf16[512,2048]{1,0:T(8,128)(2,1)}, bf16[512,2048]{1,0:T(8,128)(2,1)}, u32[]{:S(2)}, u32[]{:S(2)}) %collective-permute-start.7) | collective-permute-done | bytes 2097184 | tf_op jit(solution)/shard_map/ppermute | solution.py:1054
  78.2 2.5 pack.1
  84.0 2.4 power_multiply_fusion.1
  97.5 18.3 %project.2 = (bf16[2048,2048]{1,0:T(8,128)(2,1)}, bf16[2048,768]{1,0:T(8,128)(2,1)}) custom-call(s32[1]{0:T(128)} %bitcast.14.refs_0_.place, bf16[512,2048]{1,0:T(8,128)(2,1)} %get-tuple-element.221.refs_1_, bf16[512,2048]{1,0:T(8,128)(2,1)} %collective-permute-done.6.refs_2_, bf16[512,2048]{1,0:T(8,128)(2,1)} %collective-permute-done.7.refs_3_, ...), custom_call_target="tpu_custom_call" | custom-call | flops 4026531840 | tf_op jit(solution)/shard_map/project/pallas_call | solution.py:481
  115.9 31.2 %attend.2 = (bf16[512,256]{1,0:T(8,128)(2,1)}, bf16[512,256]{1,0:T(8,128)(2,1)}, bf16[512,256]{1,0:T(8,128)(2,1)}, bf16[512,256]{1,0:T(8,128)(2,1)}, f32[4,2048]{1,0:T(4,128)}) custom-call(s32[2]{0:T(128)} %pad_add_fusion.refs_0_, bf16[2048,768]{1,0:T(8,128)(2,1)} %get-tuple-element.100.refs_1_), custom_call_target="tpu_custom_call" | custom-call | flops 7784628224 | tf_op jit(solution)/shard_map/attend/pallas_call | solution.py:481
  147.1 9.6 %collective-permute-done.13.refs_0_.refs_3_ = bf16[512,2048]{1,0:T(8,128)(2,1)} collective-permute-done((bf16[512,2048]{1,0:T(8,128)(2,1)S(1)}, bf16[512,2048]{1,0:T(8,128)(2,1)}, u32[]{:S(2)}, u32[]{:S(2)}) %collective-permute-start.13) | collective-permute-done | bytes 2097184 | tf_op jit(solution)/shard_map/ppermute | solution.py:1054
  156.7 3.8 relay.5.refs_11_
  162.3 2.5 collective-permute-start.10
  166.2 18.6 %project.3 = (bf16[2048,2048]{1,0:T(8,128)(2,1)}, bf16[2048,768]{1,0:T(8,128)(2,1)}) custom-call(s32[1]{0:T(128)} %bitcast.14.refs_0_.place, bf16[512,2048]{1,0:T(8,128)(2,1)} %get-tuple-element.220.refs_2_.refs_1_, bf16[512,2048]{1,0:T(8,128)(2,1)} %collective-permute-done.12.refs_2_, bf16[512,2048]{1,0:T(8,128)(2,1)} %collective-permute-done.13.refs_0_.refs_3_, ...), custom_call_target="tpu_custom_call" | custom-call | flops 4026531840 | tf_op jit(solution)/shard_map/project/pallas_call | solution.py:481
  184.8 29.4 %attend.3 = (bf16[512,256]{1,0:T(8,128)(2,1)}, bf16[512,256]{1,0:T(8,128)(2,1)}, bf16[512,256]{1,0:T(8,128)(2,1)}, bf16[512,256]{1,0:T(8,128)(2,1)}, f32[4,2048]{1,0:T(4,128)}) custom-call(s32[2]{0:T(128)} %pad_add_fusion.1.refs_0_, bf16[2048,768]{1,0:T(8,128)(2,1)} %get-tuple-element.106.refs_1_), custom_call_target="tpu_custom_call" | custom-call | flops 7784628224 | tf_op jit(solution)/shard_map/attend/pallas_call | solution.py:481
  214.4 3.3 collective-permute-start.16
  217.8 12.8 %collective-permute-done.16.refs_7_.refs_3_ = bf16[512,256]{1,0:T(8,128)(2,1)S(1)} collective-permute-done((bf16[512,256]{1,0:T(8,128)(2,1)}, bf16[512,256]{1,0:T(8,128)(2,1)S(1)}, u32[]{:S(2)}, u32[]{:S(2)}) %collective-permute-start.16) | collective-permute-done | bytes 262176 | tf_op jit(solution)/shard_map/ppermute | solution.py:1054
  230.6 10.9 %collective-permute-done.17.refs_8_.refs_4_ = bf16[512,256]{1,0:T(8,128)(2,1)S(1)} collective-permute-done((bf16[512,256]{1,0:T(8,128)(2,1)}, bf16[512,256]{1,0:T(8,128)(2,1)S(1)}, u32[]{:S(2)}, u32[]{:S(2)}) %collective-permute-start.17) | collective-permute-done | bytes 262176 | tf_op jit(solution)/shard_map/ppermute | solution.py:1054
  242.1 2.6 collect.2
  245.1 2.6 collect.3
  252.4 6.6 out_branch.3
  260.7 4.9 out_branch.4
  265.9 5.0 out_branch.5
  272.7 35.0 %collective-permute-done.20.refs_2_ = bf16[512,2048]{1,0:T(8,128)(2,1)S(1)} collective-permute-done((bf16[512,2048]{1,0:T(8,128)(2,1)}, bf16[512,2048]{1,0:T(8,128)(2,1)S(1)}, u32[]{:S(2)}, u32[]{:S(2)}) %collective-permute-start.20) | collective-permute-done | bytes 2097184 | tf_op jit(solution)/shard_map/ppermute | solution.py:1054
  309.1 22.9 %widen.3 = (f32[512,2048]{1,0:T(8,128)}, bf16[512,2048]{1,0:T(8,128)(2,1)}, bf16[512,4096]{1,0:T(8,128)(2,1)}, bf16[512,4096]{1,0:T(8,128)(2,1)}, f32[2,512]{1,0:T(2,128)}) custom-call(bf16[1024,2048]{1,0:T(8,128)(2,1)} %bitcast.63, bf16[512,2048]{1,0:T(8,128)(2,1)} %get-tuple-element.115.refs_5_.refs_1_, bf16[512,2048]{1,0:T(8,128)(2,1)} %copy-done.7, ...), custom_call_target="tpu_custom_call" | custom-call | flops 5798205952 | tf_op jit(solution)/shard_map/widen/pallas_call | solution.py:481
  334.8 14.4 %widen.4 = (f32[512,2048]{1,0:T(8,128)}, bf16[512,2048]{1,0:T(8,128)(2,1)}, bf16[512,4096]{1,0:T(8,128)(2,1)}, bf16[512,4096]{1,0:T(8,128)(2,1)}, f32[2,512]{1,0:T(2,128)}) custom-call(bf16[1024,2048]{1,0:T(8,128)(2,1)} %bitcast.64, bf16[256,2048]{1,0:T(8,128)(2,1)} %get-tuple-element.118.refs_6_.refs_1_, bf16[256,2048]{1,0:T(8,128)(2,1)} %copy-done.19, ...), custom_call_target="tpu_custom_call" | custom-call | flops 2899102976 | tf_op jit(solution)/shard_map/widen/pallas_call | solution.py:481
  352.9 14.2 %widen.5 = (f32[512,2048]{1,0:T(8,128)}, bf16[512,2048]{1,0:T(8,128)(2,1)}, bf16[512,4096]{1,0:T(8,128)(2,1)}, bf16[512,4096]{1,0:T(8,128)(2,1)}, f32[2,512]{1,0:T(2,128)}) custom-call(bf16[1024,2048]{1,0:T(8,128)(2,1)} %bitcast.65, ...), custom_call_target="tpu_custom_call", output_to_operand_aliasing={{0}: (5, {}), {1}: (6, {}), {2}: (7, {}), {3}: (8, {}), {4}... | custom-call | flops 2899102976 | tf_op jit(solution)/shard_map/widen/pallas_call | solution.py:481
  371.6 25.9 %weight_grad.3 = (bf16[1024,4096]{1,0:T(8,128)(2,1)}, bf16[1024,4096]{1,0:T(8,128)(2,1)}) custom-call(s32[1]{0:T(128)} %bitcast.14.refs_0_.place, bf16[1024,2048]{1,0:T(8,128)(2,1)} %bitcast.68, bf16[1024,2048]{1,0:T(8,128)(2,1)} %bitcast.69, bf16[512,4096]{1,0:T(8,128)(2,1)} %get-tuple-element.120.refs_2_.refs_3_.refs_1_, ...), custom_call_target="tpu_custom_call" | custom-call | flops 6227702784 | tf_op jit(solution)/shard_map/weight_grad/pallas_call | solution.py:441
  397.5 26.4 %wide_back.1 = (bf16[512,4096]{1,0:T(8,128)(2,1)}, bf16[512,4096]{1,0:T(8,128)(2,1)}, f32[2,512]{1,0:T(2,128)}, f32[2,512]{1,0:T(2,128)}, f32[1,4096]{1,0:T(1,128)}) custom-call(bf16[1024,2048]{1,0:T(8,128)(2,1)} %bitcast.70, bf16[4096,2048]{1,0:T(8,128)(2,1)} %all-gather.4.cloned.1.call-done.refs_1_, f32[1,4096]{1,0:T(1,128)} %reshape.280.refs_8_.refs_2_.refs_0_, ...), custom_call_target="tpu_custom_call" | custom-call | flops 7516192768 | tf_op jit(solution)/shard_map/wide_back/pallas_call | solution.py:481
  423.9 11.3 %add.201.refs_8_ = bf16[1024,4096]{1,0:T(8,128)(2,1)} custom-call(bf16[1024,4096]{1,0:T(8,128)(2,1)} %get-tuple-element.136.refs_0_, bf16[1024,4096]{1,0:T(8,128)(2,1)} %collective-permute-done.27.refs_1_, f32[2,512]{1,0:T(2,128)} %get-tuple-element.132.refs_2_.refs_5_), custom_call_target="tpu_custom_call" | custom-call | flops 1572864000 | tf_op jit(solution)/shard_map/add/pallas_call | solution.py:481
  441.7 19.7 %pre_back.2 = (bf16[512,4096]{1,0:T(8,128)(2,1)}, bf16[512,2048]{1,0:T(8,128)(2,1)}) custom-call(bf16[512,4096]{1,0:T(8,128)(2,1)} %get-tuple-element.133.refs_0_, bf16[512,4096]{1,0:T(8,128)(2,1)} %get-tuple-element.120.refs_2_.refs_3_.refs_1_, bf16[512,4096]{1,0:T(8,128)(2,1)} %get-tuple-element.134.refs_2_, ...), custom_call_target="tpu_custom_call" | custom-call | flops 4939212288 | tf_op jit(solution)/shard_map/pre_back/pallas_call | solution.py:481
  461.5 18.8 %pre_back.3 = (bf16[512,4096]{1,0:T(8,128)(2,1)}, bf16[512,2048]{1,0:T(8,128)(2,1)}) custom-call(bf16[512,4096]{1,0:T(8,128)(2,1)} %get-tuple-element.130.refs_0_, bf16[512,4096]{1,0:T(8,128)(2,1)} %get-tuple-element.127.refs_3_.refs_4_.refs_1_, bf16[512,4096]{1,0:T(8,128)(2,1)} %get-tuple-element.131.refs_2_, ...), custom_call_target="tpu_custom_call" | custom-call | flops 4939212288 | tf_op jit(solution)/shard_map/pre_back/pallas_call | solution.py:481
  482.3 25.9 %narrow.1.refs_10_.refs_0_ = bf16[1024,2048]{1,0:T(8,128)(2,1)} custom-call(f32[1,4096]{1,0:T(1,128)} %reshape.280.refs_8_.refs_2_.refs_0_, bf16[4096,2048]{1,0:T(8,128)(2,1)} %all-gather.4.cloned.1.call-done.refs_1_, bf16[512,4096]{1,0:T(8,128)(2,1)} %get-tuple-element.120.refs_2_.refs_3_.refs_1_, ...), custom_call_target="tpu_custom_call" | custom-call | flops 6871947776 | tf_op jit(solution)/shard_map/narrow/pallas_call | solution.py:481
  511.6 13.1 %middle.2 = (f32[512,2048]{1,0:T(8,128)}, bf16[512,2048]{1,0:T(8,128)(2,1)}, f32[512,1024]{1,0:T(8,128)}, f32[2,512]{1,0:T(2,128)}, f32[1,2048]{1,0:T(1,128)}, /*index=5*/f32[1,1024]{1,0:T(1,128)}) custom-call(bf16[1024,2048]{1,0:T(8,128)(2,1)} %bitcast.71, bf16[512,2048]{1,0:T(8,128)(2,1)} %get-tuple-element.137.refs_8_.refs_1_, ...), custom_call_target="tpu_custom_call" | custom-call | flops 3221225472 | tf_op jit(solution)/shard_map/middle/pallas_call | solution.py:481
  524.8 23.8 %weight_grad.4 = (bf16[1024,4096]{1,0:T(8,128)(2,1)}, bf16[1024,4096]{1,0:T(8,128)(2,1)}) custom-call(s32[1]{0:T(128)} %bitcast.14.refs_0_.place, bf16[512,2048]{1,0:T(8,128)(2,1)} %get-tuple-element.143.refs_0_, bf16[512,2048]{1,0:T(8,128)(2,1)} %get-tuple-element.144.refs_1_, bf16[512,4096]{1,0:T(8,128)(2,1)} %get-tuple-element.145.refs_2_, ...), custom_call_target="tpu_custom_call" | custom-call | flops 6227702784 | tf_op jit(solution)/shard_map/weight_grad/pallas_call | solution.py:441
  548.6 3.9 collective-permute-done.29.refs_8_.refs_2_
  553.8 4.1 share_out.2
  557.9 12.5 %middle.3 = (f32[512,2048]{1,0:T(8,128)}, bf16[512,2048]{1,0:T(8,128)(2,1)}, f32[512,1024]{1,0:T(8,128)}, f32[2,512]{1,0:T(2,128)}, f32[1,2048]{1,0:T(1,128)}, /*index=5*/f32[1,1024]{1,0:T(1,128)}) custom-call(bf16[1024,2048]{1,0:T(8,128)(2,1)} %bitcast.72, bf16[512,2048]{1,0:T(8,128)(2,1)} %get-tuple-element.138.refs_8_.refs_1_, ...), custom_call_target="tpu_custom_call" | custom-call | flops 3221225472 | tf_op jit(solution)/shard_map/middle/pallas_call | solution.py:481
  573.0 6.0 add.202.refs_7_
  579.7 4.0 share_out.3
  585.9 9.7 %weight_grad.5 = (bf16[1024,1024]{1,0:T(8,128)(2,1)}, bf16[1024,1024]{1,0:T(8,128)(2,1)}) custom-call(s32[1]{0:T(128)} %bitcast.14.refs_0_.place, bf16[512,2048]{1,0:T(8,128)(2,1)} %get-tuple-element.159.refs_0_, bf16[512,2048]{1,0:T(8,128)(2,1)} %get-tuple-element.160.refs_1_, bf16[512,1024]{1,0:T(8,128)(2,1)} %get-tuple-element.161.refs_2_, ...), custom_call_target="tpu_custom_call" | custom-call | flops 1556925696 | tf_op jit(solution)/shard_map/weight_grad/pallas_call | solution.py:441
  599.0 45.3 %attend_back.2.refs_2_.refs_1_.refs_0_ = bf16[2048,768]{1,0:T(8,128)(2,1)} custom-call(s32[2]{0:T(128)} %pad_add_fusion.refs_0_, bf16[2048,768]{1,0:T(8,128)(2,1)} %get-tuple-element.100.refs_1_, bf16[512,256]{1,0:T(8,128)(2,1)} %get-tuple-element.148.refs_10_.refs_2_, bf16[512,256]{1,0:T(8,128)(2,1)} %copy-done.49, bf16[512,256]{1,0:T(8,128)(2,1)} %copy-done.51, ...), custom_call_target="tpu_custom_call" | custom-call | flops 281857228800 | tf_op jit(solution)/shard_map/attend_back/pallas_call | solution.py:481
  644.4 6.2 add.203.refs_5_
  652.7 17.4 %first_back.2 = (bf16[512,1024]{1,0:T(8,128)(2,1)}, bf16[512,1024]{1,0:T(8,128)(2,1)}, bf16[512,1024]{1,0:T(8,128)(2,1)}, bf16[512,1024]{1,0:T(8,128)(2,1)}, bf1...) custom-call(s32[4]{0:T(128)} %broadcast_xor_fusion.refs_0_, bf16[2048,768]{1,0:T(8,128)(2,1)} %attend_back.2.refs_2_.refs_1_.refs_0_, ...), custom_call_target="tpu_custom_call" | custom-call | flops 3623878656 | tf_op jit(solution)/shard_map/first_back/pallas_call | solution.py:481
  670.8 2.3 collective-permute-done.42.refs_1_
  675.5 4.2 add_halves.2
  680.5 8.9 collective-permute-done.37.refs_2_
  690.8 7.3 add.204.refs_15_
  698.1 41.4 %attend_back.3.refs_5_.refs_1_ = bf16[2048,768]{1,0:T(8,128)(2,1)} custom-call(s32[2]{0:T(128)} %pad_add_fusion.1.refs_0_, bf16[2048,768]{1,0:T(8,128)(2,1)} %get-tuple-element.106.refs_1_, bf16[512,256]{1,0:T(8,128)(2,1)} %get-tuple-element.152.refs_4_.refs_2_, bf16[512,256]{1,0:T(8,128)(2,1)} %copy-done.46, bf16[512,256]{1,0:T(8,128)(2,1)} %copy-done.47, ...), custom_call_target="tpu_custom_call" | custom-call | flops 11274289152 | tf_op jit(solution)/shard_map/attend_back/pallas_call | solution.py:481
  741.3 5.0 join_halves.1.refs_5_.refs_3_
  747.8 17.5 %first_back.3 = (bf16[512,1024]{1,0:T(8,128)(2,1)}, bf16[512,1024]{1,0:T(8,128)(2,1)}, bf16[512,1024]{1,0:T(8,128)(2,1)}, bf16[512,1024]{1,0:T(8,128)(2,1)}, bf1...) custom-call(s32[4]{0:T(128)} %broadcast_xor_fusion.refs_0_, bf16[2048,768]{1,0:T(8,128)(2,1)} %attend_back.3.refs_5_.refs_1_, ...), custom_call_target="tpu_custom_call" | custom-call | flops 3623878656 | tf_op jit(solution)/shard_map/first_back/pallas_call | solution.py:481
  765.9 10.4 %result.1.refs_3_ = bf16[1024,2048]{1,0:T(8,128)(2,1)} custom-call(bf16[1024,2048]{1,0:T(8,128)(2,1)} %narrow.1.refs_10_.refs_0_, bf16[1024,2048]{1,0:T(8,128)(2,1)} %collective-permute-done.28.refs_1_, f32[512,2048]{1,0:T(8,128)} %get-tuple-element.139.refs_3_.refs_2_, f32[512,2048]{1,0:T(8,128)} %get-tuple-element.140.refs_3_, ...), custom_call_target="tpu_custom_call" | custom-call | flops 74999996416 | tf_op jit(solution)/shard_map/result/pallas_call | solution.py:481
  778.2 4.2 add_halves.3
  783.0 18.8 %heads_grad.1.refs_3_ = bf16[2048,768]{1,0:T(8,128)(2,1)} custom-call(bf16[2048,768]{1,0:T(8,128)(2,1)} %attend_back.2.refs_2_.refs_1_.refs_0_, bf16[2048,768]{1,0:T(8,128)(2,1)} %attend_back.3.refs_5_.refs_1_, bf16[2048,2048]{1,0:T(8,128)(2,1)} %get-tuple-element.164.refs_2_, bf16[2048,2048]{1,0:T(8,128)(2,1)} %get-tuple-element.170.refs_2_.refs_3_, ...), custom_call_target="tpu_custom_call" | custom-call | flops 4831838208 | tf_op jit(solution)/shard_map/heads_grad/pallas_call | solution.py:481
  803.2 3.1 collective-permute-done.52.refs_4_
  809.8 3.9 add.205.refs_1_.refs_3_
  819.7 9.7 %collective-permute-start.58 = (f32[16,576]{1,0:T(8,128)}, f32[16,576]{1,0:T(8,128)S(1)}, u32[]{:S(2)}, u32[]{:S(2)}) collective-permute-start(f32[16,576]{1,0:T(8,128)} %relay.6.refs_5_), channel_id=1, source_target_pairs={{0,24},{8,16},{16,8},{24,0},{1,25},{9,17},{17,9},{25,1},{2,26},{10... | collective-permute-start | bytes 110600 | tf_op jit(solution)/shard_map/ppermute | solution.py:1054
  830.4 2.3 collective-permute-done.58
  832.7 7.3 input_grad.2.refs_5_.refs_7_
  841.5 4.0 add.206.refs_1_.refs_5_
  851.7 14.7 %collective-permute-done.65.refs_1_ = bf16[128,4096]{1,0:T(8,128)(2,1)} collective-permute-done((bf16[128,4096]{1,0:T(8,128)(2,1)}, bf16[128,4096]{1,0:T(8,128)(2,1)}, u32[]{:S(2)}, u32[]{:S(2)}) %collective-permute-start.65) | collective-permute-done | bytes 1048608 | tf_op jit(solution)/shard_map/ppermute | solution.py:1054
  866.5 6.2 finish.2.refs_2_
  882.1 7.2 input_grad.3
  (367 shorter events, 120.6 us)
Async XLA Ops:
  7.2 90.3 %all-gather.6.cloned.1.call-start = ((), (), s32[]{:S(2)}) async-start(), calls=%async_computation.5 | async-start | bytes 3932160 | tf_op jit(solution)/shard_map/all_gather | solution.py:1365
  12.1 8.0 collective-permute-start
  12.7 8.9 collective-permute-start.1
  15.3 10.5 %collective-permute-start.2 = (bf16[144,768]{1,0:T(8,128)(2,1)S(1)}, bf16[144,768]{1,0:T(8,128)(2,1)S(1)}, u32[]{:S(2)}, u32[]{:S(2)}) collective-permute-start(bf16[144,768]{1,0:T(8,128)(2,1)S(1)} %get-tuple-element.249), channel_id=1, source_target_pairs={{0,6},{2,4},{4,2},{6,0},{1,7},{3,5},{5,3},{7,1},{8,14},{10,12},{12... | collective-permute-start | bytes 663560 | tf_op jit(solution)/shard_map/ppermute | solution.py:1054
  30.2 222.3 %all-gather.8.cloned.1.call-start = ((), (), s32[]{:S(2)}) async-start(), calls=%async_computation.6 | async-start | bytes 22282240 | tf_op jit(solution)/shard_map/all_gather | solution.py:1378
  30.2 48.0 %collective-permute-start.7 = (bf16[512,2048]{1,0:T(8,128)(2,1)}, bf16[512,2048]{1,0:T(8,128)(2,1)}, u32[]{:S(2)}, u32[]{:S(2)}) collective-permute-start(bf16[512,2048]{1,0:T(8,128)(2,1)} %get-tuple-element.221.refs_1_), channel_id=1, source_target_pairs={{0,4},{2,6},{4,0},{6,2},{1,5},{3,7},{5,1},{7,3},{8,12},{10,14},{12... | collective-permute-start | bytes 6291464 | tf_op jit(solution)/shard_map/ppermute | solution.py:1054
  35.0 5.8 collective-permute-start.5
  80.7 316.8 %all-gather.4.cloned.1.call-start = ((), (), s32[]{:S(2)}) async-start(), calls=%async_computation.4 | async-start | bytes 17825792 | tf_op jit(solution)/shard_map/all_gather | solution.py:1381
  81.5 504.4 %reduce-scatter.5.cloned.1.call-start = ((), (), s32[]{:S(2)}) async-start(), calls=%async_computation.7 | async-start | bytes 10485760 | tf_op jit(solution)/shard_map/reduce_scatter | solution.py:1245
  81.7 15.8 %collective-permute-start.6 = (bf16[512,2048]{1,0:T(8,128)(2,1)}, bf16[512,2048]{1,0:T(8,128)(2,1)}, u32[]{:S(2)}, u32[]{:S(2)}) collective-permute-start(bf16[512,2048]{1,0:T(8,128)(2,1)} %get-tuple-element.221.refs_1_), channel_id=1, source_target_pairs={{0,2},{2,0},{4,6},{6,4},{1,3},{3,1},{5,7},{7,5},{8,10},{10,8},{12,... | collective-permute-start | bytes 6291464 | tf_op jit(solution)/shard_map/ppermute | solution.py:1054
  81.8 15.8 %collective-permute-start.8 = (bf16[512,2048]{1,0:T(8,128)(2,1)}, bf16[512,2048]{1,0:T(8,128)(2,1)}, u32[]{:S(2)}, u32[]{:S(2)}) collective-permute-start(bf16[512,2048]{1,0:T(8,128)(2,1)} %collective-permute-done.7.refs_3_), channel_id=1, source_target_pairs={{0,2},{2,0},{4,6},{6,4},{1,3},{3,1},{5,7},{7,5},{8,10},{10,8},{12,... | collective-permute-start | bytes 6291464 | tf_op jit(solution)/shard_map/ppermute | solution.py:1054
  82.3 74.4 %collective-permute-start.13 = (bf16[512,2048]{1,0:T(8,128)(2,1)S(1)}, bf16[512,2048]{1,0:T(8,128)(2,1)}, u32[]{:S(2)}, u32[]{:S(2)}) collective-permute-start(bf16[512,2048]{1,0:T(8,128)(2,1)S(1)} %copy-done), channel_id=1, source_target_pairs={{0,4},{2,6},{4,0},{6,2},{1,5},{3,7},{5,1},{7,3},{8,12},{10,14},{12... | collective-permute-start | bytes 6291464 | tf_op jit(solution)/shard_map/ppermute | solution.py:1054
  84.0 80.8 %collective-permute-start.12 = (bf16[512,2048]{1,0:T(8,128)(2,1)S(1)}, bf16[512,2048]{1,0:T(8,128)(2,1)}, u32[]{:S(2)}, u32[]{:S(2)}) collective-permute-start(bf16[512,2048]{1,0:T(8,128)(2,1)S(1)} %copy-done), channel_id=1, source_target_pairs={{0,2},{2,0},{4,6},{6,4},{1,3},{3,1},{5,7},{7,5},{8,10},{10,8},{12,... | collective-permute-start | bytes 6291464 | tf_op jit(solution)/shard_map/ppermute | solution.py:1054
  161.7 55.9 %collective-permute-start.9 = (bf16[512,256]{1,0:T(8,128)(2,1)S(1)}, bf16[512,256]{1,0:T(8,128)(2,1)S(1)}, u32[]{:S(2)}, u32[]{:S(2)}) collective-permute-start(bf16[512,256]{1,0:T(8,128)(2,1)S(1)} %copy-done.43), channel_id=1, source_target_pairs={{0,2},{2,0},{4,6},{6,4},{1,3},{3,1},{5,7},{7,5},{8,10},{10,8},{12,... | collective-permute-start | bytes 786440 | tf_op jit(solution)/shard_map/ppermute | solution.py:1054
  162.3 55.5 %collective-permute-start.10 = (bf16[512,256]{1,0:T(8,128)(2,1)S(1)}, bf16[512,256]{1,0:T(8,128)(2,1)S(1)}, u32[]{:S(2)}, u32[]{:S(2)}) collective-permute-start(bf16[512,256]{1,0:T(8,128)(2,1)S(1)} %copy-done.44), channel_id=1, source_target_pairs={{0,4},{2,6},{4,0},{6,2},{1,5},{3,7},{5,1},{7,3},{8,12},{10,14},{12... | collective-permute-start | bytes 786440 | tf_op jit(solution)/shard_map/ppermute | solution.py:1054
  164.8 52.9 %collective-permute-start.11 = (bf16[512,256]{1,0:T(8,128)(2,1)S(1)}, bf16[512,256]{1,0:T(8,128)(2,1)S(1)}, u32[]{:S(2)}, u32[]{:S(2)}) collective-permute-start(bf16[512,256]{1,0:T(8,128)(2,1)S(1)} %copy-done.45), channel_id=1, source_target_pairs={{0,6},{2,4},{4,2},{6,0},{1,7},{3,5},{5,3},{7,1},{8,14},{10,12},{12... | collective-permute-start | bytes 786440 | tf_op jit(solution)/shard_map/ppermute | solution.py:1054
  214.4 16.2 %collective-permute-start.16 = (bf16[512,256]{1,0:T(8,128)(2,1)}, bf16[512,256]{1,0:T(8,128)(2,1)S(1)}, u32[]{:S(2)}, u32[]{:S(2)}) collective-permute-start(bf16[512,256]{1,0:T(8,128)(2,1)} %get-tuple-element.109.refs_8_), channel_id=1, source_target_pairs={{0,4},{2,6},{4,0},{6,2},{1,5},{3,7},{5,1},{7,3},{8,12},{10,14},{12... | collective-permute-start | bytes 786440 | tf_op jit(solution)/shard_map/ppermute | solution.py:1054
  217.7 23.8 %collective-permute-start.17 = (bf16[512,256]{1,0:T(8,128)(2,1)}, bf16[512,256]{1,0:T(8,128)(2,1)S(1)}, u32[]{:S(2)}, u32[]{:S(2)}) collective-permute-start(bf16[512,256]{1,0:T(8,128)(2,1)} %get-tuple-element.110.refs_9_), channel_id=1, source_target_pairs={{0,6},{2,4},{4,2},{6,0},{1,7},{3,5},{5,3},{7,1},{8,14},{10,12},{12... | collective-permute-start | bytes 786440 | tf_op jit(solution)/shard_map/ppermute | solution.py:1054
  259.0 48.7 %collective-permute-start.20 = (bf16[512,2048]{1,0:T(8,128)(2,1)}, bf16[512,2048]{1,0:T(8,128)(2,1)S(1)}, u32[]{:S(2)}, u32[]{:S(2)}) collective-permute-start(bf16[512,2048]{1,0:T(8,128)(2,1)} %get-tuple-element.115.refs_5_.refs_1_), channel_id=1, source_target_pairs={{0,1},{1,0},{2,3},{3,2},{4,5},{5,4},{6,7},{7,6},{8,9},{9,8},{10,11... | collective-permute-start | bytes 6291464 | tf_op jit(solution)/shard_map/ppermute | solution.py:1054
  265.6 68.2 %collective-permute-start.22 = (bf16[256,2048]{1,0:T(8,128)(2,1)}, bf16[256,2048]{1,0:T(8,128)(2,1)S(1)}, u32[]{:S(2)}, u32[]{:S(2)}) collective-permute-start(bf16[256,2048]{1,0:T(8,128)(2,1)} %get-tuple-element.118.refs_6_.refs_1_), channel_id=1, source_target_pairs={{0,1},{1,0},{2,3},{3,2},{4,5},{5,4},{6,7},{7,6},{8,9},{9,8},{10,11... | collective-permute-start | bytes 3145736 | tf_op jit(solution)/shard_map/ppermute | solution.py:1054
  270.9 81.1 %collective-permute-start.21 = (bf16[256,2048]{1,0:T(8,128)(2,1)}, bf16[256,2048]{1,0:T(8,128)(2,1)S(1)}, u32[]{:S(2)}, u32[]{:S(2)}) collective-permute-start(bf16[256,2048]{1,0:T(8,128)(2,1)} %get-tuple-element.119.refs_5_.refs_1_), channel_id=1, source_target_pairs={{0,1},{1,0},{2,3},{3,2},{4,5},{5,4},{6,7},{7,6},{8,9},{9,8},{10,11... | collective-permute-start | bytes 3145736 | tf_op jit(solution)/shard_map/ppermute | solution.py:1054
  332.0 38.4 %collective-permute-start.23 = (f32[2,512]{1,0:T(2,128)}, f32[2,512]{1,0:T(2,128)S(1)}, u32[]{:S(2)}, u32[]{:S(2)}) collective-permute-start(f32[2,512]{1,0:T(2,128)} %get-tuple-element.121.refs_5_.refs_4_.refs_3_), channel_id=1, source_target_pairs={{0,1},{1,0},{2,3},{3,2},{4,5},{5,4},{6,7},{7,6},{8,9},{9,8},{10,11... | collective-permute-start | bytes 12296 | tf_op jit(solution)/shard_map/ppermute | solution.py:1054
  397.5 26.4 %collective-permute-start.27 = (bf16[1024,4096]{1,0:T(8,128)(2,1)}, bf16[1024,4096]{1,0:T(8,128)(2,1)}, u32[]{:S(2)}, u32[]{:S(2)}) collective-permute-start(bf16[1024,4096]{1,0:T(8,128)(2,1)} %get-tuple-element.129.refs_9_), channel_id=1, source_target_pairs={{0,2},{2,0},{4,6},{6,4},{1,3},{3,1},{5,7},{7,5},{8,10},{10,8},{12,... | collective-permute-start | bytes 25165832 | tf_op jit(solution)/shard_map/ppermute | solution.py:1054
  435.2 347.8 %reduce-scatter.9.cloned.1.call-start = ((), (), s32[]{:S(2)}) async-start(), calls=%async_computation.9 | async-start | bytes 2621440 | tf_op jit(solution)/shard_map/reduce_scatter | solution.py:1245
  461.4 48.8 %collective-permute-start.30 = (bf16[512,2048]{1,0:T(8,128)(2,1)}, bf16[512,2048]{1,0:T(8,128)(2,1)S(1)}, u32[]{:S(2)}, u32[]{:S(2)}) collective-permute-start(bf16[512,2048]{1,0:T(8,128)(2,1)} %get-tuple-element.137.refs_8_.refs_1_), channel_id=1, source_target_pairs={{0,1},{1,0},{2,3},{3,2},{4,5},{5,4},{6,7},{7,6},{8,9},{9,8},{10,11... | collective-permute-start | bytes 6291464 | tf_op jit(solution)/shard_map/ppermute | solution.py:1054
  480.3 72.3 %collective-permute-start.29 = (bf16[512,2048]{1,0:T(8,128)(2,1)}, bf16[512,2048]{1,0:T(8,128)(2,1)S(1)}, u32[]{:S(2)}, u32[]{:S(2)}) collective-permute-start(bf16[512,2048]{1,0:T(8,128)(2,1)} %get-tuple-element.138.refs_8_.refs_1_), channel_id=1, source_target_pairs={{0,1},{1,0},{2,3},{3,2},{4,5},{5,4},{6,7},{7,6},{8,9},{9,8},{10,11... | collective-permute-start | bytes 6291464 | tf_op jit(solution)/shard_map/ppermute | solution.py:1054
  524.7 27.8 %collective-permute-start.31 = (f32[2,512]{1,0:T(2,128)}, f32[2,512]{1,0:T(2,128)S(1)}, u32[]{:S(2)}, u32[]{:S(2)}) collective-permute-start(f32[2,512]{1,0:T(2,128)} %get-tuple-element.142.refs_4_.refs_5_), channel_id=1, source_target_pairs={{0,1},{1,0},{2,3},{3,2},{4,5},{5,4},{6,7},{7,6},{8,9},{9,8},{10,11... | collective-permute-start | bytes 12296 | tf_op jit(solution)/shard_map/ppermute | solution.py:1054
  548.6 24.4 %collective-permute-start.33 = (bf16[1024,4096]{1,0:T(8,128)(2,1)}, bf16[1024,4096]{1,0:T(8,128)(2,1)}, u32[]{:S(2)}, u32[]{:S(2)}) collective-permute-start(bf16[1024,4096]{1,0:T(8,128)(2,1)} %get-tuple-element.147.refs_7_), channel_id=1, source_target_pairs={{0,2},{2,0},{4,6},{6,4},{1,3},{3,1},{5,7},{7,5},{8,10},{10,8},{12,... | collective-permute-start | bytes 25165832 | tf_op jit(solution)/shard_map/ppermute | solution.py:1054
  557.9 28.0 %collective-permute-start.38 = (bf16[512,256]{1,0:T(8,128)(2,1)}, bf16[512,256]{1,0:T(8,128)(2,1)S(1)}, u32[]{:S(2)}, u32[]{:S(2)}) collective-permute-start(bf16[512,256]{1,0:T(8,128)(2,1)} %get-tuple-element.156), channel_id=1, source_target_pairs={{0,2},{2,0},{4,6},{6,4},{1,3},{3,1},{5,7},{7,5},{8,10},{10,8},{12,... | collective-permute-start | bytes 786440 | tf_op jit(solution)/shard_map/ppermute | solution.py:1054
  570.5 8.6 collective-permute-start.32
  570.9 24.7 %collective-permute-start.39 = (bf16[512,256]{1,0:T(8,128)(2,1)S(1)}, bf16[512,256]{1,0:T(8,128)(2,1)S(1)}, u32[]{:S(2)}, u32[]{:S(2)}) collective-permute-start(bf16[512,256]{1,0:T(8,128)(2,1)S(1)} %copy-done.53), channel_id=1, source_target_pairs={{0,4},{2,6},{4,0},{6,2},{1,5},{3,7},{5,1},{7,3},{8,12},{10,14},{12... | collective-permute-start | bytes 786440 | tf_op jit(solution)/shard_map/ppermute | solution.py:1054
  573.0 24.0 %collective-permute-start.40 = (bf16[512,256]{1,0:T(8,128)(2,1)S(1)}, bf16[512,256]{1,0:T(8,128)(2,1)S(1)}, u32[]{:S(2)}, u32[]{:S(2)}) collective-permute-start(bf16[512,256]{1,0:T(8,128)(2,1)S(1)} %copy-done.50), channel_id=1, source_target_pairs={{0,6},{2,4},{4,2},{6,0},{1,7},{3,5},{5,3},{7,1},{8,14},{10,12},{12... | collective-permute-start | bytes 786440 | tf_op jit(solution)/shard_map/ppermute | solution.py:1054
  583.7 13.8 %collective-permute-start.34 = (bf16[512,256]{1,0:T(8,128)(2,1)}, bf16[512,256]{1,0:T(8,128)(2,1)S(1)}, u32[]{:S(2)}, u32[]{:S(2)}) collective-permute-start(bf16[512,256]{1,0:T(8,128)(2,1)} %get-tuple-element.153), channel_id=1, source_target_pairs={{0,2},{2,0},{4,6},{6,4},{1,3},{3,1},{5,7},{7,5},{8,10},{10,8},{12,... | collective-permute-start | bytes 786440 | tf_op jit(solution)/shard_map/ppermute | solution.py:1054
  583.9 13.6 %collective-permute-start.35 = (bf16[512,256]{1,0:T(8,128)(2,1)}, bf16[512,256]{1,0:T(8,128)(2,1)S(1)}, u32[]{:S(2)}, u32[]{:S(2)}) collective-permute-start(bf16[512,256]{1,0:T(8,128)(2,1)} %get-tuple-element.154), channel_id=1, source_target_pairs={{0,4},{2,6},{4,0},{6,2},{1,5},{3,7},{5,1},{7,3},{8,12},{10,14},{12... | collective-permute-start | bytes 786440 | tf_op jit(solution)/shard_map/ppermute | solution.py:1054
  585.9 11.7 %collective-permute-start.36 = (bf16[512,256]{1,0:T(8,128)(2,1)}, bf16[512,256]{1,0:T(8,128)(2,1)S(1)}, u32[]{:S(2)}, u32[]{:S(2)}) collective-permute-start(bf16[512,256]{1,0:T(8,128)(2,1)} %get-tuple-element.155), channel_id=1, source_target_pairs={{0,6},{2,4},{4,2},{6,0},{1,7},{3,5},{5,3},{7,1},{8,14},{10,12},{12... | collective-permute-start | bytes 786440 | tf_op jit(solution)/shard_map/ppermute | solution.py:1054
  595.6 93.8 %collective-permute-start.37 = (bf16[512,4096]{1,0:T(8,128)(2,1)}, bf16[512,4096]{1,0:T(8,128)(2,1)}, u32[]{:S(2)}, u32[]{:S(2)}) collective-permute-start(bf16[512,4096]{1,0:T(8,128)(2,1)} %add.202.refs_7_), channel_id=1, source_target_pairs={{0,4},{2,6},{4,0},{6,2},{1,5},{3,7},{5,1},{7,3},{8,12},{10,14},{12... | collective-permute-start | bytes 12582920 | tf_op jit(solution)/shard_map/ppermute | solution.py:1054
  597.0 47.4 %collective-permute-start.41 = (bf16[1024,1024]{1,0:T(8,128)(2,1)}, bf16[1024,1024]{1,0:T(8,128)(2,1)}, u32[]{:S(2)}, u32[]{:S(2)}) collective-permute-start(bf16[1024,1024]{1,0:T(8,128)(2,1)} %get-tuple-element.163.refs_15_), channel_id=1, source_target_pairs={{0,2},{2,0},{4,6},{6,4},{1,3},{3,1},{5,7},{7,5},{8,10},{10,8},{12,... | collective-permute-start | bytes 6291464 | tf_op jit(solution)/shard_map/ppermute | solution.py:1054
  650.6 132.4 %reduce-scatter.7.cloned.1.call-start = ((), (), s32[]{:S(2)}) async-start(), calls=%async_computation.8 | async-start | bytes 5242880 | tf_op jit(solution)/shard_map/reduce_scatter | solution.py:1263
  650.6 115.3 %collective-permute-start.28 = (bf16[1024,2048]{1,0:T(8,128)(2,1)}, bf16[1024,2048]{1,0:T(8,128)(2,1)}, u32[]{:S(2)}, u32[]{:S(2)}) collective-permute-start(bf16[1024,2048]{1,0:T(8,128)(2,1)} %narrow.1.refs_10_.refs_0_), channel_id=1, source_target_pairs={{0,1},{1,0},{2,3},{3,2},{4,5},{5,4},{6,7},{7,6},{8,9},{9,8},{10,11... | collective-permute-start | bytes 12582920 | tf_op jit(solution)/shard_map/ppermute | solution.py:1054
  670.7 68.9 %collective-permute-start.44 = (bf16[512,1024]{1,0:T(8,128)(2,1)}, bf16[512,1024]{1,0:T(8,128)(2,1)S(1)}, u32[]{:S(2)}, u32[]{:S(2)}) collective-permute-start(bf16[512,1024]{1,0:T(8,128)(2,1)} %get-tuple-element.171), channel_id=1, source_target_pairs={{0,2},{2,0},{4,6},{6,4},{1,3},{3,1},{5,7},{7,5},{8,10},{10,8},{12,... | collective-permute-start | bytes 3145736 | tf_op jit(solution)/shard_map/ppermute | solution.py:1054
  673.1 66.5 %collective-permute-start.45 = (bf16[512,1024]{1,0:T(8,128)(2,1)}, bf16[512,1024]{1,0:T(8,128)(2,1)S(1)}, u32[]{:S(2)}, u32[]{:S(2)}) collective-permute-start(bf16[512,1024]{1,0:T(8,128)(2,1)} %get-tuple-element.172), channel_id=1, source_target_pairs={{0,2},{2,0},{4,6},{6,4},{1,3},{3,1},{5,7},{7,5},{8,10},{10,8},{12,... | collective-permute-start | bytes 3145736 | tf_op jit(solution)/shard_map/ppermute | solution.py:1054
  679.7 59.9 %collective-permute-start.47 = (bf16[512,1024]{1,0:T(8,128)(2,1)}, bf16[512,1024]{1,0:T(8,128)(2,1)S(1)}, u32[]{:S(2)}, u32[]{:S(2)}) collective-permute-start(bf16[512,1024]{1,0:T(8,128)(2,1)} %get-tuple-element.173), channel_id=1, source_target_pairs={{0,4},{2,6},{4,0},{6,2},{1,5},{3,7},{5,1},{7,3},{8,12},{10,14},{12... | collective-permute-start | bytes 3145736 | tf_op jit(solution)/shard_map/ppermute | solution.py:1054
  689.4 50.2 %collective-permute-start.46 = (bf16[512,1024]{1,0:T(8,128)(2,1)}, bf16[512,1024]{1,0:T(8,128)(2,1)}, u32[]{:S(2)}, u32[]{:S(2)}) collective-permute-start(bf16[512,1024]{1,0:T(8,128)(2,1)} %get-tuple-element.169.refs_3_), channel_id=1, source_target_pairs={{0,4},{2,6},{4,0},{6,2},{1,5},{3,7},{5,1},{7,3},{8,12},{10,14},{12... | collective-permute-start | bytes 3145736 | tf_op jit(solution)/shard_map/ppermute | solution.py:1054
  698.1 177.3 %reduce-scatter.11.cloned.1.call-start = ((), (), s32[]{:S(2)}) async-start(), calls=%async_computation.10 | async-start | bytes 3932160 | tf_op jit(solution)/shard_map/reduce_scatter | solution.py:1520
  746.3 84.2 %collective-permute-start.59 = (bf16[512,2048]{1,0:T(8,128)(2,1)}, bf16[512,2048]{1,0:T(8,128)(2,1)}, u32[]{:S(2)}, u32[]{:S(2)}) collective-permute-start(bf16[512,2048]{1,0:T(8,128)(2,1)} %join_halves.1.refs_5_.refs_3_), channel_id=1, source_target_pairs={{0,1},{1,0},{2,3},{3,2},{4,5},{5,4},{6,7},{7,6},{8,9},{9,8},{10,11... | collective-permute-start | bytes 6291464 | tf_op jit(solution)/shard_map/ppermute | solution.py:1054
  765.3 42.5 %collective-permute-start.48 = (bf16[512,1024]{1,0:T(8,128)(2,1)}, bf16[512,1024]{1,0:T(8,128)(2,1)S(1)}, u32[]{:S(2)}, u32[]{:S(2)}) collective-permute-start(bf16[512,1024]{1,0:T(8,128)(2,1)} %get-tuple-element.176), channel_id=1, source_target_pairs={{0,2},{2,0},{4,6},{6,4},{1,3},{3,1},{5,7},{7,5},{8,10},{10,8},{12,... | collective-permute-start | bytes 3145736 | tf_op jit(solution)/shard_map/ppermute | solution.py:1054
  765.3 11.0 %collective-permute-start.49 = (bf16[512,1024]{1,0:T(8,128)(2,1)}, bf16[512,1024]{1,0:T(8,128)(2,1)S(1)}, u32[]{:S(2)}, u32[]{:S(2)}) collective-permute-start(bf16[512,1024]{1,0:T(8,128)(2,1)} %get-tuple-element.177), channel_id=1, source_target_pairs={{0,2},{2,0},{4,6},{6,4},{1,3},{3,1},{5,7},{7,5},{8,10},{10,8},{12,... | collective-permute-start | bytes 3145736 | tf_op jit(solution)/shard_map/ppermute | solution.py:1054
  765.8 10.5 %collective-permute-start.50 = (bf16[512,1024]{1,0:T(8,128)(2,1)}, bf16[512,1024]{1,0:T(8,128)(2,1)S(1)}, u32[]{:S(2)}, u32[]{:S(2)}) collective-permute-start(bf16[512,1024]{1,0:T(8,128)(2,1)} %get-tuple-element.178), channel_id=1, source_target_pairs={{0,2},{2,0},{4,6},{6,4},{1,3},{3,1},{5,7},{7,5},{8,10},{10,8},{12,... | collective-permute-start | bytes 3145736 | tf_op jit(solution)/shard_map/ppermute | solution.py:1054
  782.4 25.6 %collective-permute-start.51 = (bf16[512,1024]{1,0:T(8,128)(2,1)}, bf16[512,1024]{1,0:T(8,128)(2,1)S(1)}, u32[]{:S(2)}, u32[]{:S(2)}) collective-permute-start(bf16[512,1024]{1,0:T(8,128)(2,1)} %get-tuple-element.179.refs_4_), channel_id=1, source_target_pairs={{0,4},{2,6},{4,0},{6,2},{1,5},{3,7},{5,1},{7,3},{8,12},{10,14},{12... | collective-permute-start | bytes 3145736 | tf_op jit(solution)/shard_map/ppermute | solution.py:1054
  803.2 38.3 %collective-permute-start.54 = (bf16[512,1024]{1,0:T(8,128)(2,1)}, bf16[512,1024]{1,0:T(8,128)(2,1)}, u32[]{:S(2)}, u32[]{:S(2)}) collective-permute-start(bf16[512,1024]{1,0:T(8,128)(2,1)} %get-tuple-element.182), channel_id=1, source_target_pairs={{0,2},{2,0},{4,6},{6,4},{1,3},{3,1},{5,7},{7,5},{8,10},{10,8},{12,... | collective-permute-start | bytes 3145736 | tf_op jit(solution)/shard_map/ppermute | solution.py:1054
  806.3 35.2 %collective-permute-start.55 = (bf16[512,1024]{1,0:T(8,128)(2,1)}, bf16[512,1024]{1,0:T(8,128)(2,1)}, u32[]{:S(2)}, u32[]{:S(2)}) collective-permute-start(bf16[512,1024]{1,0:T(8,128)(2,1)} %get-tuple-element.183), channel_id=1, source_target_pairs={{0,4},{2,6},{4,0},{6,2},{1,5},{3,7},{5,1},{7,3},{8,12},{10,14},{12... | collective-permute-start | bytes 3145736 | tf_op jit(solution)/shard_map/ppermute | solution.py:1054
  813.6 27.9 %collective-permute-start.53 = (bf16[512,1024]{1,0:T(8,128)(2,1)}, bf16[512,1024]{1,0:T(8,128)(2,1)}, u32[]{:S(2)}, u32[]{:S(2)}) collective-permute-start(bf16[512,1024]{1,0:T(8,128)(2,1)} %add.205.refs_1_.refs_3_), channel_id=1, source_target_pairs={{0,1},{1,0},{2,3},{3,2},{4,5},{5,4},{6,7},{7,6},{8,9},{9,8},{10,11... | collective-permute-start | bytes 3145736 | tf_op jit(solution)/shard_map/ppermute | solution.py:1054
  819.7 13.0 %collective-permute-start.58 = (f32[16,576]{1,0:T(8,128)}, f32[16,576]{1,0:T(8,128)S(1)}, u32[]{:S(2)}, u32[]{:S(2)}) collective-permute-start(f32[16,576]{1,0:T(8,128)} %relay.6.refs_5_), channel_id=1, source_target_pairs={{0,24},{8,16},{16,8},{24,0},{1,25},{9,17},{17,9},{25,1},{2,26},{10... | collective-permute-start | bytes 110600 | tf_op jit(solution)/shard_map/ppermute | solution.py:1054
  830.4 9.6 %collective-permute-start.57 = (f32[16,576]{1,0:T(8,128)}, f32[16,576]{1,0:T(8,128)S(1)}, u32[]{:S(2)}, u32[]{:S(2)}) collective-permute-start(f32[16,576]{1,0:T(8,128)} %relay.6.refs_5_), channel_id=1, source_target_pairs={{0,16},{8,24},{16,0},{24,8},{1,17},{9,25},{17,1},{25,9},{2,18},{10... | collective-permute-start | bytes 110600 | tf_op jit(solution)/shard_map/ppermute | solution.py:1054
  832.7 8.2 collective-permute-start.56
  840.1 26.4 %collective-permute-start.65 = (bf16[128,4096]{1,0:T(8,128)(2,1)}, bf16[128,4096]{1,0:T(8,128)(2,1)}, u32[]{:S(2)}, u32[]{:S(2)}) collective-permute-start(bf16[128,4096]{1,0:T(8,128)(2,1)} %slice.147), channel_id=1, source_target_pairs={{0,4},{2,6},{4,0},{6,2},{1,5},{3,7},{5,1},{7,3},{8,12},{10,14},{12... | collective-permute-start | bytes 3145736 | tf_op jit(solution)/shard_map/ppermute | solution.py:1054
  845.5 35.6 %collective-permute-start.60 = (bf16[512,1024]{1,0:T(8,128)(2,1)}, bf16[512,1024]{1,0:T(8,128)(2,1)S(1)}, u32[]{:S(2)}, u32[]{:S(2)}) collective-permute-start(bf16[512,1024]{1,0:T(8,128)(2,1)} %add.206.refs_1_.refs_5_), channel_id=1, source_target_pairs={{0,1},{1,0},{2,3},{3,2},{4,5},{5,4},{6,7},{7,6},{8,9},{9,8},{10,11... | collective-permute-start | bytes 3145736 | tf_op jit(solution)/shard_map/ppermute | solution.py:1054
  846.7 26.0 %collective-permute-start.64 = (bf16[128,1024]{1,0:T(8,128)(2,1)S(1)}, bf16[128,1024]{1,0:T(8,128)(2,1)S(1)}, u32[]{:S(2)}, u32[]{:S(2)}) collective-permute-start(bf16[128,1024]{1,0:T(8,128)(2,1)S(1)} %slice.146), channel_id=1, source_target_pairs={{0,4},{2,6},{4,0},{6,2},{1,5},{3,7},{5,1},{7,3},{8,12},{10,14},{12... | collective-permute-start | bytes 786440 | tf_op jit(solution)/shard_map/ppermute | solution.py:1054
  850.8 26.8 %collective-permute-start.63 = (f32[16,576]{1,0:T(8,128)}, f32[16,576]{1,0:T(8,128)S(1)}, u32[]{:S(2)}, u32[]{:S(2)}) collective-permute-start(f32[16,576]{1,0:T(8,128)} %relay.7.refs_2_), channel_id=1, source_target_pairs={{0,6},{2,4},{4,2},{6,0},{1,7},{3,5},{5,3},{7,1},{8,14},{10,12},{12... | collective-permute-start | bytes 110600 | tf_op jit(solution)/shard_map/ppermute | solution.py:1054
  850.8 28.0 %collective-permute-start.62 = (f32[16,576]{1,0:T(8,128)}, f32[16,576]{1,0:T(8,128)S(1)}, u32[]{:S(2)}, u32[]{:S(2)}) collective-permute-start(f32[16,576]{1,0:T(8,128)} %relay.7.refs_2_), channel_id=1, source_target_pairs={{0,4},{2,6},{4,0},{6,2},{1,5},{3,7},{5,1},{7,3},{8,12},{10,14},{12... | collective-permute-start | bytes 110600 | tf_op jit(solution)/shard_map/ppermute | solution.py:1054
  866.5 12.3 %collective-permute-start.61 = (f32[16,576]{1,0:T(8,128)}, f32[16,576]{1,0:T(8,128)S(1)}, u32[]{:S(2)}, u32[]{:S(2)}) collective-permute-start(f32[16,576]{1,0:T(8,128)} %relay.7.refs_2_), channel_id=1, source_target_pairs={{0,2},{2,0},{4,6},{6,4},{1,3},{3,1},{5,7},{7,5},{8,10},{10,8},{12,... | collective-permute-start | bytes 110600 | tf_op jit(solution)/shard_map/ppermute | solution.py:1054
  876.6 12.7 %collective-permute-start.68 = (bf16[128,768]{1,0:T(8,128)(2,1)S(1)}, bf16[128,768]{1,0:T(8,128)(2,1)S(1)}, u32[]{:S(2)}, u32[]{:S(2)}) collective-permute-start(bf16[128,768]{1,0:T(8,128)(2,1)S(1)} %get-tuple-element.235), channel_id=1, source_target_pairs={{0,6},{2,4},{4,2},{6,0},{1,7},{3,5},{5,3},{7,1},{8,14},{10,12},{12... | collective-permute-start | bytes 589832 | tf_op jit(solution)/shard_map/ppermute | solution.py:1054
  877.6 11.8 %collective-permute-start.67 = (bf16[128,768]{1,0:T(8,128)(2,1)S(1)}, bf16[128,768]{1,0:T(8,128)(2,1)S(1)}, u32[]{:S(2)}, u32[]{:S(2)}) collective-permute-start(bf16[128,768]{1,0:T(8,128)(2,1)S(1)} %get-tuple-element.236), channel_id=1, source_target_pairs={{0,4},{2,6},{4,0},{6,2},{1,5},{3,7},{5,1},{7,3},{8,12},{10,14},{12... | collective-permute-start | bytes 589832 | tf_op jit(solution)/shard_map/ppermute | solution.py:1054
  878.8 10.6 %collective-permute-start.66 = (bf16[128,768]{1,0:T(8,128)(2,1)S(1)}, bf16[128,768]{1,0:T(8,128)(2,1)S(1)}, u32[]{:S(2)}, u32[]{:S(2)}) collective-permute-start(bf16[128,768]{1,0:T(8,128)(2,1)S(1)} %get-tuple-element.237), channel_id=1, source_target_pairs={{0,2},{2,0},{4,6},{6,4},{1,3},{3,1},{5,7},{7,5},{8,10},{10,8},{12,... | collective-permute-start | bytes 589832 | tf_op jit(solution)/shard_map/ppermute | solution.py:1054
  (75 other events, 466.4 us)
Sparse Core Ops, SparseCore 0:
  30.3 64.7 all-gather.5
  97.3 155.0 all-gather.7
  254.6 131.7 all-gather.3
  435.3 147.7 reduce-scatter.4
  650.7 46.9 reduce-scatter.8
  700.0 77.6 reduce-scatter.6
  802.0 69.1 reduce-scatter.10
